TPU v7x, 32 devices: a whole 2x2x4 slice. The times are simulated.
32 devices in a mesh: section: 4 (over z), dp: 8 (over y, x, core).
Axes of the slice: x: 2, y: 2, z: 4, core: 2. Of those that a mesh axis runs over, the one named last changes fastest.
Arguments:
- tokens: bfloat16 [2560, 3072], P('dp'), may hold values from -6 to 6
- cotangent: bfloat16 [2560, 3072], P('dp'), may hold values from -6 to 6
- live_counts: int32 [8, 4], P('dp'), may hold values from 1 to 80, 240 in all within a row
- weight: bfloat16 [4, 3072, 3072], P('section'), may hold values from -0.0546875 to 0.0546875
- inverse_in: float32 [4, 16, 192, 192], P('section', 'dp'), may hold values from -3 to 4, as said below
- inverse_out: float32 [4, 16, 192, 192], P('section'), may hold values from -3 to 4, as said below
Outputs:
- update: bfloat16 [4, 3072, 3072], P('section', 'dp')
- factor_in: float32 [4, 16, 192, 192], P('section', 'dp')
- factor_out: float32 [4, 16, 192, 192], P('section', 'dp')
Inputs may be any that keep to these rules, and one draw needn't show every extreme that they name: `live_counts`: on each data rank the live counts of the micro-batches sum to 240, and one of them is 80. `inverse_in`: each block is symmetric. `inverse_out`: each block is symmetric.
All inputs are finite; a program needn't handle non-finite values.
Results may differ from a plain program's by a relative error of at most 0.025.
Values may be sent and summed in bfloat16 or wider, within the bound.
No kernel may reach another device: no remote copies, remote signals or barrier semaphores. Data moves between devices by JAX's collectives and lax.ppermute only.
A program may use at most 192 MiB of HBM per device.

v0:
```python
import jax
import jax.numpy as jnp
from jax import lax
from jax.sharding import PartitionSpec as P

D = 3072
BLOCK = 192
MICRO = 4
ROWS = 80
TOK_DEV = 320
NBLK = 16


C_ZERO = 0.7978845608028654
C_ONE = 0.044715


def from_behind(x, axis, by):
    peers = lax.axis_size(axis)
    pairs = [(i, i + by) for i in range(peers) if 0 <= i + by < peers]
    return lax.ppermute(x, axis, pairs)


def activate(value):
    return 0.5 * value * (1.0 + jnp.tanh(C_ZERO * (value + C_ONE * value * value * value)))


def slope(value):
    hyper = jnp.tanh(C_ZERO * (value + C_ONE * value * value * value))
    return 0.5 * (1.0 + hyper) + 0.5 * value * (1.0 - hyper * hyper) * C_ZERO * (
        1.0 + 3.0 * C_ONE * value * value
    )


def block_gram(rows_data, total):
    blocks = rows_data.reshape(rows_data.shape[0], NBLK, BLOCK)
    return jnp.einsum("tkb,tkc->kbc", blocks, blocks, preferred_element_type=jnp.float32) / total


def shards(tokens, cotangent, live_counts, weight, inverse_in, inverse_out):
    section_count = lax.axis_size("section")
    section_here = lax.axis_index("section")
    rank_count = lax.axis_size("dp")
    matrix = weight[0]
    counts = live_counts[0]
    slots = jnp.arange(ROWS, dtype=jnp.int32)
    live = (slots[None, :] < counts[:, None]).astype(jnp.float32)[:, :, None]
    input_blocks = tokens.reshape(MICRO, ROWS, D)
    cot_blocks = cotangent.reshape(MICRO, ROWS, D)
    ticks = MICRO + section_count - 1
    total = jnp.float32(TOK_DEV * rank_count)

    def forward_tick(tick, carry):
        outgoing, stored_in, stored_pre = carry
        arrived = from_behind(outgoing, "section", 1)
        micro = tick - section_here
        valid = jnp.logical_and(micro >= 0, micro < MICRO)
        index = jnp.clip(micro, 0, MICRO - 1)
        first = lax.dynamic_index_in_dim(input_blocks, index, 0, keepdims=False)
        current = jnp.where(section_here == 0, first, arrived)
        pre = lax.cond(
            valid,
            lambda v: jnp.dot(v, matrix, preferred_element_type=jnp.float32),
            lambda v: jnp.zeros((ROWS, D), jnp.float32),
            current,
        )
        result = (current.astype(jnp.float32) + activate(pre)).astype(jnp.bfloat16)
        old_in = lax.dynamic_index_in_dim(stored_in, index, 0, keepdims=False)
        old_pre = lax.dynamic_index_in_dim(stored_pre, index, 0, keepdims=False)
        stored_in = lax.dynamic_update_index_in_dim(
            stored_in, jnp.where(valid, current, old_in), index, 0
        )
        stored_pre = lax.dynamic_update_index_in_dim(
            stored_pre, jnp.where(valid, pre, old_pre), index, 0
        )
        return (result, stored_in, stored_pre)

    start_fwd = (
        jnp.zeros((ROWS, D), jnp.bfloat16),
        jnp.zeros((MICRO, ROWS, D), jnp.bfloat16),
        jnp.zeros((MICRO, ROWS, D), jnp.float32),
    )
    unused, stored_in, stored_pre = lax.fori_loop(0, ticks, forward_tick, start_fwd)
    in_flat = stored_in.reshape(TOK_DEV, D)
    live_in = (stored_in * live.astype(jnp.bfloat16)).reshape(TOK_DEV, D)
    gram_in = block_gram(live_in, total)

    def backward_tick(tick, carry):
        outgoing, stored_scaled = carry
        arrived = from_behind(outgoing, "section", -1)
        micro = tick - (section_count - 1 - section_here)
        valid = jnp.logical_and(micro >= 0, micro < MICRO)
        index = jnp.clip(micro, 0, MICRO - 1)
        last = lax.dynamic_index_in_dim(cot_blocks, index, 0, keepdims=False)
        current = jnp.where(section_here == section_count - 1, last, arrived)
        pre = lax.dynamic_index_in_dim(stored_pre, index, 0, keepdims=False)
        mask = lax.dynamic_index_in_dim(live, index, 0, keepdims=False)
        scaled = (current.astype(jnp.float32) * slope(pre) * mask).astype(jnp.bfloat16)
        back = lax.cond(
            valid,
            lambda v: lax.dot_general(
                v, matrix, (((1,), (1,)), ((), ())), preferred_element_type=jnp.float32
            ),
            lambda v: jnp.zeros((ROWS, D), jnp.float32),
            scaled,
        )
        result = (current.astype(jnp.float32) + back).astype(jnp.bfloat16)
        old = lax.dynamic_index_in_dim(stored_scaled, index, 0, keepdims=False)
        stored_scaled = lax.dynamic_update_index_in_dim(
            stored_scaled, jnp.where(valid, scaled, old), index, 0
        )
        return (result, stored_scaled)

    start_bwd = (jnp.zeros((ROWS, D), jnp.bfloat16), jnp.zeros((MICRO, ROWS, D), jnp.bfloat16))
    unused_flow, stored_scaled = lax.fori_loop(0, ticks, backward_tick, start_bwd)
    scaled_flat = stored_scaled.reshape(TOK_DEV, D)
    gram_out = block_gram(scaled_flat, total)
    owned_in, owned_out = (
        lax.psum_scatter(
            gram_in.astype(jnp.bfloat16), "dp", scatter_dimension=0, tiled=True
        ).astype(jnp.float32),
        lax.psum_scatter(
            gram_out.astype(jnp.bfloat16), "dp", scatter_dimension=0, tiled=True
        ).astype(jnp.float32),
    )
    owned_rows = D // rank_count
    left = in_flat
    grad_rows = lax.psum_scatter(
        lax.dot_general(
            left, scaled_flat, (((0,), (0,)), ((), ())), preferred_element_type=jnp.float32
        ).astype(jnp.bfloat16),
        "dp",
        scatter_dimension=0,
        tiled=True,
    ).astype(jnp.float32)
    left = jnp.einsum(
        "kbc,kcd->kbd",
        inverse_in[0],
        grad_rows.reshape(owned_rows // BLOCK, BLOCK, D),
        precision=lax.Precision.HIGHEST,
    )
    right = jnp.einsum(
        "rkc,kce->rke",
        left.reshape(owned_rows, NBLK, BLOCK),
        inverse_out[0],
        precision=lax.Precision.HIGHEST,
    )
    update = (right.reshape(owned_rows, D) / jnp.sqrt(total)).astype(jnp.bfloat16)
    return (update[None], owned_in[None], owned_out[None])


def solution(mesh):
    in_specs = (
        P("dp", None),
        P("dp", None),
        P("dp", None),
        P("section", None, None),
        P("section", "dp", None, None),
        P("section", None, None, None),
    )
    out_specs = (
        P("section", "dp", None),
        P("section", "dp", None, None),
        P("section", "dp", None, None),
    )
    return jax.shard_map(shards, mesh=mesh, in_specs=in_specs, out_specs=out_specs, check_vma=False)
```

profile of v0, /device:TPU:9, one launch (start us, length us, event | category | flops | bytes accessed | tf_op | source)
XLA Modules:
  0.0 678.0 jit_solution(6323294147671043201)
XLA Ops:
  11.9 201.0 %while.37 = (s32[]{:T(128)}, bf16[80,3072]{1,0:T(8,128)(2,1)}, bf16[4,80,3072]{2,1,0:T(8,128)(2,1)}, f32[4,80,3072]{2,1,0:T(8,128)}, pred[]{:T(512)}, /*index=5*...) while((s32[]{:T(128)}, bf16[80,3072]{1,0:T(8,128)(2,1)}, ...), condition=%wide.region_3.4_spmd.clone, body=%wide.region_0.3_spmd.clone.sunk | while | flops 1513635840 | bytes 41485124 | solution.py:83
  43.4 13.2 %collective-permute-done = bf16[80,3072]{1,0:T(8,128)(2,1)} collective-permute-done((bf16[80,3072]{1,0:T(8,128)(2,1)}, bf16[80,3072]{1,0:T(8,128)(2,1)}, u32[]{:S(2)}, u32[]{:S(2)}) %collective-permute-start) | collective-permute-done | bytes 491552 | tf_op jit(solution)/shard_map/while/body/eval_jaxpr/ppermute | solution.py:21
  59.1 10.9 %conditional.6 = (f32[80,3072]{1,0:T(8,128)}) conditional(s32[]{:T(128)} %convert_element_type.157, () %tuple.100, (bf16[80,3072]{1,0:T(8,128)(2,1)}, bf16[3072,3072]{1,0:T(8,128)(2,1)}) %tuple.101), branch_computations={%region_1.1_spmd, %region_2.2_spmd} | conditional | flops 1509949440 | bytes 20348936 | solution.py:61
  59.1 10.9 %fusion.34 = f32[80,3072]{1,0:T(8,128)} fusion(bf16[80,3072]{1,0:T(8,128)(2,1)} %get-tuple-element.357, bf16[3072,3072]{1,0:T(8,128)(2,1)} %get-tuple-element.358), kind=kOutput, calls=%fused_computation.56 | convolution fusion | flops 1509949440 | bytes 20348928 | tf_op jit(solution)/shard_map/while/body/eval_jaxpr/cond/branch_1_fun/dot_general | solution.py:63
  90.8 10.9 %conditional.6 = (f32[80,3072]{1,0:T(8,128)}) conditional(s32[]{:T(128)} %convert_element_type.157, () %tuple.100, (bf16[80,3072]{1,0:T(8,128)(2,1)}, bf16[3072,3072]{1,0:T(8,128)(2,1)}) %tuple.101), branch_computations={%region_1.1_spmd, %region_2.2_spmd} | conditional | flops 1509949440 | bytes 20348936 | solution.py:61
  90.8 10.9 %fusion.34 = f32[80,3072]{1,0:T(8,128)} fusion(bf16[80,3072]{1,0:T(8,128)(2,1)} %get-tuple-element.357, bf16[3072,3072]{1,0:T(8,128)(2,1)} %get-tuple-element.358), kind=kOutput, calls=%fused_computation.56 | convolution fusion | flops 1509949440 | bytes 20348928 | tf_op jit(solution)/shard_map/while/body/eval_jaxpr/cond/branch_1_fun/dot_general | solution.py:63
  151.3 10.9 %conditional.6 = (f32[80,3072]{1,0:T(8,128)}) conditional(s32[]{:T(128)} %convert_element_type.157, () %tuple.100, (bf16[80,3072]{1,0:T(8,128)(2,1)}, bf16[3072,3072]{1,0:T(8,128)(2,1)}) %tuple.101), branch_computations={%region_1.1_spmd, %region_2.2_spmd} | conditional | flops 1509949440 | bytes 20348936 | solution.py:61
  151.3 10.9 %fusion.34 = f32[80,3072]{1,0:T(8,128)} fusion(bf16[80,3072]{1,0:T(8,128)(2,1)} %get-tuple-element.357, bf16[3072,3072]{1,0:T(8,128)(2,1)} %get-tuple-element.358), kind=kOutput, calls=%fused_computation.56 | convolution fusion | flops 1509949440 | bytes 20348928 | tf_op jit(solution)/shard_map/while/body/eval_jaxpr/cond/branch_1_fun/dot_general | solution.py:63
  186.7 12.9 %collective-permute-start = (bf16[80,3072]{1,0:T(8,128)(2,1)}, bf16[80,3072]{1,0:T(8,128)(2,1)}, u32[]{:S(2)}, u32[]{:S(2)}) collective-permute-start(bf16[80,3072]{1,0:T(8,128)(2,1)} %broadcast_select_fusion.4), channel_id=1, source_target_pairs={{0,8},{8,16},{16,24},{1,9},{9,17},{17,25},{2,10},{10,18},{18,26},{... | collective-permute-start | bytes 1474568 | tf_op jit(solution)/shard_map/while/body/eval_jaxpr/ppermute | solution.py:21
  230.3 208.8 %while.38 = (s32[]{:T(128)}, bf16[80,3072]{1,0:T(8,128)(2,1)}, bf16[4,80,3072]{2,1,0:T(8,128)(2,1)}, pred[]{:T(512)}, s32[]{:T(128)}, /*index=5*/bf16[4,80,3072]...) while((s32[]{:T(128)}, bf16[80,3072]{1,0:T(8,128)(2,1)}, ...), condition=%wide.region_7.8_spmd.clone, body=%wide.region_4.7_spmd.clone.sunk | while | flops 1516830720 | bytes 30181076 | solution.py:115
  253.0 15.6 %collective-permute-done.1 = bf16[80,3072]{1,0:T(8,128)(2,1)} collective-permute-done((bf16[80,3072]{1,0:T(8,128)(2,1)}, bf16[80,3072]{1,0:T(8,128)(2,1)}, u32[]{:S(2)}, u32[]{:S(2)}) %collective-permute-start.1) | collective-permute-done | bytes 491552 | tf_op jit(solution)/shard_map/while/body/eval_jaxpr/ppermute | solution.py:21
  280.2 29.3 %collective-permute-done.1 = bf16[80,3072]{1,0:T(8,128)(2,1)} collective-permute-done((bf16[80,3072]{1,0:T(8,128)(2,1)}, bf16[80,3072]{1,0:T(8,128)(2,1)}, u32[]{:S(2)}, u32[]{:S(2)}) %collective-permute-start.1) | collective-permute-done | bytes 491552 | tf_op jit(solution)/shard_map/while/body/eval_jaxpr/ppermute | solution.py:21
  312.8 13.3 %conditional.7 = (f32[80,3072]{1,0:T(8,128)}) conditional(s32[]{:T(128)} %convert_element_type.160, () %tuple.104, (bf16[80,3072]{1,0:T(8,128)(2,1)}, bf16[3072,3072]{1,0:T(8,128)(2,1)}) %tuple.105), branch_computations={%region_5.5_spmd, %region_6.6_spmd} | conditional | flops 1509949440 | bytes 20348936 | solution.py:99
  312.8 13.3 %fusion.35 = f32[80,3072]{1,0:T(8,128)} fusion(bf16[80,3072]{1,0:T(8,128)(2,1)} %get-tuple-element.368, bf16[3072,3072]{1,0:T(8,128)(2,1)} %get-tuple-element.369), kind=kOutput, calls=%fused_computation.57 | convolution fusion | flops 1509949440 | bytes 20348928 | tf_op jit(solution)/shard_map/while/body/eval_jaxpr/cond/branch_1_fun/dot_general | solution.py:101
  343.5 13.3 %conditional.7 = (f32[80,3072]{1,0:T(8,128)}) conditional(s32[]{:T(128)} %convert_element_type.160, () %tuple.104, (bf16[80,3072]{1,0:T(8,128)(2,1)}, bf16[3072,3072]{1,0:T(8,128)(2,1)}) %tuple.105), branch_computations={%region_5.5_spmd, %region_6.6_spmd} | conditional | flops 1509949440 | bytes 20348936 | solution.py:99
  343.5 13.3 %fusion.35 = f32[80,3072]{1,0:T(8,128)} fusion(bf16[80,3072]{1,0:T(8,128)(2,1)} %get-tuple-element.368, bf16[3072,3072]{1,0:T(8,128)(2,1)} %get-tuple-element.369), kind=kOutput, calls=%fused_computation.57 | convolution fusion | flops 1509949440 | bytes 20348928 | tf_op jit(solution)/shard_map/while/body/eval_jaxpr/cond/branch_1_fun/dot_general | solution.py:101
  374.2 13.3 %conditional.7 = (f32[80,3072]{1,0:T(8,128)}) conditional(s32[]{:T(128)} %convert_element_type.160, () %tuple.104, (bf16[80,3072]{1,0:T(8,128)(2,1)}, bf16[3072,3072]{1,0:T(8,128)(2,1)}) %tuple.105), branch_computations={%region_5.5_spmd, %region_6.6_spmd} | conditional | flops 1509949440 | bytes 20348936 | solution.py:99
  374.2 13.3 %fusion.35 = f32[80,3072]{1,0:T(8,128)} fusion(bf16[80,3072]{1,0:T(8,128)(2,1)} %get-tuple-element.368, bf16[3072,3072]{1,0:T(8,128)(2,1)} %get-tuple-element.369), kind=kOutput, calls=%fused_computation.57 | convolution fusion | flops 1509949440 | bytes 20348928 | tf_op jit(solution)/shard_map/while/body/eval_jaxpr/cond/branch_1_fun/dot_general | solution.py:101
  404.9 13.3 %conditional.7 = (f32[80,3072]{1,0:T(8,128)}) conditional(s32[]{:T(128)} %convert_element_type.160, () %tuple.104, (bf16[80,3072]{1,0:T(8,128)(2,1)}, bf16[3072,3072]{1,0:T(8,128)(2,1)}) %tuple.105), branch_computations={%region_5.5_spmd, %region_6.6_spmd} | conditional | flops 1509949440 | bytes 20348936 | solution.py:99
  404.9 13.3 %fusion.35 = f32[80,3072]{1,0:T(8,128)} fusion(bf16[80,3072]{1,0:T(8,128)(2,1)} %get-tuple-element.368, bf16[3072,3072]{1,0:T(8,128)(2,1)} %get-tuple-element.369), kind=kOutput, calls=%fused_computation.57 | convolution fusion | flops 1509949440 | bytes 20348928 | tf_op jit(solution)/shard_map/while/body/eval_jaxpr/cond/branch_1_fun/dot_general | solution.py:101
  451.6 16.0 %bitcast_convert_fusion = bf16[3072,3072]{1,0:T(8,128)(2,1)} fusion(bf16[4,80,3072]{2,1,0:T(8,128)(2,1)} %get-tuple-element.386, bf16[4,80,3072]{2,1,0:T(8,128)(2,1)} %get-tuple-element.388), kind=kOutput, calls=%fused_computation.37 | convolution fusion | flops 6049234944 | bytes 22806528 | tf_op jit(solution)/shard_map/dot_general | solution.py:129
  469.4 42.4 %reduce-scatter.8.cloned.1.call-done = bf16[2,192,192]{2,1,0:T(8,128)(2,1)} async-done(((bf16[16,192,192]{2,1,0:T(8,128)(2,1)}), bf16[2,192,192]{2,1,0:T(8,128)(2,1)}) %reduce-scatter.8.cloned.1.call-update) | async-done | bytes 147472 | tf_op jit(solution)/shard_map/reduce_scatter | solution.py:122
  513.6 128.0 %reduce-scatter.4.cloned.1.call-done = bf16[384,3072]{1,0:T(8,128)(2,1)} async-done(((bf16[3072,3072]{1,0:T(8,128)(2,1)}), bf16[384,3072]{1,0:T(8,128)(2,1)}) %reduce-scatter.4.cloned.1.call-update) | async-done | bytes 2359312 | tf_op jit(solution)/shard_map/reduce_scatter | solution.py:128
  655.1 12.2 %multiply_convert_fusion = bf16[16,384,192]{1,2,0:T(8,128)(2,1)} fusion(f32[1,16,192,192]{3,2,1,0:T(8,128)S(1)} %copy-done, f32[384,16,192]{2,1,0:T(8,128)} %reshape.101), kind=kOutput, calls=%fused_computation.40 | convolution fusion | flops 2720268288 | bytes 9437184 | tf_op jit(solution)/shard_map/rkc,kce->rke/dot_general | solution.py:142
  (173 shorter events, 325.4 us)
Async XLA Ops:
  7.2 647.9 %copy-start = (f32[1,16,192,192]{3,2,1,0:T(8,128)S(1)}, f32[1,16,192,192]{3,2,1,0:T(8,128)}, u32[]{:S(2)}) copy-start(f32[1,16,192,192]{3,2,1,0:T(8,128)} %param.19) | copy-start | bytes 7077892
  7.2 460.5 %reduce-scatter.6.cloned.1.call-start = ((), (), s32[]{:S(2)}) async-start(), calls=%async_computation.4 | async-start | bytes 1769472 | tf_op jit(solution)/shard_map/reduce_scatter | solution.py:119
  12.8 14.3 %collective-permute-start = (bf16[80,3072]{1,0:T(8,128)(2,1)}, bf16[80,3072]{1,0:T(8,128)(2,1)}, u32[]{:S(2)}, u32[]{:S(2)}) collective-permute-start(bf16[80,3072]{1,0:T(8,128)(2,1)} %broadcast_select_fusion.4), channel_id=1, source_target_pairs={{0,8},{8,16},{16,24},{1,9},{9,17},{17,25},{2,10},{10,18},{18,26},{... | collective-permute-start | bytes 1474568 | tf_op jit(solution)/shard_map/while/body/eval_jaxpr/ppermute | solution.py:21
  30.6 2.6 copy-start.2
  36.1 20.5 %collective-permute-start = (bf16[80,3072]{1,0:T(8,128)(2,1)}, bf16[80,3072]{1,0:T(8,128)(2,1)}, u32[]{:S(2)}, u32[]{:S(2)}) collective-permute-start(bf16[80,3072]{1,0:T(8,128)(2,1)} %broadcast_select_fusion.4), channel_id=1, source_target_pairs={{0,8},{8,16},{16,24},{1,9},{9,17},{17,25},{2,10},{10,18},{18,26},{... | collective-permute-start | bytes 1474568 | tf_op jit(solution)/shard_map/while/body/eval_jaxpr/ppermute | solution.py:21
  70.0 2.6 copy-start.2
  75.5 12.7 %collective-permute-start = (bf16[80,3072]{1,0:T(8,128)(2,1)}, bf16[80,3072]{1,0:T(8,128)(2,1)}, u32[]{:S(2)}, u32[]{:S(2)}) collective-permute-start(bf16[80,3072]{1,0:T(8,128)(2,1)} %broadcast_select_fusion.4), channel_id=1, source_target_pairs={{0,8},{8,16},{16,24},{1,9},{9,17},{17,25},{2,10},{10,18},{18,26},{... | collective-permute-start | bytes 1474568 | tf_op jit(solution)/shard_map/while/body/eval_jaxpr/ppermute | solution.py:21
  101.6 2.6 copy-start.2
  107.2 11.8 %collective-permute-start = (bf16[80,3072]{1,0:T(8,128)(2,1)}, bf16[80,3072]{1,0:T(8,128)(2,1)}, u32[]{:S(2)}, u32[]{:S(2)}) collective-permute-start(bf16[80,3072]{1,0:T(8,128)(2,1)} %broadcast_select_fusion.4), channel_id=1, source_target_pairs={{0,8},{8,16},{16,24},{1,9},{9,17},{17,25},{2,10},{10,18},{18,26},{... | collective-permute-start | bytes 1474568 | tf_op jit(solution)/shard_map/while/body/eval_jaxpr/ppermute | solution.py:21
  132.4 2.6 copy-start.2
  138.0 10.9 %collective-permute-start = (bf16[80,3072]{1,0:T(8,128)(2,1)}, bf16[80,3072]{1,0:T(8,128)(2,1)}, u32[]{:S(2)}, u32[]{:S(2)}) collective-permute-start(bf16[80,3072]{1,0:T(8,128)(2,1)} %broadcast_select_fusion.4), channel_id=1, source_target_pairs={{0,8},{8,16},{16,24},{1,9},{9,17},{17,25},{2,10},{10,18},{18,26},{... | collective-permute-start | bytes 1474568 | tf_op jit(solution)/shard_map/while/body/eval_jaxpr/ppermute | solution.py:21
  167.8 9.9 %collective-permute-start = (bf16[80,3072]{1,0:T(8,128)(2,1)}, bf16[80,3072]{1,0:T(8,128)(2,1)}, u32[]{:S(2)}, u32[]{:S(2)}) collective-permute-start(bf16[80,3072]{1,0:T(8,128)(2,1)} %broadcast_select_fusion.4), channel_id=1, source_target_pairs={{0,8},{8,16},{16,24},{1,9},{9,17},{17,25},{2,10},{10,18},{18,26},{... | collective-permute-start | bytes 1474568 | tf_op jit(solution)/shard_map/while/body/eval_jaxpr/ppermute | solution.py:21
  186.7 19.0 %collective-permute-start = (bf16[80,3072]{1,0:T(8,128)(2,1)}, bf16[80,3072]{1,0:T(8,128)(2,1)}, u32[]{:S(2)}, u32[]{:S(2)}) collective-permute-start(bf16[80,3072]{1,0:T(8,128)(2,1)} %broadcast_select_fusion.4), channel_id=1, source_target_pairs={{0,8},{8,16},{16,24},{1,9},{9,17},{17,25},{2,10},{10,18},{18,26},{... | collective-permute-start | bytes 1474568 | tf_op jit(solution)/shard_map/while/body/eval_jaxpr/ppermute | solution.py:21
  221.6 7.1 %copy-start.4 = (s32[1,4]{1,0:T(1,128)S(1)}, s32[1,4]{1,0:T(1,128)}, u32[]{:S(2)}) copy-start(s32[1,4]{1,0:T(1,128)} %param.16) | copy-start | bytes 52
  228.4 283.4 %reduce-scatter.8.cloned.1.call-start = ((), (), s32[]{:S(2)}) async-start(), calls=%async_computation.5 | async-start | bytes 1769472 | tf_op jit(solution)/shard_map/reduce_scatter | solution.py:122
  231.1 10.3 %collective-permute-start.1 = (bf16[80,3072]{1,0:T(8,128)(2,1)}, bf16[80,3072]{1,0:T(8,128)(2,1)}, u32[]{:S(2)}, u32[]{:S(2)}) collective-permute-start(bf16[80,3072]{1,0:T(8,128)(2,1)} %broadcast_select_fusion.5), channel_id=1, source_target_pairs={{8,0},{16,8},{24,16},{9,1},{17,9},{25,17},{10,2},{18,10},{26,18},{... | collective-permute-start | bytes 1474568 | tf_op jit(solution)/shard_map/while/body/eval_jaxpr/ppermute | solution.py:21
  250.0 18.6 %collective-permute-start.1 = (bf16[80,3072]{1,0:T(8,128)(2,1)}, bf16[80,3072]{1,0:T(8,128)(2,1)}, u32[]{:S(2)}, u32[]{:S(2)}) collective-permute-start(bf16[80,3072]{1,0:T(8,128)(2,1)} %broadcast_select_fusion.5), channel_id=1, source_target_pairs={{8,0},{16,8},{24,16},{9,1},{17,9},{25,17},{10,2},{18,10},{26,18},{... | collective-permute-start | bytes 1474568 | tf_op jit(solution)/shard_map/while/body/eval_jaxpr/ppermute | solution.py:21
  277.2 32.4 %collective-permute-start.1 = (bf16[80,3072]{1,0:T(8,128)(2,1)}, bf16[80,3072]{1,0:T(8,128)(2,1)}, u32[]{:S(2)}, u32[]{:S(2)}) collective-permute-start(bf16[80,3072]{1,0:T(8,128)(2,1)} %broadcast_select_fusion.5), channel_id=1, source_target_pairs={{8,0},{16,8},{24,16},{9,1},{17,9},{25,17},{10,2},{18,10},{26,18},{... | collective-permute-start | bytes 1474568 | tf_op jit(solution)/shard_map/while/body/eval_jaxpr/ppermute | solution.py:21
  330.4 9.9 %collective-permute-start.1 = (bf16[80,3072]{1,0:T(8,128)(2,1)}, bf16[80,3072]{1,0:T(8,128)(2,1)}, u32[]{:S(2)}, u32[]{:S(2)}) collective-permute-start(bf16[80,3072]{1,0:T(8,128)(2,1)} %broadcast_select_fusion.5), channel_id=1, source_target_pairs={{8,0},{16,8},{24,16},{9,1},{17,9},{25,17},{10,2},{18,10},{26,18},{... | collective-permute-start | bytes 1474568 | tf_op jit(solution)/shard_map/while/body/eval_jaxpr/ppermute | solution.py:21
  361.1 9.9 %collective-permute-start.1 = (bf16[80,3072]{1,0:T(8,128)(2,1)}, bf16[80,3072]{1,0:T(8,128)(2,1)}, u32[]{:S(2)}, u32[]{:S(2)}) collective-permute-start(bf16[80,3072]{1,0:T(8,128)(2,1)} %broadcast_select_fusion.5), channel_id=1, source_target_pairs={{8,0},{16,8},{24,16},{9,1},{17,9},{25,17},{10,2},{18,10},{26,18},{... | collective-permute-start | bytes 1474568 | tf_op jit(solution)/shard_map/while/body/eval_jaxpr/ppermute | solution.py:21
  391.8 9.9 %collective-permute-start.1 = (bf16[80,3072]{1,0:T(8,128)(2,1)}, bf16[80,3072]{1,0:T(8,128)(2,1)}, u32[]{:S(2)}, u32[]{:S(2)}) collective-permute-start(bf16[80,3072]{1,0:T(8,128)(2,1)} %broadcast_select_fusion.5), channel_id=1, source_target_pairs={{8,0},{16,8},{24,16},{9,1},{17,9},{25,17},{10,2},{18,10},{26,18},{... | collective-permute-start | bytes 1474568 | tf_op jit(solution)/shard_map/while/body/eval_jaxpr/ppermute | solution.py:21
  422.5 9.9 %collective-permute-start.1 = (bf16[80,3072]{1,0:T(8,128)(2,1)}, bf16[80,3072]{1,0:T(8,128)(2,1)}, u32[]{:S(2)}, u32[]{:S(2)}) collective-permute-start(bf16[80,3072]{1,0:T(8,128)(2,1)} %broadcast_select_fusion.5), channel_id=1, source_target_pairs={{8,0},{16,8},{24,16},{9,1},{17,9},{25,17},{10,2},{18,10},{26,18},{... | collective-permute-start | bytes 1474568 | tf_op jit(solution)/shard_map/while/body/eval_jaxpr/ppermute | solution.py:21
  451.4 190.2 %reduce-scatter.4.cloned.1.call-start = ((), (), s32[]{:S(2)}) async-start(), calls=%async_computation.3 | async-start | bytes 21233664 | tf_op jit(solution)/shard_map/reduce_scatter | solution.py:128
  467.6 174.0 %copy-start.3 = (f32[1,2,192,192]{3,2,1,0:T(8,128)S(1)}, f32[1,2,192,192]{3,2,1,0:T(8,128)}, u32[]{:S(2)}) copy-start(f32[1,2,192,192]{3,2,1,0:T(8,128)} %param.18) | copy-start | bytes 884740
  (10 other events, 26.4 us)
Sparse Core Ops, SparseCore 0:
  228.6 55.3 reduce-scatter.5
  451.5 60.3 reduce-scatter.7
  515.5 126.0 reduce-scatter.3
where the time goes:
time: 683 us; the launch traced here: 678 us
  waiting for transfers between devices  292 us (43%)
  matrix products  144 us (21%)
  other arithmetic  114 us (17%)
  local copies, waits for them, and re-layouts  70.5 us (10%)
  starting transfers between devices  42.5 us (6%)
  between operations  13.8 us (2%)
    reduce_scatter x1, waiting for transfers between devices, shards(): lax.psum_scatter(lax.dot_general(left, scaled_flat, (((0,), (0,)), ((), (...  128 us
    ppermute x14, waiting for transfers between devices, from_behind(): return lax.ppermute(x, axis, pairs)  122 us
    dot_general x4, matrix products, backward_tick(): lax.dot_general(v, matrix, (((1,), (1,)), ((), ())), preferred_element_ty...  53.2 us
    dot_general x4, matrix products, forward_tick(): jnp.dot(v, matrix, preferred_element_type=jnp.float32)  43.5 us
    reduce_scatter x1, waiting for transfers between devices, shards(): lax.psum_scatter(gram_out.astype(jnp.bfloat16), 'dp', scatter_dimension=0...  42.4 us
    ppermute x14, starting transfers between devices, from_behind(): return lax.ppermute(x, axis, pairs)  42 us
    while x14, other arithmetic  23.7 us
    dynamic_update_slice x7, other arithmetic, backward_tick(): lax.dynamic_update_index_in_dim(stored_scaled, jnp.where(valid, scaled, o...  23 us
  transfers between devices with their start and end apart: 17, of which 16 were waited for; matrix products, arithmetic and copies ran while one was open for 26% of the time, Pallas kernels for 0%

commit v1 on v0

v1 whole, which is shorter than its diff:
```python
import functools
import math

import jax
import jax.numpy as jnp
from jax import lax
from jax.experimental import pallas as pl
from jax.experimental.pallas import tpu as pltpu
from jax.sharding import PartitionSpec as P

D = 3072
BLOCK = 192
MICRO = 4
ROWS = 80
TOK_DEV = 320
LIVE = 240
NBLK = 16

PIECE = 48
PIECES = LIVE // PIECE
WIDE = 1024
PAIR = 2 * BLOCK

C_ZERO = 0.7978845608028654
C_ONE = 0.044715

BF = jnp.bfloat16
F32 = jnp.float32
VM = pl.BlockSpec(memory_space=pltpu.VMEM)
SM = pl.BlockSpec(memory_space=pltpu.SMEM)
HB = pl.BlockSpec(memory_space=pl.ANY)
MIB = 1 << 20


def resident(x):
    return pltpu.with_memory_space_constraint(x, pltpu.VMEM)


def cost(flops, moved):
    return pl.CostEstimate(flops=int(flops), bytes_accessed=int(moved), transcendentals=0)


def pack_kernel(sections, counts_ref, tokens_ref, cot_ref, tok_out, cot_out, *unset):
    here = lax.axis_index("section")

    def pack(source, target):
        row = lax.broadcasted_iota(jnp.int32, (LIVE, TOK_DEV), 0)
        column = lax.broadcasted_iota(jnp.int32, (LIVE, TOK_DEV), 1)
        origin = row
        edge = jnp.int32(0)
        for micro in range(MICRO):
            count = counts_ref[0, micro]
            edge = edge + count
            origin = origin + jnp.where(row >= edge, ROWS - count, 0)
        pick = (column == origin).astype(F32).astype(BF)
        for start in range(0, D, WIDE):
            part = jnp.dot(
                pick, source[:, start : start + WIDE], preferred_element_type=F32
            ).astype(BF)
            for piece in range(PIECES):
                target[piece, :, start : start + WIDE] = part[piece * PIECE : (piece + 1) * PIECE]

    @pl.when(here == 0)
    def _():
        pack(tokens_ref, tok_out)

    @pl.when(here == sections - 1)
    def _():
        pack(cot_ref, cot_out)


def pack(sections, ranks, counts, tokens, cotangent):
    shape = jax.ShapeDtypeStruct((PIECES, PIECE, D), BF)
    store = jax.ShapeDtypeStruct((ranks, LIVE, D // ranks), BF)
    slopes = jax.ShapeDtypeStruct((PIECES, PIECE, D), F32)
    kept = [jax.ShapeDtypeStruct((PIECE, D), BF)] * PIECES
    return pl.pallas_call(
        functools.partial(pack_kernel, sections),
        out_shape=(shape, shape, store, slopes, *kept),
        in_specs=[SM, VM, VM],
        out_specs=(VM, VM, *[HB] * (2 + PIECES)),
        compiler_params=pltpu.CompilerParams(vmem_limit_bytes=24 * MIB),
        cost_estimate=cost(2 * LIVE * TOK_DEV * D, 8e6),
    )(counts, tokens, cotangent)


def forward_kernel(tick, sections, ranks, *refs):
    if tick == 0:
        tok_ref, w_ref, _, _, next_ref, store_ref, slope_ref, held = refs
        from_ref = None
    else:
        from_ref, tok_ref, w_ref, _, _, next_ref, store_ref, slope_ref, held = refs
    here = lax.axis_index("section")
    piece = tick - here
    own = D // ranks

    @pl.when(jnp.logical_and(piece >= 0, piece < PIECES))
    def _():
        if tick < PIECES:

            @pl.when(here == 0)
            def _():
                held[...] = tok_ref[tick]

        if tick > 0:

            @pl.when(here > 0)
            def _():
                held[...] = from_ref[...]

        rows = pl.ds(pl.multiple_of(piece * PIECE, PIECE), PIECE)
        for rank in range(ranks):
            store_ref[rank, rows, :] = held[:, rank * own : (rank + 1) * own]

        @pl.loop(0, D // WIDE)
        def _(step):
            columns = pl.ds(pl.multiple_of(step * WIDE, WIDE), WIDE)
            pre = jnp.dot(held[...], w_ref[:, columns], preferred_element_type=F32)
            square = pre * pre
            hyper = jnp.tanh(C_ZERO * (pre + C_ONE * pre * square))
            half = 0.5 * (1.0 + hyper)
            next_ref[:, columns] = (held[:, columns].astype(F32) + pre * half).astype(BF)
            slope_ref[piece, :, columns] = half + 0.5 * pre * (1.0 - hyper * hyper) * C_ZERO * (
                1.0 + 3.0 * C_ONE * square
            )


def forward(tick, sections, ranks, arrived, tokens, matrix, store, slopes):
    first = [] if tick == 0 else [arrived]
    base = len(first)
    return pl.pallas_call(
        functools.partial(forward_kernel, tick, sections, ranks),
        out_shape=(
            jax.ShapeDtypeStruct((PIECE, D), BF),
            jax.ShapeDtypeStruct(store.shape, store.dtype),
            jax.ShapeDtypeStruct(slopes.shape, slopes.dtype),
        ),
        in_specs=[VM] * (base + 4),
        out_specs=(VM, VM, VM),
        scratch_shapes=[pltpu.VMEM((PIECE, D), BF)],
        input_output_aliases={base + 2: 1, base + 3: 2},
        compiler_params=pltpu.CompilerParams(vmem_limit_bytes=12 * MIB),
        cost_estimate=cost(2 * 256 * D * D, 0),
    )(*first, resident(tokens), resident(matrix), resident(store), resident(slopes))


def backward_kernel(tick, sections, span, *refs):
    keeps = len(span)
    lead = 4 if tick > sections - 1 else 3
    ins = refs[:lead]
    w_ref, slope_ref, cot_ref = ins[:3]
    from_ref = ins[3] if lead == 4 else None
    next_ref = refs[lead + keeps]
    outs = refs[lead + keeps + 1 : lead + 2 * keeps + 1]
    flow, scaled, sem = refs[lead + 2 * keeps + 1 :]
    here = lax.axis_index("section")
    piece = tick - 2 * (sections - 1) + here

    @pl.when(jnp.logical_and(piece >= 0, piece < PIECES))
    def _():
        if 0 <= tick - (sections - 1) < PIECES:

            @pl.when(here == sections - 1)
            def _():
                flow[...] = cot_ref[tick - (sections - 1)]

        if from_ref is not None:

            @pl.when(here < sections - 1)
            def _():
                flow[...] = from_ref[...]

        scaled[...] = (flow[...].astype(F32) * slope_ref[piece]).astype(BF)
        for out, index in zip(outs, span):

            @pl.when(piece == index)
            def _():
                pltpu.make_async_copy(scaled, out, sem).start()

        @pl.when(here > 0)
        def _():
            @pl.loop(0, D // WIDE)
            def _(step):
                part = pl.ds(pl.multiple_of(step * WIDE, WIDE), WIDE)
                back = lax.dot_general(
                    scaled[...], w_ref[part, :], (((1,), (1,)), ((), ())), preferred_element_type=F32
                )
                next_ref[:, part] = (flow[:, part].astype(F32) + back).astype(BF)

        for out, index in zip(outs, span):

            @pl.when(piece == index)
            def _():
                pltpu.make_async_copy(scaled, out, sem).wait()


def backward(tick, sections, arrived, matrix, slopes, cotangent, kept):
    low = max(0, tick - 2 * (sections - 1))
    high = min(PIECES - 1, tick - (sections - 1))
    span = list(range(low, high + 1))
    first = [] if arrived is None else [arrived]
    base = 3 + len(first)
    out = pl.pallas_call(
        functools.partial(backward_kernel, tick, sections, span),
        out_shape=(
            jax.ShapeDtypeStruct((PIECE, D), BF),
            *[jax.ShapeDtypeStruct((PIECE, D), BF) for _ in span],
        ),
        in_specs=[VM] * base + [HB] * len(span),
        out_specs=(VM, *[HB for _ in span]),
        scratch_shapes=[
            pltpu.VMEM((PIECE, D), BF),
            pltpu.VMEM((PIECE, D), BF),
            pltpu.SemaphoreType.DMA,
        ],
        input_output_aliases={base + k: 1 + k for k in range(len(span))},
        compiler_params=pltpu.CompilerParams(vmem_limit_bytes=12 * MIB),
        cost_estimate=cost(2 * 256 * D * D, 0),
    )(resident(matrix), resident(slopes), resident(cotangent), *first, *[kept[k] for k in span])
    kept = list(kept)
    for k, index in enumerate(span):
        kept[index] = out[1 + k]
    return out[0], kept


def prepare_kernel(ranks, total, x_ref, pin_ref, pout_ref, xt_ref, factor_ref, left_ref, right_ref):
    own = D // ranks
    width = ranks * PIECE
    for piece in range(PIECES):
        part = x_ref[:, piece * PIECE : (piece + 1) * PIECE, :].reshape(width, own)
        xt_ref[:, piece * width : (piece + 1) * width] = part.T
    for block in range(own // BLOCK):
        rows = xt_ref[block * BLOCK : (block + 1) * BLOCK, :]
        gram = lax.dot_general(rows, rows, (((1,), (1,)), ((), ())), preferred_element_type=F32)
        factor_ref[block] = gram * (1.0 / total)
        left_ref[block] = pin_ref[block].astype(BF)
    row = lax.broadcasted_iota(jnp.int32, (BLOCK, PAIR), 0)
    column = lax.broadcasted_iota(jnp.int32, (BLOCK, PAIR), 1)

    @pl.loop(0, NBLK // 2)
    def _(pair):
        for side in range(2):
            place = (column == row + side * BLOCK).astype(F32).astype(BF)
            wide = jnp.dot(pout_ref[2 * pair + side].astype(BF), place, preferred_element_type=F32)
            right_ref[pair, side * BLOCK : (side + 1) * BLOCK, :] = wide.astype(BF)


def prepare(ranks, total, gathered, inverse_in, inverse_out):
    own = D // ranks
    blocks = own // BLOCK
    return pl.pallas_call(
        functools.partial(prepare_kernel, ranks, total),
        out_shape=(
            jax.ShapeDtypeStruct((own, ranks * LIVE), BF),
            jax.ShapeDtypeStruct((blocks, BLOCK, BLOCK), F32),
            jax.ShapeDtypeStruct((blocks, BLOCK, BLOCK), BF),
            jax.ShapeDtypeStruct((NBLK // 2, PAIR, PAIR), BF),
        ),
        in_specs=[VM, VM, VM],
        out_specs=(VM, VM, VM, VM),
        compiler_params=pltpu.CompilerParams(vmem_limit_bytes=24 * MIB),
        cost_estimate=cost(2 * ranks * LIVE * own * BLOCK, 6e6),
    )(gathered, inverse_in, inverse_out)


def finish_kernel(ranks, total, *refs):
    parts = refs[:PIECES]
    xt_ref, left_ref, right_ref, update_ref, factor_ref, every, sems = refs[PIECES:]
    own = D // ranks
    width = ranks * PIECE
    copies = [
        pltpu.make_async_copy(parts[k], every.at[pl.ds(k * width, width), :], sems.at[k])
        for k in range(PIECES)
    ]
    for copy in copies:
        copy.start()
    for copy in copies:
        copy.wait()
    rank = lax.axis_index("dp")
    if own % 128 == 0:
        columns = pl.ds(pl.multiple_of(rank * own, 128), own)
        turned = every[:, columns].T
    else:
        columns = pl.ds(pl.multiple_of((rank // 2) * (2 * own), 128), 2 * own)
        both = every[:, columns].T
        turned = jnp.where(lax.rem(rank, 2) == 0, both[:own], both[own:])
    for block in range(own // BLOCK):
        rows = turned[block * BLOCK : (block + 1) * BLOCK]
        gram = lax.dot_general(rows, rows, (((1,), (1,)), ((), ())), preferred_element_type=F32)
        factor_ref[block] = gram * (1.0 / total)

    @pl.loop(0, D // (2 * PAIR))
    def _(step):
        columns = pl.ds(pl.multiple_of(step * 2 * PAIR, 2 * PAIR), 2 * PAIR)
        grad = jnp.dot(xt_ref[...], every[:, columns], preferred_element_type=F32).astype(BF)
        for block in range(own // BLOCK):
            rows = slice(block * BLOCK, (block + 1) * BLOCK)
            left = jnp.dot(left_ref[block], grad[rows], preferred_element_type=F32).astype(BF)
            for side in range(2):
                right = jnp.dot(
                    left[:, side * PAIR : (side + 1) * PAIR],
                    right_ref[2 * step + side],
                    preferred_element_type=F32,
                )
                place = pl.ds(pl.multiple_of((2 * step + side) * PAIR, PAIR), PAIR)
                update_ref[rows, place] = (right * (1.0 / math.sqrt(total))).astype(BF)


def finish(ranks, total, parts, turned, left, right):
    own = D // ranks
    blocks = own // BLOCK
    return pl.pallas_call(
        functools.partial(finish_kernel, ranks, total),
        out_shape=(
            jax.ShapeDtypeStruct((own, D), BF),
            jax.ShapeDtypeStruct((blocks, BLOCK, BLOCK), F32),
        ),
        in_specs=[HB] * PIECES + [VM] * 3,
        out_specs=(VM, VM),
        scratch_shapes=[
            pltpu.VMEM((ranks * LIVE, D), BF),
            pltpu.SemaphoreType.DMA((PIECES,)),
        ],
        compiler_params=pltpu.CompilerParams(vmem_limit_bytes=48 * MIB),
        cost_estimate=cost(2 * ranks * LIVE * own * D, 18e6),
    )(*parts, turned, left, right)


def shards(sections, ranks, tokens, cotangent, live_counts, weight, inverse_in, inverse_out):
    matrix = weight[0]
    total = float(TOK_DEV * ranks)
    packed_tokens, packed_cot, store, slopes, *kept = pack(
        sections, ranks, live_counts, tokens, cotangent
    )
    parts = []
    ahead, behind = None, None
    gathered = None
    for tick in range(PIECES + 2 * (sections - 1)):
        arrived_ahead = arrived_behind = None
        if 0 < tick < PIECES + sections - 1:
            pairs = [(s - 1, s) for s in range(1, sections) if 0 <= tick - s < PIECES]
            arrived_ahead = lax.ppermute(ahead, "section", pairs)
        if tick > sections - 1:
            pairs = [
                (s + 1, s)
                for s in range(sections - 1)
                if 0 <= tick - 2 * (sections - 1) + s < PIECES
            ]
            arrived_behind = lax.ppermute(behind, "section", pairs)
        if tick < PIECES + sections - 1:
            ahead, store, slopes = forward(
                tick, sections, ranks, arrived_ahead, packed_tokens, matrix, store, slopes
            )
        if tick == PIECES + sections - 2:
            gathered = lax.all_to_all(store, "dp", split_axis=0, concat_axis=0, tiled=True)
        if tick >= sections - 1:
            behind, kept = backward(
                tick, sections, arrived_behind, matrix, slopes, packed_cot, kept
            )
        done = tick - 2 * (sections - 1)
        if 0 <= done < PIECES:
            parts.append(lax.all_gather(kept[done], "dp", axis=0, tiled=True))
    turned, factor_in, left, right = prepare(ranks, total, gathered, inverse_in[0], inverse_out[0])
    update, factor_out = finish(ranks, total, parts, turned, left, right)
    return (update[None], factor_in[None], factor_out[None])


def solution(mesh):
    in_specs = (
        P("dp", None),
        P("dp", None),
        P("dp", None),
        P("section", None, None),
        P("section", "dp", None, None),
        P("section", None, None, None),
    )
    out_specs = (
        P("section", "dp", None),
        P("section", "dp", None, None),
        P("section", "dp", None, None),
    )
    body = functools.partial(shards, mesh.shape["section"], mesh.shape["dp"])
    return jax.shard_map(body, mesh=mesh, in_specs=in_specs, out_specs=out_specs, check_vma=False)
```

time: 683 us -> 317 us (0.46)
  waiting for transfers between devices: 292 us -> 110 us
  matrix products: 144 us -> 0 us
  other arithmetic: 114 us -> 0.01 us
  Pallas kernels: 0 us -> 74.2 us
  blocking collectives: 0 us -> 29.6 us
  starting transfers between devices: 42.5 us -> 28.9 us
  local copies, waits for them, and re-layouts: 70.5 us -> 58 us
    reduce_scatter x3 -> x0, waiting for transfers between devices: 170 us -> none  [the longest x1 128 us: shards(): lax.psum_scatter(lax.dot_general(left, scaled_flat, (((0,), (0,)), ((), (...]
    dot_general x13 -> x0, matrix products: 144 us -> none  [the longest x4 53.2 us: backward_tick(): lax.dot_general(v, matrix, (((1,), (1,)), ((), ())), preferred_element_ty...]
    pallas_call x0 -> x19, Pallas kernels: none -> 74.2 us  [the longest x8 31.4 us: backward(): pl.pallas_call(functools.partial(backward_kernel, tick, sections, span),...]
    ppermute x14, waiting for transfers between devices: 122 us -> 61.2 us  [the longest x7 33.9 us: shards(): arrived_ahead = lax.ppermute(ahead, 'section', pairs)]
    unnamed x7 -> x64, local copies, waits for them, and re-layouts: 4.28 us -> 58 us
    all_gather x0 -> x5, waiting for transfers between devices: none -> 48.8 us  [shards(): parts.append(lax.all_gather(kept[done], 'dp', axis=0, tiled=True))]
    dynamic_update_slice x21 -> x0, other arithmetic: 47.9 us -> none  [the longest x7 23 us: backward_tick(): lax.dynamic_update_index_in_dim(stored_scaled, jnp.where(valid, scaled, o...]
    convert_element_type x16 -> x0, other arithmetic: 36.2 us -> none  [the longest x7 18.5 us: forward_tick(): result = (current.astype(jnp.float32) + activate(pre)).astype(jnp.bfloat16)]
  transfers between devices with their start and end apart: 17 -> 19, of which waited for: 16 -> 11; matrix products, arithmetic and copies ran while one was open for 26% -> 0% of each run, Pallas kernels for 0% -> 12%
where the time goes in v1:
time: 317 us; the launch traced here: 315 us
  waiting for transfers between devices  110 us (35%)
  Pallas kernels  74.2 us (23%)
  local copies, waits for them, and re-layouts  58 us (18%)
  blocking collectives  29.6 us (9%)
  starting transfers between devices  28.9 us (9%)
  between operations  14.2 us (4%)
    unnamed x64, local copies, waits for them, and re-layouts  58 us
    all_gather x5, waiting for transfers between devices, shards(): parts.append(lax.all_gather(kept[done], 'dp', axis=0, tiled=True))  48.8 us
    ppermute x7, waiting for transfers between devices, shards(): arrived_ahead = lax.ppermute(ahead, 'section', pairs)  33.9 us
    pallas_call x8, Pallas kernels, backward(): pl.pallas_call(functools.partial(backward_kernel, tick, sections, span),...  31.4 us
    all_to_all x1, blocking collectives, shards(): lax.all_to_all(store, 'dp', split_axis=0, concat_axis=0, tiled=True)  29.6 us
    ppermute x7, waiting for transfers between devices, shards(): arrived_behind = lax.ppermute(behind, 'section', pairs)  27.3 us
    pallas_call x8, Pallas kernels, forward(): pl.pallas_call(functools.partial(forward_kernel, tick, sections, ranks),...  20.4 us
    pallas_call x1, Pallas kernels, finish(): pl.pallas_call(functools.partial(finish_kernel, ranks, total), out_shape=...  18.6 us
  transfers between devices with their start and end apart: 19, of which 11 were waited for; matrix products, arithmetic and copies ran while one was open for 0% of the time, Pallas kernels for 12%

profile of v1, /device:TPU:9, one launch (start us, length us, event | category | flops | bytes accessed | tf_op | source)
XLA Modules:
  0.0 315.0 jit_solution(845541367096022247)
XLA Ops:
  11.6 7.4 %copy-done = bf16[1,3072,3072]{2,1,0:T(8,128)(2,1)S(1)} copy-done((bf16[1,3072,3072]{2,1,0:T(8,128)(2,1)S(1)}, bf16[1,3072,3072]{2,1,0:T(8,128)(2,1)}, u32[]{:S(2)}) %copy-start) | copy-done | bytes 18874392
  20.3 11.5 %collective-permute-done.refs_0_ = bf16[48,3072]{1,0:T(8,128)(2,1)S(1)} collective-permute-done((bf16[48,3072]{1,0:T(8,128)(2,1)S(1)}, bf16[48,3072]{1,0:T(8,128)(2,1)S(1)}, u32[]{:S(2)}, u32[]{:S(2)}) %collective-permute-start) | collective-permute-done | bytes 294944 | tf_op jit(solution)/shard_map/ppermute | solution.py:342
  37.6 7.9 %collective-permute-done.1.refs_0_ = bf16[48,3072]{1,0:T(8,128)(2,1)S(1)} collective-permute-done((bf16[48,3072]{1,0:T(8,128)(2,1)S(1)}, bf16[48,3072]{1,0:T(8,128)(2,1)S(1)}, u32[]{:S(2)}, u32[]{:S(2)}) %collective-permute-start.1) | collective-permute-done | bytes 294944 | tf_op jit(solution)/shard_map/ppermute | solution.py:342
  45.5 3.9 %shard_map.88 = (bf16[48,3072]{1,0:T(8,128)(2,1)S(1)}, bf16[8,240,384]{2,1,0:T(8,128)(2,1)S(1)}, f32[5,48,3072]{2,1,0:T(8,128)S(1)}) custom-call(bf16[48,3072]{1,0:T(8,128)(2,1)S(1)} %collective-permute-done.1.refs_0_, bf16[5,48,3072]{2,1,0:T(8,128)(2,1)S(1)} %get-tuple-element.68.refs_0_.refs_1_, ...), custom_call_target="tpu_custom_call", output_to_operand_aliasing={{1}: (3, {}), {2}: (4, {})} | custom-call | flops 4831838208 | tf_op jit(solution)/shard_map/pallas_call | solution.py:131
  51.7 6.6 %collective-permute-done.2.refs_0_ = bf16[48,3072]{1,0:T(8,128)(2,1)S(1)} collective-permute-done((bf16[48,3072]{1,0:T(8,128)(2,1)S(1)}, bf16[48,3072]{1,0:T(8,128)(2,1)S(1)}, u32[]{:S(2)}, u32[]{:S(2)}) %collective-permute-start.2) | collective-permute-done | bytes 294944 | tf_op jit(solution)/shard_map/ppermute | solution.py:342
  65.6 4.6 %collective-permute-done.3.refs_0_ = bf16[48,3072]{1,0:T(8,128)(2,1)S(1)} collective-permute-done((bf16[48,3072]{1,0:T(8,128)(2,1)S(1)}, bf16[48,3072]{1,0:T(8,128)(2,1)S(1)}, u32[]{:S(2)}, u32[]{:S(2)}) %collective-permute-start.3) | collective-permute-done | bytes 294944 | tf_op jit(solution)/shard_map/ppermute | solution.py:342
  85.6 6.2 %collective-permute-start.5 = (bf16[48,3072]{1,0:T(8,128)(2,1)S(1)}, bf16[48,3072]{1,0:T(8,128)(2,1)S(1)}, u32[]{:S(2)}, u32[]{:S(2)}) collective-permute-start(bf16[48,3072]{1,0:T(8,128)(2,1)S(1)} %get-tuple-element.86), channel_id=1, source_target_pairs={{8,16},{16,24},{9,17},{17,25},{10,18},{18,26},{11,19},{19,27},{12,... | collective-permute-start | bytes 884744 | tf_op jit(solution)/shard_map/ppermute | solution.py:342
  91.9 6.3 %shard_map.95 = (bf16[48,3072]{1,0:T(8,128)(2,1)S(1)}, bf16[48,3072]{1,0:T(8,128)(2,1)}, bf16[48,3072]{1,0:T(8,128)(2,1)}, bf16[48,3072]{1,0:T(8,128)(2,1)}) custom-call(bf16[3072,3072]{1,0:T(8,128)(2,1)S(1)} %bitcast.16, f32[5,48,3072]{2,1,0:T(8,128)S(1)} %get-tuple-element.88.refs_4_.refs_1_, ...), custom_call_target="tpu_custom_call", output_to_operand_aliasing={{1}: (4, {}), {2}: (5, {}), {3}: (6, {})} | custom-call | flops 4831838208 | tf_op jit(solution)/shard_map/pallas_call | solution.py:203
  100.1 5.5 %collective-permute-done.8.refs_3_ = bf16[48,3072]{1,0:T(8,128)(2,1)S(1)} collective-permute-done((bf16[48,3072]{1,0:T(8,128)(2,1)S(1)}, bf16[48,3072]{1,0:T(8,128)(2,1)S(1)}, u32[]{:S(2)}, u32[]{:S(2)}) %collective-permute-start.8) | collective-permute-done | bytes 294944 | tf_op jit(solution)/shard_map/ppermute | solution.py:349
  105.6 6.1 %shard_map.96 = (bf16[48,3072]{1,0:T(8,128)(2,1)S(1)}, bf16[48,3072]{1,0:T(8,128)(2,1)}, bf16[48,3072]{1,0:T(8,128)(2,1)}, bf16[48,3072]{1,0:T(8,128)(2,1)}, bf16[48,3072]{1,0:T(8,128)(2,1)}) custom-call(bf16[3072,3072]{1,0:T(8,128)(2,1)S(1)} %bitcast.18, ...), custom_call_target="tpu_custom_call", output_to_operand_aliasing={{1}: (4, {}), {2}: (5, {}), {3}: (6, {}), {4}: (7, {})} | custom-call | flops 4831838208 | tf_op jit(solution)/shard_map/pallas_call | solution.py:203
  114.4 6.4 %copy-done.1 = bf16[1,3072,3072]{2,1,0:T(8,128)(2,1)S(1)} copy-done((bf16[1,3072,3072]{2,1,0:T(8,128)(2,1)S(1)}, bf16[1,3072,3072]{2,1,0:T(8,128)(2,1)}, u32[]{:S(2)}) %copy-start.1) | copy-done | bytes 18874392
  125.1 6.4 %copy-done.2 = bf16[1,3072,3072]{2,1,0:T(8,128)(2,1)S(1)} copy-done((bf16[1,3072,3072]{2,1,0:T(8,128)(2,1)S(1)}, bf16[1,3072,3072]{2,1,0:T(8,128)(2,1)}, u32[]{:S(2)}) %copy-start.2) | copy-done | bytes 18874392
  131.5 6.1 %shard_map.98 = (bf16[48,3072]{1,0:T(8,128)(2,1)S(1)}, bf16[48,3072]{1,0:T(8,128)(2,1)}, bf16[48,3072]{1,0:T(8,128)(2,1)}, bf16[48,3072]{1,0:T(8,128)(2,1)}, bf16[48,3072]{1,0:T(8,128)(2,1)}) custom-call(bf16[3072,3072]{1,0:T(8,128)(2,1)S(1)} %bitcast.20, ...), custom_call_target="tpu_custom_call", output_to_operand_aliasing={{1}: (4, {}), {2}: (5, {}), {3}: (6, {}), {4}: (7, {})} | custom-call | flops 4831838208 | tf_op jit(solution)/shard_map/pallas_call | solution.py:203
  139.6 8.6 %collective-permute-done.11.refs_3_ = bf16[48,3072]{1,0:T(8,128)(2,1)S(1)} collective-permute-done((bf16[48,3072]{1,0:T(8,128)(2,1)S(1)}, bf16[48,3072]{1,0:T(8,128)(2,1)S(1)}, u32[]{:S(2)}, u32[]{:S(2)}) %collective-permute-start.11) | collective-permute-done | bytes 294944 | tf_op jit(solution)/shard_map/ppermute | solution.py:349
  148.1 6.4 %copy-done.3 = bf16[1,3072,3072]{2,1,0:T(8,128)(2,1)S(1)} copy-done((bf16[1,3072,3072]{2,1,0:T(8,128)(2,1)S(1)}, bf16[1,3072,3072]{2,1,0:T(8,128)(2,1)}, u32[]{:S(2)}) %copy-start.3) | copy-done | bytes 18874392
  155.9 6.1 %shard_map.99 = (bf16[48,3072]{1,0:T(8,128)(2,1)S(1)}, bf16[48,3072]{1,0:T(8,128)(2,1)}, bf16[48,3072]{1,0:T(8,128)(2,1)}, bf16[48,3072]{1,0:T(8,128)(2,1)}) custom-call(bf16[3072,3072]{1,0:T(8,128)(2,1)S(1)} %bitcast.21, f32[5,48,3072]{2,1,0:T(8,128)S(1)} %get-tuple-element.107.refs_1_, ...), custom_call_target="tpu_custom_call", output_to_operand_aliasing={{1}: (4, {}), {2}: (5, {}), {3}: (6, {})} | custom-call | flops 4831838208 | tf_op jit(solution)/shard_map/pallas_call | solution.py:203
  164.0 9.6 %collective-permute-done.12.refs_3_ = bf16[48,3072]{1,0:T(8,128)(2,1)S(1)} collective-permute-done((bf16[48,3072]{1,0:T(8,128)(2,1)S(1)}, bf16[48,3072]{1,0:T(8,128)(2,1)S(1)}, u32[]{:S(2)}, u32[]{:S(2)}) %collective-permute-start.12) | collective-permute-done | bytes 294944 | tf_op jit(solution)/shard_map/ppermute | solution.py:349
  173.6 6.5 %copy-done.4 = bf16[1,3072,3072]{2,1,0:T(8,128)(2,1)S(1)} copy-done((bf16[1,3072,3072]{2,1,0:T(8,128)(2,1)S(1)}, bf16[1,3072,3072]{2,1,0:T(8,128)(2,1)}, u32[]{:S(2)}) %copy-start.4) | copy-done | bytes 18874392
  181.5 6.1 %shard_map.100 = (bf16[48,3072]{1,0:T(8,128)(2,1)S(1)}, bf16[48,3072]{1,0:T(8,128)(2,1)}, bf16[48,3072]{1,0:T(8,128)(2,1)}) custom-call(bf16[3072,3072]{1,0:T(8,128)(2,1)S(1)} %bitcast.22, f32[5,48,3072]{2,1,0:T(8,128)S(1)} %get-tuple-element.107.refs_1_, bf16[5,48,3072]{2,1,0:T(8,128)(2,1)S(1)} %copy-done.12, ...), custom_call_target="tpu_custom_call", output_to_operand_aliasing={{1}: (4, {}), {2}: (5, {})} | custom-call | flops 4831838208 | tf_op jit(solution)/shard_map/pallas_call | solution.py:203
  192.6 6.4 %copy-done.5 = bf16[1,3072,3072]{2,1,0:T(8,128)(2,1)S(1)} copy-done((bf16[1,3072,3072]{2,1,0:T(8,128)(2,1)S(1)}, bf16[1,3072,3072]{2,1,0:T(8,128)(2,1)}, u32[]{:S(2)}) %copy-start.5) | copy-done | bytes 18874392
  201.1 29.6 %all_to_all.5.x_ref = bf16[8,240,384]{2,1,0:T(8,128)(2,1)S(1)} all-to-all(bf16[8,240,384]{2,1,0:T(8,128)(2,1)} %copy-done.8), channel_id=1, replica_groups=mesh['section'=4,'dp'=8] {'dp'}, dimensions={0} | all-to-all | bytes 2949120 | tf_op jit(solution)/shard_map/all_to_all | solution.py:355
  237.1 18.0 %all-gather.12.cloned.1.call-done.refs_3_ = bf16[384,3072]{1,0:T(8,128)(2,1)} async-done(((bf16[48,3072]{1,0:T(8,128)(2,1)}), bf16[384,3072]{1,0:T(8,128)(2,1)}) %all-gather.12.cloned.1.call-update) | async-done | bytes 2359312 | tf_op jit(solution)/shard_map/all_gather | solution.py:362
  255.1 30.8 %all-gather.14.cloned.1.call-done.refs_4_ = bf16[384,3072]{1,0:T(8,128)(2,1)} async-done(((bf16[48,3072]{1,0:T(8,128)(2,1)}), bf16[384,3072]{1,0:T(8,128)(2,1)}) %all-gather.14.cloned.1.call-update) | async-done | bytes 2359312 | tf_op jit(solution)/shard_map/all_gather | solution.py:362
  289.8 18.6 %shard_map.103 = (bf16[384,3072]{1,0:T(8,128)(2,1)}, f32[2,192,192]{2,1,0:T(8,128)}) custom-call(bf16[384,3072]{1,0:T(8,128)(2,1)S(1)} %copy-done.21, bf16[384,3072]{1,0:T(8,128)(2,1)} %all-gather.8.cloned.1.call-done.refs_1_, bf16[384,3072]{1,0:T(8,128)(2,1)} %all-gather.10.cloned.1.call-done.refs_2_, ...), custom_call_target="tpu_custom_call" | custom-call | flops 4529848320 | bytes 18000000 | tf_op jit(solution)/shard_map/pallas_call | solution.py:312
  (104 shorter events, 69.3 us)
Async XLA Ops:
  7.2 229.9 %all-gather.6.cloned.1.call-start = ((), (), s32[]{:S(2)}) async-start(), calls=%async_computation.1 | async-start | bytes 2654208 | tf_op jit(solution)/shard_map/all_gather | solution.py:362
  11.5 88.6 %copy-start.14 = (bf16[5,48,3072]{2,1,0:T(8,128)(2,1)}, bf16[5,48,3072]{2,1,0:T(8,128)(2,1)S(1)}, u32[]{:S(2)}) copy-start(bf16[5,48,3072]{2,1,0:T(8,128)(2,1)S(1)} %get-tuple-element.68.refs_0_.refs_1_) | copy-start | bytes 4423684
  11.5 94.1 %copy-start.9 = (bf16[5,48,3072]{2,1,0:T(8,128)(2,1)}, bf16[5,48,3072]{2,1,0:T(8,128)(2,1)S(1)}, u32[]{:S(2)}) copy-start(bf16[5,48,3072]{2,1,0:T(8,128)(2,1)S(1)} %get-tuple-element.90.refs_2_) | copy-start | bytes 4423684
  19.0 12.8 %collective-permute-start = (bf16[48,3072]{1,0:T(8,128)(2,1)S(1)}, bf16[48,3072]{1,0:T(8,128)(2,1)S(1)}, u32[]{:S(2)}, u32[]{:S(2)}) collective-permute-start(bf16[48,3072]{1,0:T(8,128)(2,1)S(1)} %get-tuple-element.71), channel_id=1, source_target_pairs={{0,8},{1,9},{2,10},{3,11},{4,12},{5,13},{6,14},{7,15}} | collective-permute-start | bytes 884744 | tf_op jit(solution)/shard_map/ppermute | solution.py:342
  35.7 9.8 %collective-permute-start.1 = (bf16[48,3072]{1,0:T(8,128)(2,1)S(1)}, bf16[48,3072]{1,0:T(8,128)(2,1)S(1)}, u32[]{:S(2)}, u32[]{:S(2)}) collective-permute-start(bf16[48,3072]{1,0:T(8,128)(2,1)S(1)} %get-tuple-element.74), channel_id=1, source_target_pairs={{0,8},{8,16},{1,9},{9,17},{2,10},{10,18},{3,11},{11,19},{4,12},{12... | collective-permute-start | bytes 884744 | tf_op jit(solution)/shard_map/ppermute | solution.py:342
  45.5 19.4 %slice-start.2 = ((s8[18874368]{0:T(1024)(128)(4,1)}), s8[4194304]{0:T(1024)(128)(4,1)S(1)}, s32[]{:S(2)}) async-start(s8[18874368]{0:T(1024)(128)(4,1)} %bitcast.10), calls=%async_computation.8 | async-start | bytes 8388608
  49.5 8.9 %collective-permute-start.2 = (bf16[48,3072]{1,0:T(8,128)(2,1)S(1)}, bf16[48,3072]{1,0:T(8,128)(2,1)S(1)}, u32[]{:S(2)}, u32[]{:S(2)}) collective-permute-start(bf16[48,3072]{1,0:T(8,128)(2,1)S(1)} %get-tuple-element.77), channel_id=1, source_target_pairs={{0,8},{8,16},{16,24},{1,9},{9,17},{17,25},{2,10},{10,18},{18,26},{... | collective-permute-start | bytes 884744 | tf_op jit(solution)/shard_map/ppermute | solution.py:342
  62.3 8.0 %collective-permute-start.3 = (bf16[48,3072]{1,0:T(8,128)(2,1)S(1)}, bf16[48,3072]{1,0:T(8,128)(2,1)S(1)}, u32[]{:S(2)}, u32[]{:S(2)}) collective-permute-start(bf16[48,3072]{1,0:T(8,128)(2,1)S(1)} %get-tuple-element.80), channel_id=1, source_target_pairs={{0,8},{8,16},{16,24},{1,9},{9,17},{17,25},{2,10},{10,18},{18,26},{... | collective-permute-start | bytes 884744 | tf_op jit(solution)/shard_map/ppermute | solution.py:342
  65.0 12.1 %collective-permute-start.6 = (bf16[48,3072]{1,0:T(8,128)(2,1)S(1)}, bf16[48,3072]{1,0:T(8,128)(2,1)S(1)}, u32[]{:S(2)}, u32[]{:S(2)}) collective-permute-start(bf16[48,3072]{1,0:T(8,128)(2,1)S(1)} %get-tuple-element.92), channel_id=1, source_target_pairs={{24,16},{25,17},{26,18},{27,19},{28,20},{29,21},{30,22},{31,23}} | collective-permute-start | bytes 884744 | tf_op jit(solution)/shard_map/ppermute | solution.py:349
  74.2 7.5 %collective-permute-start.4 = (bf16[48,3072]{1,0:T(8,128)(2,1)S(1)}, bf16[48,3072]{1,0:T(8,128)(2,1)S(1)}, u32[]{:S(2)}, u32[]{:S(2)}) collective-permute-start(bf16[48,3072]{1,0:T(8,128)(2,1)S(1)} %get-tuple-element.83), channel_id=1, source_target_pairs={{0,8},{8,16},{16,24},{1,9},{9,17},{17,25},{2,10},{10,18},{18,26},{... | collective-permute-start | bytes 884744 | tf_op jit(solution)/shard_map/ppermute | solution.py:342
  77.1 14.7 %collective-permute-start.7 = (bf16[48,3072]{1,0:T(8,128)(2,1)S(1)}, bf16[48,3072]{1,0:T(8,128)(2,1)S(1)}, u32[]{:S(2)}, u32[]{:S(2)}) collective-permute-start(bf16[48,3072]{1,0:T(8,128)(2,1)S(1)} %get-tuple-element.95), channel_id=1, source_target_pairs={{16,8},{24,16},{17,9},{25,17},{18,10},{26,18},{19,11},{27,19},{20,... | collective-permute-start | bytes 884744 | tf_op jit(solution)/shard_map/ppermute | solution.py:349
  85.6 14.5 %collective-permute-start.5 = (bf16[48,3072]{1,0:T(8,128)(2,1)S(1)}, bf16[48,3072]{1,0:T(8,128)(2,1)S(1)}, u32[]{:S(2)}, u32[]{:S(2)}) collective-permute-start(bf16[48,3072]{1,0:T(8,128)(2,1)S(1)} %get-tuple-element.86), channel_id=1, source_target_pairs={{8,16},{16,24},{9,17},{17,25},{10,18},{18,26},{11,19},{19,27},{12,... | collective-permute-start | bytes 884744 | tf_op jit(solution)/shard_map/ppermute | solution.py:342
  98.2 7.5 %collective-permute-start.8 = (bf16[48,3072]{1,0:T(8,128)(2,1)S(1)}, bf16[48,3072]{1,0:T(8,128)(2,1)S(1)}, u32[]{:S(2)}, u32[]{:S(2)}) collective-permute-start(bf16[48,3072]{1,0:T(8,128)(2,1)S(1)} %get-tuple-element.99), channel_id=1, source_target_pairs={{8,0},{16,8},{24,16},{9,1},{17,9},{25,17},{10,2},{18,10},{26,18},{... | collective-permute-start | bytes 884744 | tf_op jit(solution)/shard_map/ppermute | solution.py:349
  111.8 125.3 %all-gather.8.cloned.1.call-start = ((), (), s32[]{:S(2)}) async-start(), calls=%async_computation.2 | async-start | bytes 2654208 | tf_op jit(solution)/shard_map/all_gather | solution.py:362
  111.8 2.6 collective-permute-start.9
  112.5 11.9 %collective-permute-start.10 = (bf16[48,3072]{1,0:T(8,128)(2,1)S(1)}, bf16[48,3072]{1,0:T(8,128)(2,1)S(1)}, u32[]{:S(2)}, u32[]{:S(2)}) collective-permute-start(bf16[48,3072]{1,0:T(8,128)(2,1)S(1)} %get-tuple-element.108), channel_id=1, source_target_pairs={{8,0},{16,8},{24,16},{9,1},{17,9},{25,17},{10,2},{18,10},{26,18},{... | collective-permute-start | bytes 884744 | tf_op jit(solution)/shard_map/ppermute | solution.py:349
  137.6 99.4 %all-gather.10.cloned.1.call-start = ((), (), s32[]{:S(2)}) async-start(), calls=%async_computation.3 | async-start | bytes 2654208 | tf_op jit(solution)/shard_map/all_gather | solution.py:362
  137.7 10.5 %collective-permute-start.11 = (bf16[48,3072]{1,0:T(8,128)(2,1)S(1)}, bf16[48,3072]{1,0:T(8,128)(2,1)S(1)}, u32[]{:S(2)}, u32[]{:S(2)}) collective-permute-start(bf16[48,3072]{1,0:T(8,128)(2,1)S(1)} %get-tuple-element.114), channel_id=1, source_target_pairs={{8,0},{16,8},{24,16},{9,1},{17,9},{25,17},{10,2},{18,10},{26,18},{... | collective-permute-start | bytes 884744 | tf_op jit(solution)/shard_map/ppermute | solution.py:349
  162.0 93.1 %all-gather.12.cloned.1.call-start = ((), (), s32[]{:S(2)}) async-start(), calls=%async_computation.4 | async-start | bytes 2654208 | tf_op jit(solution)/shard_map/all_gather | solution.py:362
  162.1 11.5 %collective-permute-start.12 = (bf16[48,3072]{1,0:T(8,128)(2,1)S(1)}, bf16[48,3072]{1,0:T(8,128)(2,1)S(1)}, u32[]{:S(2)}, u32[]{:S(2)}) collective-permute-start(bf16[48,3072]{1,0:T(8,128)(2,1)S(1)} %get-tuple-element.119), channel_id=1, source_target_pairs={{8,0},{16,8},{9,1},{17,9},{10,2},{18,10},{11,3},{19,11},{12,4},{20... | collective-permute-start | bytes 884744 | tf_op jit(solution)/shard_map/ppermute | solution.py:349
  187.6 98.3 %all-gather.14.cloned.1.call-start = ((), (), s32[]{:S(2)}) async-start(), calls=%async_computation.5 | async-start | bytes 2654208 | tf_op jit(solution)/shard_map/all_gather | solution.py:362
  187.6 4.9 %collective-permute-start.13 = (bf16[48,3072]{1,0:T(8,128)(2,1)S(1)}, bf16[48,3072]{1,0:T(8,128)(2,1)S(1)}, u32[]{:S(2)}, u32[]{:S(2)}) collective-permute-start(bf16[48,3072]{1,0:T(8,128)(2,1)S(1)} %get-tuple-element.123), channel_id=1, source_target_pairs={{8,0},{9,1},{10,2},{11,3},{12,4},{13,5},{14,6},{15,7}} | collective-permute-start | bytes 884744 | tf_op jit(solution)/shard_map/ppermute | solution.py:349
  200.3 30.3 %copy-start.19 = (f32[1,2,192,192]{3,2,1,0:T(8,128)S(1)}, f32[1,2,192,192]{3,2,1,0:T(8,128)}, u32[]{:S(2)}) copy-start(f32[1,2,192,192]{3,2,1,0:T(8,128)} %param.10) | copy-start | bytes 884740
  201.1 29.6 %copy-start.16 = (f32[1,16,192,192]{3,2,1,0:T(8,128)S(1)}, f32[1,16,192,192]{3,2,1,0:T(8,128)}, u32[]{:S(2)}) copy-start(f32[1,16,192,192]{3,2,1,0:T(8,128)} %param.11) | copy-start | bytes 7077892
  (27 other events, 135.3 us)
Sparse Core Ops, SparseCore 0:
  111.9 32.4 all-gather.5
  146.2 32.8 all-gather.7
  181.1 36.8 all-gather.9
  219.7 35.3 all-gather.11
  256.8 29.0 all-gather.13

commit v2 on v1

v2 whole, which is shorter than its diff:
```python
import functools
import math

import jax
import jax.numpy as jnp
from jax import lax
from jax.experimental import pallas as pl
from jax.experimental.pallas import tpu as pltpu
from jax.sharding import PartitionSpec as P

D = 3072
BLOCK = 192
MICRO = 4
ROWS = 80
TOK_DEV = 320
LIVE = 240
NBLK = 16

PIECE = 80
PIECES = LIVE // PIECE
WIDE = 1024
LOAD = 512
PAIR = 2 * BLOCK
SIDE = 256

C_ZERO = 0.7978845608028654
C_ONE = 0.044715

BF = jnp.bfloat16
F32 = jnp.float32
VM = pl.BlockSpec(memory_space=pltpu.VMEM)
SM = pl.BlockSpec(memory_space=pltpu.SMEM)
HB = pl.BlockSpec(memory_space=pl.ANY)
MIB = 1 << 20


def resident(x):
    return pltpu.with_memory_space_constraint(x, pltpu.VMEM)


def distant(x):
    return pltpu.with_memory_space_constraint(x, pltpu.HBM)


SMALL = pl.CostEstimate(flops=1000, bytes_accessed=1000, transcendentals=0)


def shape(*sizes, kind=BF):
    return jax.ShapeDtypeStruct(sizes, kind)


def near(*sizes, kind=BF):
    return pltpu.VMEM(sizes, kind)


def limit(size):
    return pltpu.CompilerParams(vmem_limit_bytes=size * MIB)


def swap(x, ranks, flip):
    return lax.ppermute(x, "dp", [(r, r ^ flip) for r in range(ranks)])


def contract_last(a, b):
    return lax.dot_general(a, b, (((1,), (1,)), ((), ())), preferred_element_type=F32)


def forward_columns(columns, held, w_ref, next_ref, slope_ref, piece):
    pre = jnp.dot(held[...], w_ref[:, columns], preferred_element_type=F32)
    square = pre * pre
    hyper = jnp.tanh(C_ZERO * (pre + C_ONE * pre * square))
    half = 0.5 * (1.0 + hyper)
    next_ref[:, columns] = (held[:, columns].astype(F32) + pre * half).astype(BF)
    slope_ref[piece, :, columns] = half + 0.5 * pre * (1.0 - hyper * hyper) * C_ZERO * (
        1.0 + 3.0 * C_ONE * square
    )


def keep_columns(piece, held, stores):
    chips = len(stores)
    width = D // chips
    chip = lax.div(lax.axis_index("dp"), 2)
    rows = pl.ds(pl.multiple_of(piece * PIECE, 16), PIECE)
    for offset, store in enumerate(stores):
        columns = pl.ds(pl.multiple_of((chip ^ offset) * width, 128), width)
        store[rows, :] = held[:, columns]


def begin_kernel(sections, chips, counts_ref, tokens_ref, cot_ref, weight_ref, *refs):
    w_ref, next_ref, tok_out, cot_out, slope_ref = refs[:5]
    stores = refs[5 : 5 + chips]
    held, raw, raw_sem, sems = refs[5 + chips + PIECES :]
    here = lax.axis_index("section")
    core = lax.rem(lax.axis_index("dp"), 2)
    loads = [
        pltpu.make_async_copy(
            weight_ref.at[:, pl.ds(k * LOAD, LOAD)], w_ref.at[:, pl.ds(k * LOAD, LOAD)], sems.at[k]
        )
        for k in range(D // LOAD)
    ]

    def pack(source, target):
        copy = pltpu.make_async_copy(source, raw, raw_sem)
        copy.start()
        for load in loads:
            load.start()
        row = lax.broadcasted_iota(jnp.int32, (LIVE, TOK_DEV), 0)
        column = lax.broadcasted_iota(jnp.int32, (LIVE, TOK_DEV), 1)
        origin = row
        edge = jnp.int32(0)
        for micro in range(MICRO):
            count = counts_ref[0, micro]
            edge = edge + count
            origin = origin + jnp.where(row >= edge, ROWS - count, 0)
        pick = (column == origin).astype(F32).astype(BF)
        copy.wait()
        for start in range(0, D, WIDE):
            part = jnp.dot(
                pick, raw[:, start : start + WIDE], preferred_element_type=F32
            ).astype(BF)
            for piece in range(PIECES):
                target[piece, :, start : start + WIDE] = part[piece * PIECE : (piece + 1) * PIECE]

    @pl.when(here == 0)
    def _():
        pack(tokens_ref, tok_out)
        held[...] = tok_out[0]
        keep_columns(0, held, stores)

    @pl.when(here == sections - 1)
    def _():
        if sections > 1:
            pack(cot_ref, cot_out)

    @pl.when(jnp.logical_and(here > 0, here < sections - 1))
    def _():
        for load in loads:
            load.start()

    lead = jnp.logical_and(here == 0, core == 0)
    for k, load in enumerate(loads):
        load.wait()

        @pl.when(lead)
        def _():
            forward_columns(pl.ds(k * LOAD, LOAD), held, w_ref, next_ref, slope_ref, 0)

    @pl.when(jnp.logical_and(here == 0, core != 0))
    def _():
        @pl.loop(0, D // WIDE)
        def _(step):
            columns = pl.ds(pl.multiple_of(step * WIDE, WIDE), WIDE)
            forward_columns(columns, held, w_ref, next_ref, slope_ref, 0)


def begin(sections, chips, counts, tokens, cotangent, matrix):
    packed = near(PIECES, PIECE, D)
    return pl.pallas_call(
        functools.partial(begin_kernel, sections, chips),
        out_shape=(
            near(D, D),
            near(PIECE, D),
            packed,
            packed,
            near(PIECES, PIECE, D, kind=F32),
            *[near(LIVE, D // chips)] * chips,
            *[near(PIECE, D)] * PIECES,
        ),
        in_specs=[SM, HB, HB, HB],
        out_specs=[VM] * (5 + chips) + [HB] * PIECES,
        scratch_shapes=[
            pltpu.VMEM((PIECE, D), BF),
            pltpu.VMEM((TOK_DEV, D), BF),
            pltpu.SemaphoreType.DMA,
            pltpu.SemaphoreType.DMA((D // LOAD,)),
        ],
        compiler_params=limit(6),
        cost_estimate=SMALL,
    )(counts, distant(tokens), distant(cotangent), distant(matrix))


def forward_kernel(tick, chips, from_ref, tok_ref, w_ref, *refs):
    next_ref, _, slope_ref = refs[1 + chips : 4 + chips]
    stores = refs[4 + chips : 4 + 2 * chips]
    (held,) = refs[4 + 2 * chips :]
    here = lax.axis_index("section")
    piece = tick - here

    @pl.when(jnp.logical_and(piece >= 0, piece < PIECES))
    def _():
        if tick < PIECES:

            @pl.when(here == 0)
            def _():
                held[...] = tok_ref[tick]

        @pl.when(here > 0)
        def _():
            held[...] = from_ref[...]

        @pl.loop(0, D // WIDE)
        def _(step):
            columns = pl.ds(pl.multiple_of(step * WIDE, WIDE), WIDE)
            forward_columns(columns, held, w_ref, next_ref, slope_ref, piece)

        keep_columns(piece, held, stores)


def forward(tick, arrived, tokens, matrix, slopes, stores):
    chips = len(stores)
    outs = pl.pallas_call(
        functools.partial(forward_kernel, tick, chips),
        out_shape=(
            near(PIECE, D),
            near(*matrix.shape),
            near(*slopes.shape, kind=F32),
            *[near(*s.shape) for s in stores],
        ),
        in_specs=[VM] * (4 + chips),
        out_specs=[VM] * (3 + chips),
        scratch_shapes=[pltpu.VMEM((PIECE, D), BF)],
        input_output_aliases={2 + k: 1 + k for k in range(2 + chips)},
        compiler_params=limit(6),
        cost_estimate=SMALL,
    )(
        resident(arrived),
        resident(tokens),
        resident(matrix),
        resident(slopes),
        *[resident(s) for s in stores],
    )
    return outs[0], outs[1], outs[2], list(outs[3:])


def backward_kernel(tick, sections, span, late, *refs):
    keeps = len(span)
    lead = 4 if tick > sections - 1 else 3
    w_ref, slope_ref, cot_ref = refs[:3]
    from_ref = refs[3] if lead == 4 else None
    outs = refs[lead + keeps + late :]
    next_ref, kept = outs[0], outs[2 : 2 + keeps]
    flow, scaled = outs[2 + keeps :]
    here = lax.axis_index("section")
    piece = tick - 2 * (sections - 1) + here

    @pl.when(jnp.logical_and(piece >= 0, piece < PIECES))
    def _():
        if 0 <= tick - (sections - 1) < PIECES:

            @pl.when(here == sections - 1)
            def _():
                flow[...] = cot_ref[tick - (sections - 1)]

        if from_ref is not None:

            @pl.when(here < sections - 1)
            def _():
                flow[...] = from_ref[...]

        scaled[...] = (flow[...].astype(F32) * slope_ref[piece]).astype(BF)
        for out, index in zip(kept, span):

            @pl.when(piece == index)
            def _():
                out[...] = scaled[...]

        @pl.when(here > 0)
        def _():
            @pl.loop(0, D // WIDE)
            def _(step):
                part = pl.ds(pl.multiple_of(step * WIDE, WIDE), WIDE)
                back = contract_last(scaled[...], w_ref[part, :])
                next_ref[:, part] = (flow[:, part].astype(F32) + back).astype(BF)


def backward(tick, sections, arrived, matrix, slopes, cotangent, kept, after):
    low = max(0, tick - 2 * (sections - 1))
    high = min(PIECES - 1, tick - (sections - 1))
    span = list(range(low, high + 1))
    first = [] if arrived is None else [resident(arrived)]
    base = 3 + len(first)
    out = pl.pallas_call(
        functools.partial(backward_kernel, tick, sections, span, len(after)),
        out_shape=(near(PIECE, D), near(D, D), *[near(PIECE, D) for _ in span]),
        in_specs=[VM] * (base + len(span)) + [HB] * len(after),
        out_specs=[VM] * (2 + len(span)),
        scratch_shapes=[pltpu.VMEM((PIECE, D), BF), pltpu.VMEM((PIECE, D), BF)],
        input_output_aliases={0: 1, **{base + k: 2 + k for k in range(len(span))}},
        compiler_params=limit(6),
        cost_estimate=SMALL,
    )(
        resident(matrix),
        resident(slopes),
        resident(cotangent),
        *first,
        *[resident(kept[k]) for k in span],
        *after,
    )
    kept = list(kept)
    for k, index in enumerate(span):
        kept[index] = out[2 + k]
    return out[0], out[1], kept


def prepare_kernel(chips, blocks, *refs):
    parts = refs[:chips]
    pin_ref, pout_ref, xt_ref, gram_ref, left_ref, right_ref = refs[chips:]
    for piece in range(PIECES):
        rows = slice(piece * PIECE, (piece + 1) * PIECE)
        both = jnp.concatenate([part[rows, :] for part in parts], axis=0)
        xt_ref[piece] = both.T
    for block in range(2 * blocks):
        rows = slice(block * BLOCK, (block + 1) * BLOCK)
        gram = jnp.zeros((BLOCK, BLOCK), F32)
        for piece in range(PIECES):
            some = xt_ref[piece, rows, :]
            gram = gram + contract_last(some, some)
        gram_ref[rows, :] = gram
    for block in range(blocks):
        left_ref[block] = pin_ref[block].astype(BF)
    row = lax.broadcasted_iota(jnp.int32, (BLOCK, PAIR), 0)
    column = lax.broadcasted_iota(jnp.int32, (BLOCK, PAIR), 1)

    @pl.loop(0, NBLK // 2)
    def _(pair):
        for side in range(2):
            place = (column == row + side * BLOCK).astype(F32).astype(BF)
            wide = jnp.dot(pout_ref[2 * pair + side].astype(BF), place, preferred_element_type=F32)
            right_ref[pair, side * BLOCK : (side + 1) * BLOCK, :] = wide.astype(BF)


def prepare(parts, inverse_in, inverse_out):
    chips = len(parts)
    width = D // chips
    blocks = inverse_in.shape[0]
    return pl.pallas_call(
        functools.partial(prepare_kernel, chips, blocks),
        out_shape=(
            near(PIECES, width, chips * PIECE),
            near(width, BLOCK, kind=F32),
            near(blocks, BLOCK, BLOCK),
            near(NBLK // 2, PAIR, PAIR),
        ),
        in_specs=[VM] * (chips + 2),
        out_specs=(VM, VM, VM, VM),
        compiler_params=limit(8),
        cost_estimate=SMALL,
    )(*[resident(p) for p in parts], inverse_in, inverse_out)


def add_gram(chips, every, gram_ref, begins):
    width = D // chips
    chip = lax.div(lax.axis_index("dp"), 2)
    columns = pl.ds(pl.multiple_of(chip * width, 128), width)
    turned = every[:, columns].T
    for block in range(width // BLOCK):
        rows = slice(block * BLOCK, (block + 1) * BLOCK)
        gram = contract_last(turned[rows], turned[rows])
        gram_ref[rows, :] = gram if begins else gram + gram_ref[rows, :]


def gather_kernel(chips, index, *refs):
    parts = refs[:chips]
    xt_ref = refs[chips]
    acc_ref, gram_ref, every = refs[-3:]
    for k, part in enumerate(parts):
        every[k * PIECE : (k + 1) * PIECE, :] = part[...]
    add_gram(chips, every, gram_ref, index == 0)

    @pl.loop(0, D // LOAD)
    def _(step):
        columns = pl.ds(pl.multiple_of(step * LOAD, LOAD), LOAD)
        term = jnp.dot(xt_ref[index], every[:, columns], preferred_element_type=F32)
        acc_ref[:, columns] = term if index == 0 else acc_ref[:, columns] + term


def gather(chips, index, parts, turned, so_far):
    width = D // chips
    return pl.pallas_call(
        functools.partial(gather_kernel, chips, index),
        out_shape=(near(width, D, kind=F32), near(width, BLOCK, kind=F32)),
        in_specs=[VM] * (chips + 1 + len(so_far)),
        out_specs=(VM, VM),
        scratch_shapes=[pltpu.VMEM((chips * PIECE, D), BF)],
        input_output_aliases={chips + 1 + k: k for k in range(len(so_far))},
        compiler_params=limit(8),
        cost_estimate=SMALL,
    )(*[resident(p) for p in parts], resident(turned), *[resident(a) for a in so_far])


def other_kernel(chips, *refs):
    parts = refs[:chips]
    xt_ref, acc_ref, gram_in_ref, gram_ref, _, _, out_ref, every = refs[chips:]
    own = D // chips // 2
    rows = pl.ds(pl.multiple_of((1 - lax.rem(lax.axis_index("dp"), 2)) * own, 16), own)
    for k, part in enumerate(parts):
        every[k * PIECE : (k + 1) * PIECE, :] = part[...]
    add_gram(chips, every, gram_ref, False)
    out_ref[:, D : D + BLOCK] = gram_ref[rows, :].astype(BF)
    out_ref[:, D + SIDE : D + SIDE + BLOCK] = gram_in_ref[rows, :].astype(BF)

    @pl.loop(0, D // LOAD)
    def _(step):
        columns = pl.ds(pl.multiple_of(step * LOAD, LOAD), LOAD)
        term = jnp.dot(xt_ref[PIECES - 1, rows, :], every[:, columns], preferred_element_type=F32)
        out_ref[:, columns] = (term + acc_ref[rows, columns]).astype(BF)


def other_half(chips, parts, turned, acc, gram_in, gram_out):
    width = D // chips
    return pl.pallas_call(
        functools.partial(other_kernel, chips),
        out_shape=(
            near(width, D, kind=F32),
            near(width, BLOCK, kind=F32),
            near(width // 2, D + 2 * SIDE),
        ),
        in_specs=[VM] * (chips + 4),
        out_specs=(VM, VM, VM),
        scratch_shapes=[pltpu.VMEM((chips * PIECE, D), BF)],
        input_output_aliases={chips + 1: 0, chips + 3: 1},
        compiler_params=limit(8),
        cost_estimate=SMALL,
    )(
        *[resident(p) for p in parts],
        resident(turned),
        resident(acc),
        resident(gram_in),
        resident(gram_out),
    )


def own_kernel(chips, *refs):
    parts = refs[:chips]
    xt_ref, acc_ref, out_ref, every = refs[chips:]
    own = D // chips // 2
    rows = pl.ds(pl.multiple_of(lax.rem(lax.axis_index("dp"), 2) * own, 16), own)
    for k, part in enumerate(parts):
        every[k * PIECE : (k + 1) * PIECE, :] = part[...]

    @pl.loop(0, D // LOAD)
    def _(step):
        columns = pl.ds(pl.multiple_of(step * LOAD, LOAD), LOAD)
        term = jnp.dot(xt_ref[PIECES - 1, rows, :], every[:, columns], preferred_element_type=F32)
        out_ref[:, columns] = term + acc_ref[rows, columns]


def own_half(chips, parts, turned, acc):
    width = D // chips
    return pl.pallas_call(
        functools.partial(own_kernel, chips),
        out_shape=near(width // 2, D, kind=F32),
        in_specs=[VM] * (chips + 2),
        out_specs=VM,
        scratch_shapes=[pltpu.VMEM((chips * PIECE, D), BF)],
        compiler_params=limit(8),
        cost_estimate=SMALL,
    )(*[resident(p) for p in parts], resident(turned), resident(acc))


def finish_kernel(blocks, total, own_ref, other_ref, left_ref, right_ref, *refs):
    gram_in_ref, gram_out_ref, update_ref, factor_in_ref, factor_out_ref, ready, sems = refs
    step_width = 2 * PAIR
    copies = []
    core = lax.rem(lax.axis_index("dp"), 2)
    for step in range(D // step_width):
        columns = slice(step * step_width, (step + 1) * step_width)
        grad = (own_ref[:, columns] + other_ref[:, columns].astype(F32)).astype(BF)
        for block in range(blocks):
            rows = slice(block * BLOCK, (block + 1) * BLOCK)
            left = jnp.dot(left_ref[block], grad[rows], preferred_element_type=F32).astype(BF)
            for side in range(2):
                right = jnp.dot(
                    left[:, side * PAIR : (side + 1) * PAIR],
                    right_ref[2 * step + side],
                    preferred_element_type=F32,
                )
                ready[step, rows, side * PAIR : (side + 1) * PAIR] = (
                    right * (1.0 / math.sqrt(total))
                ).astype(BF)
        copy = pltpu.make_async_copy(ready.at[step], update_ref.at[:, columns], sems.at[step])
        copy.start()
        copies.append(copy)
    for block in range(blocks):
        rows = slice(block * BLOCK, (block + 1) * BLOCK)
        start = pl.multiple_of((core * blocks + block) * BLOCK, BLOCK)
        mine = pl.ds(start, BLOCK)
        factor_out_ref[block] = (
            gram_out_ref[mine, :] + other_ref[rows, D : D + BLOCK].astype(F32)
        ) * (1.0 / total)
        factor_in_ref[block] = (
            gram_in_ref[mine, :] + other_ref[rows, D + SIDE : D + SIDE + BLOCK].astype(F32)
        ) * (1.0 / total)
    for copy in copies:
        copy.wait()


def finish(blocks, total, own, other, left, right, gram_in, gram_out):
    factor = shape(blocks, BLOCK, BLOCK, kind=F32)
    steps = D // (2 * PAIR)
    return pl.pallas_call(
        functools.partial(finish_kernel, blocks, total),
        out_shape=(shape(blocks * BLOCK, D), factor, factor),
        in_specs=[VM] * 6,
        out_specs=(HB, VM, VM),
        scratch_shapes=[
            pltpu.VMEM((steps, blocks * BLOCK, 2 * PAIR), BF),
            pltpu.SemaphoreType.DMA((steps,)),
        ],
        compiler_params=limit(8),
        cost_estimate=SMALL,
    )(
        resident(own),
        resident(other),
        resident(left),
        resident(right),
        resident(gram_in),
        resident(gram_out),
    )


def shards(sections, ranks, tokens, cotangent, live_counts, weight, inverse_in, inverse_out):
    total = float(TOK_DEV * ranks)
    chips = ranks // 2
    begun = begin(sections, chips, live_counts, tokens, cotangent, weight[0])
    matrix, ahead, packed_tokens, packed_cot, slopes = begun[:5]
    stores = list(begun[5 : 5 + chips])
    kept = list(begun[5 + chips :])
    behind = None
    parts = []
    last_turn = 2 * (sections - 1)
    crossed = None
    acc = []
    for tick in range(PIECES + last_turn):
        done = tick - last_turn
        arrived_ahead = arrived_behind = None
        if 0 < tick < PIECES + sections - 1:
            pairs = [(s - 1, s) for s in range(1, sections) if 0 <= tick - s < PIECES]
            arrived_ahead = lax.ppermute(ahead, "section", pairs)
            ahead, matrix, slopes, stores = forward(
                tick, arrived_ahead, packed_tokens, matrix, slopes, stores
            )
        if tick > sections - 1:
            pairs = [(s + 1, s) for s in range(sections - 1) if 0 <= tick - last_turn + s < PIECES]
            arrived_behind = lax.ppermute(behind, "section", pairs)
        if tick >= sections - 1:
            after = []
            if tick == PIECES + sections - 1:
                after = crossed[1:]
            if done >= 1:
                after = after + [parts[done - 1][1 << b] for b in range(chips.bit_length() - 1)]
            if done >= 2:
                acc = gather(chips, done - 2, parts[done - 2], rows_turned, acc)
                after = after + [acc[1]]
            behind, matrix, kept = backward(
                tick, sections, arrived_behind, matrix, slopes, packed_cot, kept, after
            )
        if tick == PIECES + sections - 2:
            crossed = [stores[0]] + [swap(stores[o], ranks, 2 * o) for o in range(1, chips)]
            rows_turned, gram_in, left, right = prepare(crossed, inverse_in[0], inverse_out[0])
        if 0 <= done < PIECES:
            piece = [kept[done]]
            for offset in range(1, chips):
                bit = offset & -offset if done % 2 else 1 << (offset.bit_length() - 1)
                piece.append(swap(piece[offset ^ bit], ranks, 2 * bit))
            parts.append(piece)
    acc = gather(chips, PIECES - 2, parts[PIECES - 2], rows_turned, acc)
    acc, gram_out, other = other_half(chips, parts[-1], rows_turned, acc[0], gram_in, acc[1])
    other = swap(other, ranks, 1)
    own = own_half(chips, parts[-1], rows_turned, acc)
    update, factor_in, factor_out = finish(
        inverse_in.shape[1], total, own, other, left, right, gram_in, gram_out
    )
    return (update[None], factor_in[None], factor_out[None])


def solution(mesh):
    in_specs = (
        P("dp", None),
        P("dp", None),
        P("dp", None),
        P("section", None, None),
        P("section", "dp", None, None),
        P("section", None, None, None),
    )
    out_specs = (
        P("section", "dp", None),
        P("section", "dp", None, None),
        P("section", "dp", None, None),
    )
    body = functools.partial(shards, mesh.shape["section"], mesh.shape["dp"])
    return jax.shard_map(body, mesh=mesh, in_specs=in_specs, out_specs=out_specs, check_vma=False)
```

time: 317 us -> 205 us (0.65)
  local copies, waits for them, and re-layouts: 58 us -> 0.66 us
  blocking collectives: 29.6 us -> 0 us
  Pallas kernels: 74.2 us -> 60.8 us
  between operations: 14.2 us -> 1.07 us
  starting transfers between devices: 28.9 us -> 40.3 us
  waiting for transfers between devices: 110 us -> 101 us
    unnamed x64 -> x6, local copies, waits for them, and re-layouts: 58 us -> 0.66 us
    all_gather x5 -> x0, waiting for transfers between devices: 48.8 us -> none  [shards(): parts.append(lax.all_gather(kept[done], 'dp', axis=0, tiled=True))]
    ppermute x0 -> x13, waiting for transfers between devices: none -> 32.6 us  [swap(): return lax.ppermute(x, 'dp', [(r, r ^ flip) for r in range(ranks)])]
    all_to_all x1 -> x0, blocking collectives: 29.6 us -> none  [shards(): lax.all_to_all(store, 'dp', split_axis=0, concat_axis=0, tiled=True)]
    ppermute x0 -> x13, starting transfers between devices: none -> 24.5 us  [swap(): return lax.ppermute(x, 'dp', [(r, r ^ flip) for r in range(ranks)])]
    pallas_call x19 -> x18, Pallas kernels: 74.2 us -> 60.8 us  [the longest x6 19.6 us: backward(): pl.pallas_call(functools.partial(backward_kernel, tick, sections, span, l...]
    ppermute x7 -> x5, waiting for transfers between devices: 33.9 us -> 45.2 us  [shards(): arrived_ahead = lax.ppermute(ahead, 'section', pairs)]
    ppermute x7 -> x5, starting transfers between devices: 17.8 us -> 8.69 us  [shards(): arrived_ahead = lax.ppermute(ahead, 'section', pairs)]
  transfers between devices with their start and end apart: 19 -> 23, of which waited for: 11 -> 15; matrix products, arithmetic and copies ran while one was open for 0% -> 0% of each run, Pallas kernels for 12% -> 10%
where the time goes in v2:
time: 205 us; the launch traced here: 204 us
  waiting for transfers between devices  101 us (49%)
  Pallas kernels  60.8 us (30%)
  starting transfers between devices  40.3 us (20%)
    ppermute x5, waiting for transfers between devices, shards(): arrived_ahead = lax.ppermute(ahead, 'section', pairs)  45.2 us
    ppermute x13, waiting for transfers between devices, swap(): return lax.ppermute(x, 'dp', [(r, r ^ flip) for r in range(ranks)])  32.6 us
    ppermute x13, starting transfers between devices, swap(): return lax.ppermute(x, 'dp', [(r, r ^ flip) for r in range(ranks)])  24.5 us
    ppermute x5, waiting for transfers between devices, shards(): arrived_behind = lax.ppermute(behind, 'section', pairs)  23.5 us
    pallas_call x6, Pallas kernels, backward(): pl.pallas_call(functools.partial(backward_kernel, tick, sections, span, l...  19.6 us
    pallas_call x5, Pallas kernels, forward(): pl.pallas_call(functools.partial(forward_kernel, tick, chips), out_shape=...  13.7 us
    ppermute x5, starting transfers between devices, shards(): arrived_ahead = lax.ppermute(ahead, 'section', pairs)  8.69 us
    pallas_call x2, Pallas kernels, gather(): pl.pallas_call(functools.partial(gather_kernel, chips, index), out_shape=...  8 us
  transfers between devices with their start and end apart: 23, of which 15 were waited for; matrix products, arithmetic and copies ran while one was open for 0% of the time, Pallas kernels for 10%

profile of v2, /device:TPU:9, one launch (start us, length us, event | category | flops | bytes accessed | tf_op | source)
XLA Modules:
  0.0 204.2 jit_solution(636211590171885606)
XLA Ops:
  1.3 7.1 %shard_map.85 = (bf16[3072,3072]{1,0:T(8,128)(2,1)S(1)}, bf16[80,3072]{1,0:T(8,128)(2,1)S(1)}, bf16[3,80,3072]{2,1,0:T(8,128)(2,1)S(1)}, bf16[3,80,3072]{2,1,0:T...) custom-call(s32[1,4]{1,0:T(1,128)S(1)} %copy-done.2, ...), custom_call_target="tpu_custom_call" | custom-call | flops 1000 | bytes 1000 | tf_op jit(solution)/shard_map/pallas_call | solution.py:158
  9.7 15.5 %collective-permute-done.from_ref = bf16[80,3072]{1,0:T(8,128)(2,1)S(1)} collective-permute-done((bf16[80,3072]{1,0:T(8,128)(2,1)S(1)}, bf16[80,3072]{1,0:T(8,128)(2,1)S(1)}, u32[]{:S(2)}, u32[]{:S(2)}) %collective-permute-start) | collective-permute-done | bytes 491552 | tf_op jit(solution)/shard_map/ppermute | solution.py:539
  25.2 4.3 %shard_map.86 = (bf16[80,3072]{1,0:T(8,128)(2,1)S(1)}, bf16[3072,3072]{1,0:T(8,128)(2,1)S(1)}, f32[3,80,3072]{2,1,0:T(8,128)S(1)}, bf16[240,768]{1,0:T(8,128)(2,...) custom-call(bf16[80,3072]{1,0:T(8,128)(2,1)S(1)} %collective-permute, ...), custom_call_target="tpu_custom_call", output_to_operand_aliasing={{1}: (2, {}), {2}: (3, {}), {3}: (4, {}), {4}: (5, {}), {5}... | custom-call | flops 1000 | bytes 1000 | tf_op jit(solution)/shard_map/pallas_call | solution.py:211
  31.4 11.8 %collective-permute-done.1.from_ref = bf16[80,3072]{1,0:T(8,128)(2,1)S(1)} collective-permute-done((bf16[80,3072]{1,0:T(8,128)(2,1)S(1)}, bf16[80,3072]{1,0:T(8,128)(2,1)S(1)}, u32[]{:S(2)}, u32[]{:S(2)}) %collective-permute-start.1) | collective-permute-done | bytes 491552 | tf_op jit(solution)/shard_map/ppermute | solution.py:539
  43.3 4.3 %shard_map.87 = (bf16[80,3072]{1,0:T(8,128)(2,1)S(1)}, bf16[3072,3072]{1,0:T(8,128)(2,1)S(1)}, f32[3,80,3072]{2,1,0:T(8,128)S(1)}, bf16[240,768]{1,0:T(8,128)(2,...) custom-call(bf16[80,3072]{1,0:T(8,128)(2,1)S(1)} %collective-permute, ...), custom_call_target="tpu_custom_call", output_to_operand_aliasing={{1}: (2, {}), {2}: (3, {}), {3}: (4, {}), {4}: (5, {}), {5}... | custom-call | flops 1000 | bytes 1000 | tf_op jit(solution)/shard_map/pallas_call | solution.py:211
  49.8 10.6 %collective-permute-done.2.from_ref = bf16[80,3072]{1,0:T(8,128)(2,1)S(1)} collective-permute-done((bf16[80,3072]{1,0:T(8,128)(2,1)S(1)}, bf16[80,3072]{1,0:T(8,128)(2,1)S(1)}, u32[]{:S(2)}, u32[]{:S(2)}) %collective-permute-start.2) | collective-permute-done | bytes 491552 | tf_op jit(solution)/shard_map/ppermute | solution.py:539
  60.4 4.3 %shard_map.88 = (bf16[80,3072]{1,0:T(8,128)(2,1)S(1)}, bf16[3072,3072]{1,0:T(8,128)(2,1)S(1)}, f32[3,80,3072]{2,1,0:T(8,128)S(1)}, bf16[240,768]{1,0:T(8,128)(2,...) custom-call(bf16[80,3072]{1,0:T(8,128)(2,1)S(1)} %collective-permute, ...), custom_call_target="tpu_custom_call", output_to_operand_aliasing={{1}: (2, {}), {2}: (3, {}), {3}: (4, {}), {4}: (5, {}), {5}... | custom-call | flops 1000 | bytes 1000 | tf_op jit(solution)/shard_map/pallas_call | solution.py:211
  68.0 7.3 %collective-permute-done.3.from_ref = bf16[80,3072]{1,0:T(8,128)(2,1)S(1)} collective-permute-done((bf16[80,3072]{1,0:T(8,128)(2,1)S(1)}, bf16[80,3072]{1,0:T(8,128)(2,1)S(1)}, u32[]{:S(2)}, u32[]{:S(2)}) %collective-permute-start.3) | collective-permute-done | bytes 491552 | tf_op jit(solution)/shard_map/ppermute | solution.py:539
  78.2 22.8 %collective-permute-done.6.refs_3_ = bf16[80,3072]{1,0:T(8,128)(2,1)S(1)} collective-permute-done((bf16[80,3072]{1,0:T(8,128)(2,1)S(1)}, bf16[80,3072]{1,0:T(8,128)(2,1)S(1)}, u32[]{:S(2)}, u32[]{:S(2)}) %collective-permute-start.6) | collective-permute-done | bytes 491552 | tf_op jit(solution)/shard_map/ppermute | solution.py:545
  101.0 6.3 %shard_map.93 = (bf16[80,3072]{1,0:T(8,128)(2,1)S(1)}, bf16[3072,3072]{1,0:T(8,128)(2,1)S(1)}, bf16[80,3072]{1,0:T(8,128)(2,1)S(1)}, bf16[80,3072]{1,0:T(8,128)(2,1)S(1)}, bf16[80,3072]{1,0:T(8,128)(2,1)S(1)}) custom-call(bf16[3072,3072]{1,0:T(8,128)(2,1)S(1)} %get-tuple-element.128.refs_0_, ...), custom_call_target="tpu_custom_call", output_to_operand_aliasing={{1}: (0, {}), {2}: (4, {}), {3}: (5, {}), {4}: (6, {})} | custom-call | flops 1000 | bytes 1000 | tf_op jit(solution)/shard_map/pallas_call | solution.py:282
  111.9 3.7 %collective-permute-done.8.refs_7_.refs_1_ = bf16[240,768]{1,0:T(8,128)(2,1)S(1)} collective-permute-done((bf16[240,768]{1,0:T(8,128)(2,1)S(1)}, bf16[240,768]{1,0:T(8,128)(2,1)S(1)}, u32[]{:S(2)}, u32[]{:S(2)}) %collective-permute-start.8) | collective-permute-done | bytes 368672 | tf_op jit(solution)/shard_map/ppermute | solution.py:61
  115.6 5.7 %collective-permute-done.9.refs_8_.refs_2_ = bf16[240,768]{1,0:T(8,128)(2,1)S(1)} collective-permute-done((bf16[240,768]{1,0:T(8,128)(2,1)S(1)}, bf16[240,768]{1,0:T(8,128)(2,1)S(1)}, u32[]{:S(2)}, u32[]{:S(2)}) %collective-permute-start.9) | collective-permute-done | bytes 368672 | tf_op jit(solution)/shard_map/ppermute | solution.py:61
  121.4 6.3 %shard_map.94 = (bf16[80,3072]{1,0:T(8,128)(2,1)S(1)}, bf16[3072,3072]{1,0:T(8,128)(2,1)S(1)}, bf16[80,3072]{1,0:T(8,128)(2,1)S(1)}, bf16[80,3072]{1,0:T(8,128)(2,1)S(1)}, bf16[80,3072]{1,0:T(8,128)(2,1)S(1)}) custom-call(bf16[3072,3072]{1,0:T(8,128)(2,1)S(1)} %get-tuple-element.134.refs_0_, ...), custom_call_target="tpu_custom_call", output_to_operand_aliasing={{1}: (0, {}), {2}: (4, {}), {3}: (5, {}), {4}: (6, {})} | custom-call | flops 1000 | bytes 1000 | tf_op jit(solution)/shard_map/pallas_call | solution.py:282
  135.4 2.8 %collective-permute-start.17 = (bf16[80,3072]{1,0:T(8,128)(2,1)S(1)}, bf16[80,3072]{1,0:T(8,128)(2,1)S(1)}, u32[]{:S(2)}, u32[]{:S(2)}) collective-permute-start(bf16[80,3072]{1,0:T(8,128)(2,1)S(1)} %collective-permute-done.12.refs_6_.refs_1_), channel_id=1, source_target_pairs={{0,4},{1,5},{2,6},{3,7},{4,0},{5,1},{6,2},{7,3},{8,12},{9,13},{10,... | collective-permute-start | bytes 1474568 | tf_op jit(solution)/shard_map/ppermute | solution.py:61
  139.3 6.3 %shard_map.95 = (bf16[80,3072]{1,0:T(8,128)(2,1)S(1)}, bf16[3072,3072]{1,0:T(8,128)(2,1)S(1)}, bf16[80,3072]{1,0:T(8,128)(2,1)S(1)}, bf16[80,3072]{1,0:T(8,128)(2,1)S(1)}) custom-call(bf16[3072,3072]{1,0:T(8,128)(2,1)S(1)} %get-tuple-element.142.refs_0_, ...), custom_call_target="tpu_custom_call", output_to_operand_aliasing={{1}: (0, {}), {2}: (4, {}), {3}: (5, {})} | custom-call | flops 1000 | bytes 1000 | tf_op jit(solution)/shard_map/pallas_call | solution.py:282
  149.7 2.9 %shard_map.96 = (bf16[3,768,320]{2,1,0:T(8,128)(2,1)S(1)}, f32[768,192]{1,0:T(8,128)S(1)}, bf16[2,192,192]{2,1,0:T(8,128)(2,1)S(1)}, bf16[8,384,384]{2,1,0:T(8,128)(2,1)S(1)}) custom-call(bf16[240,768]{1,0:T(8,128)(2,1)S(1)} %get-tuple-element.151.refs_0_, bf16[240,768]{1,0:T(8,128)(2,1)S(1)} %collective-permute-done.8.refs_7_.refs_1_, ...), custom_call_target="tpu_custom_call" | custom-call | flops 1000 | bytes 1000 | tf_op jit(solution)/shard_map/pallas_call | solution.py:336
  152.5 4.0 %shard_map.97 = (f32[768,3072]{1,0:T(8,128)S(1)}, f32[768,192]{1,0:T(8,128)S(1)}) custom-call(bf16[80,3072]{1,0:T(8,128)(2,1)S(1)} %get-tuple-element.146.refs_0_, bf16[80,3072]{1,0:T(8,128)(2,1)S(1)} %collective-permute-done.12.refs_6_.refs_1_, bf16[80,3072]{1,0:T(8,128)(2,1)S(1)} %collective-permute-done.13.refs_7_.refs_2_, ...), custom_call_target="tpu_custom_call" | custom-call | flops 1000 | bytes 1000 | tf_op jit(solution)/shard_map/pallas_call | solution.py:379
  156.5 3.7 %collective-permute-done.16.refs_6_.refs_2_ = bf16[80,3072]{1,0:T(8,128)(2,1)S(1)} collective-permute-done((bf16[80,3072]{1,0:T(8,128)(2,1)S(1)}, bf16[80,3072]{1,0:T(8,128)(2,1)S(1)}, u32[]{:S(2)}, u32[]{:S(2)}) %collective-permute-start.16) | collective-permute-done | bytes 491552 | tf_op jit(solution)/shard_map/ppermute | solution.py:61
  164.0 7.5 %collective-permute-done.18.refs_1_ = bf16[80,3072]{1,0:T(8,128)(2,1)S(1)} collective-permute-done((bf16[80,3072]{1,0:T(8,128)(2,1)S(1)}, bf16[80,3072]{1,0:T(8,128)(2,1)S(1)}, u32[]{:S(2)}, u32[]{:S(2)}) %collective-permute-start.18) | collective-permute-done | bytes 491552 | tf_op jit(solution)/shard_map/ppermute | solution.py:61
  172.9 6.4 %collective-permute-done.21.refs_3_ = bf16[80,3072]{1,0:T(8,128)(2,1)S(1)} collective-permute-done((bf16[80,3072]{1,0:T(8,128)(2,1)S(1)}, bf16[80,3072]{1,0:T(8,128)(2,1)S(1)}, u32[]{:S(2)}, u32[]{:S(2)}) %collective-permute-start.21) | collective-permute-done | bytes 491552 | tf_op jit(solution)/shard_map/ppermute | solution.py:61
  179.4 4.0 %shard_map.99 = (f32[768,3072]{1,0:T(8,128)S(1)}, f32[768,192]{1,0:T(8,128)S(1)}) custom-call(bf16[80,3072]{1,0:T(8,128)(2,1)S(1)} %get-tuple-element.150.refs_0_, bf16[80,3072]{1,0:T(8,128)(2,1)S(1)} %collective-permute-done.15.refs_5_.refs_1_, ...), custom_call_target="tpu_custom_call", output_to_operand_aliasing={{0}: (5, {}), {1}: (6, {})} | custom-call | flops 1000 | bytes 1000 | tf_op jit(solution)/shard_map/pallas_call | solution.py:379
  183.4 2.8 %shard_map.100 = (f32[768,3072]{1,0:T(8,128)S(1)}, f32[768,192]{1,0:T(8,128)S(1)}, bf16[384,3584]{1,0:T(8,128)(2,1)S(1)}) custom-call(bf16[80,3072]{1,0:T(8,128)(2,1)S(1)} %get-tuple-element.154.refs_0_, bf16[80,3072]{1,0:T(8,128)(2,1)S(1)} %collective-permute-done.18.refs_1_, ...), custom_call_target="tpu_custom_call", output_to_operand_aliasing={{0}: (5, {}), {1}: (7, {})} | custom-call | flops 1000 | bytes 1000 | tf_op jit(solution)/shard_map/pallas_call | solution.py:411
  186.3 8.6 %collective-permute-start.22 = (bf16[384,3584]{1,0:T(8,128)(2,1)S(1)}, bf16[384,3584]{1,0:T(8,128)(2,1)S(1)}, u32[]{:S(2)}, u32[]{:S(2)}) collective-permute-start(bf16[384,3584]{1,0:T(8,128)(2,1)S(1)} %get-tuple-element.160), channel_id=1, source_target_pairs={{0,1},{1,0},{2,3},{3,2},{4,5},{5,4},{6,7},{7,6},{8,9},{9,8},{10,11... | collective-permute-start | bytes 8257544 | tf_op jit(solution)/shard_map/ppermute | solution.py:61
  199.7 4.4 %shard_map.102 = (bf16[384,3072]{1,0:T(8,128)(2,1)}, f32[2,192,192]{2,1,0:T(8,128)}, f32[2,192,192]{2,1,0:T(8,128)}) custom-call(f32[384,3072]{1,0:T(8,128)S(1)} %shard_map.101.own_ref, bf16[384,3584]{1,0:T(8,128)(2,1)S(1)} %collective-permute-done.22.other_ref, bf16[2,192,192]{2,1,0:T(8,128)(2,1)S(1)} %get-tuple-element.161.left_ref, ...), custom_call_target="tpu_custom_call" | custom-call | flops 1000 | bytes 1000 | tf_op jit(solution)/shard_map/pallas_call | solution.py:501
  (46 shorter events, 39.6 us)
Async XLA Ops:
  8.4 16.8 %collective-permute-start = (bf16[80,3072]{1,0:T(8,128)(2,1)S(1)}, bf16[80,3072]{1,0:T(8,128)(2,1)S(1)}, u32[]{:S(2)}, u32[]{:S(2)}) collective-permute-start(bf16[80,3072]{1,0:T(8,128)(2,1)S(1)} %get-tuple-element.85), channel_id=1, source_target_pairs={{0,8},{1,9},{2,10},{3,11},{4,12},{5,13},{6,14},{7,15}} | collective-permute-start | bytes 1474568 | tf_op jit(solution)/shard_map/ppermute | solution.py:539
  29.5 13.7 %collective-permute-start.1 = (bf16[80,3072]{1,0:T(8,128)(2,1)S(1)}, bf16[80,3072]{1,0:T(8,128)(2,1)S(1)}, u32[]{:S(2)}, u32[]{:S(2)}) collective-permute-start(bf16[80,3072]{1,0:T(8,128)(2,1)S(1)} %get-tuple-element.93), channel_id=1, source_target_pairs={{0,8},{8,16},{1,9},{9,17},{2,10},{10,18},{3,11},{11,19},{4,12},{12... | collective-permute-start | bytes 1474568 | tf_op jit(solution)/shard_map/ppermute | solution.py:539
  47.6 12.8 %collective-permute-start.2 = (bf16[80,3072]{1,0:T(8,128)(2,1)S(1)}, bf16[80,3072]{1,0:T(8,128)(2,1)S(1)}, u32[]{:S(2)}, u32[]{:S(2)}) collective-permute-start(bf16[80,3072]{1,0:T(8,128)(2,1)S(1)} %get-tuple-element.100), channel_id=1, source_target_pairs={{0,8},{8,16},{16,24},{1,9},{9,17},{17,25},{2,10},{10,18},{18,26},{... | collective-permute-start | bytes 1474568 | tf_op jit(solution)/shard_map/ppermute | solution.py:539
  64.7 10.6 %collective-permute-start.3 = (bf16[80,3072]{1,0:T(8,128)(2,1)S(1)}, bf16[80,3072]{1,0:T(8,128)(2,1)S(1)}, u32[]{:S(2)}, u32[]{:S(2)}) collective-permute-start(bf16[80,3072]{1,0:T(8,128)(2,1)S(1)} %get-tuple-element.107), channel_id=1, source_target_pairs={{8,16},{16,24},{9,17},{17,25},{10,18},{18,26},{11,19},{19,27},{12,... | collective-permute-start | bytes 1474568 | tf_op jit(solution)/shard_map/ppermute | solution.py:539
  67.3 8.7 %collective-permute-start.5 = (bf16[80,3072]{1,0:T(8,128)(2,1)S(1)}, bf16[80,3072]{1,0:T(8,128)(2,1)S(1)}, u32[]{:S(2)}, u32[]{:S(2)}) collective-permute-start(bf16[80,3072]{1,0:T(8,128)(2,1)S(1)} %get-tuple-element.120), channel_id=1, source_target_pairs={{24,16},{25,17},{26,18},{27,19},{28,20},{29,21},{30,22},{31,23}} | collective-permute-start | bytes 1474568 | tf_op jit(solution)/shard_map/ppermute | solution.py:545
  75.3 2.0 collective-permute-start.4
  76.1 25.0 %collective-permute-start.6 = (bf16[80,3072]{1,0:T(8,128)(2,1)S(1)}, bf16[80,3072]{1,0:T(8,128)(2,1)S(1)}, u32[]{:S(2)}, u32[]{:S(2)}) collective-permute-start(bf16[80,3072]{1,0:T(8,128)(2,1)S(1)} %get-tuple-element.130), channel_id=1, source_target_pairs={{16,8},{24,16},{17,9},{25,17},{18,10},{26,18},{19,11},{27,19},{20,... | collective-permute-start | bytes 1474568 | tf_op jit(solution)/shard_map/ppermute | solution.py:545
  107.3 14.1 %collective-permute-start.7 = (bf16[80,3072]{1,0:T(8,128)(2,1)S(1)}, bf16[80,3072]{1,0:T(8,128)(2,1)S(1)}, u32[]{:S(2)}, u32[]{:S(2)}) collective-permute-start(bf16[80,3072]{1,0:T(8,128)(2,1)S(1)} %get-tuple-element.135), channel_id=1, source_target_pairs={{8,0},{16,8},{24,16},{9,1},{17,9},{25,17},{10,2},{18,10},{26,18},{... | collective-permute-start | bytes 1474568 | tf_op jit(solution)/shard_map/ppermute | solution.py:545
  109.2 6.4 %collective-permute-start.8 = (bf16[240,768]{1,0:T(8,128)(2,1)S(1)}, bf16[240,768]{1,0:T(8,128)(2,1)S(1)}, u32[]{:S(2)}, u32[]{:S(2)}) collective-permute-start(bf16[240,768]{1,0:T(8,128)(2,1)S(1)} %get-tuple-element.139), channel_id=1, source_target_pairs={{0,2},{1,3},{2,0},{3,1},{4,6},{5,7},{6,4},{7,5},{8,10},{9,11},{10,... | collective-permute-start | bytes 1105928 | tf_op jit(solution)/shard_map/ppermute | solution.py:61
  109.3 12.1 %collective-permute-start.9 = (bf16[240,768]{1,0:T(8,128)(2,1)S(1)}, bf16[240,768]{1,0:T(8,128)(2,1)S(1)}, u32[]{:S(2)}, u32[]{:S(2)}) collective-permute-start(bf16[240,768]{1,0:T(8,128)(2,1)S(1)} %get-tuple-element.140), channel_id=1, source_target_pairs={{0,4},{1,5},{2,6},{3,7},{4,0},{5,1},{6,2},{7,3},{8,12},{9,13},{10,... | collective-permute-start | bytes 1105928 | tf_op jit(solution)/shard_map/ppermute | solution.py:61
  109.4 12.0 %collective-permute-start.10 = (bf16[240,768]{1,0:T(8,128)(2,1)S(1)}, bf16[240,768]{1,0:T(8,128)(2,1)S(1)}, u32[]{:S(2)}, u32[]{:S(2)}) collective-permute-start(bf16[240,768]{1,0:T(8,128)(2,1)S(1)} %get-tuple-element.141), channel_id=1, source_target_pairs={{0,6},{1,7},{2,4},{3,5},{4,2},{5,3},{6,0},{7,1},{8,14},{9,15},{10,... | collective-permute-start | bytes 1105928 | tf_op jit(solution)/shard_map/ppermute | solution.py:61
  127.7 7.7 %collective-permute-start.12 = (bf16[80,3072]{1,0:T(8,128)(2,1)S(1)}, bf16[80,3072]{1,0:T(8,128)(2,1)S(1)}, u32[]{:S(2)}, u32[]{:S(2)}) collective-permute-start(bf16[80,3072]{1,0:T(8,128)(2,1)S(1)} %get-tuple-element.146.refs_0_), channel_id=1, source_target_pairs={{0,2},{1,3},{2,0},{3,1},{4,6},{5,7},{6,4},{7,5},{8,10},{9,11},{10,... | collective-permute-start | bytes 1474568 | tf_op jit(solution)/shard_map/ppermute | solution.py:61
  129.0 9.9 %collective-permute-start.11 = (bf16[80,3072]{1,0:T(8,128)(2,1)S(1)}, bf16[80,3072]{1,0:T(8,128)(2,1)S(1)}, u32[]{:S(2)}, u32[]{:S(2)}) collective-permute-start(bf16[80,3072]{1,0:T(8,128)(2,1)S(1)} %get-tuple-element.143), channel_id=1, source_target_pairs={{8,0},{16,8},{9,1},{17,9},{10,2},{18,10},{11,3},{19,11},{12,4},{20... | collective-permute-start | bytes 1474568 | tf_op jit(solution)/shard_map/ppermute | solution.py:545
  130.9 8.4 %collective-permute-start.13 = (bf16[80,3072]{1,0:T(8,128)(2,1)S(1)}, bf16[80,3072]{1,0:T(8,128)(2,1)S(1)}, u32[]{:S(2)}, u32[]{:S(2)}) collective-permute-start(bf16[80,3072]{1,0:T(8,128)(2,1)S(1)} %get-tuple-element.146.refs_0_), channel_id=1, source_target_pairs={{0,4},{1,5},{2,6},{3,7},{4,0},{5,1},{6,2},{7,3},{8,12},{9,13},{10,... | collective-permute-start | bytes 1474568 | tf_op jit(solution)/shard_map/ppermute | solution.py:61
  135.4 17.1 %collective-permute-start.17 = (bf16[80,3072]{1,0:T(8,128)(2,1)S(1)}, bf16[80,3072]{1,0:T(8,128)(2,1)S(1)}, u32[]{:S(2)}, u32[]{:S(2)}) collective-permute-start(bf16[80,3072]{1,0:T(8,128)(2,1)S(1)} %collective-permute-done.12.refs_6_.refs_1_), channel_id=1, source_target_pairs={{0,4},{1,5},{2,6},{3,7},{4,0},{5,1},{6,2},{7,3},{8,12},{9,13},{10,... | collective-permute-start | bytes 1474568 | tf_op jit(solution)/shard_map/ppermute | solution.py:61
  139.3 10.3 %copy-start.1 = (f32[1,2,192,192]{3,2,1,0:T(8,128)S(1)}, f32[1,2,192,192]{3,2,1,0:T(8,128)}, u32[]{:S(2)}) copy-start(f32[1,2,192,192]{3,2,1,0:T(8,128)} %param.10) | copy-start | bytes 884740
  145.6 10.9 %collective-permute-start.14 = (bf16[80,3072]{1,0:T(8,128)(2,1)S(1)}, bf16[80,3072]{1,0:T(8,128)(2,1)S(1)}, u32[]{:S(2)}, u32[]{:S(2)}) collective-permute-start(bf16[80,3072]{1,0:T(8,128)(2,1)S(1)} %get-tuple-element.148), channel_id=1, source_target_pairs={{8,0},{9,1},{10,2},{11,3},{12,4},{13,5},{14,6},{15,7}} | collective-permute-start | bytes 1474568 | tf_op jit(solution)/shard_map/ppermute | solution.py:545
  146.9 9.6 %collective-permute-start.15 = (bf16[80,3072]{1,0:T(8,128)(2,1)S(1)}, bf16[80,3072]{1,0:T(8,128)(2,1)S(1)}, u32[]{:S(2)}, u32[]{:S(2)}) collective-permute-start(bf16[80,3072]{1,0:T(8,128)(2,1)S(1)} %get-tuple-element.150.refs_0_), channel_id=1, source_target_pairs={{0,2},{1,3},{2,0},{3,1},{4,6},{5,7},{6,4},{7,5},{8,10},{9,11},{10,... | collective-permute-start | bytes 1474568 | tf_op jit(solution)/shard_map/ppermute | solution.py:61
  148.2 12.1 %collective-permute-start.16 = (bf16[80,3072]{1,0:T(8,128)(2,1)S(1)}, bf16[80,3072]{1,0:T(8,128)(2,1)S(1)}, u32[]{:S(2)}, u32[]{:S(2)}) collective-permute-start(bf16[80,3072]{1,0:T(8,128)(2,1)S(1)} %get-tuple-element.150.refs_0_), channel_id=1, source_target_pairs={{0,4},{1,5},{2,6},{3,7},{4,0},{5,1},{6,2},{7,3},{8,12},{9,13},{10,... | collective-permute-start | bytes 1474568 | tf_op jit(solution)/shard_map/ppermute | solution.py:61
  161.0 10.5 %collective-permute-start.18 = (bf16[80,3072]{1,0:T(8,128)(2,1)S(1)}, bf16[80,3072]{1,0:T(8,128)(2,1)S(1)}, u32[]{:S(2)}, u32[]{:S(2)}) collective-permute-start(bf16[80,3072]{1,0:T(8,128)(2,1)S(1)} %get-tuple-element.154.refs_0_), channel_id=1, source_target_pairs={{0,2},{1,3},{2,0},{3,1},{4,6},{5,7},{6,4},{7,5},{8,10},{9,11},{10,... | collective-permute-start | bytes 1474568 | tf_op jit(solution)/shard_map/ppermute | solution.py:61
  162.2 17.2 %collective-permute-start.21 = (bf16[80,3072]{1,0:T(8,128)(2,1)S(1)}, bf16[80,3072]{1,0:T(8,128)(2,1)S(1)}, u32[]{:S(2)}, u32[]{:S(2)}) collective-permute-start(bf16[80,3072]{1,0:T(8,128)(2,1)S(1)} %collective-permute-done.16.refs_6_.refs_2_), channel_id=1, source_target_pairs={{0,2},{1,3},{2,0},{3,1},{4,6},{5,7},{6,4},{7,5},{8,10},{9,11},{10,... | collective-permute-start | bytes 1474568 | tf_op jit(solution)/shard_map/ppermute | solution.py:61
  162.5 20.9 %collective-permute-start.19 = (bf16[80,3072]{1,0:T(8,128)(2,1)S(1)}, bf16[80,3072]{1,0:T(8,128)(2,1)S(1)}, u32[]{:S(2)}, u32[]{:S(2)}) collective-permute-start(bf16[80,3072]{1,0:T(8,128)(2,1)S(1)} %get-tuple-element.154.refs_0_), channel_id=1, source_target_pairs={{0,4},{1,5},{2,6},{3,7},{4,0},{5,1},{6,2},{7,3},{8,12},{9,13},{10,... | collective-permute-start | bytes 1474568 | tf_op jit(solution)/shard_map/ppermute | solution.py:61
  171.5 11.9 %collective-permute-start.20 = (bf16[80,3072]{1,0:T(8,128)(2,1)S(1)}, bf16[80,3072]{1,0:T(8,128)(2,1)S(1)}, u32[]{:S(2)}, u32[]{:S(2)}) collective-permute-start(bf16[80,3072]{1,0:T(8,128)(2,1)S(1)} %collective-permute-done.18.refs_1_), channel_id=1, source_target_pairs={{0,4},{1,5},{2,6},{3,7},{4,0},{5,1},{6,2},{7,3},{8,12},{9,13},{10,... | collective-permute-start | bytes 1474568 | tf_op jit(solution)/shard_map/ppermute | solution.py:61
  186.3 13.4 %collective-permute-start.22 = (bf16[384,3584]{1,0:T(8,128)(2,1)S(1)}, bf16[384,3584]{1,0:T(8,128)(2,1)S(1)}, u32[]{:S(2)}, u32[]{:S(2)}) collective-permute-start(bf16[384,3584]{1,0:T(8,128)(2,1)S(1)} %get-tuple-element.160), channel_id=1, source_target_pairs={{0,1},{1,0},{2,3},{3,2},{4,5},{5,4},{6,7},{7,6},{8,9},{9,8},{10,11... | collective-permute-start | bytes 8257544 | tf_op jit(solution)/shard_map/ppermute | solution.py:61
  (2 other events, 11.0 us)

commit v3 on v2

--- a/solution.py
+++ b/solution.py
@@ -22,6 +22,7 @@
 LOAD = 512
 PAIR = 2 * BLOCK
 SIDE = 256
+FLIGHT = 4
 
 C_ZERO = 0.7978845608028654
 C_ONE = 0.044715
@@ -76,34 +77,34 @@
     )
 
 
-def keep_columns(piece, held, stores):
-    chips = len(stores)
+def keep_columns(piece, span, held, stores):
+    chips = len(stores) // len(span)
     width = D // chips
     chip = lax.div(lax.axis_index("dp"), 2)
-    rows = pl.ds(pl.multiple_of(piece * PIECE, 16), PIECE)
-    for offset, store in enumerate(stores):
-        columns = pl.ds(pl.multiple_of((chip ^ offset) * width, 128), width)
-        store[rows, :] = held[:, columns]
+    for k, index in enumerate(span):
+
+        @pl.when(piece == index)
+        def _():
+            for offset in range(chips):
+                columns = pl.ds(pl.multiple_of((chip ^ offset) * width, 128), width)
+                stores[k * chips + offset][...] = held[:, columns]
 
 
 def begin_kernel(sections, chips, counts_ref, tokens_ref, cot_ref, weight_ref, *refs):
     w_ref, next_ref, tok_out, cot_out, slope_ref = refs[:5]
     stores = refs[5 : 5 + chips]
-    held, raw, raw_sem, sems = refs[5 + chips + PIECES :]
+    held, raw, raw_sem, sems = refs[-4:]
     here = lax.axis_index("section")
-    core = lax.rem(lax.axis_index("dp"), 2)
     loads = [
         pltpu.make_async_copy(
             weight_ref.at[:, pl.ds(k * LOAD, LOAD)], w_ref.at[:, pl.ds(k * LOAD, LOAD)], sems.at[k]
         )
         for k in range(D // LOAD)
     ]
-
-    def pack(source, target):
-        copy = pltpu.make_async_copy(source, raw, raw_sem)
-        copy.start()
-        for load in loads:
-            load.start()
+    copy_tokens = pltpu.make_async_copy(tokens_ref, raw, raw_sem)
+    copy_cot = pltpu.make_async_copy(cot_ref, raw, raw_sem)
+
+    def pack(copy, target):
         row = lax.broadcasted_iota(jnp.int32, (LIVE, TOK_DEV), 0)
         column = lax.broadcasted_iota(jnp.int32, (LIVE, TOK_DEV), 1)
         origin = row
@@ -123,34 +124,33 @@
 
     @pl.when(here == 0)
     def _():
-        pack(tokens_ref, tok_out)
+        copy_tokens.start()
+
+    for load in loads[:FLIGHT]:
+        load.start()
+
+    @pl.when(here == 0)
+    def _():
+        pack(copy_tokens, tok_out)
         held[...] = tok_out[0]
-        keep_columns(0, held, stores)
-
-    @pl.when(here == sections - 1)
-    def _():
-        if sections > 1:
-            pack(cot_ref, cot_out)
-
-    @pl.when(jnp.logical_and(here > 0, here < sections - 1))
-    def _():
-        for load in loads:
-            load.start()
-
-    lead = jnp.logical_and(here == 0, core == 0)
+
     for k, load in enumerate(loads):
         load.wait()
-
-        @pl.when(lead)
+        if k + FLIGHT < len(loads):
+            loads[k + FLIGHT].start()
+
+        @pl.when(here == 0)
         def _():
             forward_columns(pl.ds(k * LOAD, LOAD), held, w_ref, next_ref, slope_ref, 0)
 
-    @pl.when(jnp.logical_and(here == 0, core != 0))
+    @pl.when(here == 0)
     def _():
-        @pl.loop(0, D // WIDE)
-        def _(step):
-            columns = pl.ds(pl.multiple_of(step * WIDE, WIDE), WIDE)
-            forward_columns(columns, held, w_ref, next_ref, slope_ref, 0)
+        keep_columns(0, [0], held, stores)
+
+    @pl.when(jnp.logical_and(here == sections - 1, sections > 1))
+    def _():
+        copy_cot.start()
+        pack(copy_cot, cot_out)
 
 
 def begin(sections, chips, counts, tokens, cotangent, matrix):
@@ -163,26 +163,26 @@
             packed,
             packed,
             near(PIECES, PIECE, D, kind=F32),
-            *[near(LIVE, D // chips)] * chips,
+            *[near(PIECE, D // chips)] * (chips * PIECES),
             *[near(PIECE, D)] * PIECES,
         ),
         in_specs=[SM, HB, HB, HB],
-        out_specs=[VM] * (5 + chips) + [HB] * PIECES,
+        out_specs=[VM] * (5 + chips) + [HB] * (chips * (PIECES - 1) + PIECES),
         scratch_shapes=[
             pltpu.VMEM((PIECE, D), BF),
             pltpu.VMEM((TOK_DEV, D), BF),
             pltpu.SemaphoreType.DMA,
             pltpu.SemaphoreType.DMA((D // LOAD,)),
         ],
-        compiler_params=limit(6),
+        compiler_params=limit(8),
         cost_estimate=SMALL,
     )(counts, distant(tokens), distant(cotangent), distant(matrix))
 
 
-def forward_kernel(tick, chips, from_ref, tok_ref, w_ref, *refs):
-    next_ref, _, slope_ref = refs[1 + chips : 4 + chips]
-    stores = refs[4 + chips : 4 + 2 * chips]
-    (held,) = refs[4 + 2 * chips :]
+def forward_kernel(tick, span, count, from_ref, tok_ref, w_ref, *refs):
+    next_ref, _, slope_ref = refs[1 + count : 4 + count]
+    stores = refs[4 + count : 4 + 2 * count]
+    (held,) = refs[4 + 2 * count :]
     here = lax.axis_index("section")
     piece = tick - here
 
@@ -203,23 +203,25 @@
             columns = pl.ds(pl.multiple_of(step * WIDE, WIDE), WIDE)
             forward_columns(columns, held, w_ref, next_ref, slope_ref, piece)
 
-        keep_columns(piece, held, stores)
-
-
-def forward(tick, arrived, tokens, matrix, slopes, stores):
-    chips = len(stores)
+        keep_columns(piece, span, held, stores)
+
+
+def forward(tick, sections, arrived, tokens, matrix, slopes, stores):
+    span = list(range(max(0, tick - sections + 1), min(PIECES - 1, tick) + 1))
+    flat = [s for k in span for s in stores[k]]
+    count = len(flat)
     outs = pl.pallas_call(
-        functools.partial(forward_kernel, tick, chips),
+        functools.partial(forward_kernel, tick, span, count),
         out_shape=(
             near(PIECE, D),
             near(*matrix.shape),
             near(*slopes.shape, kind=F32),
-            *[near(*s.shape) for s in stores],
+            *[near(*s.shape) for s in flat],
         ),
-        in_specs=[VM] * (4 + chips),
-        out_specs=[VM] * (3 + chips),
+        in_specs=[VM] * (4 + count),
+        out_specs=[VM] * (3 + count),
         scratch_shapes=[pltpu.VMEM((PIECE, D), BF)],
-        input_output_aliases={2 + k: 1 + k for k in range(2 + chips)},
+        input_output_aliases={2 + k: 1 + k for k in range(2 + count)},
         compiler_params=limit(6),
         cost_estimate=SMALL,
     )(
@@ -227,9 +229,13 @@
         resident(tokens),
         resident(matrix),
         resident(slopes),
-        *[resident(s) for s in stores],
-    )
-    return outs[0], outs[1], outs[2], list(outs[3:])
+        *[resident(s) for s in flat],
+    )
+    stores = list(stores)
+    chips = count // len(span)
+    for k, index in enumerate(span):
+        stores[index] = list(outs[3 + k * chips : 3 + (k + 1) * chips])
+    return outs[0], outs[1], outs[2], stores
 
 
 def backward_kernel(tick, sections, span, late, *refs):
@@ -303,11 +309,12 @@
 
 
 def prepare_kernel(chips, blocks, *refs):
-    parts = refs[:chips]
-    pin_ref, pout_ref, xt_ref, gram_ref, left_ref, right_ref = refs[chips:]
+    parts = refs[: chips * PIECES]
+    pin_ref, pout_ref, xt_ref, gram_ref, left_ref, right_ref = refs[chips * PIECES :]
     for piece in range(PIECES):
-        rows = slice(piece * PIECE, (piece + 1) * PIECE)
-        both = jnp.concatenate([part[rows, :] for part in parts], axis=0)
+        both = jnp.concatenate(
+            [part[...] for part in parts[piece * chips : (piece + 1) * chips]], axis=0
+        )
         xt_ref[piece] = both.T
     for block in range(2 * blocks):
         rows = slice(block * BLOCK, (block + 1) * BLOCK)
@@ -330,9 +337,10 @@
 
 
 def prepare(parts, inverse_in, inverse_out):
-    chips = len(parts)
+    chips = len(parts[0])
     width = D // chips
     blocks = inverse_in.shape[0]
+    flat = [p for piece in parts for p in piece]
     return pl.pallas_call(
         functools.partial(prepare_kernel, chips, blocks),
         out_shape=(
@@ -341,11 +349,11 @@
             near(blocks, BLOCK, BLOCK),
             near(NBLK // 2, PAIR, PAIR),
         ),
-        in_specs=[VM] * (chips + 2),
+        in_specs=[VM] * (len(flat) + 2),
         out_specs=(VM, VM, VM, VM),
         compiler_params=limit(8),
         cost_estimate=SMALL,
-    )(*[resident(p) for p in parts], inverse_in, inverse_out)
+    )(*[resident(p) for p in flat], inverse_in, inverse_out)
 
 
 def add_gram(chips, every, gram_ref, begins):
@@ -359,28 +367,40 @@
         gram_ref[rows, :] = gram if begins else gram + gram_ref[rows, :]
 
 
+def fill(parts, every):
+    for k, part in enumerate(parts):
+        every[k * PIECE : (k + 1) * PIECE, :] = part[...]
+
+
+def half_rows(mine, own):
+    core = lax.rem(lax.axis_index("dp"), 2)
+    return pl.ds(pl.multiple_of((core if mine else 1 - core) * own, 16), own)
+
+
 def gather_kernel(chips, index, *refs):
     parts = refs[:chips]
     xt_ref = refs[chips]
-    acc_ref, gram_ref, every = refs[-3:]
-    for k, part in enumerate(parts):
-        every[k * PIECE : (k + 1) * PIECE, :] = part[...]
+    own_ref, other_ref, gram_ref, every = refs[-4:]
+    fill(parts, every)
     add_gram(chips, every, gram_ref, index == 0)
-
-    @pl.loop(0, D // LOAD)
-    def _(step):
-        columns = pl.ds(pl.multiple_of(step * LOAD, LOAD), LOAD)
-        term = jnp.dot(xt_ref[index], every[:, columns], preferred_element_type=F32)
-        acc_ref[:, columns] = term if index == 0 else acc_ref[:, columns] + term
+    for mine, acc_ref in ((True, own_ref), (False, other_ref)):
+        rows = half_rows(mine, acc_ref.shape[0])
+
+        @pl.loop(0, D // LOAD)
+        def _(step):
+            columns = pl.ds(pl.multiple_of(step * LOAD, LOAD), LOAD)
+            term = jnp.dot(xt_ref[index, rows, :], every[:, columns], preferred_element_type=F32)
+            acc_ref[:, columns] = term if index == 0 else acc_ref[:, columns] + term
 
 
 def gather(chips, index, parts, turned, so_far):
     width = D // chips
+    half = near(width // 2, D, kind=F32)
     return pl.pallas_call(
         functools.partial(gather_kernel, chips, index),
-        out_shape=(near(width, D, kind=F32), near(width, BLOCK, kind=F32)),
+        out_shape=(half, half, near(width, BLOCK, kind=F32)),
         in_specs=[VM] * (chips + 1 + len(so_far)),
-        out_specs=(VM, VM),
+        out_specs=(VM, VM, VM),
         scratch_shapes=[pltpu.VMEM((chips * PIECE, D), BF)],
         input_output_aliases={chips + 1 + k: k for k in range(len(so_far))},
         compiler_params=limit(8),
@@ -390,11 +410,9 @@
 
 def other_kernel(chips, *refs):
     parts = refs[:chips]
-    xt_ref, acc_ref, gram_in_ref, gram_ref, _, _, out_ref, every = refs[chips:]
-    own = D // chips // 2
-    rows = pl.ds(pl.multiple_of((1 - lax.rem(lax.axis_index("dp"), 2)) * own, 16), own)
-    for k, part in enumerate(parts):
-        every[k * PIECE : (k + 1) * PIECE, :] = part[...]
+    xt_ref, acc_ref, gram_in_ref, gram_ref, _, out_ref, every = refs[chips:]
+    rows = half_rows(False, acc_ref.shape[0])
+    fill(parts, every)
     add_gram(chips, every, gram_ref, False)
     out_ref[:, D : D + BLOCK] = gram_ref[rows, :].astype(BF)
     out_ref[:, D + SIDE : D + SIDE + BLOCK] = gram_in_ref[rows, :].astype(BF)
@@ -403,22 +421,18 @@
     def _(step):
         columns = pl.ds(pl.multiple_of(step * LOAD, LOAD), LOAD)
         term = jnp.dot(xt_ref[PIECES - 1, rows, :], every[:, columns], preferred_element_type=F32)
-        out_ref[:, columns] = (term + acc_ref[rows, columns]).astype(BF)
+        out_ref[:, columns] = (term + acc_ref[:, columns]).astype(BF)
 
 
 def other_half(chips, parts, turned, acc, gram_in, gram_out):
     width = D // chips
     return pl.pallas_call(
         functools.partial(other_kernel, chips),
-        out_shape=(
-            near(width, D, kind=F32),
-            near(width, BLOCK, kind=F32),
-            near(width // 2, D + 2 * SIDE),
-        ),
+        out_shape=(near(width, BLOCK, kind=F32), near(width // 2, D + 2 * SIDE)),
         in_specs=[VM] * (chips + 4),
-        out_specs=(VM, VM, VM),
+        out_specs=(VM, VM),
         scratch_shapes=[pltpu.VMEM((chips * PIECE, D), BF)],
-        input_output_aliases={chips + 1: 0, chips + 3: 1},
+        input_output_aliases={chips + 3: 0},
         compiler_params=limit(8),
         cost_estimate=SMALL,
     )(
@@ -433,26 +447,24 @@
 def own_kernel(chips, *refs):
     parts = refs[:chips]
     xt_ref, acc_ref, out_ref, every = refs[chips:]
-    own = D // chips // 2
-    rows = pl.ds(pl.multiple_of(lax.rem(lax.axis_index("dp"), 2) * own, 16), own)
-    for k, part in enumerate(parts):
-        every[k * PIECE : (k + 1) * PIECE, :] = part[...]
+    rows = half_rows(True, acc_ref.shape[0])
+    fill(parts, every)
 
     @pl.loop(0, D // LOAD)
     def _(step):
         columns = pl.ds(pl.multiple_of(step * LOAD, LOAD), LOAD)
         term = jnp.dot(xt_ref[PIECES - 1, rows, :], every[:, columns], preferred_element_type=F32)
-        out_ref[:, columns] = term + acc_ref[rows, columns]
+        out_ref[:, columns] = term + acc_ref[:, columns]
 
 
 def own_half(chips, parts, turned, acc):
-    width = D // chips
     return pl.pallas_call(
         functools.partial(own_kernel, chips),
-        out_shape=near(width // 2, D, kind=F32),
+        out_shape=near(*acc.shape, kind=F32),
         in_specs=[VM] * (chips + 2),
         out_specs=VM,
         scratch_shapes=[pltpu.VMEM((chips * PIECE, D), BF)],
+        input_output_aliases={chips + 1: 0},
         compiler_params=limit(8),
         cost_estimate=SMALL,
     )(*[resident(p) for p in parts], resident(turned), resident(acc))
@@ -524,40 +536,44 @@
     chips = ranks // 2
     begun = begin(sections, chips, live_counts, tokens, cotangent, weight[0])
     matrix, ahead, packed_tokens, packed_cot, slopes = begun[:5]
-    stores = list(begun[5 : 5 + chips])
-    kept = list(begun[5 + chips :])
+    stores = [list(begun[5 + k * chips : 5 + (k + 1) * chips]) for k in range(PIECES)]
+    kept = list(begun[5 + chips * PIECES :])
     behind = None
     parts = []
+    crossed = []
     last_turn = 2 * (sections - 1)
-    crossed = None
+    single = [1 << b for b in range(chips.bit_length() - 1)]
     acc = []
     for tick in range(PIECES + last_turn):
         done = tick - last_turn
+        known = tick - (sections - 1)
         arrived_ahead = arrived_behind = None
         if 0 < tick < PIECES + sections - 1:
             pairs = [(s - 1, s) for s in range(1, sections) if 0 <= tick - s < PIECES]
             arrived_ahead = lax.ppermute(ahead, "section", pairs)
             ahead, matrix, slopes, stores = forward(
-                tick, arrived_ahead, packed_tokens, matrix, slopes, stores
+                tick, sections, arrived_ahead, packed_tokens, matrix, slopes, stores
             )
         if tick > sections - 1:
             pairs = [(s + 1, s) for s in range(sections - 1) if 0 <= tick - last_turn + s < PIECES]
             arrived_behind = lax.ppermute(behind, "section", pairs)
         if tick >= sections - 1:
             after = []
-            if tick == PIECES + sections - 1:
-                after = crossed[1:]
+            if 1 <= known <= PIECES:
+                after = crossed[known - 1][1:]
+            if known == PIECES:
+                rows_turned, gram_in, left, right = prepare(crossed, inverse_in[0], inverse_out[0])
             if done >= 1:
-                after = after + [parts[done - 1][1 << b] for b in range(chips.bit_length() - 1)]
+                after = after + [parts[done - 1][o] for o in single]
             if done >= 2:
                 acc = gather(chips, done - 2, parts[done - 2], rows_turned, acc)
-                after = after + [acc[1]]
+                after = after + [acc[2]]
             behind, matrix, kept = backward(
                 tick, sections, arrived_behind, matrix, slopes, packed_cot, kept, after
             )
-        if tick == PIECES + sections - 2:
-            crossed = [stores[0]] + [swap(stores[o], ranks, 2 * o) for o in range(1, chips)]
-            rows_turned, gram_in, left, right = prepare(crossed, inverse_in[0], inverse_out[0])
+        if 0 <= known < PIECES:
+            swapped = [swap(stores[known][o], ranks, 2 * o) for o in range(1, chips)]
+            crossed.append([stores[known][0]] + swapped)
         if 0 <= done < PIECES:
             piece = [kept[done]]
             for offset in range(1, chips):
@@ -565,9 +581,9 @@
                 piece.append(swap(piece[offset ^ bit], ranks, 2 * bit))
             parts.append(piece)
     acc = gather(chips, PIECES - 2, parts[PIECES - 2], rows_turned, acc)
-    acc, gram_out, other = other_half(chips, parts[-1], rows_turned, acc[0], gram_in, acc[1])
+    gram_out, other = other_half(chips, parts[-1], rows_turned, acc[1], gram_in, acc[2])
     other = swap(other, ranks, 1)
-    own = own_half(chips, parts[-1], rows_turned, acc)
+    own = own_half(chips, parts[-1], rows_turned, acc[0])
     update, factor_in, factor_out = finish(
         inverse_in.shape[1], total, own, other, left, right, gram_in, gram_out
     )

time: 205 us -> 202 us (0.985)
  starting transfers between devices: 40.3 us -> 35.4 us
  Pallas kernels: 60.8 us -> 63.2 us
    ppermute x13 -> x19, starting transfers between devices: 24.5 us -> 19.5 us  [swap(): return lax.ppermute(x, 'dp', [(r, r ^ flip) for r in range(ranks)])]
    ppermute x5, waiting for transfers between devices: 45.2 us -> 42.9 us  [shards(): arrived_ahead = lax.ppermute(ahead, 'section', pairs)]
    ppermute x13 -> x19, waiting for transfers between devices: 32.6 us -> 33.4 us  [swap(): return lax.ppermute(x, 'dp', [(r, r ^ flip) for r in range(ranks)])]
  transfers between devices with their start and end apart: 23 -> 29, of which waited for: 15 -> 18; matrix products, arithmetic and copies ran while one was open for 0% -> 0% of each run, Pallas kernels for 10% -> 11%
where the time goes in v3:
time: 202 us; the launch traced here: 201 us
  waiting for transfers between devices  101 us (50%)
  Pallas kernels  63.2 us (31%)
  starting transfers between devices  35.4 us (18%)
    ppermute x5, waiting for transfers between devices, shards(): arrived_ahead = lax.ppermute(ahead, 'section', pairs)  42.9 us
    ppermute x19, waiting for transfers between devices, swap(): return lax.ppermute(x, 'dp', [(r, r ^ flip) for r in range(ranks)])  33.4 us
    ppermute x5, waiting for transfers between devices, shards(): arrived_behind = lax.ppermute(behind, 'section', pairs)  24.3 us
    pallas_call x6, Pallas kernels, backward(): pl.pallas_call(functools.partial(backward_kernel, tick, sections, span, l...  19.8 us
    ppermute x19, starting transfers between devices, swap(): return lax.ppermute(x, 'dp', [(r, r ^ flip) for r in range(ranks)])  19.5 us
    pallas_call x5, Pallas kernels, forward(): pl.pallas_call(functools.partial(forward_kernel, tick, span, count), out_...  13.7 us
    pallas_call x2, Pallas kernels, gather(): pl.pallas_call(functools.partial(gather_kernel, chips, index), out_shape=...  9.95 us
    ppermute x5, starting transfers between devices, shards(): arrived_ahead = lax.ppermute(ahead, 'section', pairs)  8.72 us
  transfers between devices with their start and end apart: 29, of which 18 were waited for; matrix products, arithmetic and copies ran while one was open for 0% of the time, Pallas kernels for 11%

profile of v3, /device:TPU:9, one launch (start us, length us, event | category | flops | bytes accessed | tf_op | source)
XLA Modules:
  0.0 200.9 jit_solution(7197486908226541287)
XLA Ops:
  1.3 7.3 %shard_map.85 = (bf16[3072,3072]{1,0:T(8,128)(2,1)S(1)}, bf16[80,3072]{1,0:T(8,128)(2,1)S(1)}, bf16[3,80,3072]{2,1,0:T(8,128)(2,1)S(1)}, bf16[3,80,3072]{2,1,0:T...) custom-call(s32[1,4]{1,0:T(1,128)S(1)} %copy-done.2, ...), custom_call_target="tpu_custom_call" | custom-call | flops 1000 | bytes 1000 | tf_op jit(solution)/shard_map/pallas_call | solution.py:158
  9.9 15.0 %collective-permute-done.from_ref = bf16[80,3072]{1,0:T(8,128)(2,1)S(1)} collective-permute-done((bf16[80,3072]{1,0:T(8,128)(2,1)S(1)}, bf16[80,3072]{1,0:T(8,128)(2,1)S(1)}, u32[]{:S(2)}, u32[]{:S(2)}) %collective-permute-start) | collective-permute-done | bytes 491552 | tf_op jit(solution)/shard_map/ppermute | solution.py:553
  24.9 4.3 %shard_map.86 = (bf16[80,3072]{1,0:T(8,128)(2,1)S(1)}, bf16[3072,3072]{1,0:T(8,128)(2,1)S(1)}, f32[3,80,3072]{2,1,0:T(8,128)S(1)}, bf16[80,768]{1,0:T(8,128)(2,1...) custom-call(bf16[80,3072]{1,0:T(8,128)(2,1)S(1)} %collective-permute, ...), custom_call_target="tpu_custom_call", output_to_operand_aliasing={{1}: (2, {}), {2}: (3, {}), {3}: (4, {}), {4}: (5, {}), {5}... | custom-call | flops 1000 | bytes 1000 | tf_op jit(solution)/shard_map/pallas_call | solution.py:213
  31.1 12.1 %collective-permute-done.1.from_ref = bf16[80,3072]{1,0:T(8,128)(2,1)S(1)} collective-permute-done((bf16[80,3072]{1,0:T(8,128)(2,1)S(1)}, bf16[80,3072]{1,0:T(8,128)(2,1)S(1)}, u32[]{:S(2)}, u32[]{:S(2)}) %collective-permute-start.1) | collective-permute-done | bytes 491552 | tf_op jit(solution)/shard_map/ppermute | solution.py:553
  43.3 4.3 %shard_map.87 = (bf16[80,3072]{1,0:T(8,128)(2,1)S(1)}, bf16[3072,3072]{1,0:T(8,128)(2,1)S(1)}, f32[3,80,3072]{2,1,0:T(8,128)S(1)}, bf16[80,768]{1,0:T(8,128)(2,1...) custom-call(bf16[80,3072]{1,0:T(8,128)(2,1)S(1)} %collective-permute, ...), custom_call_target="tpu_custom_call", output_to_operand_aliasing={{1}: (2, {}), {2}: (3, {}), {3}: (4, {}), {4}: (5, {}), {5}... | custom-call | flops 1000 | bytes 1000 | tf_op jit(solution)/shard_map/pallas_call | solution.py:213
  49.8 10.9 %collective-permute-done.2.from_ref = bf16[80,3072]{1,0:T(8,128)(2,1)S(1)} collective-permute-done((bf16[80,3072]{1,0:T(8,128)(2,1)S(1)}, bf16[80,3072]{1,0:T(8,128)(2,1)S(1)}, u32[]{:S(2)}, u32[]{:S(2)}) %collective-permute-start.2) | collective-permute-done | bytes 491552 | tf_op jit(solution)/shard_map/ppermute | solution.py:553
  60.7 4.3 %shard_map.88 = (bf16[80,3072]{1,0:T(8,128)(2,1)S(1)}, bf16[3072,3072]{1,0:T(8,128)(2,1)S(1)}, f32[3,80,3072]{2,1,0:T(8,128)S(1)}, bf16[80,768]{1,0:T(8,128)(2,1...) custom-call(bf16[80,3072]{1,0:T(8,128)(2,1)S(1)} %collective-permute, ...), custom_call_target="tpu_custom_call", output_to_operand_aliasing={{1}: (2, {}), {2}: (3, {}), {3}: (4, {}), {4}: (5, {}), {5}... | custom-call | flops 1000 | bytes 1000 | tf_op jit(solution)/shard_map/pallas_call | solution.py:213
  65.0 2.6 %collective-permute-start.3 = (bf16[80,3072]{1,0:T(8,128)(2,1)S(1)}, bf16[80,3072]{1,0:T(8,128)(2,1)S(1)}, u32[]{:S(2)}, u32[]{:S(2)}) collective-permute-start(bf16[80,3072]{1,0:T(8,128)(2,1)S(1)} %get-tuple-element.160), channel_id=1, source_target_pairs={{8,16},{16,24},{9,17},{17,25},{10,18},{18,26},{11,19},{19,27},{12,... | collective-permute-start | bytes 1474568 | tf_op jit(solution)/shard_map/ppermute | solution.py:553
  71.1 4.9 %collective-permute-done.3.from_ref = bf16[80,3072]{1,0:T(8,128)(2,1)S(1)} collective-permute-done((bf16[80,3072]{1,0:T(8,128)(2,1)S(1)}, bf16[80,3072]{1,0:T(8,128)(2,1)S(1)}, u32[]{:S(2)}, u32[]{:S(2)}) %collective-permute-start.3) | collective-permute-done | bytes 491552 | tf_op jit(solution)/shard_map/ppermute | solution.py:553
  83.4 18.6 %collective-permute-done.9.refs_3_ = bf16[80,3072]{1,0:T(8,128)(2,1)S(1)} collective-permute-done((bf16[80,3072]{1,0:T(8,128)(2,1)S(1)}, bf16[80,3072]{1,0:T(8,128)(2,1)S(1)}, u32[]{:S(2)}, u32[]{:S(2)}) %collective-permute-start.9) | collective-permute-done | bytes 491552 | tf_op jit(solution)/shard_map/ppermute | solution.py:559
  102.0 6.3 %shard_map.93 = (bf16[80,3072]{1,0:T(8,128)(2,1)S(1)}, bf16[3072,3072]{1,0:T(8,128)(2,1)S(1)}, bf16[80,3072]{1,0:T(8,128)(2,1)S(1)}, bf16[80,3072]{1,0:T(8,128)(2,1)S(1)}, bf16[80,3072]{1,0:T(8,128)(2,1)S(1)}) custom-call(bf16[3072,3072]{1,0:T(8,128)(2,1)S(1)} %get-tuple-element.188.refs_0_, ...), custom_call_target="tpu_custom_call", output_to_operand_aliasing={{1}: (0, {}), {2}: (4, {}), {3}: (5, {}), {4}: (6, {})} | custom-call | flops 1000 | bytes 1000 | tf_op jit(solution)/shard_map/pallas_call | solution.py:288
  115.4 3.8 %collective-permute-done.13.refs_3_ = bf16[80,3072]{1,0:T(8,128)(2,1)S(1)} collective-permute-done((bf16[80,3072]{1,0:T(8,128)(2,1)S(1)}, bf16[80,3072]{1,0:T(8,128)(2,1)S(1)}, u32[]{:S(2)}, u32[]{:S(2)}) %collective-permute-start.13) | collective-permute-done | bytes 491552 | tf_op jit(solution)/shard_map/ppermute | solution.py:559
  119.2 6.3 %shard_map.94 = (bf16[80,3072]{1,0:T(8,128)(2,1)S(1)}, bf16[3072,3072]{1,0:T(8,128)(2,1)S(1)}, bf16[80,3072]{1,0:T(8,128)(2,1)S(1)}, bf16[80,3072]{1,0:T(8,128)(2,1)S(1)}, bf16[80,3072]{1,0:T(8,128)(2,1)S(1)}) custom-call(bf16[3072,3072]{1,0:T(8,128)(2,1)S(1)} %get-tuple-element.197.refs_0_, ...), custom_call_target="tpu_custom_call", output_to_operand_aliasing={{1}: (0, {}), {2}: (4, {}), {3}: (5, {}), {4}: (6, {})} | custom-call | flops 1000 | bytes 1000 | tf_op jit(solution)/shard_map/pallas_call | solution.py:288
  127.6 6.1 %collective-permute-done.18.refs_6_.refs_1_ = bf16[80,3072]{1,0:T(8,128)(2,1)S(1)} collective-permute-done((bf16[80,3072]{1,0:T(8,128)(2,1)S(1)}, bf16[80,3072]{1,0:T(8,128)(2,1)S(1)}, u32[]{:S(2)}, u32[]{:S(2)}) %collective-permute-start.18) | collective-permute-done | bytes 491552 | tf_op jit(solution)/shard_map/ppermute | solution.py:62
  135.7 6.3 %shard_map.95 = (bf16[80,3072]{1,0:T(8,128)(2,1)S(1)}, bf16[3072,3072]{1,0:T(8,128)(2,1)S(1)}, bf16[80,3072]{1,0:T(8,128)(2,1)S(1)}, bf16[80,3072]{1,0:T(8,128)(2,1)S(1)}) custom-call(bf16[3072,3072]{1,0:T(8,128)(2,1)S(1)} %get-tuple-element.205.refs_0_, ...), custom_call_target="tpu_custom_call", output_to_operand_aliasing={{1}: (0, {}), {2}: (4, {}), {3}: (5, {})} | custom-call | flops 1000 | bytes 1000 | tf_op jit(solution)/shard_map/pallas_call | solution.py:288
  144.8 2.9 %shard_map.96 = (bf16[3,768,320]{2,1,0:T(8,128)(2,1)S(1)}, f32[768,192]{1,0:T(8,128)S(1)}, bf16[2,192,192]{2,1,0:T(8,128)(2,1)S(1)}, bf16[8,384,384]{2,1,0:T(8,128)(2,1)S(1)}) custom-call(bf16[80,768]{1,0:T(8,128)(2,1)S(1)} %get-tuple-element.214.refs_0_, bf16[80,768]{1,0:T(8,128)(2,1)S(1)} %collective-permute-done.6.refs_6_.refs_1_, ...), custom_call_target="tpu_custom_call" | custom-call | flops 1000 | bytes 1000 | tf_op jit(solution)/shard_map/pallas_call | solution.py:344
  147.7 5.0 %shard_map.97 = (f32[384,3072]{1,0:T(8,128)S(1)}, f32[384,3072]{1,0:T(8,128)S(1)}, f32[768,192]{1,0:T(8,128)S(1)}) custom-call(bf16[80,3072]{1,0:T(8,128)(2,1)S(1)} %get-tuple-element.209.refs_0_, bf16[80,3072]{1,0:T(8,128)(2,1)S(1)} %collective-permute-done.18.refs_6_.refs_1_, bf16[80,3072]{1,0:T(8,128)(2,1)S(1)} %collective-permute-done.19.refs_7_.refs_2_, ...), custom_call_target="tpu_custom_call" | custom-call | flops 1000 | bytes 1000 | tf_op jit(solution)/shard_map/pallas_call | solution.py:399
  152.7 3.6 %collective-permute-done.22.refs_6_.refs_2_ = bf16[80,3072]{1,0:T(8,128)(2,1)S(1)} collective-permute-done((bf16[80,3072]{1,0:T(8,128)(2,1)S(1)}, bf16[80,3072]{1,0:T(8,128)(2,1)S(1)}, u32[]{:S(2)}, u32[]{:S(2)}) %collective-permute-start.22) | collective-permute-done | bytes 491552 | tf_op jit(solution)/shard_map/ppermute | solution.py:62
  158.8 8.5 %collective-permute-done.24.refs_1_ = bf16[80,3072]{1,0:T(8,128)(2,1)S(1)} collective-permute-done((bf16[80,3072]{1,0:T(8,128)(2,1)S(1)}, bf16[80,3072]{1,0:T(8,128)(2,1)S(1)}, u32[]{:S(2)}, u32[]{:S(2)}) %collective-permute-start.24) | collective-permute-done | bytes 491552 | tf_op jit(solution)/shard_map/ppermute | solution.py:62
  167.3 8.4 %collective-permute-done.27.refs_3_ = bf16[80,3072]{1,0:T(8,128)(2,1)S(1)} collective-permute-done((bf16[80,3072]{1,0:T(8,128)(2,1)S(1)}, bf16[80,3072]{1,0:T(8,128)(2,1)S(1)}, u32[]{:S(2)}, u32[]{:S(2)}) %collective-permute-start.27) | collective-permute-done | bytes 491552 | tf_op jit(solution)/shard_map/ppermute | solution.py:62
  175.7 5.0 %shard_map.99 = (f32[384,3072]{1,0:T(8,128)S(1)}, f32[384,3072]{1,0:T(8,128)S(1)}, f32[768,192]{1,0:T(8,128)S(1)}) custom-call(bf16[80,3072]{1,0:T(8,128)(2,1)S(1)} %get-tuple-element.213.refs_0_, bf16[80,3072]{1,0:T(8,128)(2,1)S(1)} %collective-permute-done.21.refs_5_.refs_1_, ...), custom_call_target="tpu_custom_call", output_to_operand_aliasing={{0}: (5, {}), {1}: (6, {}), {2}: (7, {})} | custom-call | flops 1000 | bytes 1000 | tf_op jit(solution)/shard_map/pallas_call | solution.py:399
  180.7 2.8 %shard_map.101 = (f32[768,192]{1,0:T(8,128)S(1)}, bf16[384,3584]{1,0:T(8,128)(2,1)S(1)}) custom-call(bf16[80,3072]{1,0:T(8,128)(2,1)S(1)} %get-tuple-element.219.refs_0_, bf16[80,3072]{1,0:T(8,128)(2,1)S(1)} %collective-permute-done.24.refs_1_, bf16[80,3072]{1,0:T(8,128)(2,1)S(1)} %collective-permute-done.25.refs_2_, ...), custom_call_target="tpu_custom_call", output_to_operand_aliasing={{0}: (7, {})} | custom-call | flops 1000 | bytes 1000 | tf_op jit(solution)/shard_map/pallas_call | solution.py:429
  183.6 8.1 %collective-permute-start.28 = (bf16[384,3584]{1,0:T(8,128)(2,1)S(1)}, bf16[384,3584]{1,0:T(8,128)(2,1)S(1)}, u32[]{:S(2)}, u32[]{:S(2)}) collective-permute-start(bf16[384,3584]{1,0:T(8,128)(2,1)S(1)} %get-tuple-element.226), channel_id=1, source_target_pairs={{0,1},{1,0},{2,3},{3,2},{4,5},{5,4},{6,7},{7,6},{8,9},{9,8},{10,11... | collective-permute-start | bytes 8257544 | tf_op jit(solution)/shard_map/ppermute | solution.py:62
  196.4 4.4 %shard_map.102 = (bf16[384,3072]{1,0:T(8,128)(2,1)}, f32[2,192,192]{2,1,0:T(8,128)}, f32[2,192,192]{2,1,0:T(8,128)}) custom-call(f32[384,3072]{1,0:T(8,128)S(1)} %shard_map.100.own_ref, bf16[384,3584]{1,0:T(8,128)(2,1)S(1)} %collective-permute-done.28.other_ref, bf16[2,192,192]{2,1,0:T(8,128)(2,1)S(1)} %get-tuple-element.227.left_ref, ...), custom_call_target="tpu_custom_call" | custom-call | flops 1000 | bytes 1000 | tf_op jit(solution)/shard_map/pallas_call | solution.py:513
  (58 shorter events, 38.1 us)
Async XLA Ops:
  8.6 16.3 %collective-permute-start = (bf16[80,3072]{1,0:T(8,128)(2,1)S(1)}, bf16[80,3072]{1,0:T(8,128)(2,1)S(1)}, u32[]{:S(2)}, u32[]{:S(2)}) collective-permute-start(bf16[80,3072]{1,0:T(8,128)(2,1)S(1)} %get-tuple-element.118), channel_id=1, source_target_pairs={{0,8},{1,9},{2,10},{3,11},{4,12},{5,13},{6,14},{7,15}} | collective-permute-start | bytes 1474568 | tf_op jit(solution)/shard_map/ppermute | solution.py:553
  29.2 14.1 %collective-permute-start.1 = (bf16[80,3072]{1,0:T(8,128)(2,1)S(1)}, bf16[80,3072]{1,0:T(8,128)(2,1)S(1)}, u32[]{:S(2)}, u32[]{:S(2)}) collective-permute-start(bf16[80,3072]{1,0:T(8,128)(2,1)S(1)} %get-tuple-element.130), channel_id=1, source_target_pairs={{0,8},{8,16},{1,9},{9,17},{2,10},{10,18},{3,11},{11,19},{4,12},{12... | collective-permute-start | bytes 1474568 | tf_op jit(solution)/shard_map/ppermute | solution.py:553
  47.6 13.1 %collective-permute-start.2 = (bf16[80,3072]{1,0:T(8,128)(2,1)S(1)}, bf16[80,3072]{1,0:T(8,128)(2,1)S(1)}, u32[]{:S(2)}, u32[]{:S(2)}) collective-permute-start(bf16[80,3072]{1,0:T(8,128)(2,1)S(1)} %get-tuple-element.145), channel_id=1, source_target_pairs={{0,8},{8,16},{16,24},{1,9},{9,17},{17,25},{2,10},{10,18},{18,26},{... | collective-permute-start | bytes 1474568 | tf_op jit(solution)/shard_map/ppermute | solution.py:553
  65.0 11.0 %collective-permute-start.3 = (bf16[80,3072]{1,0:T(8,128)(2,1)S(1)}, bf16[80,3072]{1,0:T(8,128)(2,1)S(1)}, u32[]{:S(2)}, u32[]{:S(2)}) collective-permute-start(bf16[80,3072]{1,0:T(8,128)(2,1)S(1)} %get-tuple-element.160), channel_id=1, source_target_pairs={{8,16},{16,24},{9,17},{17,25},{10,18},{18,26},{11,19},{19,27},{12,... | collective-permute-start | bytes 1474568 | tf_op jit(solution)/shard_map/ppermute | solution.py:553
  67.7 9.1 %collective-permute-start.5 = (bf16[80,3072]{1,0:T(8,128)(2,1)S(1)}, bf16[80,3072]{1,0:T(8,128)(2,1)S(1)}, u32[]{:S(2)}, u32[]{:S(2)}) collective-permute-start(bf16[80,3072]{1,0:T(8,128)(2,1)S(1)} %get-tuple-element.177), channel_id=1, source_target_pairs={{24,16},{25,17},{26,18},{27,19},{28,20},{29,21},{30,22},{31,23}} | collective-permute-start | bytes 1474568 | tf_op jit(solution)/shard_map/ppermute | solution.py:559
  68.4 8.3 %collective-permute-start.6 = (bf16[80,768]{1,0:T(8,128)(2,1)S(1)}, bf16[80,768]{1,0:T(8,128)(2,1)S(1)}, u32[]{:S(2)}, u32[]{:S(2)}) collective-permute-start(bf16[80,768]{1,0:T(8,128)(2,1)S(1)} %get-tuple-element.180), channel_id=1, source_target_pairs={{0,2},{1,3},{2,0},{3,1},{4,6},{5,7},{6,4},{7,5},{8,10},{9,11},{10,... | collective-permute-start | bytes 368648 | tf_op jit(solution)/shard_map/ppermute | solution.py:62
  68.4 8.3 %collective-permute-start.7 = (bf16[80,768]{1,0:T(8,128)(2,1)S(1)}, bf16[80,768]{1,0:T(8,128)(2,1)S(1)}, u32[]{:S(2)}, u32[]{:S(2)}) collective-permute-start(bf16[80,768]{1,0:T(8,128)(2,1)S(1)} %get-tuple-element.181), channel_id=1, source_target_pairs={{0,4},{1,5},{2,6},{3,7},{4,0},{5,1},{6,2},{7,3},{8,12},{9,13},{10,... | collective-permute-start | bytes 368648 | tf_op jit(solution)/shard_map/ppermute | solution.py:62
  69.6 7.1 %collective-permute-start.8 = (bf16[80,768]{1,0:T(8,128)(2,1)S(1)}, bf16[80,768]{1,0:T(8,128)(2,1)S(1)}, u32[]{:S(2)}, u32[]{:S(2)}) collective-permute-start(bf16[80,768]{1,0:T(8,128)(2,1)S(1)} %get-tuple-element.182), channel_id=1, source_target_pairs={{0,6},{1,7},{2,4},{3,5},{4,2},{5,3},{6,0},{7,1},{8,14},{9,15},{10,... | collective-permute-start | bytes 368648 | tf_op jit(solution)/shard_map/ppermute | solution.py:62
  76.9 25.1 %collective-permute-start.9 = (bf16[80,3072]{1,0:T(8,128)(2,1)S(1)}, bf16[80,3072]{1,0:T(8,128)(2,1)S(1)}, u32[]{:S(2)}, u32[]{:S(2)}) collective-permute-start(bf16[80,3072]{1,0:T(8,128)(2,1)S(1)} %get-tuple-element.190), channel_id=1, source_target_pairs={{16,8},{24,16},{17,9},{25,17},{18,10},{26,18},{19,11},{27,19},{20,... | collective-permute-start | bytes 1474568 | tf_op jit(solution)/shard_map/ppermute | solution.py:559
  108.3 11.0 %collective-permute-start.13 = (bf16[80,3072]{1,0:T(8,128)(2,1)S(1)}, bf16[80,3072]{1,0:T(8,128)(2,1)S(1)}, u32[]{:S(2)}, u32[]{:S(2)}) collective-permute-start(bf16[80,3072]{1,0:T(8,128)(2,1)S(1)} %get-tuple-element.198), channel_id=1, source_target_pairs={{8,0},{16,8},{24,16},{9,1},{17,9},{25,17},{10,2},{18,10},{26,18},{... | collective-permute-start | bytes 1474568 | tf_op jit(solution)/shard_map/ppermute | solution.py:559
  110.3 5.1 %collective-permute-start.15 = (bf16[80,768]{1,0:T(8,128)(2,1)S(1)}, bf16[80,768]{1,0:T(8,128)(2,1)S(1)}, u32[]{:S(2)}, u32[]{:S(2)}) collective-permute-start(bf16[80,768]{1,0:T(8,128)(2,1)S(1)} %get-tuple-element.203), channel_id=1, source_target_pairs={{0,4},{1,5},{2,6},{3,7},{4,0},{5,1},{6,2},{7,3},{8,12},{9,13},{10,... | collective-permute-start | bytes 368648 | tf_op jit(solution)/shard_map/ppermute | solution.py:62
  110.4 5.0 %collective-permute-start.16 = (bf16[80,768]{1,0:T(8,128)(2,1)S(1)}, bf16[80,768]{1,0:T(8,128)(2,1)S(1)}, u32[]{:S(2)}, u32[]{:S(2)}) collective-permute-start(bf16[80,768]{1,0:T(8,128)(2,1)S(1)} %get-tuple-element.204), channel_id=1, source_target_pairs={{0,6},{1,7},{2,4},{3,5},{4,2},{5,3},{6,0},{7,1},{8,14},{9,15},{10,... | collective-permute-start | bytes 368648 | tf_op jit(solution)/shard_map/ppermute | solution.py:62
  125.5 8.2 %collective-permute-start.18 = (bf16[80,3072]{1,0:T(8,128)(2,1)S(1)}, bf16[80,3072]{1,0:T(8,128)(2,1)S(1)}, u32[]{:S(2)}, u32[]{:S(2)}) collective-permute-start(bf16[80,3072]{1,0:T(8,128)(2,1)S(1)} %get-tuple-element.209.refs_0_), channel_id=1, source_target_pairs={{0,2},{1,3},{2,0},{3,1},{4,6},{5,7},{6,4},{7,5},{8,10},{9,11},{10,... | collective-permute-start | bytes 1474568 | tf_op jit(solution)/shard_map/ppermute | solution.py:62
  125.6 10.0 %collective-permute-start.17 = (bf16[80,3072]{1,0:T(8,128)(2,1)S(1)}, bf16[80,3072]{1,0:T(8,128)(2,1)S(1)}, u32[]{:S(2)}, u32[]{:S(2)}) collective-permute-start(bf16[80,3072]{1,0:T(8,128)(2,1)S(1)} %get-tuple-element.206), channel_id=1, source_target_pairs={{8,0},{16,8},{9,1},{17,9},{10,2},{18,10},{11,3},{19,11},{12,4},{20... | collective-permute-start | bytes 1474568 | tf_op jit(solution)/shard_map/ppermute | solution.py:559
  127.5 8.2 %collective-permute-start.19 = (bf16[80,3072]{1,0:T(8,128)(2,1)S(1)}, bf16[80,3072]{1,0:T(8,128)(2,1)S(1)}, u32[]{:S(2)}, u32[]{:S(2)}) collective-permute-start(bf16[80,3072]{1,0:T(8,128)(2,1)S(1)} %get-tuple-element.209.refs_0_), channel_id=1, source_target_pairs={{0,4},{1,5},{2,6},{3,7},{4,0},{5,1},{6,2},{7,3},{8,12},{9,13},{10,... | collective-permute-start | bytes 1474568 | tf_op jit(solution)/shard_map/ppermute | solution.py:62
  133.7 14.0 %collective-permute-start.23 = (bf16[80,3072]{1,0:T(8,128)(2,1)S(1)}, bf16[80,3072]{1,0:T(8,128)(2,1)S(1)}, u32[]{:S(2)}, u32[]{:S(2)}) collective-permute-start(bf16[80,3072]{1,0:T(8,128)(2,1)S(1)} %collective-permute-done.18.refs_6_.refs_1_), channel_id=1, source_target_pairs={{0,4},{1,5},{2,6},{3,7},{4,0},{5,1},{6,2},{7,3},{8,12},{9,13},{10,... | collective-permute-start | bytes 1474568 | tf_op jit(solution)/shard_map/ppermute | solution.py:62
  142.0 10.7 %collective-permute-start.20 = (bf16[80,3072]{1,0:T(8,128)(2,1)S(1)}, bf16[80,3072]{1,0:T(8,128)(2,1)S(1)}, u32[]{:S(2)}, u32[]{:S(2)}) collective-permute-start(bf16[80,3072]{1,0:T(8,128)(2,1)S(1)} %get-tuple-element.211), channel_id=1, source_target_pairs={{8,0},{9,1},{10,2},{11,3},{12,4},{13,5},{14,6},{15,7}} | collective-permute-start | bytes 1474568 | tf_op jit(solution)/shard_map/ppermute | solution.py:559
  143.3 9.4 %collective-permute-start.21 = (bf16[80,3072]{1,0:T(8,128)(2,1)S(1)}, bf16[80,3072]{1,0:T(8,128)(2,1)S(1)}, u32[]{:S(2)}, u32[]{:S(2)}) collective-permute-start(bf16[80,3072]{1,0:T(8,128)(2,1)S(1)} %get-tuple-element.213.refs_0_), channel_id=1, source_target_pairs={{0,2},{1,3},{2,0},{3,1},{4,6},{5,7},{6,4},{7,5},{8,10},{9,11},{10,... | collective-permute-start | bytes 1474568 | tf_op jit(solution)/shard_map/ppermute | solution.py:62
  144.7 11.7 %collective-permute-start.22 = (bf16[80,3072]{1,0:T(8,128)(2,1)S(1)}, bf16[80,3072]{1,0:T(8,128)(2,1)S(1)}, u32[]{:S(2)}, u32[]{:S(2)}) collective-permute-start(bf16[80,3072]{1,0:T(8,128)(2,1)S(1)} %get-tuple-element.213.refs_0_), channel_id=1, source_target_pairs={{0,4},{1,5},{2,6},{3,7},{4,0},{5,1},{6,2},{7,3},{8,12},{9,13},{10,... | collective-permute-start | bytes 1474568 | tf_op jit(solution)/shard_map/ppermute | solution.py:62
  157.1 10.2 %collective-permute-start.24 = (bf16[80,3072]{1,0:T(8,128)(2,1)S(1)}, bf16[80,3072]{1,0:T(8,128)(2,1)S(1)}, u32[]{:S(2)}, u32[]{:S(2)}) collective-permute-start(bf16[80,3072]{1,0:T(8,128)(2,1)S(1)} %get-tuple-element.219.refs_0_), channel_id=1, source_target_pairs={{0,2},{1,3},{2,0},{3,1},{4,6},{5,7},{6,4},{7,5},{8,10},{9,11},{10,... | collective-permute-start | bytes 1474568 | tf_op jit(solution)/shard_map/ppermute | solution.py:62
  158.7 17.0 %collective-permute-start.27 = (bf16[80,3072]{1,0:T(8,128)(2,1)S(1)}, bf16[80,3072]{1,0:T(8,128)(2,1)S(1)}, u32[]{:S(2)}, u32[]{:S(2)}) collective-permute-start(bf16[80,3072]{1,0:T(8,128)(2,1)S(1)} %collective-permute-done.22.refs_6_.refs_2_), channel_id=1, source_target_pairs={{0,2},{1,3},{2,0},{3,1},{4,6},{5,7},{6,4},{7,5},{8,10},{9,11},{10,... | collective-permute-start | bytes 1474568 | tf_op jit(solution)/shard_map/ppermute | solution.py:62
  158.8 21.9 %collective-permute-start.25 = (bf16[80,3072]{1,0:T(8,128)(2,1)S(1)}, bf16[80,3072]{1,0:T(8,128)(2,1)S(1)}, u32[]{:S(2)}, u32[]{:S(2)}) collective-permute-start(bf16[80,3072]{1,0:T(8,128)(2,1)S(1)} %get-tuple-element.219.refs_0_), channel_id=1, source_target_pairs={{0,4},{1,5},{2,6},{3,7},{4,0},{5,1},{6,2},{7,3},{8,12},{9,13},{10,... | collective-permute-start | bytes 1474568 | tf_op jit(solution)/shard_map/ppermute | solution.py:62
  167.3 13.4 %collective-permute-start.26 = (bf16[80,3072]{1,0:T(8,128)(2,1)S(1)}, bf16[80,3072]{1,0:T(8,128)(2,1)S(1)}, u32[]{:S(2)}, u32[]{:S(2)}) collective-permute-start(bf16[80,3072]{1,0:T(8,128)(2,1)S(1)} %collective-permute-done.24.refs_1_), channel_id=1, source_target_pairs={{0,4},{1,5},{2,6},{3,7},{4,0},{5,1},{6,2},{7,3},{8,12},{9,13},{10,... | collective-permute-start | bytes 1474568 | tf_op jit(solution)/shard_map/ppermute | solution.py:62
  183.6 12.8 %collective-permute-start.28 = (bf16[384,3584]{1,0:T(8,128)(2,1)S(1)}, bf16[384,3584]{1,0:T(8,128)(2,1)S(1)}, u32[]{:S(2)}, u32[]{:S(2)}) collective-permute-start(bf16[384,3584]{1,0:T(8,128)(2,1)S(1)} %get-tuple-element.226), channel_id=1, source_target_pairs={{0,1},{1,0},{2,3},{3,2},{4,5},{5,4},{6,7},{7,6},{8,9},{9,8},{10,11... | collective-permute-start | bytes 8257544 | tf_op jit(solution)/shard_map/ppermute | solution.py:62
  (8 other events, 39.9 us)

commit v4 on v3

--- a/solution.py
+++ b/solution.py
@@ -72,9 +72,8 @@
     hyper = jnp.tanh(C_ZERO * (pre + C_ONE * pre * square))
     half = 0.5 * (1.0 + hyper)
     next_ref[:, columns] = (held[:, columns].astype(F32) + pre * half).astype(BF)
-    slope_ref[piece, :, columns] = half + 0.5 * pre * (1.0 - hyper * hyper) * C_ZERO * (
-        1.0 + 3.0 * C_ONE * square
-    )
+    slope = half + 0.5 * pre * (1.0 - hyper * hyper) * C_ZERO * (1.0 + 3.0 * C_ONE * square)
+    slope_ref[piece, :, columns] = slope.astype(BF)
 
 
 def keep_columns(piece, span, held, stores):
@@ -104,7 +103,7 @@
     copy_tokens = pltpu.make_async_copy(tokens_ref, raw, raw_sem)
     copy_cot = pltpu.make_async_copy(cot_ref, raw, raw_sem)
 
-    def pack(copy, target):
+    def pack(target):
         row = lax.broadcasted_iota(jnp.int32, (LIVE, TOK_DEV), 0)
         column = lax.broadcasted_iota(jnp.int32, (LIVE, TOK_DEV), 1)
         origin = row
@@ -114,7 +113,6 @@
             edge = edge + count
             origin = origin + jnp.where(row >= edge, ROWS - count, 0)
         pick = (column == origin).astype(F32).astype(BF)
-        copy.wait()
         for start in range(0, D, WIDE):
             part = jnp.dot(
                 pick, raw[:, start : start + WIDE], preferred_element_type=F32
@@ -125,13 +123,14 @@
     @pl.when(here == 0)
     def _():
         copy_tokens.start()
+        copy_tokens.wait()
 
     for load in loads[:FLIGHT]:
         load.start()
 
     @pl.when(here == 0)
     def _():
-        pack(copy_tokens, tok_out)
+        pack(tok_out)
         held[...] = tok_out[0]
 
     for k, load in enumerate(loads):
@@ -150,7 +149,8 @@
     @pl.when(jnp.logical_and(here == sections - 1, sections > 1))
     def _():
         copy_cot.start()
-        pack(copy_cot, cot_out)
+        copy_cot.wait()
+        pack(cot_out)
 
 
 def begin(sections, chips, counts, tokens, cotangent, matrix):
@@ -162,7 +162,7 @@
             near(PIECE, D),
             packed,
             packed,
-            near(PIECES, PIECE, D, kind=F32),
+            near(PIECES, PIECE, D),
             *[near(PIECE, D // chips)] * (chips * PIECES),
             *[near(PIECE, D)] * PIECES,
         ),
@@ -215,14 +215,14 @@
         out_shape=(
             near(PIECE, D),
             near(*matrix.shape),
-            near(*slopes.shape, kind=F32),
+            near(*slopes.shape),
             *[near(*s.shape) for s in flat],
         ),
         in_specs=[VM] * (4 + count),
         out_specs=[VM] * (3 + count),
         scratch_shapes=[pltpu.VMEM((PIECE, D), BF)],
         input_output_aliases={2 + k: 1 + k for k in range(2 + count)},
-        compiler_params=limit(6),
+        compiler_params=limit(4),
         cost_estimate=SMALL,
     )(
         resident(arrived),
@@ -238,6 +238,31 @@
     return outs[0], outs[1], outs[2], stores
 
 
+def turn_kernel(w_ref, _, out_ref):
+    @pl.when(lax.axis_index("section") > 0)
+    def _():
+        @pl.loop(0, D // LOAD)
+        def _(step):
+            rows = pl.ds(pl.multiple_of(step * LOAD, LOAD), LOAD)
+
+            @pl.loop(0, D // LOAD)
+            def _(other):
+                columns = pl.ds(pl.multiple_of(other * LOAD, LOAD), LOAD)
+                out_ref[columns, rows] = w_ref[rows, columns].T
+
+
+def turn(matrix):
+    return pl.pallas_call(
+        turn_kernel,
+        out_shape=(near(*matrix.shape), near(*matrix.shape)),
+        in_specs=[VM],
+        out_specs=(VM, VM),
+        input_output_aliases={0: 0},
+        compiler_params=limit(3),
+        cost_estimate=SMALL,
+    )(resident(matrix))
+
+
 def backward_kernel(tick, sections, span, late, *refs):
     keeps = len(span)
     lead = 4 if tick > sections - 1 else 3
@@ -263,7 +288,7 @@
             def _():
                 flow[...] = from_ref[...]
 
-        scaled[...] = (flow[...].astype(F32) * slope_ref[piece]).astype(BF)
+        scaled[...] = (flow[...].astype(F32) * slope_ref[piece].astype(F32)).astype(BF)
         for out, index in zip(kept, span):
 
             @pl.when(piece == index)
@@ -275,7 +300,7 @@
             @pl.loop(0, D // WIDE)
             def _(step):
                 part = pl.ds(pl.multiple_of(step * WIDE, WIDE), WIDE)
-                back = contract_last(scaled[...], w_ref[part, :])
+                back = jnp.dot(scaled[...], w_ref[:, part], preferred_element_type=F32)
                 next_ref[:, part] = (flow[:, part].astype(F32) + back).astype(BF)
 
 
@@ -292,7 +317,7 @@
         out_specs=[VM] * (2 + len(span)),
         scratch_shapes=[pltpu.VMEM((PIECE, D), BF), pltpu.VMEM((PIECE, D), BF)],
         input_output_aliases={0: 1, **{base + k: 2 + k for k in range(len(span))}},
-        compiler_params=limit(6),
+        compiler_params=limit(4),
         cost_estimate=SMALL,
     )(
         resident(matrix),
@@ -554,6 +579,8 @@
             ahead, matrix, slopes, stores = forward(
                 tick, sections, arrived_ahead, packed_tokens, matrix, slopes, stores
             )
+        if tick == sections - 2:
+            matrix, turned = turn(matrix)
         if tick > sections - 1:
             pairs = [(s + 1, s) for s in range(sections - 1) if 0 <= tick - last_turn + s < PIECES]
             arrived_behind = lax.ppermute(behind, "section", pairs)
@@ -568,8 +595,8 @@
             if done >= 2:
                 acc = gather(chips, done - 2, parts[done - 2], rows_turned, acc)
                 after = after + [acc[2]]
-            behind, matrix, kept = backward(
-                tick, sections, arrived_behind, matrix, slopes, packed_cot, kept, after
+            behind, turned, kept = backward(
+                tick, sections, arrived_behind, turned, slopes, packed_cot, kept, after
             )
         if 0 <= known < PIECES:
             swapped = [swap(stores[known][o], ranks, 2 * o) for o in range(1, chips)]

time: 202 us -> 190 us (0.941)
  waiting for transfers between devices: 101 us -> 79.9 us
  starting transfers between devices: 35.4 us -> 45.4 us
    ppermute x5, waiting for transfers between devices: 42.9 us -> 29.1 us  [shards(): arrived_ahead = lax.ppermute(ahead, 'section', pairs)]
    ppermute x5, waiting for transfers between devices: 24.3 us -> 13.5 us  [shards(): arrived_behind = lax.ppermute(behind, 'section', pairs)]
    ppermute x19, starting transfers between devices: 19.5 us -> 29.5 us  [swap(): return lax.ppermute(x, 'dp', [(r, r ^ flip) for r in range(ranks)])]
    pallas_call x6, Pallas kernels: 19.8 us -> 12.3 us  [backward(): pl.pallas_call(functools.partial(backward_kernel, tick, sections, span, l...]
    pallas_call x0 -> x1, Pallas kernels: none -> 7.28 us  [turn(): pl.pallas_call(turn_kernel, out_shape=(near(*matrix.shape), near(*matrix....]
    ppermute x19, waiting for transfers between devices: 33.4 us -> 37.3 us  [swap(): return lax.ppermute(x, 'dp', [(r, r ^ flip) for r in range(ranks)])]
  transfers between devices with their start and end apart: 29 -> 29, of which waited for: 18 -> 19; matrix products, arithmetic and copies ran while one was open for 0% -> 0% of each run, Pallas kernels for 11% -> 14%
where the time goes in v4:
time: 190 us
  waiting for transfers between devices  79.9 us (42%)
  Pallas kernels  62.8 us (33%)
  starting transfers between devices  45.4 us (24%)
    ppermute x19, waiting for transfers between devices, swap(): return lax.ppermute(x, 'dp', [(r, r ^ flip) for r in range(ranks)])  37.3 us
    ppermute x19, starting transfers between devices, swap(): return lax.ppermute(x, 'dp', [(r, r ^ flip) for r in range(ranks)])  29.5 us
    ppermute x5, waiting for transfers between devices, shards(): arrived_ahead = lax.ppermute(ahead, 'section', pairs)  29.1 us
    pallas_call x5, Pallas kernels, forward(): pl.pallas_call(functools.partial(forward_kernel, tick, span, count), out_...  13.5 us
    ppermute x5, waiting for transfers between devices, shards(): arrived_behind = lax.ppermute(behind, 'section', pairs)  13.5 us
    pallas_call x6, Pallas kernels, backward(): pl.pallas_call(functools.partial(backward_kernel, tick, sections, span, l...  12.3 us
    pallas_call x2, Pallas kernels, gather(): pl.pallas_call(functools.partial(gather_kernel, chips, index), out_shape=...  9.95 us
    ppermute x5, starting transfers between devices, shards(): arrived_ahead = lax.ppermute(ahead, 'section', pairs)  8.62 us
  transfers between devices with their start and end apart: 29, of which 19 were waited for; matrix products, arithmetic and copies ran while one was open for 0% of the time, Pallas kernels for 14%

profile of v4, /device:TPU:9, one launch (start us, length us, event | category | flops | bytes accessed | tf_op | source)
XLA Modules:
  0.0 189.9 jit_solution(8230915703835440782)
XLA Ops:
  1.3 7.4 %shard_map.85 = (bf16[3072,3072]{1,0:T(8,128)(2,1)S(1)}, bf16[80,3072]{1,0:T(8,128)(2,1)S(1)}, bf16[3,80,3072]{2,1,0:T(8,128)(2,1)S(1)}, bf16[3,80,3072]{2,1,0:T...) custom-call(s32[1,4]{1,0:T(1,128)S(1)} %copy-done.4, ...), custom_call_target="tpu_custom_call" | custom-call | flops 1000 | bytes 1000 | tf_op jit(solution)/shard_map/pallas_call | solution.py:158
  10.0 12.7 %collective-permute-done.from_ref = bf16[80,3072]{1,0:T(8,128)(2,1)S(1)} collective-permute-done((bf16[80,3072]{1,0:T(8,128)(2,1)S(1)}, bf16[80,3072]{1,0:T(8,128)(2,1)S(1)}, u32[]{:S(2)}, u32[]{:S(2)}) %collective-permute-start) | collective-permute-done | bytes 491552 | tf_op jit(solution)/shard_map/ppermute | solution.py:578
  22.6 4.2 %shard_map.86 = (bf16[80,3072]{1,0:T(8,128)(2,1)S(1)}, bf16[3072,3072]{1,0:T(8,128)(2,1)S(1)}, bf16[3,80,3072]{2,1,0:T(8,128)(2,1)S(1)}, bf16[80,768]{1,0:T(8,12...) custom-call(bf16[80,3072]{1,0:T(8,128)(2,1)S(1)} %collective-permute, ...), custom_call_target="tpu_custom_call", output_to_operand_aliasing={{1}: (2, {}), {2}: (3, {}), {3}: (4, {}), {4}: (5, {}), {5}... | custom-call | flops 1000 | bytes 1000 | tf_op jit(solution)/shard_map/pallas_call | solution.py:213
  28.8 11.1 %collective-permute-done.1.from_ref = bf16[80,3072]{1,0:T(8,128)(2,1)S(1)} collective-permute-done((bf16[80,3072]{1,0:T(8,128)(2,1)S(1)}, bf16[80,3072]{1,0:T(8,128)(2,1)S(1)}, u32[]{:S(2)}, u32[]{:S(2)}) %collective-permute-start.1) | collective-permute-done | bytes 491552 | tf_op jit(solution)/shard_map/ppermute | solution.py:578
  39.9 4.2 %shard_map.87 = (bf16[80,3072]{1,0:T(8,128)(2,1)S(1)}, bf16[3072,3072]{1,0:T(8,128)(2,1)S(1)}, bf16[3,80,3072]{2,1,0:T(8,128)(2,1)S(1)}, bf16[80,768]{1,0:T(8,12...) custom-call(bf16[80,3072]{1,0:T(8,128)(2,1)S(1)} %collective-permute, ...), custom_call_target="tpu_custom_call", output_to_operand_aliasing={{1}: (2, {}), {2}: (3, {}), {3}: (4, {}), {4}: (5, {}), {5}... | custom-call | flops 1000 | bytes 1000 | tf_op jit(solution)/shard_map/pallas_call | solution.py:213
  46.4 7.3 %shard_map.88 = (bf16[3072,3072]{1,0:T(8,128)(2,1)S(1)}, bf16[3072,3072]{1,0:T(8,128)(2,1)S(1)}) custom-call(bf16[3072,3072]{1,0:T(8,128)(2,1)S(1)} %get-tuple-element.146.w_ref), custom_call_target="tpu_custom_call", output_to_operand_aliasing={{0}: (0, {})} | custom-call | flops 1000 | bytes 1000 | tf_op jit(solution)/shard_map/pallas_call | solution.py:255
  56.3 4.2 %shard_map.89 = (bf16[80,3072]{1,0:T(8,128)(2,1)S(1)}, bf16[3072,3072]{1,0:T(8,128)(2,1)S(1)}, bf16[3,80,3072]{2,1,0:T(8,128)(2,1)S(1)}, bf16[80,768]{1,0:T(8,12...) custom-call(bf16[80,3072]{1,0:T(8,128)(2,1)S(1)} %collective-permute, ...), custom_call_target="tpu_custom_call", output_to_operand_aliasing={{1}: (2, {}), {2}: (3, {}), {3}: (4, {}), {4}: (5, {}), {5}... | custom-call | flops 1000 | bytes 1000 | tf_op jit(solution)/shard_map/pallas_call | solution.py:213
  63.8 2.7 %collective-permute-start.5 = (bf16[80,768]{1,0:T(8,128)(2,1)S(1)}, bf16[80,768]{1,0:T(8,128)(2,1)S(1)}, u32[]{:S(2)}, u32[]{:S(2)}) collective-permute-start(bf16[80,768]{1,0:T(8,128)(2,1)S(1)} %get-tuple-element.181), channel_id=1, source_target_pairs={{0,2},{1,3},{2,0},{3,1},{4,6},{5,7},{6,4},{7,5},{8,10},{9,11},{10,... | collective-permute-start | bytes 368648 | tf_op jit(solution)/shard_map/ppermute | solution.py:62
  67.8 2.7 %collective-permute-done.3.from_ref = bf16[80,3072]{1,0:T(8,128)(2,1)S(1)} collective-permute-done((bf16[80,3072]{1,0:T(8,128)(2,1)S(1)}, bf16[80,3072]{1,0:T(8,128)(2,1)S(1)}, u32[]{:S(2)}, u32[]{:S(2)}) %collective-permute-start.3) | collective-permute-done | bytes 491552 | tf_op jit(solution)/shard_map/ppermute | solution.py:578
  81.6 11.3 %collective-permute-done.9.refs_3_ = bf16[80,3072]{1,0:T(8,128)(2,1)S(1)} collective-permute-done((bf16[80,3072]{1,0:T(8,128)(2,1)S(1)}, bf16[80,3072]{1,0:T(8,128)(2,1)S(1)}, u32[]{:S(2)}, u32[]{:S(2)}) %collective-permute-start.9) | collective-permute-done | bytes 491552 | tf_op jit(solution)/shard_map/ppermute | solution.py:586
  92.9 3.8 %shard_map.94 = (bf16[80,3072]{1,0:T(8,128)(2,1)S(1)}, bf16[3072,3072]{1,0:T(8,128)(2,1)S(1)}, bf16[80,3072]{1,0:T(8,128)(2,1)S(1)}, bf16[80,3072]{1,0:T(8,128)(2,1)S(1)}, bf16[80,3072]{1,0:T(8,128)(2,1)S(1)}) custom-call(bf16[3072,3072]{1,0:T(8,128)(2,1)S(1)} %get-tuple-element.184.refs_0_, ...), custom_call_target="tpu_custom_call", output_to_operand_aliasing={{1}: (0, {}), {2}: (4, {}), {3}: (5, {}), {4}: (6, {})} | custom-call | flops 1000 | bytes 1000 | tf_op jit(solution)/shard_map/pallas_call | solution.py:313
  98.7 3.3 %collective-permute-start.14 = (bf16[80,768]{1,0:T(8,128)(2,1)S(1)}, bf16[80,768]{1,0:T(8,128)(2,1)S(1)}, u32[]{:S(2)}, u32[]{:S(2)}) collective-permute-start(bf16[80,768]{1,0:T(8,128)(2,1)S(1)} %get-tuple-element.204), channel_id=1, source_target_pairs={{0,2},{1,3},{2,0},{3,1},{4,6},{5,7},{6,4},{7,5},{8,10},{9,11},{10,... | collective-permute-start | bytes 368648 | tf_op jit(solution)/shard_map/ppermute | solution.py:62
  107.9 3.8 %shard_map.95 = (bf16[80,3072]{1,0:T(8,128)(2,1)S(1)}, bf16[3072,3072]{1,0:T(8,128)(2,1)S(1)}, bf16[80,3072]{1,0:T(8,128)(2,1)S(1)}, bf16[80,3072]{1,0:T(8,128)(2,1)S(1)}, bf16[80,3072]{1,0:T(8,128)(2,1)S(1)}) custom-call(bf16[3072,3072]{1,0:T(8,128)(2,1)S(1)} %get-tuple-element.199.refs_0_, ...), custom_call_target="tpu_custom_call", output_to_operand_aliasing={{1}: (0, {}), {2}: (4, {}), {3}: (5, {}), {4}: (6, {})} | custom-call | flops 1000 | bytes 1000 | tf_op jit(solution)/shard_map/pallas_call | solution.py:313
  117.4 3.0 %collective-permute-done.18.refs_6_.refs_1_ = bf16[80,3072]{1,0:T(8,128)(2,1)S(1)} collective-permute-done((bf16[80,3072]{1,0:T(8,128)(2,1)S(1)}, bf16[80,3072]{1,0:T(8,128)(2,1)S(1)}, u32[]{:S(2)}, u32[]{:S(2)}) %collective-permute-start.18) | collective-permute-done | bytes 491552 | tf_op jit(solution)/shard_map/ppermute | solution.py:62
  124.2 3.8 %shard_map.96 = (bf16[80,3072]{1,0:T(8,128)(2,1)S(1)}, bf16[3072,3072]{1,0:T(8,128)(2,1)S(1)}, bf16[80,3072]{1,0:T(8,128)(2,1)S(1)}, bf16[80,3072]{1,0:T(8,128)(2,1)S(1)}) custom-call(bf16[3072,3072]{1,0:T(8,128)(2,1)S(1)} %get-tuple-element.207.refs_0_, ...), custom_call_target="tpu_custom_call", output_to_operand_aliasing={{1}: (0, {}), {2}: (4, {}), {3}: (5, {})} | custom-call | flops 1000 | bytes 1000 | tf_op jit(solution)/shard_map/pallas_call | solution.py:313
  131.0 2.9 %shard_map.97 = (bf16[3,768,320]{2,1,0:T(8,128)(2,1)S(1)}, f32[768,192]{1,0:T(8,128)S(1)}, bf16[2,192,192]{2,1,0:T(8,128)(2,1)S(1)}, bf16[8,384,384]{2,1,0:T(8,128)(2,1)S(1)}) custom-call(bf16[80,768]{1,0:T(8,128)(2,1)S(1)} %get-tuple-element.216.refs_0_, bf16[80,768]{1,0:T(8,128)(2,1)S(1)} %collective-permute-done.5.refs_6_.refs_1_, ...), custom_call_target="tpu_custom_call" | custom-call | flops 1000 | bytes 1000 | tf_op jit(solution)/shard_map/pallas_call | solution.py:369
  133.9 5.0 %shard_map.98 = (f32[384,3072]{1,0:T(8,128)S(1)}, f32[384,3072]{1,0:T(8,128)S(1)}, f32[768,192]{1,0:T(8,128)S(1)}) custom-call(bf16[80,3072]{1,0:T(8,128)(2,1)S(1)} %get-tuple-element.211.refs_0_, bf16[80,3072]{1,0:T(8,128)(2,1)S(1)} %collective-permute-done.18.refs_6_.refs_1_, bf16[80,3072]{1,0:T(8,128)(2,1)S(1)} %collective-permute-done.19.refs_7_.refs_2_, ...), custom_call_target="tpu_custom_call" | custom-call | flops 1000 | bytes 1000 | tf_op jit(solution)/shard_map/pallas_call | solution.py:424
  138.9 5.5 %collective-permute-done.22.refs_6_.refs_2_ = bf16[80,3072]{1,0:T(8,128)(2,1)S(1)} collective-permute-done((bf16[80,3072]{1,0:T(8,128)(2,1)S(1)}, bf16[80,3072]{1,0:T(8,128)(2,1)S(1)}, u32[]{:S(2)}, u32[]{:S(2)}) %collective-permute-start.22) | collective-permute-done | bytes 491552 | tf_op jit(solution)/shard_map/ppermute | solution.py:62
  147.9 8.3 %collective-permute-done.24.refs_1_ = bf16[80,3072]{1,0:T(8,128)(2,1)S(1)} collective-permute-done((bf16[80,3072]{1,0:T(8,128)(2,1)S(1)}, bf16[80,3072]{1,0:T(8,128)(2,1)S(1)}, u32[]{:S(2)}, u32[]{:S(2)}) %collective-permute-start.24) | collective-permute-done | bytes 491552 | tf_op jit(solution)/shard_map/ppermute | solution.py:62
  156.4 8.2 %collective-permute-done.27.refs_3_ = bf16[80,3072]{1,0:T(8,128)(2,1)S(1)} collective-permute-done((bf16[80,3072]{1,0:T(8,128)(2,1)S(1)}, bf16[80,3072]{1,0:T(8,128)(2,1)S(1)}, u32[]{:S(2)}, u32[]{:S(2)}) %collective-permute-start.27) | collective-permute-done | bytes 491552 | tf_op jit(solution)/shard_map/ppermute | solution.py:62
  164.6 5.0 %shard_map.100 = (f32[384,3072]{1,0:T(8,128)S(1)}, f32[384,3072]{1,0:T(8,128)S(1)}, f32[768,192]{1,0:T(8,128)S(1)}) custom-call(bf16[80,3072]{1,0:T(8,128)(2,1)S(1)} %get-tuple-element.215.refs_0_, bf16[80,3072]{1,0:T(8,128)(2,1)S(1)} %collective-permute-done.21.refs_5_.refs_1_, ...), custom_call_target="tpu_custom_call", output_to_operand_aliasing={{0}: (5, {}), {1}: (6, {}), {2}: (7, {})} | custom-call | flops 1000 | bytes 1000 | tf_op jit(solution)/shard_map/pallas_call | solution.py:424
  169.6 2.8 %shard_map.102 = (f32[768,192]{1,0:T(8,128)S(1)}, bf16[384,3584]{1,0:T(8,128)(2,1)S(1)}) custom-call(bf16[80,3072]{1,0:T(8,128)(2,1)S(1)} %get-tuple-element.221.refs_0_, bf16[80,3072]{1,0:T(8,128)(2,1)S(1)} %collective-permute-done.24.refs_1_, bf16[80,3072]{1,0:T(8,128)(2,1)S(1)} %collective-permute-done.25.refs_2_, ...), custom_call_target="tpu_custom_call", output_to_operand_aliasing={{0}: (7, {})} | custom-call | flops 1000 | bytes 1000 | tf_op jit(solution)/shard_map/pallas_call | solution.py:454
  172.5 8.1 %collective-permute-start.28 = (bf16[384,3584]{1,0:T(8,128)(2,1)S(1)}, bf16[384,3584]{1,0:T(8,128)(2,1)S(1)}, u32[]{:S(2)}, u32[]{:S(2)}) collective-permute-start(bf16[384,3584]{1,0:T(8,128)(2,1)S(1)} %get-tuple-element.228), channel_id=1, source_target_pairs={{0,1},{1,0},{2,3},{3,2},{4,5},{5,4},{6,7},{7,6},{8,9},{9,8},{10,11... | collective-permute-start | bytes 8257544 | tf_op jit(solution)/shard_map/ppermute | solution.py:62
  185.3 4.4 %shard_map.103 = (bf16[384,3072]{1,0:T(8,128)(2,1)}, f32[2,192,192]{2,1,0:T(8,128)}, f32[2,192,192]{2,1,0:T(8,128)}) custom-call(f32[384,3072]{1,0:T(8,128)S(1)} %shard_map.101.own_ref, bf16[384,3584]{1,0:T(8,128)(2,1)S(1)} %collective-permute-done.28.other_ref, bf16[2,192,192]{2,1,0:T(8,128)(2,1)S(1)} %get-tuple-element.229.left_ref, ...), custom_call_target="tpu_custom_call" | custom-call | flops 1000 | bytes 1000 | tf_op jit(solution)/shard_map/pallas_call | solution.py:538
  (63 shorter events, 52.9 us)
Async XLA Ops:
  8.7 14.0 %collective-permute-start = (bf16[80,3072]{1,0:T(8,128)(2,1)S(1)}, bf16[80,3072]{1,0:T(8,128)(2,1)S(1)}, u32[]{:S(2)}, u32[]{:S(2)}) collective-permute-start(bf16[80,3072]{1,0:T(8,128)(2,1)S(1)} %get-tuple-element.119), channel_id=1, source_target_pairs={{0,8},{1,9},{2,10},{3,11},{4,12},{5,13},{6,14},{7,15}} | collective-permute-start | bytes 1474568 | tf_op jit(solution)/shard_map/ppermute | solution.py:578
  26.9 13.1 %collective-permute-start.1 = (bf16[80,3072]{1,0:T(8,128)(2,1)S(1)}, bf16[80,3072]{1,0:T(8,128)(2,1)S(1)}, u32[]{:S(2)}, u32[]{:S(2)}) collective-permute-start(bf16[80,3072]{1,0:T(8,128)(2,1)S(1)} %get-tuple-element.131), channel_id=1, source_target_pairs={{0,8},{8,16},{1,9},{9,17},{2,10},{10,18},{3,11},{11,19},{4,12},{12... | collective-permute-start | bytes 1474568 | tf_op jit(solution)/shard_map/ppermute | solution.py:578
  44.2 12.1 %collective-permute-start.2 = (bf16[80,3072]{1,0:T(8,128)(2,1)S(1)}, bf16[80,3072]{1,0:T(8,128)(2,1)S(1)}, u32[]{:S(2)}, u32[]{:S(2)}) collective-permute-start(bf16[80,3072]{1,0:T(8,128)(2,1)S(1)} %get-tuple-element.148), channel_id=1, source_target_pairs={{0,8},{8,16},{16,24},{1,9},{9,17},{17,25},{2,10},{10,18},{18,26},{... | collective-permute-start | bytes 1474568 | tf_op jit(solution)/shard_map/ppermute | solution.py:578
  60.6 9.9 %collective-permute-start.3 = (bf16[80,3072]{1,0:T(8,128)(2,1)S(1)}, bf16[80,3072]{1,0:T(8,128)(2,1)S(1)}, u32[]{:S(2)}, u32[]{:S(2)}) collective-permute-start(bf16[80,3072]{1,0:T(8,128)(2,1)S(1)} %get-tuple-element.167), channel_id=1, source_target_pairs={{8,16},{16,24},{9,17},{17,25},{10,18},{18,26},{11,19},{19,27},{12,... | collective-permute-start | bytes 1474568 | tf_op jit(solution)/shard_map/ppermute | solution.py:578
  63.1 9.4 %collective-permute-start.4 = (bf16[80,3072]{1,0:T(8,128)(2,1)S(1)}, bf16[80,3072]{1,0:T(8,128)(2,1)S(1)}, u32[]{:S(2)}, u32[]{:S(2)}) collective-permute-start(bf16[80,3072]{1,0:T(8,128)(2,1)S(1)} %get-tuple-element.178), channel_id=1, source_target_pairs={{24,16},{25,17},{26,18},{27,19},{28,20},{29,21},{30,22},{31,23}} | collective-permute-start | bytes 1474568 | tf_op jit(solution)/shard_map/ppermute | solution.py:586
  63.8 7.3 %collective-permute-start.5 = (bf16[80,768]{1,0:T(8,128)(2,1)S(1)}, bf16[80,768]{1,0:T(8,128)(2,1)S(1)}, u32[]{:S(2)}, u32[]{:S(2)}) collective-permute-start(bf16[80,768]{1,0:T(8,128)(2,1)S(1)} %get-tuple-element.181), channel_id=1, source_target_pairs={{0,2},{1,3},{2,0},{3,1},{4,6},{5,7},{6,4},{7,5},{8,10},{9,11},{10,... | collective-permute-start | bytes 368648 | tf_op jit(solution)/shard_map/ppermute | solution.py:62
  66.5 4.7 %collective-permute-start.6 = (bf16[80,768]{1,0:T(8,128)(2,1)S(1)}, bf16[80,768]{1,0:T(8,128)(2,1)S(1)}, u32[]{:S(2)}, u32[]{:S(2)}) collective-permute-start(bf16[80,768]{1,0:T(8,128)(2,1)S(1)} %get-tuple-element.182), channel_id=1, source_target_pairs={{0,4},{1,5},{2,6},{3,7},{4,0},{5,1},{6,2},{7,3},{8,12},{9,13},{10,... | collective-permute-start | bytes 368648 | tf_op jit(solution)/shard_map/ppermute | solution.py:62
  67.7 4.8 %collective-permute-start.7 = (bf16[80,768]{1,0:T(8,128)(2,1)S(1)}, bf16[80,768]{1,0:T(8,128)(2,1)S(1)}, u32[]{:S(2)}, u32[]{:S(2)}) collective-permute-start(bf16[80,768]{1,0:T(8,128)(2,1)S(1)} %get-tuple-element.183), channel_id=1, source_target_pairs={{0,6},{1,7},{2,4},{3,5},{4,2},{5,3},{6,0},{7,1},{8,14},{9,15},{10,... | collective-permute-start | bytes 368648 | tf_op jit(solution)/shard_map/ppermute | solution.py:62
  70.5 6.5 %collective-permute-start.8 = (bf16[80,3072]{1,0:T(8,128)(2,1)S(1)}, bf16[80,3072]{1,0:T(8,128)(2,1)S(1)}, u32[]{:S(2)}, u32[]{:S(2)}) collective-permute-start(bf16[80,3072]{1,0:T(8,128)(2,1)S(1)} %get-tuple-element.185), channel_id=1, source_target_pairs={{16,24},{17,25},{18,26},{19,27},{20,28},{21,29},{22,30},{23,31}} | collective-permute-start | bytes 1474568 | tf_op jit(solution)/shard_map/ppermute | solution.py:578
  72.5 20.4 %collective-permute-start.9 = (bf16[80,3072]{1,0:T(8,128)(2,1)S(1)}, bf16[80,3072]{1,0:T(8,128)(2,1)S(1)}, u32[]{:S(2)}, u32[]{:S(2)}) collective-permute-start(bf16[80,3072]{1,0:T(8,128)(2,1)S(1)} %get-tuple-element.192), channel_id=1, source_target_pairs={{16,8},{24,16},{17,9},{25,17},{18,10},{26,18},{19,11},{27,19},{20,... | collective-permute-start | bytes 1474568 | tf_op jit(solution)/shard_map/ppermute | solution.py:586
  96.7 11.1 %collective-permute-start.13 = (bf16[80,3072]{1,0:T(8,128)(2,1)S(1)}, bf16[80,3072]{1,0:T(8,128)(2,1)S(1)}, u32[]{:S(2)}, u32[]{:S(2)}) collective-permute-start(bf16[80,3072]{1,0:T(8,128)(2,1)S(1)} %get-tuple-element.200), channel_id=1, source_target_pairs={{8,0},{16,8},{24,16},{9,1},{17,9},{25,17},{10,2},{18,10},{26,18},{... | collective-permute-start | bytes 1474568 | tf_op jit(solution)/shard_map/ppermute | solution.py:586
  98.7 5.6 %collective-permute-start.14 = (bf16[80,768]{1,0:T(8,128)(2,1)S(1)}, bf16[80,768]{1,0:T(8,128)(2,1)S(1)}, u32[]{:S(2)}, u32[]{:S(2)}) collective-permute-start(bf16[80,768]{1,0:T(8,128)(2,1)S(1)} %get-tuple-element.204), channel_id=1, source_target_pairs={{0,2},{1,3},{2,0},{3,1},{4,6},{5,7},{6,4},{7,5},{8,10},{9,11},{10,... | collective-permute-start | bytes 368648 | tf_op jit(solution)/shard_map/ppermute | solution.py:62
  111.7 8.7 %collective-permute-start.18 = (bf16[80,3072]{1,0:T(8,128)(2,1)S(1)}, bf16[80,3072]{1,0:T(8,128)(2,1)S(1)}, u32[]{:S(2)}, u32[]{:S(2)}) collective-permute-start(bf16[80,3072]{1,0:T(8,128)(2,1)S(1)} %get-tuple-element.211.refs_0_), channel_id=1, source_target_pairs={{0,2},{1,3},{2,0},{3,1},{4,6},{5,7},{6,4},{7,5},{8,10},{9,11},{10,... | collective-permute-start | bytes 1474568 | tf_op jit(solution)/shard_map/ppermute | solution.py:62
  114.2 9.9 %collective-permute-start.17 = (bf16[80,3072]{1,0:T(8,128)(2,1)S(1)}, bf16[80,3072]{1,0:T(8,128)(2,1)S(1)}, u32[]{:S(2)}, u32[]{:S(2)}) collective-permute-start(bf16[80,3072]{1,0:T(8,128)(2,1)S(1)} %get-tuple-element.208), channel_id=1, source_target_pairs={{8,0},{16,8},{9,1},{17,9},{10,2},{18,10},{11,3},{19,11},{12,4},{20... | collective-permute-start | bytes 1474568 | tf_op jit(solution)/shard_map/ppermute | solution.py:586
  116.1 8.0 %collective-permute-start.19 = (bf16[80,3072]{1,0:T(8,128)(2,1)S(1)}, bf16[80,3072]{1,0:T(8,128)(2,1)S(1)}, u32[]{:S(2)}, u32[]{:S(2)}) collective-permute-start(bf16[80,3072]{1,0:T(8,128)(2,1)S(1)} %get-tuple-element.211.refs_0_), channel_id=1, source_target_pairs={{0,4},{1,5},{2,6},{3,7},{4,0},{5,1},{6,2},{7,3},{8,12},{9,13},{10,... | collective-permute-start | bytes 1474568 | tf_op jit(solution)/shard_map/ppermute | solution.py:62
  120.4 13.5 %collective-permute-start.23 = (bf16[80,3072]{1,0:T(8,128)(2,1)S(1)}, bf16[80,3072]{1,0:T(8,128)(2,1)S(1)}, u32[]{:S(2)}, u32[]{:S(2)}) collective-permute-start(bf16[80,3072]{1,0:T(8,128)(2,1)S(1)} %collective-permute-done.18.refs_6_.refs_1_), channel_id=1, source_target_pairs={{0,4},{1,5},{2,6},{3,7},{4,0},{5,1},{6,2},{7,3},{8,12},{9,13},{10,... | collective-permute-start | bytes 1474568 | tf_op jit(solution)/shard_map/ppermute | solution.py:62
  128.0 10.9 %collective-permute-start.20 = (bf16[80,3072]{1,0:T(8,128)(2,1)S(1)}, bf16[80,3072]{1,0:T(8,128)(2,1)S(1)}, u32[]{:S(2)}, u32[]{:S(2)}) collective-permute-start(bf16[80,3072]{1,0:T(8,128)(2,1)S(1)} %get-tuple-element.213), channel_id=1, source_target_pairs={{8,0},{9,1},{10,2},{11,3},{12,4},{13,5},{14,6},{15,7}} | collective-permute-start | bytes 1474568 | tf_op jit(solution)/shard_map/ppermute | solution.py:586
  129.5 14.9 %collective-permute-start.22 = (bf16[80,3072]{1,0:T(8,128)(2,1)S(1)}, bf16[80,3072]{1,0:T(8,128)(2,1)S(1)}, u32[]{:S(2)}, u32[]{:S(2)}) collective-permute-start(bf16[80,3072]{1,0:T(8,128)(2,1)S(1)} %get-tuple-element.215.refs_0_), channel_id=1, source_target_pairs={{0,4},{1,5},{2,6},{3,7},{4,0},{5,1},{6,2},{7,3},{8,12},{9,13},{10,... | collective-permute-start | bytes 1474568 | tf_op jit(solution)/shard_map/ppermute | solution.py:62
  130.8 13.6 %collective-permute-start.21 = (bf16[80,3072]{1,0:T(8,128)(2,1)S(1)}, bf16[80,3072]{1,0:T(8,128)(2,1)S(1)}, u32[]{:S(2)}, u32[]{:S(2)}) collective-permute-start(bf16[80,3072]{1,0:T(8,128)(2,1)S(1)} %get-tuple-element.215.refs_0_), channel_id=1, source_target_pairs={{0,2},{1,3},{2,0},{3,1},{4,6},{5,7},{6,4},{7,5},{8,10},{9,11},{10,... | collective-permute-start | bytes 1474568 | tf_op jit(solution)/shard_map/ppermute | solution.py:62
  145.2 11.0 %collective-permute-start.24 = (bf16[80,3072]{1,0:T(8,128)(2,1)S(1)}, bf16[80,3072]{1,0:T(8,128)(2,1)S(1)}, u32[]{:S(2)}, u32[]{:S(2)}) collective-permute-start(bf16[80,3072]{1,0:T(8,128)(2,1)S(1)} %get-tuple-element.221.refs_0_), channel_id=1, source_target_pairs={{0,2},{1,3},{2,0},{3,1},{4,6},{5,7},{6,4},{7,5},{8,10},{9,11},{10,... | collective-permute-start | bytes 1474568 | tf_op jit(solution)/shard_map/ppermute | solution.py:62
  146.3 18.3 %collective-permute-start.27 = (bf16[80,3072]{1,0:T(8,128)(2,1)S(1)}, bf16[80,3072]{1,0:T(8,128)(2,1)S(1)}, u32[]{:S(2)}, u32[]{:S(2)}) collective-permute-start(bf16[80,3072]{1,0:T(8,128)(2,1)S(1)} %collective-permute-done.22.refs_6_.refs_2_), channel_id=1, source_target_pairs={{0,2},{1,3},{2,0},{3,1},{4,6},{5,7},{6,4},{7,5},{8,10},{9,11},{10,... | collective-permute-start | bytes 1474568 | tf_op jit(solution)/shard_map/ppermute | solution.py:62
  146.7 23.0 %collective-permute-start.25 = (bf16[80,3072]{1,0:T(8,128)(2,1)S(1)}, bf16[80,3072]{1,0:T(8,128)(2,1)S(1)}, u32[]{:S(2)}, u32[]{:S(2)}) collective-permute-start(bf16[80,3072]{1,0:T(8,128)(2,1)S(1)} %get-tuple-element.221.refs_0_), channel_id=1, source_target_pairs={{0,4},{1,5},{2,6},{3,7},{4,0},{5,1},{6,2},{7,3},{8,12},{9,13},{10,... | collective-permute-start | bytes 1474568 | tf_op jit(solution)/shard_map/ppermute | solution.py:62
  156.2 13.4 %collective-permute-start.26 = (bf16[80,3072]{1,0:T(8,128)(2,1)S(1)}, bf16[80,3072]{1,0:T(8,128)(2,1)S(1)}, u32[]{:S(2)}, u32[]{:S(2)}) collective-permute-start(bf16[80,3072]{1,0:T(8,128)(2,1)S(1)} %collective-permute-done.24.refs_1_), channel_id=1, source_target_pairs={{0,4},{1,5},{2,6},{3,7},{4,0},{5,1},{6,2},{7,3},{8,12},{9,13},{10,... | collective-permute-start | bytes 1474568 | tf_op jit(solution)/shard_map/ppermute | solution.py:62
  172.5 12.8 %collective-permute-start.28 = (bf16[384,3584]{1,0:T(8,128)(2,1)S(1)}, bf16[384,3584]{1,0:T(8,128)(2,1)S(1)}, u32[]{:S(2)}, u32[]{:S(2)}) collective-permute-start(bf16[384,3584]{1,0:T(8,128)(2,1)S(1)} %get-tuple-element.228), channel_id=1, source_target_pairs={{0,1},{1,0},{2,3},{3,2},{4,5},{5,4},{6,7},{7,6},{8,9},{9,8},{10,11... | collective-permute-start | bytes 8257544 | tf_op jit(solution)/shard_map/ppermute | solution.py:62
  (10 other events, 98.1 us)

commit v5 on v4

--- a/solution.py
+++ b/solution.py
@@ -265,10 +265,13 @@
 
 def backward_kernel(tick, sections, span, late, *refs):
     keeps = len(span)
-    lead = 4 if tick > sections - 1 else 3
-    w_ref, slope_ref, cot_ref = refs[:3]
-    from_ref = refs[3] if lead == 4 else None
-    outs = refs[lead + keeps + late :]
+    refs = refs[late:]
+    w_ref, slope_ref = refs[:2]
+    chained = tick > sections - 1
+    opens = tick - (sections - 1) < PIECES
+    cot_ref = refs[2] if opens else None
+    from_ref = refs[2 + opens + keeps] if chained else None
+    outs = refs[2 + opens + keeps + chained :]
     next_ref, kept = outs[0], outs[2 : 2 + keeps]
     flow, scaled = outs[2 + keeps :]
     here = lax.axis_index("section")
@@ -276,7 +279,7 @@
 
     @pl.when(jnp.logical_and(piece >= 0, piece < PIECES))
     def _():
-        if 0 <= tick - (sections - 1) < PIECES:
+        if opens:
 
             @pl.when(here == sections - 1)
             def _():
@@ -309,23 +312,27 @@
     high = min(PIECES - 1, tick - (sections - 1))
     span = list(range(low, high + 1))
     first = [] if arrived is None else [resident(arrived)]
-    base = 3 + len(first)
+    opens = [resident(cotangent)] if tick - (sections - 1) < PIECES else []
+    base = 2 + len(after) + len(opens)
     out = pl.pallas_call(
         functools.partial(backward_kernel, tick, sections, span, len(after)),
         out_shape=(near(PIECE, D), near(D, D), *[near(PIECE, D) for _ in span]),
-        in_specs=[VM] * (base + len(span)) + [HB] * len(after),
+        in_specs=[HB] * len(after) + [VM] * (2 + len(opens) + len(span) + len(first)),
         out_specs=[VM] * (2 + len(span)),
         scratch_shapes=[pltpu.VMEM((PIECE, D), BF), pltpu.VMEM((PIECE, D), BF)],
-        input_output_aliases={0: 1, **{base + k: 2 + k for k in range(len(span))}},
+        input_output_aliases={
+            len(after): 1,
+            **{base + k: 2 + k for k in range(len(span))},
+        },
         compiler_params=limit(4),
         cost_estimate=SMALL,
     )(
+        *after,
         resident(matrix),
         resident(slopes),
-        resident(cotangent),
+        *opens,
+        *[resident(kept[k]) for k in span],
         *first,
-        *[resident(kept[k]) for k in span],
-        *after,
     )
     kept = list(kept)
     for k, index in enumerate(span):
@@ -335,17 +342,20 @@
 
 def prepare_kernel(chips, blocks, *refs):
     parts = refs[: chips * PIECES]
-    pin_ref, pout_ref, xt_ref, gram_ref, left_ref, right_ref = refs[chips * PIECES :]
+    pin_ref, pout_ref, gram_ref, left_ref, right_ref = refs[chips * PIECES : chips * PIECES + 5]
+    turned = refs[chips * PIECES + 5 :]
     for piece in range(PIECES):
-        both = jnp.concatenate(
-            [part[...] for part in parts[piece * chips : (piece + 1) * chips]], axis=0
-        )
-        xt_ref[piece] = both.T
+        some = [part[...] for part in parts[piece * chips : (piece + 1) * chips]]
+        if piece < PIECES - 1:
+            turned[piece][...] = jnp.concatenate(some, axis=0).T
+        else:
+            turned[piece][...] = jnp.concatenate(some[:-1], axis=0).T
+            turned[piece + 1][...] = some[-1].T
     for block in range(2 * blocks):
         rows = slice(block * BLOCK, (block + 1) * BLOCK)
         gram = jnp.zeros((BLOCK, BLOCK), F32)
-        for piece in range(PIECES):
-            some = xt_ref[piece, rows, :]
+        for ref in turned:
+            some = ref[rows, :]
             gram = gram + contract_last(some, some)
         gram_ref[rows, :] = gram
     for block in range(blocks):
@@ -369,20 +379,22 @@
     return pl.pallas_call(
         functools.partial(prepare_kernel, chips, blocks),
         out_shape=(
-            near(PIECES, width, chips * PIECE),
             near(width, BLOCK, kind=F32),
             near(blocks, BLOCK, BLOCK),
             near(NBLK // 2, PAIR, PAIR),
+            *[near(width, chips * PIECE)] * (PIECES - 1),
+            near(width, (chips - 1) * PIECE),
+            near(width, PIECE),
         ),
         in_specs=[VM] * (len(flat) + 2),
-        out_specs=(VM, VM, VM, VM),
+        out_specs=[VM] * (4 + PIECES),
         compiler_params=limit(8),
         cost_estimate=SMALL,
     )(*[resident(p) for p in flat], inverse_in, inverse_out)
 
 
-def add_gram(chips, every, gram_ref, begins):
-    width = D // chips
+def add_gram(every, gram_ref, begins):
+    width = gram_ref.shape[0]
     chip = lax.div(lax.axis_index("dp"), 2)
     columns = pl.ds(pl.multiple_of(chip * width, 128), width)
     turned = every[:, columns].T
@@ -402,122 +414,111 @@
     return pl.ds(pl.multiple_of((core if mine else 1 - core) * own, 16), own)
 
 
-def gather_kernel(chips, index, *refs):
-    parts = refs[:chips]
-    xt_ref = refs[chips]
+def gather_kernel(count, begins, *refs):
+    parts = refs[:count]
+    xt_ref = refs[count]
     own_ref, other_ref, gram_ref, every = refs[-4:]
     fill(parts, every)
-    add_gram(chips, every, gram_ref, index == 0)
+    add_gram(every, gram_ref, begins)
     for mine, acc_ref in ((True, own_ref), (False, other_ref)):
         rows = half_rows(mine, acc_ref.shape[0])
 
         @pl.loop(0, D // LOAD)
         def _(step):
             columns = pl.ds(pl.multiple_of(step * LOAD, LOAD), LOAD)
-            term = jnp.dot(xt_ref[index, rows, :], every[:, columns], preferred_element_type=F32)
-            acc_ref[:, columns] = term if index == 0 else acc_ref[:, columns] + term
-
-
-def gather(chips, index, parts, turned, so_far):
-    width = D // chips
+            term = jnp.dot(xt_ref[rows, :], every[:, columns], preferred_element_type=F32)
+            acc_ref[:, columns] = term if begins else acc_ref[:, columns] + term
+
+
+def gather(parts, turned, so_far):
+    count = len(parts)
+    width = turned.shape[0]
     half = near(width // 2, D, kind=F32)
     return pl.pallas_call(
-        functools.partial(gather_kernel, chips, index),
+        functools.partial(gather_kernel, count, not so_far),
         out_shape=(half, half, near(width, BLOCK, kind=F32)),
-        in_specs=[VM] * (chips + 1 + len(so_far)),
+        in_specs=[VM] * (count + 1 + len(so_far)),
         out_specs=(VM, VM, VM),
-        scratch_shapes=[pltpu.VMEM((chips * PIECE, D), BF)],
-        input_output_aliases={chips + 1 + k: k for k in range(len(so_far))},
+        scratch_shapes=[pltpu.VMEM((count * PIECE, D), BF)],
+        input_output_aliases={count + 1 + k: k for k in range(len(so_far))},
         compiler_params=limit(8),
         cost_estimate=SMALL,
     )(*[resident(p) for p in parts], resident(turned), *[resident(a) for a in so_far])
 
 
-def other_kernel(chips, *refs):
-    parts = refs[:chips]
-    xt_ref, acc_ref, gram_in_ref, gram_ref, _, out_ref, every = refs[chips:]
+def other_kernel(part, xt_ref, acc_ref, gram_in_ref, gram_ref, _, out_ref):
     rows = half_rows(False, acc_ref.shape[0])
-    fill(parts, every)
-    add_gram(chips, every, gram_ref, False)
+    add_gram(part, gram_ref, False)
     out_ref[:, D : D + BLOCK] = gram_ref[rows, :].astype(BF)
     out_ref[:, D + SIDE : D + SIDE + BLOCK] = gram_in_ref[rows, :].astype(BF)
 
     @pl.loop(0, D // LOAD)
     def _(step):
         columns = pl.ds(pl.multiple_of(step * LOAD, LOAD), LOAD)
-        term = jnp.dot(xt_ref[PIECES - 1, rows, :], every[:, columns], preferred_element_type=F32)
+        term = jnp.dot(xt_ref[rows, :], part[:, columns], preferred_element_type=F32)
         out_ref[:, columns] = (term + acc_ref[:, columns]).astype(BF)
 
 
-def other_half(chips, parts, turned, acc, gram_in, gram_out):
-    width = D // chips
+def other_half(part, turned, acc, gram_in, gram_out):
+    width = turned.shape[0]
     return pl.pallas_call(
-        functools.partial(other_kernel, chips),
+        other_kernel,
         out_shape=(near(width, BLOCK, kind=F32), near(width // 2, D + 2 * SIDE)),
-        in_specs=[VM] * (chips + 4),
+        in_specs=[VM] * 5,
         out_specs=(VM, VM),
-        scratch_shapes=[pltpu.VMEM((chips * PIECE, D), BF)],
-        input_output_aliases={chips + 3: 0},
+        input_output_aliases={4: 0},
         compiler_params=limit(8),
         cost_estimate=SMALL,
-    )(
-        *[resident(p) for p in parts],
-        resident(turned),
-        resident(acc),
-        resident(gram_in),
-        resident(gram_out),
-    )
-
-
-def own_kernel(chips, *refs):
-    parts = refs[:chips]
-    xt_ref, acc_ref, out_ref, every = refs[chips:]
+    )(resident(part), resident(turned), resident(acc), resident(gram_in), resident(gram_out))
+
+
+def own_kernel(part, xt_ref, acc_ref, out_ref):
     rows = half_rows(True, acc_ref.shape[0])
-    fill(parts, every)
 
     @pl.loop(0, D // LOAD)
     def _(step):
         columns = pl.ds(pl.multiple_of(step * LOAD, LOAD), LOAD)
-        term = jnp.dot(xt_ref[PIECES - 1, rows, :], every[:, columns], preferred_element_type=F32)
+        term = jnp.dot(xt_ref[rows, :], part[:, columns], preferred_element_type=F32)
         out_ref[:, columns] = term + acc_ref[:, columns]
 
 
-def own_half(chips, parts, turned, acc):
+def own_half(part, turned, acc):
     return pl.pallas_call(
-        functools.partial(own_kernel, chips),
+        own_kernel,
         out_shape=near(*acc.shape, kind=F32),
-        in_specs=[VM] * (chips + 2),
+        in_specs=[VM] * 3,
         out_specs=VM,
-        scratch_shapes=[pltpu.VMEM((chips * PIECE, D), BF)],
-        input_output_aliases={chips + 1: 0},
+        input_output_aliases={2: 0},
         compiler_params=limit(8),
         cost_estimate=SMALL,
-    )(*[resident(p) for p in parts], resident(turned), resident(acc))
+    )(resident(part), resident(turned), resident(acc))
 
 
 def finish_kernel(blocks, total, own_ref, other_ref, left_ref, right_ref, *refs):
     gram_in_ref, gram_out_ref, update_ref, factor_in_ref, factor_out_ref, ready, sems = refs
-    step_width = 2 * PAIR
-    copies = []
     core = lax.rem(lax.axis_index("dp"), 2)
-    for step in range(D // step_width):
-        columns = slice(step * step_width, (step + 1) * step_width)
+    scale = 1.0 / math.sqrt(total)
+    pairs = D // PAIR
+    for step in range(D // (2 * PAIR)):
+        columns = slice(step * 2 * PAIR, (step + 1) * 2 * PAIR)
         grad = (own_ref[:, columns] + other_ref[:, columns].astype(F32)).astype(BF)
         for block in range(blocks):
             rows = slice(block * BLOCK, (block + 1) * BLOCK)
-            left = jnp.dot(left_ref[block], grad[rows], preferred_element_type=F32).astype(BF)
-            for side in range(2):
-                right = jnp.dot(
-                    left[:, side * PAIR : (side + 1) * PAIR],
-                    right_ref[2 * step + side],
-                    preferred_element_type=F32,
-                )
-                ready[step, rows, side * PAIR : (side + 1) * PAIR] = (
-                    right * (1.0 / math.sqrt(total))
-                ).astype(BF)
-        copy = pltpu.make_async_copy(ready.at[step], update_ref.at[:, columns], sems.at[step])
-        copy.start()
-        copies.append(copy)
+            ready[rows, columns] = jnp.dot(
+                left_ref[block], grad[rows], preferred_element_type=F32
+            ).astype(BF)
+    copies = []
+    for pair in range(pairs):
+        columns = slice(pair * PAIR, (pair + 1) * PAIR)
+        right = jnp.dot(ready[:, columns], right_ref[pair], preferred_element_type=F32)
+        ready[:, columns] = (right * scale).astype(BF)
+        if pair % 2:
+            columns = slice((pair - 1) * PAIR, (pair + 1) * PAIR)
+            copy = pltpu.make_async_copy(
+                ready.at[:, columns], update_ref.at[:, columns], sems.at[pair // 2]
+            )
+            copy.start()
+            copies.append(copy)
     for block in range(blocks):
         rows = slice(block * BLOCK, (block + 1) * BLOCK)
         start = pl.multiple_of((core * blocks + block) * BLOCK, BLOCK)
@@ -541,7 +542,7 @@
         in_specs=[VM] * 6,
         out_specs=(HB, VM, VM),
         scratch_shapes=[
-            pltpu.VMEM((steps, blocks * BLOCK, 2 * PAIR), BF),
+            pltpu.VMEM((blocks * BLOCK, D), BF),
             pltpu.SemaphoreType.DMA((steps,)),
         ],
         compiler_params=limit(8),
@@ -589,11 +590,13 @@
             if 1 <= known <= PIECES:
                 after = crossed[known - 1][1:]
             if known == PIECES:
-                rows_turned, gram_in, left, right = prepare(crossed, inverse_in[0], inverse_out[0])
-            if done >= 1:
+                gram_in, left, right, *rows_turned = prepare(
+                    crossed, inverse_in[0], inverse_out[0]
+                )
+            if 1 <= done == PIECES - 1:
                 after = after + [parts[done - 1][o] for o in single]
             if done >= 2:
-                acc = gather(chips, done - 2, parts[done - 2], rows_turned, acc)
+                acc = gather(parts[done - 2], rows_turned[done - 2], acc)
                 after = after + [acc[2]]
             behind, turned, kept = backward(
                 tick, sections, arrived_behind, turned, slopes, packed_cot, kept, after
@@ -607,10 +610,11 @@
                 bit = offset & -offset if done % 2 else 1 << (offset.bit_length() - 1)
                 piece.append(swap(piece[offset ^ bit], ranks, 2 * bit))
             parts.append(piece)
-    acc = gather(chips, PIECES - 2, parts[PIECES - 2], rows_turned, acc)
-    gram_out, other = other_half(chips, parts[-1], rows_turned, acc[1], gram_in, acc[2])
+    acc = gather(parts[-1][:-1], rows_turned[-2], acc)
+    acc = gather(parts[-2], rows_turned[-3], acc)
+    gram_out, other = other_half(parts[-1][-1], rows_turned[-1], acc[1], gram_in, acc[2])
     other = swap(other, ranks, 1)
-    own = own_half(chips, parts[-1], rows_turned, acc[0])
+    own = own_half(parts[-1][-1], rows_turned[-1], acc[0])
     update, factor_in, factor_out = finish(
         inverse_in.shape[1], total, own, other, left, right, gram_in, gram_out
     )

time: 190 us -> 187 us (0.984)
  waiting for transfers between devices: 79.9 us -> 72.6 us
  starting transfers between devices: 45.4 us -> 47.7 us
  Pallas kernels: 62.8 us -> 64.8 us
    ppermute x19, waiting for transfers between devices: 37.3 us -> 29.7 us  [swap(): return lax.ppermute(x, 'dp', [(r, r ^ flip) for r in range(ranks)])]
    ppermute x19, starting transfers between devices: 29.5 us -> 32 us  [swap(): return lax.ppermute(x, 'dp', [(r, r ^ flip) for r in range(ranks)])]
    pallas_call x4 -> x5, Pallas kernels: 15.1 us -> 17 us  [the longest x3 13.6 us: gather(): pl.pallas_call(functools.partial(gather_kernel, count, not so_far), out_s...]
  transfers between devices with their start and end apart: 29 -> 29, of which waited for: 19 -> 20; matrix products, arithmetic and copies ran while one was open for 0% -> 0% of each run, Pallas kernels for 14% -> 16%
where the time goes in v5:
time: 187 us
  waiting for transfers between devices  72.6 us (39%)
  Pallas kernels  64.8 us (35%)
  starting transfers between devices  47.7 us (26%)
    ppermute x19, starting transfers between devices, swap(): return lax.ppermute(x, 'dp', [(r, r ^ flip) for r in range(ranks)])  32 us
    ppermute x19, waiting for transfers between devices, swap(): return lax.ppermute(x, 'dp', [(r, r ^ flip) for r in range(ranks)])  29.7 us
    ppermute x5, waiting for transfers between devices, shards(): arrived_ahead = lax.ppermute(ahead, 'section', pairs)  29.2 us
    ppermute x5, waiting for transfers between devices, shards(): arrived_behind = lax.ppermute(behind, 'section', pairs)  13.7 us
    pallas_call x5, Pallas kernels, forward(): pl.pallas_call(functools.partial(forward_kernel, tick, span, count), out_...  13.7 us
    pallas_call x3, Pallas kernels, gather(): pl.pallas_call(functools.partial(gather_kernel, count, not so_far), out_s...  13.6 us
    pallas_call x6, Pallas kernels, backward(): pl.pallas_call(functools.partial(backward_kernel, tick, sections, span, l...  12.5 us
    ppermute x5, starting transfers between devices, shards(): arrived_ahead = lax.ppermute(ahead, 'section', pairs)  8.59 us
  transfers between devices with their start and end apart: 29, of which 20 were waited for; matrix products, arithmetic and copies ran while one was open for 0% of the time, Pallas kernels for 16%

profile of v5, /device:TPU:9, one launch (start us, length us, event | category | flops | bytes accessed | tf_op | source)
XLA Modules:
  0.0 186.8 jit_solution(10804370522254755540)
XLA Ops:
  1.3 7.4 %shard_map.85 = (bf16[3072,3072]{1,0:T(8,128)(2,1)S(1)}, bf16[80,3072]{1,0:T(8,128)(2,1)S(1)}, bf16[3,80,3072]{2,1,0:T(8,128)(2,1)S(1)}, bf16[3,80,3072]{2,1,0:T...) custom-call(s32[1,4]{1,0:T(1,128)S(1)} %copy-done.4, ...), custom_call_target="tpu_custom_call" | custom-call | flops 1000 | bytes 1000 | tf_op jit(solution)/shard_map/pallas_call | solution.py:158
  10.0 12.7 %collective-permute-done.from_ref = bf16[80,3072]{1,0:T(8,128)(2,1)S(1)} collective-permute-done((bf16[80,3072]{1,0:T(8,128)(2,1)S(1)}, bf16[80,3072]{1,0:T(8,128)(2,1)S(1)}, u32[]{:S(2)}, u32[]{:S(2)}) %collective-permute-start) | collective-permute-done | bytes 491552 | tf_op jit(solution)/shard_map/ppermute | solution.py:579
  22.6 4.3 %shard_map.86 = (bf16[80,3072]{1,0:T(8,128)(2,1)S(1)}, bf16[3072,3072]{1,0:T(8,128)(2,1)S(1)}, bf16[3,80,3072]{2,1,0:T(8,128)(2,1)S(1)}, bf16[80,768]{1,0:T(8,12...) custom-call(bf16[80,3072]{1,0:T(8,128)(2,1)S(1)} %collective-permute, ...), custom_call_target="tpu_custom_call", output_to_operand_aliasing={{1}: (2, {}), {2}: (3, {}), {3}: (4, {}), {4}: (5, {}), {5}... | custom-call | flops 1000 | bytes 1000 | tf_op jit(solution)/shard_map/pallas_call | solution.py:213
  28.9 11.1 %collective-permute-done.1.from_ref = bf16[80,3072]{1,0:T(8,128)(2,1)S(1)} collective-permute-done((bf16[80,3072]{1,0:T(8,128)(2,1)S(1)}, bf16[80,3072]{1,0:T(8,128)(2,1)S(1)}, u32[]{:S(2)}, u32[]{:S(2)}) %collective-permute-start.1) | collective-permute-done | bytes 491552 | tf_op jit(solution)/shard_map/ppermute | solution.py:579
  40.0 4.3 %shard_map.87 = (bf16[80,3072]{1,0:T(8,128)(2,1)S(1)}, bf16[3072,3072]{1,0:T(8,128)(2,1)S(1)}, bf16[3,80,3072]{2,1,0:T(8,128)(2,1)S(1)}, bf16[80,768]{1,0:T(8,12...) custom-call(bf16[80,3072]{1,0:T(8,128)(2,1)S(1)} %collective-permute, ...), custom_call_target="tpu_custom_call", output_to_operand_aliasing={{1}: (2, {}), {2}: (3, {}), {3}: (4, {}), {4}: (5, {}), {5}... | custom-call | flops 1000 | bytes 1000 | tf_op jit(solution)/shard_map/pallas_call | solution.py:213
  46.6 7.3 %shard_map.88 = (bf16[3072,3072]{1,0:T(8,128)(2,1)S(1)}, bf16[3072,3072]{1,0:T(8,128)(2,1)S(1)}) custom-call(bf16[3072,3072]{1,0:T(8,128)(2,1)S(1)} %get-tuple-element.153.w_ref), custom_call_target="tpu_custom_call", output_to_operand_aliasing={{0}: (0, {})} | custom-call | flops 1000 | bytes 1000 | tf_op jit(solution)/shard_map/pallas_call | solution.py:255
  56.5 4.3 %shard_map.89 = (bf16[80,3072]{1,0:T(8,128)(2,1)S(1)}, bf16[3072,3072]{1,0:T(8,128)(2,1)S(1)}, bf16[3,80,3072]{2,1,0:T(8,128)(2,1)S(1)}, bf16[80,768]{1,0:T(8,12...) custom-call(bf16[80,3072]{1,0:T(8,128)(2,1)S(1)} %collective-permute, ...), custom_call_target="tpu_custom_call", output_to_operand_aliasing={{1}: (2, {}), {2}: (3, {}), {3}: (4, {}), {4}: (5, {}), {5}... | custom-call | flops 1000 | bytes 1000 | tf_op jit(solution)/shard_map/pallas_call | solution.py:213
  64.1 2.7 %collective-permute-start.11 = (bf16[80,768]{1,0:T(8,128)(2,1)S(1)}, bf16[80,768]{1,0:T(8,128)(2,1)S(1)}, u32[]{:S(2)}, u32[]{:S(2)}) collective-permute-start(bf16[80,768]{1,0:T(8,128)(2,1)S(1)} %get-tuple-element.192), channel_id=1, source_target_pairs={{0,2},{1,3},{2,0},{3,1},{4,6},{5,7},{6,4},{7,5},{8,10},{9,11},{10,... | collective-permute-start | bytes 368648 | tf_op jit(solution)/shard_map/ppermute | solution.py:62
  68.0 2.7 %collective-permute-done.3.from_ref = bf16[80,3072]{1,0:T(8,128)(2,1)S(1)} collective-permute-done((bf16[80,3072]{1,0:T(8,128)(2,1)S(1)}, bf16[80,3072]{1,0:T(8,128)(2,1)S(1)}, u32[]{:S(2)}, u32[]{:S(2)}) %collective-permute-start.3) | collective-permute-done | bytes 491552 | tf_op jit(solution)/shard_map/ppermute | solution.py:579
  81.8 11.5 %collective-permute-done.15.refs_9_ = bf16[80,3072]{1,0:T(8,128)(2,1)S(1)} collective-permute-done((bf16[80,3072]{1,0:T(8,128)(2,1)S(1)}, bf16[80,3072]{1,0:T(8,128)(2,1)S(1)}, u32[]{:S(2)}, u32[]{:S(2)}) %collective-permute-start.15) | collective-permute-done | bytes 491552 | tf_op jit(solution)/shard_map/ppermute | solution.py:587
  93.3 3.9 %shard_map.94 = (bf16[80,3072]{1,0:T(8,128)(2,1)S(1)}, bf16[3072,3072]{1,0:T(8,128)(2,1)S(1)}, bf16[80,3072]{1,0:T(8,128)(2,1)S(1)}, bf16[80,3072]{1,0:T(8,128)(2,1)S(1)}, bf16[80,3072]{1,0:T(8,128)(2,1)S(1)}) custom-call(bf16[80,768]{1,0:T(8,128)(2,1)S(1)} %collective-permute-done.8.refs_0_., ...), custom_call_target="tpu_custom_call", output_to_operand_aliasing={{1}: (3, {}), {2}: (6, {}), {3}: (7, {}), {4}: (8, {})} | custom-call | flops 1000 | bytes 1000 | tf_op jit(solution)/shard_map/pallas_call | solution.py:317
  99.1 3.3 %collective-permute-start.5 = (bf16[80,768]{1,0:T(8,128)(2,1)S(1)}, bf16[80,768]{1,0:T(8,128)(2,1)S(1)}, u32[]{:S(2)}, u32[]{:S(2)}) collective-permute-start(bf16[80,768]{1,0:T(8,128)(2,1)S(1)} %get-tuple-element.186), channel_id=1, source_target_pairs={{0,2},{1,3},{2,0},{3,1},{4,6},{5,7},{6,4},{7,5},{8,10},{9,11},{10,... | collective-permute-start | bytes 368648 | tf_op jit(solution)/shard_map/ppermute | solution.py:62
  108.3 3.9 %shard_map.95 = (bf16[80,3072]{1,0:T(8,128)(2,1)S(1)}, bf16[3072,3072]{1,0:T(8,128)(2,1)S(1)}, bf16[80,3072]{1,0:T(8,128)(2,1)S(1)}, bf16[80,3072]{1,0:T(8,128)(2,1)S(1)}, bf16[80,3072]{1,0:T(8,128)(2,1)S(1)}) custom-call(bf16[80,768]{1,0:T(8,128)(2,1)S(1)} %collective-permute-done.5.refs_0_., ...), custom_call_target="tpu_custom_call", output_to_operand_aliasing={{1}: (3, {}), {2}: (5, {}), {3}: (6, {}), {4}: (7, {})} | custom-call | flops 1000 | bytes 1000 | tf_op jit(solution)/shard_map/pallas_call | solution.py:317
  117.9 3.0 %collective-permute-done.20.refs_1_ = bf16[80,3072]{1,0:T(8,128)(2,1)S(1)} collective-permute-done((bf16[80,3072]{1,0:T(8,128)(2,1)S(1)}, bf16[80,3072]{1,0:T(8,128)(2,1)S(1)}, u32[]{:S(2)}, u32[]{:S(2)}) %collective-permute-start.20) | collective-permute-done | bytes 491552 | tf_op jit(solution)/shard_map/ppermute | solution.py:62
  124.5 3.9 %shard_map.96 = (bf16[80,3072]{1,0:T(8,128)(2,1)S(1)}, bf16[3072,3072]{1,0:T(8,128)(2,1)S(1)}, bf16[80,3072]{1,0:T(8,128)(2,1)S(1)}, bf16[80,3072]{1,0:T(8,128)(2,1)S(1)}) custom-call(bf16[3072,3072]{1,0:T(8,128)(2,1)S(1)} %get-tuple-element.213.refs_0_, ...), custom_call_target="tpu_custom_call", output_to_operand_aliasing={{1}: (0, {}), {2}: (2, {}), {3}: (3, {})} | custom-call | flops 1000 | bytes 1000 | tf_op jit(solution)/shard_map/pallas_call | solution.py:317
  131.2 2.9 %shard_map.97 = (f32[768,192]{1,0:T(8,128)S(1)}, bf16[2,192,192]{2,1,0:T(8,128)(2,1)S(1)}, bf16[8,384,384]{2,1,0:T(8,128)(2,1)S(1)}, bf16[768,320]{1,0:T(8,128)(...) custom-call(bf16[80,768]{1,0:T(8,128)(2,1)S(1)} %get-tuple-element.219.refs_0_, ...), custom_call_target="tpu_custom_call" | custom-call | flops 1000 | bytes 1000 | tf_op jit(solution)/shard_map/pallas_call | solution.py:379
  134.3 5.0 %shard_map.98 = (f32[384,3072]{1,0:T(8,128)S(1)}, f32[384,3072]{1,0:T(8,128)S(1)}, f32[768,192]{1,0:T(8,128)S(1)}) custom-call(bf16[80,3072]{1,0:T(8,128)(2,1)S(1)} %get-tuple-element.218.refs_0_, bf16[80,3072]{1,0:T(8,128)(2,1)S(1)} %collective-permute-done.20.refs_1_, bf16[80,3072]{1,0:T(8,128)(2,1)S(1)} %collective-permute-done.21.refs_2_, ...), custom_call_target="tpu_custom_call" | custom-call | flops 1000 | bytes 1000 | tf_op jit(solution)/shard_map/pallas_call | solution.py:437
  139.3 5.6 %collective-permute-done.19.refs_1_.refs_2_ = bf16[80,3072]{1,0:T(8,128)(2,1)S(1)} collective-permute-done((bf16[80,3072]{1,0:T(8,128)(2,1)S(1)}, bf16[80,3072]{1,0:T(8,128)(2,1)S(1)}, u32[]{:S(2)}, u32[]{:S(2)}) %collective-permute-start.19) | collective-permute-done | bytes 491552 | tf_op jit(solution)/shard_map/ppermute | solution.py:62
  148.4 5.0 %collective-permute-done.24.refs_1_ = bf16[80,3072]{1,0:T(8,128)(2,1)S(1)} collective-permute-done((bf16[80,3072]{1,0:T(8,128)(2,1)S(1)}, bf16[80,3072]{1,0:T(8,128)(2,1)S(1)}, u32[]{:S(2)}, u32[]{:S(2)}) %collective-permute-start.24) | collective-permute-done | bytes 491552 | tf_op jit(solution)/shard_map/ppermute | solution.py:62
  155.9 3.6 %shard_map.100 = (f32[384,3072]{1,0:T(8,128)S(1)}, f32[384,3072]{1,0:T(8,128)S(1)}, f32[768,192]{1,0:T(8,128)S(1)}) custom-call(bf16[80,3072]{1,0:T(8,128)(2,1)S(1)} %get-tuple-element.227.refs_0_, bf16[80,3072]{1,0:T(8,128)(2,1)S(1)} %collective-permute-done.24.refs_1_, ...), custom_call_target="tpu_custom_call", output_to_operand_aliasing={{0}: (4, {}), {1}: (5, {}), {2}: (6, {})} | custom-call | flops 1000 | bytes 1000 | tf_op jit(solution)/shard_map/pallas_call | solution.py:437
  161.0 5.0 %shard_map.101 = (f32[384,3072]{1,0:T(8,128)S(1)}, f32[384,3072]{1,0:T(8,128)S(1)}, f32[768,192]{1,0:T(8,128)S(1)}) custom-call(bf16[80,3072]{1,0:T(8,128)(2,1)S(1)} %copy-done.1, bf16[80,3072]{1,0:T(8,128)(2,1)S(1)} %collective-permute-done.18.refs_0_.refs_1_, ...), custom_call_target="tpu_custom_call", output_to_operand_aliasing={{0}: (5, {}), {1}: (6, {}), {2}: (7, {})} | custom-call | flops 1000 | bytes 1000 | tf_op jit(solution)/shard_map/pallas_call | solution.py:437
  167.9 9.9 %collective-permute-start.28 = (bf16[384,3584]{1,0:T(8,128)(2,1)S(1)}, bf16[384,3584]{1,0:T(8,128)(2,1)S(1)}, u32[]{:S(2)}, u32[]{:S(2)}) collective-permute-start(bf16[384,3584]{1,0:T(8,128)(2,1)S(1)} %get-tuple-element.240), channel_id=1, source_target_pairs={{0,1},{1,0},{2,3},{3,2},{4,5},{5,4},{6,7},{7,6},{8,9},{9,8},{10,11... | collective-permute-start | bytes 8257544 | tf_op jit(solution)/shard_map/ppermute | solution.py:62
  179.3 3.2 %collective-permute-done.28.other_ref = bf16[384,3584]{1,0:T(8,128)(2,1)S(1)} collective-permute-done((bf16[384,3584]{1,0:T(8,128)(2,1)S(1)}, bf16[384,3584]{1,0:T(8,128)(2,1)S(1)}, u32[]{:S(2)}, u32[]{:S(2)}) %collective-permute-start.28) | collective-permute-done | bytes 2752544 | tf_op jit(solution)/shard_map/ppermute | solution.py:62
  182.5 4.1 %shard_map.104 = (bf16[384,3072]{1,0:T(8,128)(2,1)}, f32[2,192,192]{2,1,0:T(8,128)}, f32[2,192,192]{2,1,0:T(8,128)}) custom-call(f32[384,3072]{1,0:T(8,128)S(1)} %shard_map.102.own_ref, bf16[384,3584]{1,0:T(8,128)(2,1)S(1)} %collective-permute-done.28.other_ref, bf16[2,192,192]{2,1,0:T(8,128)(2,1)S(1)} %get-tuple-element.241.left_ref, ...), custom_call_target="tpu_custom_call" | custom-call | flops 1000 | bytes 1000 | tf_op jit(solution)/shard_map/pallas_call | solution.py:539
  (64 shorter events, 55.3 us)
Async XLA Ops:
  8.7 14.0 %collective-permute-start = (bf16[80,3072]{1,0:T(8,128)(2,1)S(1)}, bf16[80,3072]{1,0:T(8,128)(2,1)S(1)}, u32[]{:S(2)}, u32[]{:S(2)}) collective-permute-start(bf16[80,3072]{1,0:T(8,128)(2,1)S(1)} %get-tuple-element.125), channel_id=1, source_target_pairs={{0,8},{1,9},{2,10},{3,11},{4,12},{5,13},{6,14},{7,15}} | collective-permute-start | bytes 1474568 | tf_op jit(solution)/shard_map/ppermute | solution.py:579
  27.0 13.1 %collective-permute-start.1 = (bf16[80,3072]{1,0:T(8,128)(2,1)S(1)}, bf16[80,3072]{1,0:T(8,128)(2,1)S(1)}, u32[]{:S(2)}, u32[]{:S(2)}) collective-permute-start(bf16[80,3072]{1,0:T(8,128)(2,1)S(1)} %get-tuple-element.137), channel_id=1, source_target_pairs={{0,8},{8,16},{1,9},{9,17},{2,10},{10,18},{3,11},{11,19},{4,12},{12... | collective-permute-start | bytes 1474568 | tf_op jit(solution)/shard_map/ppermute | solution.py:579
  44.4 12.1 %collective-permute-start.2 = (bf16[80,3072]{1,0:T(8,128)(2,1)S(1)}, bf16[80,3072]{1,0:T(8,128)(2,1)S(1)}, u32[]{:S(2)}, u32[]{:S(2)}) collective-permute-start(bf16[80,3072]{1,0:T(8,128)(2,1)S(1)} %get-tuple-element.152), channel_id=1, source_target_pairs={{0,8},{8,16},{16,24},{1,9},{9,17},{17,25},{2,10},{10,18},{18,26},{... | collective-permute-start | bytes 1474568 | tf_op jit(solution)/shard_map/ppermute | solution.py:579
  60.8 9.9 %collective-permute-start.3 = (bf16[80,3072]{1,0:T(8,128)(2,1)S(1)}, bf16[80,3072]{1,0:T(8,128)(2,1)S(1)}, u32[]{:S(2)}, u32[]{:S(2)}) collective-permute-start(bf16[80,3072]{1,0:T(8,128)(2,1)S(1)} %get-tuple-element.168), channel_id=1, source_target_pairs={{8,16},{16,24},{9,17},{17,25},{10,18},{18,26},{11,19},{19,27},{12,... | collective-permute-start | bytes 1474568 | tf_op jit(solution)/shard_map/ppermute | solution.py:579
  63.4 9.4 %collective-permute-start.14 = (bf16[80,3072]{1,0:T(8,128)(2,1)S(1)}, bf16[80,3072]{1,0:T(8,128)(2,1)S(1)}, u32[]{:S(2)}, u32[]{:S(2)}) collective-permute-start(bf16[80,3072]{1,0:T(8,128)(2,1)S(1)} %get-tuple-element.201), channel_id=1, source_target_pairs={{24,16},{25,17},{26,18},{27,19},{28,20},{29,21},{30,22},{31,23}} | collective-permute-start | bytes 1474568 | tf_op jit(solution)/shard_map/ppermute | solution.py:587
  64.1 7.3 %collective-permute-start.11 = (bf16[80,768]{1,0:T(8,128)(2,1)S(1)}, bf16[80,768]{1,0:T(8,128)(2,1)S(1)}, u32[]{:S(2)}, u32[]{:S(2)}) collective-permute-start(bf16[80,768]{1,0:T(8,128)(2,1)S(1)} %get-tuple-element.192), channel_id=1, source_target_pairs={{0,2},{1,3},{2,0},{3,1},{4,6},{5,7},{6,4},{7,5},{8,10},{9,11},{10,... | collective-permute-start | bytes 368648 | tf_op jit(solution)/shard_map/ppermute | solution.py:62
  66.7 4.7 %collective-permute-start.12 = (bf16[80,768]{1,0:T(8,128)(2,1)S(1)}, bf16[80,768]{1,0:T(8,128)(2,1)S(1)}, u32[]{:S(2)}, u32[]{:S(2)}) collective-permute-start(bf16[80,768]{1,0:T(8,128)(2,1)S(1)} %get-tuple-element.193), channel_id=1, source_target_pairs={{0,4},{1,5},{2,6},{3,7},{4,0},{5,1},{6,2},{7,3},{8,12},{9,13},{10,... | collective-permute-start | bytes 368648 | tf_op jit(solution)/shard_map/ppermute | solution.py:62
  68.0 4.8 %collective-permute-start.13 = (bf16[80,768]{1,0:T(8,128)(2,1)S(1)}, bf16[80,768]{1,0:T(8,128)(2,1)S(1)}, u32[]{:S(2)}, u32[]{:S(2)}) collective-permute-start(bf16[80,768]{1,0:T(8,128)(2,1)S(1)} %get-tuple-element.194), channel_id=1, source_target_pairs={{0,6},{1,7},{2,4},{3,5},{4,2},{5,3},{6,0},{7,1},{8,14},{9,15},{10,... | collective-permute-start | bytes 368648 | tf_op jit(solution)/shard_map/ppermute | solution.py:62
  70.7 6.5 %collective-permute-start.4 = (bf16[80,3072]{1,0:T(8,128)(2,1)S(1)}, bf16[80,3072]{1,0:T(8,128)(2,1)S(1)}, u32[]{:S(2)}, u32[]{:S(2)}) collective-permute-start(bf16[80,3072]{1,0:T(8,128)(2,1)S(1)} %get-tuple-element.179), channel_id=1, source_target_pairs={{16,24},{17,25},{18,26},{19,27},{20,28},{21,29},{22,30},{23,31}} | collective-permute-start | bytes 1474568 | tf_op jit(solution)/shard_map/ppermute | solution.py:579
  72.8 20.5 %collective-permute-start.15 = (bf16[80,3072]{1,0:T(8,128)(2,1)S(1)}, bf16[80,3072]{1,0:T(8,128)(2,1)S(1)}, u32[]{:S(2)}, u32[]{:S(2)}) collective-permute-start(bf16[80,3072]{1,0:T(8,128)(2,1)S(1)} %get-tuple-element.207), channel_id=1, source_target_pairs={{16,8},{24,16},{17,9},{25,17},{18,10},{26,18},{19,11},{27,19},{20,... | collective-permute-start | bytes 1474568 | tf_op jit(solution)/shard_map/ppermute | solution.py:587
  97.1 11.1 %collective-permute-start.16 = (bf16[80,3072]{1,0:T(8,128)(2,1)S(1)}, bf16[80,3072]{1,0:T(8,128)(2,1)S(1)}, u32[]{:S(2)}, u32[]{:S(2)}) collective-permute-start(bf16[80,3072]{1,0:T(8,128)(2,1)S(1)} %get-tuple-element.212), channel_id=1, source_target_pairs={{8,0},{16,8},{24,16},{9,1},{17,9},{25,17},{10,2},{18,10},{26,18},{... | collective-permute-start | bytes 1474568 | tf_op jit(solution)/shard_map/ppermute | solution.py:587
  99.1 5.6 %collective-permute-start.5 = (bf16[80,768]{1,0:T(8,128)(2,1)S(1)}, bf16[80,768]{1,0:T(8,128)(2,1)S(1)}, u32[]{:S(2)}, u32[]{:S(2)}) collective-permute-start(bf16[80,768]{1,0:T(8,128)(2,1)S(1)} %get-tuple-element.186), channel_id=1, source_target_pairs={{0,2},{1,3},{2,0},{3,1},{4,6},{5,7},{6,4},{7,5},{8,10},{9,11},{10,... | collective-permute-start | bytes 368648 | tf_op jit(solution)/shard_map/ppermute | solution.py:62
  112.2 8.7 %collective-permute-start.20 = (bf16[80,3072]{1,0:T(8,128)(2,1)S(1)}, bf16[80,3072]{1,0:T(8,128)(2,1)S(1)}, u32[]{:S(2)}, u32[]{:S(2)}) collective-permute-start(bf16[80,3072]{1,0:T(8,128)(2,1)S(1)} %get-tuple-element.218.refs_0_), channel_id=1, source_target_pairs={{0,2},{1,3},{2,0},{3,1},{4,6},{5,7},{6,4},{7,5},{8,10},{9,11},{10,... | collective-permute-start | bytes 1474568 | tf_op jit(solution)/shard_map/ppermute | solution.py:62
  114.7 9.9 %collective-permute-start.17 = (bf16[80,3072]{1,0:T(8,128)(2,1)S(1)}, bf16[80,3072]{1,0:T(8,128)(2,1)S(1)}, u32[]{:S(2)}, u32[]{:S(2)}) collective-permute-start(bf16[80,3072]{1,0:T(8,128)(2,1)S(1)} %get-tuple-element.216), channel_id=1, source_target_pairs={{8,0},{16,8},{9,1},{17,9},{10,2},{18,10},{11,3},{19,11},{12,4},{20... | collective-permute-start | bytes 1474568 | tf_op jit(solution)/shard_map/ppermute | solution.py:587
  116.6 17.5 %collective-permute-start.21 = (bf16[80,3072]{1,0:T(8,128)(2,1)S(1)}, bf16[80,3072]{1,0:T(8,128)(2,1)S(1)}, u32[]{:S(2)}, u32[]{:S(2)}) collective-permute-start(bf16[80,3072]{1,0:T(8,128)(2,1)S(1)} %get-tuple-element.218.refs_0_), channel_id=1, source_target_pairs={{0,4},{1,5},{2,6},{3,7},{4,0},{5,1},{6,2},{7,3},{8,12},{9,13},{10,... | collective-permute-start | bytes 1474568 | tf_op jit(solution)/shard_map/ppermute | solution.py:62
  120.9 13.5 %collective-permute-start.22 = (bf16[80,3072]{1,0:T(8,128)(2,1)S(1)}, bf16[80,3072]{1,0:T(8,128)(2,1)S(1)}, u32[]{:S(2)}, u32[]{:S(2)}) collective-permute-start(bf16[80,3072]{1,0:T(8,128)(2,1)S(1)} %collective-permute-done.20.refs_1_), channel_id=1, source_target_pairs={{0,4},{1,5},{2,6},{3,7},{4,0},{5,1},{6,2},{7,3},{8,12},{9,13},{10,... | collective-permute-start | bytes 1474568 | tf_op jit(solution)/shard_map/ppermute | solution.py:62
  128.4 10.9 %collective-permute-start.23 = (bf16[80,3072]{1,0:T(8,128)(2,1)S(1)}, bf16[80,3072]{1,0:T(8,128)(2,1)S(1)}, u32[]{:S(2)}, u32[]{:S(2)}) collective-permute-start(bf16[80,3072]{1,0:T(8,128)(2,1)S(1)} %get-tuple-element.226), channel_id=1, source_target_pairs={{8,0},{9,1},{10,2},{11,3},{12,4},{13,5},{14,6},{15,7}} | collective-permute-start | bytes 1474568 | tf_op jit(solution)/shard_map/ppermute | solution.py:587
  129.7 15.1 %collective-permute-start.19 = (bf16[80,3072]{1,0:T(8,128)(2,1)S(1)}, bf16[80,3072]{1,0:T(8,128)(2,1)S(1)}, u32[]{:S(2)}, u32[]{:S(2)}) collective-permute-start(bf16[80,3072]{1,0:T(8,128)(2,1)S(1)} %get-tuple-element.217.refs_0_), channel_id=1, source_target_pairs={{0,4},{1,5},{2,6},{3,7},{4,0},{5,1},{6,2},{7,3},{8,12},{9,13},{10,... | collective-permute-start | bytes 1474568 | tf_op jit(solution)/shard_map/ppermute | solution.py:62
  131.0 13.8 %collective-permute-start.18 = (bf16[80,3072]{1,0:T(8,128)(2,1)S(1)}, bf16[80,3072]{1,0:T(8,128)(2,1)S(1)}, u32[]{:S(2)}, u32[]{:S(2)}) collective-permute-start(bf16[80,3072]{1,0:T(8,128)(2,1)S(1)} %get-tuple-element.217.refs_0_), channel_id=1, source_target_pairs={{0,2},{1,3},{2,0},{3,1},{4,6},{5,7},{6,4},{7,5},{8,10},{9,11},{10,... | collective-permute-start | bytes 1474568 | tf_op jit(solution)/shard_map/ppermute | solution.py:62
  145.7 7.7 %collective-permute-start.24 = (bf16[80,3072]{1,0:T(8,128)(2,1)S(1)}, bf16[80,3072]{1,0:T(8,128)(2,1)S(1)}, u32[]{:S(2)}, u32[]{:S(2)}) collective-permute-start(bf16[80,3072]{1,0:T(8,128)(2,1)S(1)} %get-tuple-element.227.refs_0_), channel_id=1, source_target_pairs={{0,2},{1,3},{2,0},{3,1},{4,6},{5,7},{6,4},{7,5},{8,10},{9,11},{10,... | collective-permute-start | bytes 1474568 | tf_op jit(solution)/shard_map/ppermute | solution.py:62
  146.7 9.2 %collective-permute-start.27 = (bf16[80,3072]{1,0:T(8,128)(2,1)S(1)}, bf16[80,3072]{1,0:T(8,128)(2,1)S(1)}, u32[]{:S(2)}, u32[]{:S(2)}) collective-permute-start(bf16[80,3072]{1,0:T(8,128)(2,1)S(1)} %get-tuple-element.227.refs_0_), channel_id=1, source_target_pairs={{0,4},{1,5},{2,6},{3,7},{4,0},{5,1},{6,2},{7,3},{8,12},{9,13},{10,... | collective-permute-start | bytes 1474568 | tf_op jit(solution)/shard_map/ppermute | solution.py:62
  147.8 13.3 %collective-permute-start.26 = (bf16[80,3072]{1,0:T(8,128)(2,1)S(1)}, bf16[80,3072]{1,0:T(8,128)(2,1)S(1)}, u32[]{:S(2)}, u32[]{:S(2)}) collective-permute-start(bf16[80,3072]{1,0:T(8,128)(2,1)S(1)} %collective-permute-done.19.refs_1_.refs_2_), channel_id=1, source_target_pairs={{0,2},{1,3},{2,0},{3,1},{4,6},{5,7},{6,4},{7,5},{8,10},{9,11},{10,... | collective-permute-start | bytes 1474568 | tf_op jit(solution)/shard_map/ppermute | solution.py:62
  153.3 12.7 %collective-permute-start.25 = (bf16[80,3072]{1,0:T(8,128)(2,1)S(1)}, bf16[80,3072]{1,0:T(8,128)(2,1)S(1)}, u32[]{:S(2)}, u32[]{:S(2)}) collective-permute-start(bf16[80,3072]{1,0:T(8,128)(2,1)S(1)} %collective-permute-done.24.refs_1_), channel_id=1, source_target_pairs={{0,4},{1,5},{2,6},{3,7},{4,0},{5,1},{6,2},{7,3},{8,12},{9,13},{10,... | collective-permute-start | bytes 1474568 | tf_op jit(solution)/shard_map/ppermute | solution.py:62
  167.9 14.6 %collective-permute-start.28 = (bf16[384,3584]{1,0:T(8,128)(2,1)S(1)}, bf16[384,3584]{1,0:T(8,128)(2,1)S(1)}, u32[]{:S(2)}, u32[]{:S(2)}) collective-permute-start(bf16[384,3584]{1,0:T(8,128)(2,1)S(1)} %get-tuple-element.240), channel_id=1, source_target_pairs={{0,1},{1,0},{2,3},{3,2},{4,5},{5,4},{6,7},{7,6},{8,9},{9,8},{10,11... | collective-permute-start | bytes 8257544 | tf_op jit(solution)/shard_map/ppermute | solution.py:62
  (10 other events, 57.2 us)

commit v6 on v5

--- a/solution.py
+++ b/solution.py
@@ -30,7 +30,6 @@
 BF = jnp.bfloat16
 F32 = jnp.float32
 VM = pl.BlockSpec(memory_space=pltpu.VMEM)
-SM = pl.BlockSpec(memory_space=pltpu.SMEM)
 HB = pl.BlockSpec(memory_space=pl.ANY)
 MIB = 1 << 20
 
@@ -71,7 +70,8 @@
     square = pre * pre
     hyper = jnp.tanh(C_ZERO * (pre + C_ONE * pre * square))
     half = 0.5 * (1.0 + hyper)
-    next_ref[:, columns] = (held[:, columns].astype(F32) + pre * half).astype(BF)
+    if next_ref is not None:
+        next_ref[:, columns] = (held[:, columns].astype(F32) + pre * half).astype(BF)
     slope = half + 0.5 * pre * (1.0 - hyper * hyper) * C_ZERO * (1.0 + 3.0 * C_ONE * square)
     slope_ref[piece, :, columns] = slope.astype(BF)
 
@@ -92,7 +92,7 @@
 def begin_kernel(sections, chips, counts_ref, tokens_ref, cot_ref, weight_ref, *refs):
     w_ref, next_ref, tok_out, cot_out, slope_ref = refs[:5]
     stores = refs[5 : 5 + chips]
-    held, raw, raw_sem, sems = refs[-4:]
+    held, raw, counts, raw_sem, counts_sem, sems = refs[-6:]
     here = lax.axis_index("section")
     loads = [
         pltpu.make_async_copy(
@@ -102,6 +102,7 @@
     ]
     copy_tokens = pltpu.make_async_copy(tokens_ref, raw, raw_sem)
     copy_cot = pltpu.make_async_copy(cot_ref, raw, raw_sem)
+    copy_counts = pltpu.make_async_copy(counts_ref, counts, counts_sem)
 
     def pack(target):
         row = lax.broadcasted_iota(jnp.int32, (LIVE, TOK_DEV), 0)
@@ -109,7 +110,7 @@
         origin = row
         edge = jnp.int32(0)
         for micro in range(MICRO):
-            count = counts_ref[0, micro]
+            count = counts[0, micro]
             edge = edge + count
             origin = origin + jnp.where(row >= edge, ROWS - count, 0)
         pick = (column == origin).astype(F32).astype(BF)
@@ -122,7 +123,9 @@
 
     @pl.when(here == 0)
     def _():
+        copy_counts.start()
         copy_tokens.start()
+        copy_counts.wait()
         copy_tokens.wait()
 
     for load in loads[:FLIGHT]:
@@ -148,7 +151,9 @@
 
     @pl.when(jnp.logical_and(here == sections - 1, sections > 1))
     def _():
+        copy_counts.start()
         copy_cot.start()
+        copy_counts.wait()
         copy_cot.wait()
         pack(cot_out)
 
@@ -166,23 +171,27 @@
             *[near(PIECE, D // chips)] * (chips * PIECES),
             *[near(PIECE, D)] * PIECES,
         ),
-        in_specs=[SM, HB, HB, HB],
+        in_specs=[HB] * 4,
         out_specs=[VM] * (5 + chips) + [HB] * (chips * (PIECES - 1) + PIECES),
         scratch_shapes=[
             pltpu.VMEM((PIECE, D), BF),
             pltpu.VMEM((TOK_DEV, D), BF),
+            pltpu.SMEM((1, MICRO), jnp.int32),
+            pltpu.SemaphoreType.DMA,
             pltpu.SemaphoreType.DMA,
             pltpu.SemaphoreType.DMA((D // LOAD,)),
         ],
         compiler_params=limit(8),
         cost_estimate=SMALL,
-    )(counts, distant(tokens), distant(cotangent), distant(matrix))
-
-
-def forward_kernel(tick, span, count, from_ref, tok_ref, w_ref, *refs):
-    next_ref, _, slope_ref = refs[1 + count : 4 + count]
-    stores = refs[4 + count : 4 + 2 * count]
-    (held,) = refs[4 + 2 * count :]
+    )(distant(counts), distant(tokens), distant(cotangent), distant(matrix))
+
+
+def forward_kernel(tick, span, count, sends, from_ref, tok_ref, w_ref, *refs):
+    outs = refs[1 + count :]
+    slope_ref = outs[1]
+    stores = outs[2 : 2 + count]
+    next_ref = outs[2 + count] if sends else None
+    held = outs[-1]
     here = lax.axis_index("section")
     piece = tick - here
 
@@ -210,18 +219,19 @@
     span = list(range(max(0, tick - sections + 1), min(PIECES - 1, tick) + 1))
     flat = [s for k in span for s in stores[k]]
     count = len(flat)
+    sends = tick < PIECES + sections - 2
     outs = pl.pallas_call(
-        functools.partial(forward_kernel, tick, span, count),
+        functools.partial(forward_kernel, tick, span, count, sends),
         out_shape=(
-            near(PIECE, D),
             near(*matrix.shape),
             near(*slopes.shape),
             *[near(*s.shape) for s in flat],
+            *[near(PIECE, D)] * sends,
         ),
         in_specs=[VM] * (4 + count),
-        out_specs=[VM] * (3 + count),
+        out_specs=[VM] * (2 + count + sends),
         scratch_shapes=[pltpu.VMEM((PIECE, D), BF)],
-        input_output_aliases={2 + k: 1 + k for k in range(2 + count)},
+        input_output_aliases={2 + k: k for k in range(2 + count)},
         compiler_params=limit(4),
         cost_estimate=SMALL,
     )(
@@ -234,8 +244,8 @@
     stores = list(stores)
     chips = count // len(span)
     for k, index in enumerate(span):
-        stores[index] = list(outs[3 + k * chips : 3 + (k + 1) * chips])
-    return outs[0], outs[1], outs[2], stores
+        stores[index] = list(outs[2 + k * chips : 2 + (k + 1) * chips])
+    return outs[-1], outs[0], outs[1], stores
 
 
 def turn_kernel(w_ref, _, out_ref):
@@ -272,8 +282,10 @@
     cot_ref = refs[2] if opens else None
     from_ref = refs[2 + opens + keeps] if chained else None
     outs = refs[2 + opens + keeps + chained :]
-    next_ref, kept = outs[0], outs[2 : 2 + keeps]
-    flow, scaled = outs[2 + keeps :]
+    sends = tick < 2 * (sections - 1) + PIECES - 1
+    kept = outs[1 : 1 + keeps]
+    next_ref = outs[1 + keeps] if sends else None
+    flow, scaled = outs[-2:]
     here = lax.axis_index("section")
     piece = tick - 2 * (sections - 1) + here
 
@@ -298,13 +310,14 @@
             def _():
                 out[...] = scaled[...]
 
-        @pl.when(here > 0)
+        @pl.when(jnp.logical_and(here > 0, sends))
         def _():
             @pl.loop(0, D // WIDE)
             def _(step):
                 part = pl.ds(pl.multiple_of(step * WIDE, WIDE), WIDE)
                 back = jnp.dot(scaled[...], w_ref[:, part], preferred_element_type=F32)
-                next_ref[:, part] = (flow[:, part].astype(F32) + back).astype(BF)
+                if sends:
+                    next_ref[:, part] = (flow[:, part].astype(F32) + back).astype(BF)
 
 
 def backward(tick, sections, arrived, matrix, slopes, cotangent, kept, after):
@@ -312,17 +325,18 @@
     high = min(PIECES - 1, tick - (sections - 1))
     span = list(range(low, high + 1))
     first = [] if arrived is None else [resident(arrived)]
+    sends = tick < 2 * (sections - 1) + PIECES - 1
     opens = [resident(cotangent)] if tick - (sections - 1) < PIECES else []
     base = 2 + len(after) + len(opens)
     out = pl.pallas_call(
         functools.partial(backward_kernel, tick, sections, span, len(after)),
-        out_shape=(near(PIECE, D), near(D, D), *[near(PIECE, D) for _ in span]),
+        out_shape=(near(D, D), *[near(PIECE, D)] * (len(span) + sends)),
         in_specs=[HB] * len(after) + [VM] * (2 + len(opens) + len(span) + len(first)),
-        out_specs=[VM] * (2 + len(span)),
+        out_specs=[VM] * (1 + len(span) + sends),
         scratch_shapes=[pltpu.VMEM((PIECE, D), BF), pltpu.VMEM((PIECE, D), BF)],
         input_output_aliases={
-            len(after): 1,
-            **{base + k: 2 + k for k in range(len(span))},
+            len(after): 0,
+            **{base + k: 1 + k for k in range(len(span))},
         },
         compiler_params=limit(4),
         cost_estimate=SMALL,
@@ -336,21 +350,23 @@
     )
     kept = list(kept)
     for k, index in enumerate(span):
-        kept[index] = out[2 + k]
-    return out[0], out[1], kept
+        kept[index] = out[1 + k]
+    return out[-1], out[0], kept
 
 
 def prepare_kernel(chips, blocks, *refs):
     parts = refs[: chips * PIECES]
     pin_ref, pout_ref, gram_ref, left_ref, right_ref = refs[chips * PIECES : chips * PIECES + 5]
     turned = refs[chips * PIECES + 5 :]
+    final = []
     for piece in range(PIECES):
         some = [part[...] for part in parts[piece * chips : (piece + 1) * chips]]
-        if piece < PIECES - 1:
+        if piece < PIECES - 2:
             turned[piece][...] = jnp.concatenate(some, axis=0).T
         else:
             turned[piece][...] = jnp.concatenate(some[:-1], axis=0).T
-            turned[piece + 1][...] = some[-1].T
+            final.append(some[-1])
+    turned[PIECES][...] = jnp.concatenate(final, axis=0).T
     for block in range(2 * blocks):
         rows = slice(block * BLOCK, (block + 1) * BLOCK)
         gram = jnp.zeros((BLOCK, BLOCK), F32)
@@ -360,15 +376,8 @@
         gram_ref[rows, :] = gram
     for block in range(blocks):
         left_ref[block] = pin_ref[block].astype(BF)
-    row = lax.broadcasted_iota(jnp.int32, (BLOCK, PAIR), 0)
-    column = lax.broadcasted_iota(jnp.int32, (BLOCK, PAIR), 1)
-
-    @pl.loop(0, NBLK // 2)
-    def _(pair):
-        for side in range(2):
-            place = (column == row + side * BLOCK).astype(F32).astype(BF)
-            wide = jnp.dot(pout_ref[2 * pair + side].astype(BF), place, preferred_element_type=F32)
-            right_ref[pair, side * BLOCK : (side + 1) * BLOCK, :] = wide.astype(BF)
+    for block in range(NBLK):
+        right_ref[block] = pout_ref[block].astype(BF)
 
 
 def prepare(parts, inverse_in, inverse_out):
@@ -381,10 +390,10 @@
         out_shape=(
             near(width, BLOCK, kind=F32),
             near(blocks, BLOCK, BLOCK),
-            near(NBLK // 2, PAIR, PAIR),
-            *[near(width, chips * PIECE)] * (PIECES - 1),
-            near(width, (chips - 1) * PIECE),
-            near(width, PIECE),
+            near(NBLK, BLOCK, BLOCK),
+            *[near(width, chips * PIECE)] * (PIECES - 2),
+            *[near(width, (chips - 1) * PIECE)] * 2,
+            near(width, 2 * PIECE),
         ),
         in_specs=[VM] * (len(flat) + 2),
         out_specs=[VM] * (4 + PIECES),
@@ -446,8 +455,9 @@
     )(*[resident(p) for p in parts], resident(turned), *[resident(a) for a in so_far])
 
 
-def other_kernel(part, xt_ref, acc_ref, gram_in_ref, gram_ref, _, out_ref):
+def other_kernel(first, second, xt_ref, acc_ref, gram_in_ref, gram_ref, _, out_ref, part):
     rows = half_rows(False, acc_ref.shape[0])
+    fill((first, second), part)
     add_gram(part, gram_ref, False)
     out_ref[:, D : D + BLOCK] = gram_ref[rows, :].astype(BF)
     out_ref[:, D + SIDE : D + SIDE + BLOCK] = gram_in_ref[rows, :].astype(BF)
@@ -459,21 +469,29 @@
         out_ref[:, columns] = (term + acc_ref[:, columns]).astype(BF)
 
 
-def other_half(part, turned, acc, gram_in, gram_out):
+def other_half(parts, turned, acc, gram_in, gram_out):
     width = turned.shape[0]
     return pl.pallas_call(
         other_kernel,
         out_shape=(near(width, BLOCK, kind=F32), near(width // 2, D + 2 * SIDE)),
-        in_specs=[VM] * 5,
+        in_specs=[VM] * 6,
         out_specs=(VM, VM),
-        input_output_aliases={4: 0},
+        scratch_shapes=[pltpu.VMEM((2 * PIECE, D), BF)],
+        input_output_aliases={5: 0},
         compiler_params=limit(8),
         cost_estimate=SMALL,
-    )(resident(part), resident(turned), resident(acc), resident(gram_in), resident(gram_out))
-
-
-def own_kernel(part, xt_ref, acc_ref, out_ref):
+    )(
+        *[resident(p) for p in parts],
+        resident(turned),
+        resident(acc),
+        resident(gram_in),
+        resident(gram_out),
+    )
+
+
+def own_kernel(first, second, xt_ref, acc_ref, out_ref, part):
     rows = half_rows(True, acc_ref.shape[0])
+    fill((first, second), part)
 
     @pl.loop(0, D // LOAD)
     def _(step):
@@ -482,16 +500,17 @@
         out_ref[:, columns] = term + acc_ref[:, columns]
 
 
-def own_half(part, turned, acc):
+def own_half(parts, turned, acc):
     return pl.pallas_call(
         own_kernel,
         out_shape=near(*acc.shape, kind=F32),
-        in_specs=[VM] * 3,
+        in_specs=[VM] * 4,
         out_specs=VM,
-        input_output_aliases={2: 0},
+        scratch_shapes=[pltpu.VMEM((2 * PIECE, D), BF)],
+        input_output_aliases={3: 0},
         compiler_params=limit(8),
         cost_estimate=SMALL,
-    )(resident(part), resident(turned), resident(acc))
+    )(*[resident(p) for p in parts], resident(turned), resident(acc))
 
 
 def finish_kernel(blocks, total, own_ref, other_ref, left_ref, right_ref, *refs):
@@ -509,9 +528,10 @@
             ).astype(BF)
     copies = []
     for pair in range(pairs):
-        columns = slice(pair * PAIR, (pair + 1) * PAIR)
-        right = jnp.dot(ready[:, columns], right_ref[pair], preferred_element_type=F32)
-        ready[:, columns] = (right * scale).astype(BF)
+        for block in (2 * pair, 2 * pair + 1):
+            columns = slice(block * BLOCK, (block + 1) * BLOCK)
+            right = jnp.dot(ready[:, columns], right_ref[block], preferred_element_type=F32)
+            ready[:, columns] = (right * scale).astype(BF)
         if pair % 2:
             columns = slice((pair - 1) * PAIR, (pair + 1) * PAIR)
             copy = pltpu.make_async_copy(
@@ -610,11 +630,12 @@
                 bit = offset & -offset if done % 2 else 1 << (offset.bit_length() - 1)
                 piece.append(swap(piece[offset ^ bit], ranks, 2 * bit))
             parts.append(piece)
-    acc = gather(parts[-1][:-1], rows_turned[-2], acc)
-    acc = gather(parts[-2], rows_turned[-3], acc)
-    gram_out, other = other_half(parts[-1][-1], rows_turned[-1], acc[1], gram_in, acc[2])
+    for index in range(PIECES - 2, PIECES):
+        acc = gather(parts[index][:-1], rows_turned[index], acc)
+    final = [parts[-2][-1], parts[-1][-1]]
+    gram_out, other = other_half(final, rows_turned[-1], acc[1], gram_in, acc[2])
     other = swap(other, ranks, 1)
-    own = own_half(parts[-1][-1], rows_turned[-1], acc[0])
+    own = own_half(final, rows_turned[-1], acc[0])
     update, factor_in, factor_out = finish(
         inverse_in.shape[1], total, own, other, left, right, gram_in, gram_out
     )

time: 187 us -> 184 us (0.984)
  Pallas kernels: 64.8 us -> 60.3 us
  waiting for transfers between devices: 72.6 us -> 76.3 us
  starting transfers between devices: 47.7 us -> 45.5 us
    ppermute x19, waiting for transfers between devices: 29.7 us -> 33.6 us  [swap(): return lax.ppermute(x, 'dp', [(r, r ^ flip) for r in range(ranks)])]
    ppermute x19, starting transfers between devices: 32 us -> 29.8 us  [swap(): return lax.ppermute(x, 'dp', [(r, r ^ flip) for r in range(ranks)])]
    pallas_call x1, Pallas kernels: 2.86 us -> 0.94 us  [prepare(): pl.pallas_call(functools.partial(prepare_kernel, chips, blocks), out_shap...]
  transfers between devices with their start and end apart: 29 -> 29, of which waited for: 20 -> 19; matrix products, arithmetic and copies ran while one was open for 0% -> 0% of each run, Pallas kernels for 16% -> 14%
where the time goes in v6:
time: 184 us; the launch traced here: 183 us
  waiting for transfers between devices  76.3 us (41%)
  Pallas kernels  60.3 us (33%)
  starting transfers between devices  45.5 us (25%)
    ppermute x19, waiting for transfers between devices, swap(): return lax.ppermute(x, 'dp', [(r, r ^ flip) for r in range(ranks)])  33.6 us
    ppermute x19, starting transfers between devices, swap(): return lax.ppermute(x, 'dp', [(r, r ^ flip) for r in range(ranks)])  29.8 us
    ppermute x5, waiting for transfers between devices, shards(): arrived_ahead = lax.ppermute(ahead, 'section', pairs)  29.1 us
    ppermute x5, waiting for transfers between devices, shards(): arrived_behind = lax.ppermute(behind, 'section', pairs)  13.6 us
    pallas_call x5, Pallas kernels, forward(): pl.pallas_call(functools.partial(forward_kernel, tick, span, count, sends...  12.9 us
    pallas_call x3, Pallas kernels, gather(): pl.pallas_call(functools.partial(gather_kernel, count, not so_far), out_s...  12.3 us
    pallas_call x6, Pallas kernels, backward(): pl.pallas_call(functools.partial(backward_kernel, tick, sections, span, l...  11.7 us
    ppermute x5, starting transfers between devices, shards(): arrived_ahead = lax.ppermute(ahead, 'section', pairs)  8.58 us
  transfers between devices with their start and end apart: 29, of which 19 were waited for; matrix products, arithmetic and copies ran while one was open for 0% of the time, Pallas kernels for 14%

profile of v6, /device:TPU:9, one launch (start us, length us, event | category | flops | bytes accessed | tf_op | source)
XLA Modules:
  0.0 183.2 jit_solution(729564313315982398)
XLA Ops:
  0.6 6.8 %shard_map.85 = (bf16[3072,3072]{1,0:T(8,128)(2,1)S(1)}, bf16[80,3072]{1,0:T(8,128)(2,1)S(1)}, bf16[3,80,3072]{2,1,0:T(8,128)(2,1)S(1)}, bf16[3,80,3072]{2,1,0:T...) custom-call(s32[1,4]{1,0:T(1,128)} %counts_ref.1, ...), custom_call_target="tpu_custom_call" | custom-call | flops 1000 | bytes 1000 | tf_op jit(solution)/shard_map/pallas_call | solution.py:163
  8.8 12.7 %collective-permute-done.from_ref = bf16[80,3072]{1,0:T(8,128)(2,1)S(1)} collective-permute-done((bf16[80,3072]{1,0:T(8,128)(2,1)S(1)}, bf16[80,3072]{1,0:T(8,128)(2,1)S(1)}, u32[]{:S(2)}, u32[]{:S(2)}) %collective-permute-start) | collective-permute-done | bytes 491552 | tf_op jit(solution)/shard_map/ppermute | solution.py:599
  21.5 4.3 %shard_map.86 = (bf16[3072,3072]{1,0:T(8,128)(2,1)S(1)}, bf16[3,80,3072]{2,1,0:T(8,128)(2,1)S(1)}, bf16[80,768]{1,0:T(8,128)(2,1)S(1)}, bf16[80,768]{1,0:T(8,128...) custom-call(bf16[80,3072]{1,0:T(8,128)(2,1)S(1)} %collective-permute, ...), custom_call_target="tpu_custom_call", output_to_operand_aliasing={{0}: (2, {}), {1}: (3, {}), {2}: (4, {}), {3}: (5, {}), {4}... | custom-call | flops 1000 | bytes 1000 | tf_op jit(solution)/shard_map/pallas_call | solution.py:223
  27.7 11.1 %collective-permute-done.1.from_ref = bf16[80,3072]{1,0:T(8,128)(2,1)S(1)} collective-permute-done((bf16[80,3072]{1,0:T(8,128)(2,1)S(1)}, bf16[80,3072]{1,0:T(8,128)(2,1)S(1)}, u32[]{:S(2)}, u32[]{:S(2)}) %collective-permute-start.1) | collective-permute-done | bytes 491552 | tf_op jit(solution)/shard_map/ppermute | solution.py:599
  38.8 4.3 %shard_map.87 = (bf16[3072,3072]{1,0:T(8,128)(2,1)S(1)}, bf16[3,80,3072]{2,1,0:T(8,128)(2,1)S(1)}, bf16[80,768]{1,0:T(8,128)(2,1)S(1)}, bf16[80,768]{1,0:T(8,128...) custom-call(bf16[80,3072]{1,0:T(8,128)(2,1)S(1)} %collective-permute, ...), custom_call_target="tpu_custom_call", output_to_operand_aliasing={{0}: (2, {}), {1}: (3, {}), {2}: (4, {}), {3}: (5, {}), {4}... | custom-call | flops 1000 | bytes 1000 | tf_op jit(solution)/shard_map/pallas_call | solution.py:223
  45.4 7.3 %shard_map.88 = (bf16[3072,3072]{1,0:T(8,128)(2,1)S(1)}, bf16[3072,3072]{1,0:T(8,128)(2,1)S(1)}) custom-call(bf16[3072,3072]{1,0:T(8,128)(2,1)S(1)} %get-tuple-element.153.w_ref), custom_call_target="tpu_custom_call", output_to_operand_aliasing={{0}: (0, {})} | custom-call | flops 1000 | bytes 1000 | tf_op jit(solution)/shard_map/pallas_call | solution.py:265
  55.3 4.3 %shard_map.89 = (bf16[3072,3072]{1,0:T(8,128)(2,1)S(1)}, bf16[3,80,3072]{2,1,0:T(8,128)(2,1)S(1)}, bf16[80,768]{1,0:T(8,128)(2,1)S(1)}, bf16[80,768]{1,0:T(8,128...) custom-call(bf16[80,3072]{1,0:T(8,128)(2,1)S(1)} %collective-permute, ...), custom_call_target="tpu_custom_call", output_to_operand_aliasing={{0}: (2, {}), {1}: (3, {}), {2}: (4, {}), {3}: (5, {}), {4}... | custom-call | flops 1000 | bytes 1000 | tf_op jit(solution)/shard_map/pallas_call | solution.py:223
  62.9 2.7 %collective-permute-start.11 = (bf16[80,768]{1,0:T(8,128)(2,1)S(1)}, bf16[80,768]{1,0:T(8,128)(2,1)S(1)}, u32[]{:S(2)}, u32[]{:S(2)}) collective-permute-start(bf16[80,768]{1,0:T(8,128)(2,1)S(1)} %get-tuple-element.192), channel_id=1, source_target_pairs={{0,2},{1,3},{2,0},{3,1},{4,6},{5,7},{6,4},{7,5},{8,10},{9,11},{10,... | collective-permute-start | bytes 368648 | tf_op jit(solution)/shard_map/ppermute | solution.py:61
  66.8 2.7 %collective-permute-done.3.from_ref = bf16[80,3072]{1,0:T(8,128)(2,1)S(1)} collective-permute-done((bf16[80,3072]{1,0:T(8,128)(2,1)S(1)}, bf16[80,3072]{1,0:T(8,128)(2,1)S(1)}, u32[]{:S(2)}, u32[]{:S(2)}) %collective-permute-start.3) | collective-permute-done | bytes 491552 | tf_op jit(solution)/shard_map/ppermute | solution.py:599
  80.6 11.4 %collective-permute-done.15.refs_9_ = bf16[80,3072]{1,0:T(8,128)(2,1)S(1)} collective-permute-done((bf16[80,3072]{1,0:T(8,128)(2,1)S(1)}, bf16[80,3072]{1,0:T(8,128)(2,1)S(1)}, u32[]{:S(2)}, u32[]{:S(2)}) %collective-permute-start.15) | collective-permute-done | bytes 491552 | tf_op jit(solution)/shard_map/ppermute | solution.py:607
  92.0 3.9 %shard_map.94 = (bf16[3072,3072]{1,0:T(8,128)(2,1)S(1)}, bf16[80,3072]{1,0:T(8,128)(2,1)S(1)}, bf16[80,3072]{1,0:T(8,128)(2,1)S(1)}, bf16[80,3072]{1,0:T(8,128)(2,1)S(1)}, bf16[80,3072]{1,0:T(8,128)(2,1)S(1)}) custom-call(bf16[80,768]{1,0:T(8,128)(2,1)S(1)} %collective-permute-done.8.refs_0_., ...), custom_call_target="tpu_custom_call", output_to_operand_aliasing={{0}: (3, {}), {1}: (6, {}), {2}: (7, {}), {3}: (8, {})} | custom-call | flops 1000 | bytes 1000 | tf_op jit(solution)/shard_map/pallas_call | solution.py:331
  97.9 3.4 %collective-permute-start.5 = (bf16[80,768]{1,0:T(8,128)(2,1)S(1)}, bf16[80,768]{1,0:T(8,128)(2,1)S(1)}, u32[]{:S(2)}, u32[]{:S(2)}) collective-permute-start(bf16[80,768]{1,0:T(8,128)(2,1)S(1)} %get-tuple-element.186), channel_id=1, source_target_pairs={{0,2},{1,3},{2,0},{3,1},{4,6},{5,7},{6,4},{7,5},{8,10},{9,11},{10,... | collective-permute-start | bytes 368648 | tf_op jit(solution)/shard_map/ppermute | solution.py:61
  107.1 3.9 %shard_map.95 = (bf16[3072,3072]{1,0:T(8,128)(2,1)S(1)}, bf16[80,3072]{1,0:T(8,128)(2,1)S(1)}, bf16[80,3072]{1,0:T(8,128)(2,1)S(1)}, bf16[80,3072]{1,0:T(8,128)(2,1)S(1)}, bf16[80,3072]{1,0:T(8,128)(2,1)S(1)}) custom-call(bf16[80,768]{1,0:T(8,128)(2,1)S(1)} %collective-permute-done.5.refs_0_., ...), custom_call_target="tpu_custom_call", output_to_operand_aliasing={{0}: (3, {}), {1}: (5, {}), {2}: (6, {}), {3}: (7, {})} | custom-call | flops 1000 | bytes 1000 | tf_op jit(solution)/shard_map/pallas_call | solution.py:331
  116.7 3.0 %collective-permute-done.21.refs_1_ = bf16[80,3072]{1,0:T(8,128)(2,1)S(1)} collective-permute-done((bf16[80,3072]{1,0:T(8,128)(2,1)S(1)}, bf16[80,3072]{1,0:T(8,128)(2,1)S(1)}, u32[]{:S(2)}, u32[]{:S(2)}) %collective-permute-start.21) | collective-permute-done | bytes 491552 | tf_op jit(solution)/shard_map/ppermute | solution.py:61
  123.3 3.9 %shard_map.96 = (bf16[3072,3072]{1,0:T(8,128)(2,1)S(1)}, bf16[80,3072]{1,0:T(8,128)(2,1)S(1)}, bf16[80,3072]{1,0:T(8,128)(2,1)S(1)}, bf16[80,3072]{1,0:T(8,128)(2,1)S(1)}) custom-call(bf16[3072,3072]{1,0:T(8,128)(2,1)S(1)} %get-tuple-element.213.refs_0_, ...), custom_call_target="tpu_custom_call", output_to_operand_aliasing={{0}: (0, {}), {1}: (2, {}), {2}: (3, {})} | custom-call | flops 1000 | bytes 1000 | tf_op jit(solution)/shard_map/pallas_call | solution.py:331
  133.2 5.0 %shard_map.98 = (f32[384,3072]{1,0:T(8,128)S(1)}, f32[384,3072]{1,0:T(8,128)S(1)}, f32[768,192]{1,0:T(8,128)S(1)}) custom-call(bf16[80,3072]{1,0:T(8,128)(2,1)S(1)} %get-tuple-element.218.refs_0_, bf16[80,3072]{1,0:T(8,128)(2,1)S(1)} %collective-permute-done.21.refs_1_, bf16[80,3072]{1,0:T(8,128)(2,1)S(1)} %collective-permute-done.22.refs_2_, ...), custom_call_target="tpu_custom_call" | custom-call | flops 1000 | bytes 1000 | tf_op jit(solution)/shard_map/pallas_call | solution.py:446
  138.2 5.5 %collective-permute-done.18.refs_1_.refs_2_ = bf16[80,3072]{1,0:T(8,128)(2,1)S(1)} collective-permute-done((bf16[80,3072]{1,0:T(8,128)(2,1)S(1)}, bf16[80,3072]{1,0:T(8,128)(2,1)S(1)}, u32[]{:S(2)}, u32[]{:S(2)}) %collective-permute-start.18) | collective-permute-done | bytes 491552 | tf_op jit(solution)/shard_map/ppermute | solution.py:61
  146.4 5.3 %collective-permute-done.25.refs_1_ = bf16[80,3072]{1,0:T(8,128)(2,1)S(1)} collective-permute-done((bf16[80,3072]{1,0:T(8,128)(2,1)S(1)}, bf16[80,3072]{1,0:T(8,128)(2,1)S(1)}, u32[]{:S(2)}, u32[]{:S(2)}) %collective-permute-start.25) | collective-permute-done | bytes 491552 | tf_op jit(solution)/shard_map/ppermute | solution.py:61
  152.9 3.7 %shard_map.100 = (f32[384,3072]{1,0:T(8,128)S(1)}, f32[384,3072]{1,0:T(8,128)S(1)}, f32[768,192]{1,0:T(8,128)S(1)}) custom-call(bf16[80,3072]{1,0:T(8,128)(2,1)S(1)} %get-tuple-element.217.refs_0_, bf16[80,3072]{1,0:T(8,128)(2,1)S(1)} %collective-permute-done.20.refs_0_.refs_1_, ...), custom_call_target="tpu_custom_call", output_to_operand_aliasing={{0}: (4, {}), {1}: (5, {}), {2}: (6, {})} | custom-call | flops 1000 | bytes 1000 | tf_op jit(solution)/shard_map/pallas_call | solution.py:446
  156.6 3.7 %shard_map.101 = (f32[384,3072]{1,0:T(8,128)S(1)}, f32[384,3072]{1,0:T(8,128)S(1)}, f32[768,192]{1,0:T(8,128)S(1)}) custom-call(bf16[80,3072]{1,0:T(8,128)(2,1)S(1)} %get-tuple-element.227.refs_0_, bf16[80,3072]{1,0:T(8,128)(2,1)S(1)} %collective-permute-done.25.refs_1_, ...), custom_call_target="tpu_custom_call", output_to_operand_aliasing={{0}: (4, {}), {1}: (5, {}), {2}: (6, {})} | custom-call | flops 1000 | bytes 1000 | tf_op jit(solution)/shard_map/pallas_call | solution.py:446
  160.3 3.9 %collective-permute-done.26.second = bf16[80,3072]{1,0:T(8,128)(2,1)S(1)} collective-permute-done((bf16[80,3072]{1,0:T(8,128)(2,1)S(1)}, bf16[80,3072]{1,0:T(8,128)(2,1)S(1)}, u32[]{:S(2)}, u32[]{:S(2)}) %collective-permute-start.26) | collective-permute-done | bytes 491552 | tf_op jit(solution)/shard_map/ppermute | solution.py:61
  166.3 7.4 %collective-permute-start.28 = (bf16[384,3584]{1,0:T(8,128)(2,1)S(1)}, bf16[384,3584]{1,0:T(8,128)(2,1)S(1)}, u32[]{:S(2)}, u32[]{:S(2)}) collective-permute-start(bf16[384,3584]{1,0:T(8,128)(2,1)S(1)} %get-tuple-element.240), channel_id=1, source_target_pairs={{0,1},{1,0},{2,3},{3,2},{4,5},{5,4},{6,7},{7,6},{8,9},{9,8},{10,11... | collective-permute-start | bytes 8257544 | tf_op jit(solution)/shard_map/ppermute | solution.py:61
  175.3 3.1 %collective-permute-done.28.other_ref = bf16[384,3584]{1,0:T(8,128)(2,1)S(1)} collective-permute-done((bf16[384,3584]{1,0:T(8,128)(2,1)S(1)}, bf16[384,3584]{1,0:T(8,128)(2,1)S(1)}, u32[]{:S(2)}, u32[]{:S(2)}) %collective-permute-start.28) | collective-permute-done | bytes 2752544 | tf_op jit(solution)/shard_map/ppermute | solution.py:61
  178.4 4.7 %shard_map.104 = (bf16[384,3072]{1,0:T(8,128)(2,1)}, f32[2,192,192]{2,1,0:T(8,128)}, f32[2,192,192]{2,1,0:T(8,128)}) custom-call(f32[384,3072]{1,0:T(8,128)S(1)} %shard_map.102.own_ref, bf16[384,3584]{1,0:T(8,128)(2,1)S(1)} %collective-permute-done.28.other_ref, bf16[2,192,192]{2,1,0:T(8,128)(2,1)S(1)} %get-tuple-element.241.left_ref, ...), custom_call_target="tpu_custom_call" | custom-call | flops 1000 | bytes 1000 | tf_op jit(solution)/shard_map/pallas_call | solution.py:559
  (58 shorter events, 54.2 us)
Async XLA Ops:
  7.5 14.0 %collective-permute-start = (bf16[80,3072]{1,0:T(8,128)(2,1)S(1)}, bf16[80,3072]{1,0:T(8,128)(2,1)S(1)}, u32[]{:S(2)}, u32[]{:S(2)}) collective-permute-start(bf16[80,3072]{1,0:T(8,128)(2,1)S(1)} %get-tuple-element.125), channel_id=1, source_target_pairs={{0,8},{1,9},{2,10},{3,11},{4,12},{5,13},{6,14},{7,15}} | collective-permute-start | bytes 1474568 | tf_op jit(solution)/shard_map/ppermute | solution.py:599
  25.8 13.1 %collective-permute-start.1 = (bf16[80,3072]{1,0:T(8,128)(2,1)S(1)}, bf16[80,3072]{1,0:T(8,128)(2,1)S(1)}, u32[]{:S(2)}, u32[]{:S(2)}) collective-permute-start(bf16[80,3072]{1,0:T(8,128)(2,1)S(1)} %get-tuple-element.137), channel_id=1, source_target_pairs={{0,8},{8,16},{1,9},{9,17},{2,10},{10,18},{3,11},{11,19},{4,12},{12... | collective-permute-start | bytes 1474568 | tf_op jit(solution)/shard_map/ppermute | solution.py:599
  43.2 12.1 %collective-permute-start.2 = (bf16[80,3072]{1,0:T(8,128)(2,1)S(1)}, bf16[80,3072]{1,0:T(8,128)(2,1)S(1)}, u32[]{:S(2)}, u32[]{:S(2)}) collective-permute-start(bf16[80,3072]{1,0:T(8,128)(2,1)S(1)} %get-tuple-element.152), channel_id=1, source_target_pairs={{0,8},{8,16},{16,24},{1,9},{9,17},{17,25},{2,10},{10,18},{18,26},{... | collective-permute-start | bytes 1474568 | tf_op jit(solution)/shard_map/ppermute | solution.py:599
  59.6 9.8 %collective-permute-start.3 = (bf16[80,3072]{1,0:T(8,128)(2,1)S(1)}, bf16[80,3072]{1,0:T(8,128)(2,1)S(1)}, u32[]{:S(2)}, u32[]{:S(2)}) collective-permute-start(bf16[80,3072]{1,0:T(8,128)(2,1)S(1)} %get-tuple-element.168), channel_id=1, source_target_pairs={{8,16},{16,24},{9,17},{17,25},{10,18},{18,26},{11,19},{19,27},{12,... | collective-permute-start | bytes 1474568 | tf_op jit(solution)/shard_map/ppermute | solution.py:599
  62.2 9.4 %collective-permute-start.14 = (bf16[80,3072]{1,0:T(8,128)(2,1)S(1)}, bf16[80,3072]{1,0:T(8,128)(2,1)S(1)}, u32[]{:S(2)}, u32[]{:S(2)}) collective-permute-start(bf16[80,3072]{1,0:T(8,128)(2,1)S(1)} %get-tuple-element.201), channel_id=1, source_target_pairs={{24,16},{25,17},{26,18},{27,19},{28,20},{29,21},{30,22},{31,23}} | collective-permute-start | bytes 1474568 | tf_op jit(solution)/shard_map/ppermute | solution.py:607
  62.9 7.3 %collective-permute-start.11 = (bf16[80,768]{1,0:T(8,128)(2,1)S(1)}, bf16[80,768]{1,0:T(8,128)(2,1)S(1)}, u32[]{:S(2)}, u32[]{:S(2)}) collective-permute-start(bf16[80,768]{1,0:T(8,128)(2,1)S(1)} %get-tuple-element.192), channel_id=1, source_target_pairs={{0,2},{1,3},{2,0},{3,1},{4,6},{5,7},{6,4},{7,5},{8,10},{9,11},{10,... | collective-permute-start | bytes 368648 | tf_op jit(solution)/shard_map/ppermute | solution.py:61
  65.5 4.6 %collective-permute-start.12 = (bf16[80,768]{1,0:T(8,128)(2,1)S(1)}, bf16[80,768]{1,0:T(8,128)(2,1)S(1)}, u32[]{:S(2)}, u32[]{:S(2)}) collective-permute-start(bf16[80,768]{1,0:T(8,128)(2,1)S(1)} %get-tuple-element.193), channel_id=1, source_target_pairs={{0,4},{1,5},{2,6},{3,7},{4,0},{5,1},{6,2},{7,3},{8,12},{9,13},{10,... | collective-permute-start | bytes 368648 | tf_op jit(solution)/shard_map/ppermute | solution.py:61
  66.8 4.8 %collective-permute-start.13 = (bf16[80,768]{1,0:T(8,128)(2,1)S(1)}, bf16[80,768]{1,0:T(8,128)(2,1)S(1)}, u32[]{:S(2)}, u32[]{:S(2)}) collective-permute-start(bf16[80,768]{1,0:T(8,128)(2,1)S(1)} %get-tuple-element.194), channel_id=1, source_target_pairs={{0,6},{1,7},{2,4},{3,5},{4,2},{5,3},{6,0},{7,1},{8,14},{9,15},{10,... | collective-permute-start | bytes 368648 | tf_op jit(solution)/shard_map/ppermute | solution.py:61
  69.5 6.5 %collective-permute-start.4 = (bf16[80,3072]{1,0:T(8,128)(2,1)S(1)}, bf16[80,3072]{1,0:T(8,128)(2,1)S(1)}, u32[]{:S(2)}, u32[]{:S(2)}) collective-permute-start(bf16[80,3072]{1,0:T(8,128)(2,1)S(1)} %get-tuple-element.179), channel_id=1, source_target_pairs={{16,24},{17,25},{18,26},{19,27},{20,28},{21,29},{22,30},{23,31}} | collective-permute-start | bytes 1474568 | tf_op jit(solution)/shard_map/ppermute | solution.py:599
  71.6 20.5 %collective-permute-start.15 = (bf16[80,3072]{1,0:T(8,128)(2,1)S(1)}, bf16[80,3072]{1,0:T(8,128)(2,1)S(1)}, u32[]{:S(2)}, u32[]{:S(2)}) collective-permute-start(bf16[80,3072]{1,0:T(8,128)(2,1)S(1)} %get-tuple-element.207), channel_id=1, source_target_pairs={{16,8},{24,16},{17,9},{25,17},{18,10},{26,18},{19,11},{27,19},{20,... | collective-permute-start | bytes 1474568 | tf_op jit(solution)/shard_map/ppermute | solution.py:607
  95.9 11.2 %collective-permute-start.16 = (bf16[80,3072]{1,0:T(8,128)(2,1)S(1)}, bf16[80,3072]{1,0:T(8,128)(2,1)S(1)}, u32[]{:S(2)}, u32[]{:S(2)}) collective-permute-start(bf16[80,3072]{1,0:T(8,128)(2,1)S(1)} %get-tuple-element.212), channel_id=1, source_target_pairs={{8,0},{16,8},{24,16},{9,1},{17,9},{25,17},{10,2},{18,10},{26,18},{... | collective-permute-start | bytes 1474568 | tf_op jit(solution)/shard_map/ppermute | solution.py:607
  97.9 5.7 %collective-permute-start.5 = (bf16[80,768]{1,0:T(8,128)(2,1)S(1)}, bf16[80,768]{1,0:T(8,128)(2,1)S(1)}, u32[]{:S(2)}, u32[]{:S(2)}) collective-permute-start(bf16[80,768]{1,0:T(8,128)(2,1)S(1)} %get-tuple-element.186), channel_id=1, source_target_pairs={{0,2},{1,3},{2,0},{3,1},{4,6},{5,7},{6,4},{7,5},{8,10},{9,11},{10,... | collective-permute-start | bytes 368648 | tf_op jit(solution)/shard_map/ppermute | solution.py:61
  111.0 8.7 %collective-permute-start.21 = (bf16[80,3072]{1,0:T(8,128)(2,1)S(1)}, bf16[80,3072]{1,0:T(8,128)(2,1)S(1)}, u32[]{:S(2)}, u32[]{:S(2)}) collective-permute-start(bf16[80,3072]{1,0:T(8,128)(2,1)S(1)} %get-tuple-element.218.refs_0_), channel_id=1, source_target_pairs={{0,2},{1,3},{2,0},{3,1},{4,6},{5,7},{6,4},{7,5},{8,10},{9,11},{10,... | collective-permute-start | bytes 1474568 | tf_op jit(solution)/shard_map/ppermute | solution.py:61
  113.5 9.9 %collective-permute-start.17 = (bf16[80,3072]{1,0:T(8,128)(2,1)S(1)}, bf16[80,3072]{1,0:T(8,128)(2,1)S(1)}, u32[]{:S(2)}, u32[]{:S(2)}) collective-permute-start(bf16[80,3072]{1,0:T(8,128)(2,1)S(1)} %get-tuple-element.216), channel_id=1, source_target_pairs={{8,0},{16,8},{9,1},{17,9},{10,2},{18,10},{11,3},{19,11},{12,4},{20... | collective-permute-start | bytes 1474568 | tf_op jit(solution)/shard_map/ppermute | solution.py:607
  115.4 15.7 %collective-permute-start.22 = (bf16[80,3072]{1,0:T(8,128)(2,1)S(1)}, bf16[80,3072]{1,0:T(8,128)(2,1)S(1)}, u32[]{:S(2)}, u32[]{:S(2)}) collective-permute-start(bf16[80,3072]{1,0:T(8,128)(2,1)S(1)} %get-tuple-element.218.refs_0_), channel_id=1, source_target_pairs={{0,4},{1,5},{2,6},{3,7},{4,0},{5,1},{6,2},{7,3},{8,12},{9,13},{10,... | collective-permute-start | bytes 1474568 | tf_op jit(solution)/shard_map/ppermute | solution.py:61
  119.7 13.5 %collective-permute-start.23 = (bf16[80,3072]{1,0:T(8,128)(2,1)S(1)}, bf16[80,3072]{1,0:T(8,128)(2,1)S(1)}, u32[]{:S(2)}, u32[]{:S(2)}) collective-permute-start(bf16[80,3072]{1,0:T(8,128)(2,1)S(1)} %collective-permute-done.21.refs_1_), channel_id=1, source_target_pairs={{0,4},{1,5},{2,6},{3,7},{4,0},{5,1},{6,2},{7,3},{8,12},{9,13},{10,... | collective-permute-start | bytes 1474568 | tf_op jit(solution)/shard_map/ppermute | solution.py:61
  127.2 10.9 %collective-permute-start.24 = (bf16[80,3072]{1,0:T(8,128)(2,1)S(1)}, bf16[80,3072]{1,0:T(8,128)(2,1)S(1)}, u32[]{:S(2)}, u32[]{:S(2)}) collective-permute-start(bf16[80,3072]{1,0:T(8,128)(2,1)S(1)} %get-tuple-element.226), channel_id=1, source_target_pairs={{8,0},{9,1},{10,2},{11,3},{12,4},{13,5},{14,6},{15,7}} | collective-permute-start | bytes 1474568 | tf_op jit(solution)/shard_map/ppermute | solution.py:607
  128.6 9.6 %collective-permute-start.20 = (bf16[80,3072]{1,0:T(8,128)(2,1)S(1)}, bf16[80,3072]{1,0:T(8,128)(2,1)S(1)}, u32[]{:S(2)}, u32[]{:S(2)}) collective-permute-start(bf16[80,3072]{1,0:T(8,128)(2,1)S(1)} %get-tuple-element.217.refs_0_), channel_id=1, source_target_pairs={{0,2},{1,3},{2,0},{3,1},{4,6},{5,7},{6,4},{7,5},{8,10},{9,11},{10,... | collective-permute-start | bytes 1474568 | tf_op jit(solution)/shard_map/ppermute | solution.py:61
  128.7 15.0 %collective-permute-start.18 = (bf16[80,3072]{1,0:T(8,128)(2,1)S(1)}, bf16[80,3072]{1,0:T(8,128)(2,1)S(1)}, u32[]{:S(2)}, u32[]{:S(2)}) collective-permute-start(bf16[80,3072]{1,0:T(8,128)(2,1)S(1)} %get-tuple-element.217.refs_0_), channel_id=1, source_target_pairs={{0,4},{1,5},{2,6},{3,7},{4,0},{5,1},{6,2},{7,3},{8,12},{9,13},{10,... | collective-permute-start | bytes 1474568 | tf_op jit(solution)/shard_map/ppermute | solution.py:61
  143.7 8.0 %collective-permute-start.25 = (bf16[80,3072]{1,0:T(8,128)(2,1)S(1)}, bf16[80,3072]{1,0:T(8,128)(2,1)S(1)}, u32[]{:S(2)}, u32[]{:S(2)}) collective-permute-start(bf16[80,3072]{1,0:T(8,128)(2,1)S(1)} %get-tuple-element.227.refs_0_), channel_id=1, source_target_pairs={{0,2},{1,3},{2,0},{3,1},{4,6},{5,7},{6,4},{7,5},{8,10},{9,11},{10,... | collective-permute-start | bytes 1474568 | tf_op jit(solution)/shard_map/ppermute | solution.py:61
  144.8 11.8 %collective-permute-start.27 = (bf16[80,3072]{1,0:T(8,128)(2,1)S(1)}, bf16[80,3072]{1,0:T(8,128)(2,1)S(1)}, u32[]{:S(2)}, u32[]{:S(2)}) collective-permute-start(bf16[80,3072]{1,0:T(8,128)(2,1)S(1)} %get-tuple-element.227.refs_0_), channel_id=1, source_target_pairs={{0,4},{1,5},{2,6},{3,7},{4,0},{5,1},{6,2},{7,3},{8,12},{9,13},{10,... | collective-permute-start | bytes 1474568 | tf_op jit(solution)/shard_map/ppermute | solution.py:61
  145.7 14.6 %collective-permute-start.19 = (bf16[80,3072]{1,0:T(8,128)(2,1)S(1)}, bf16[80,3072]{1,0:T(8,128)(2,1)S(1)}, u32[]{:S(2)}, u32[]{:S(2)}) collective-permute-start(bf16[80,3072]{1,0:T(8,128)(2,1)S(1)} %collective-permute-done.18.refs_1_.refs_2_), channel_id=1, source_target_pairs={{0,2},{1,3},{2,0},{3,1},{4,6},{5,7},{6,4},{7,5},{8,10},{9,11},{10,... | collective-permute-start | bytes 1474568 | tf_op jit(solution)/shard_map/ppermute | solution.py:61
  151.7 12.6 %collective-permute-start.26 = (bf16[80,3072]{1,0:T(8,128)(2,1)S(1)}, bf16[80,3072]{1,0:T(8,128)(2,1)S(1)}, u32[]{:S(2)}, u32[]{:S(2)}) collective-permute-start(bf16[80,3072]{1,0:T(8,128)(2,1)S(1)} %collective-permute-done.25.refs_1_), channel_id=1, source_target_pairs={{0,4},{1,5},{2,6},{3,7},{4,0},{5,1},{6,2},{7,3},{8,12},{9,13},{10,... | collective-permute-start | bytes 1474568 | tf_op jit(solution)/shard_map/ppermute | solution.py:61
  166.3 12.1 %collective-permute-start.28 = (bf16[384,3584]{1,0:T(8,128)(2,1)S(1)}, bf16[384,3584]{1,0:T(8,128)(2,1)S(1)}, u32[]{:S(2)}, u32[]{:S(2)}) collective-permute-start(bf16[384,3584]{1,0:T(8,128)(2,1)S(1)} %get-tuple-element.240), channel_id=1, source_target_pairs={{0,1},{1,0},{2,3},{3,2},{4,5},{5,4},{6,7},{7,6},{8,9},{9,8},{10,11... | collective-permute-start | bytes 8257544 | tf_op jit(solution)/shard_map/ppermute | solution.py:61
  (7 other events, 34.4 us)

commit v7 on v6

--- a/solution.py
+++ b/solution.py
@@ -125,10 +125,17 @@
     def _():
         copy_counts.start()
         copy_tokens.start()
+        for load in loads[:2]:
+            load.start()
         copy_counts.wait()
         copy_tokens.wait()
 
-    for load in loads[:FLIGHT]:
+    @pl.when(here > 0)
+    def _():
+        for load in loads[:2]:
+            load.start()
+
+    for load in loads[2:FLIGHT]:
         load.start()
 
     @pl.when(here == 0)
@@ -376,8 +383,15 @@
         gram_ref[rows, :] = gram
     for block in range(blocks):
         left_ref[block] = pin_ref[block].astype(BF)
-    for block in range(NBLK):
-        right_ref[block] = pout_ref[block].astype(BF)
+    row = lax.broadcasted_iota(jnp.int32, (BLOCK, PAIR), 0)
+    column = lax.broadcasted_iota(jnp.int32, (BLOCK, PAIR), 1)
+
+    @pl.loop(0, NBLK // 2)
+    def _(pair):
+        for side in range(2):
+            place = (column == row + side * BLOCK).astype(F32).astype(BF)
+            wide = jnp.dot(pout_ref[2 * pair + side].astype(BF), place, preferred_element_type=F32)
+            right_ref[pair, side * BLOCK : (side + 1) * BLOCK, :] = wide.astype(BF)
 
 
 def prepare(parts, inverse_in, inverse_out):
@@ -390,7 +404,7 @@
         out_shape=(
             near(width, BLOCK, kind=F32),
             near(blocks, BLOCK, BLOCK),
-            near(NBLK, BLOCK, BLOCK),
+            near(NBLK // 2, PAIR, PAIR),
             *[near(width, chips * PIECE)] * (PIECES - 2),
             *[near(width, (chips - 1) * PIECE)] * 2,
             near(width, 2 * PIECE),
@@ -514,10 +528,25 @@
 
 
 def finish_kernel(blocks, total, own_ref, other_ref, left_ref, right_ref, *refs):
-    gram_in_ref, gram_out_ref, update_ref, factor_in_ref, factor_out_ref, ready, sems = refs
+    gram_in_ref, gram_out_ref, update_ref, factor_in_ref, factor_out_ref, ready, grams, sems = refs
     core = lax.rem(lax.axis_index("dp"), 2)
     scale = 1.0 / math.sqrt(total)
     pairs = D // PAIR
+    copies = []
+    for block in range(blocks):
+        rows = slice(block * BLOCK, (block + 1) * BLOCK)
+        start = pl.multiple_of((core * blocks + block) * BLOCK, BLOCK)
+        mine = pl.ds(start, BLOCK)
+        grams[1, block] = (
+            gram_out_ref[mine, :] + other_ref[rows, D : D + BLOCK].astype(F32)
+        ) * (1.0 / total)
+        grams[0, block] = (
+            gram_in_ref[mine, :] + other_ref[rows, D + SIDE : D + SIDE + BLOCK].astype(F32)
+        ) * (1.0 / total)
+    for k, ref in enumerate((factor_in_ref, factor_out_ref)):
+        copy = pltpu.make_async_copy(grams.at[k], ref, sems.at[pairs + k])
+        copy.start()
+        copies.append(copy)
     for step in range(D // (2 * PAIR)):
         columns = slice(step * 2 * PAIR, (step + 1) * 2 * PAIR)
         grad = (own_ref[:, columns] + other_ref[:, columns].astype(F32)).astype(BF)
@@ -526,44 +555,30 @@
             ready[rows, columns] = jnp.dot(
                 left_ref[block], grad[rows], preferred_element_type=F32
             ).astype(BF)
-    copies = []
     for pair in range(pairs):
-        for block in (2 * pair, 2 * pair + 1):
-            columns = slice(block * BLOCK, (block + 1) * BLOCK)
-            right = jnp.dot(ready[:, columns], right_ref[block], preferred_element_type=F32)
-            ready[:, columns] = (right * scale).astype(BF)
-        if pair % 2:
-            columns = slice((pair - 1) * PAIR, (pair + 1) * PAIR)
-            copy = pltpu.make_async_copy(
-                ready.at[:, columns], update_ref.at[:, columns], sems.at[pair // 2]
-            )
-            copy.start()
-            copies.append(copy)
-    for block in range(blocks):
-        rows = slice(block * BLOCK, (block + 1) * BLOCK)
-        start = pl.multiple_of((core * blocks + block) * BLOCK, BLOCK)
-        mine = pl.ds(start, BLOCK)
-        factor_out_ref[block] = (
-            gram_out_ref[mine, :] + other_ref[rows, D : D + BLOCK].astype(F32)
-        ) * (1.0 / total)
-        factor_in_ref[block] = (
-            gram_in_ref[mine, :] + other_ref[rows, D + SIDE : D + SIDE + BLOCK].astype(F32)
-        ) * (1.0 / total)
+        columns = slice(pair * PAIR, (pair + 1) * PAIR)
+        right = jnp.dot(ready[:, columns], right_ref[pair], preferred_element_type=F32)
+        ready[:, columns] = (right * scale).astype(BF)
+        copy = pltpu.make_async_copy(
+            ready.at[:, columns], update_ref.at[:, columns], sems.at[pair]
+        )
+        copy.start()
+        copies.append(copy)
     for copy in copies:
         copy.wait()
 
 
 def finish(blocks, total, own, other, left, right, gram_in, gram_out):
     factor = shape(blocks, BLOCK, BLOCK, kind=F32)
-    steps = D // (2 * PAIR)
     return pl.pallas_call(
         functools.partial(finish_kernel, blocks, total),
         out_shape=(shape(blocks * BLOCK, D), factor, factor),
         in_specs=[VM] * 6,
-        out_specs=(HB, VM, VM),
+        out_specs=(HB, HB, HB),
         scratch_shapes=[
             pltpu.VMEM((blocks * BLOCK, D), BF),
-            pltpu.SemaphoreType.DMA((steps,)),
+            pltpu.VMEM((2, blocks, BLOCK, BLOCK), F32),
+            pltpu.SemaphoreType.DMA((D // PAIR + 2,)),
         ],
         compiler_params=limit(8),
         cost_estimate=SMALL,

time: 184 us -> 180 us (0.978)
  starting transfers between devices: 45.5 us -> 40.6 us
    ppermute x19, starting transfers between devices: 29.8 us -> 24.9 us  [swap(): return lax.ppermute(x, 'dp', [(r, r ^ flip) for r in range(ranks)])]
    ppermute x19, waiting for transfers between devices: 33.6 us -> 29.8 us  [swap(): return lax.ppermute(x, 'dp', [(r, r ^ flip) for r in range(ranks)])]
    ppermute x5, waiting for transfers between devices: 13.6 us -> 16.2 us  [shards(): arrived_behind = lax.ppermute(behind, 'section', pairs)]
    pallas_call x1, Pallas kernels: 0.94 us -> 2.81 us  [prepare(): pl.pallas_call(functools.partial(prepare_kernel, chips, blocks), out_shap...]
  transfers between devices with their start and end apart: 29 -> 29, of which waited for: 19 -> 18; matrix products, arithmetic and copies ran while one was open for 0% -> 0% of each run, Pallas kernels for 14% -> 16%
where the time goes in v7:
time: 180 us; the launch traced here: 179 us
  waiting for transfers between devices  76.4 us (42%)
  Pallas kernels  60.9 us (34%)
  starting transfers between devices  40.6 us (23%)
    ppermute x5, waiting for transfers between devices, shards(): arrived_ahead = lax.ppermute(ahead, 'section', pairs)  30.4 us
    ppermute x19, waiting for transfers between devices, swap(): return lax.ppermute(x, 'dp', [(r, r ^ flip) for r in range(ranks)])  29.8 us
    ppermute x19, starting transfers between devices, swap(): return lax.ppermute(x, 'dp', [(r, r ^ flip) for r in range(ranks)])  24.9 us
    ppermute x5, waiting for transfers between devices, shards(): arrived_behind = lax.ppermute(behind, 'section', pairs)  16.2 us
    pallas_call x5, Pallas kernels, forward(): pl.pallas_call(functools.partial(forward_kernel, tick, span, count, sends...  12.9 us
    pallas_call x3, Pallas kernels, gather(): pl.pallas_call(functools.partial(gather_kernel, count, not so_far), out_s...  12.3 us
    pallas_call x6, Pallas kernels, backward(): pl.pallas_call(functools.partial(backward_kernel, tick, sections, span, l...  11.9 us
    ppermute x5, starting transfers between devices, shards(): arrived_ahead = lax.ppermute(ahead, 'section', pairs)  8.58 us
  transfers between devices with their start and end apart: 29, of which 18 were waited for; matrix products, arithmetic and copies ran while one was open for 0% of the time, Pallas kernels for 16%

profile of v7, /device:TPU:9, one launch (start us, length us, event | category | flops | bytes accessed | tf_op | source)
XLA Modules:
  0.0 179.1 jit_solution(16694984246678065965)
XLA Ops:
  0.6 6.8 %shard_map.85 = (bf16[3072,3072]{1,0:T(8,128)(2,1)S(1)}, bf16[80,3072]{1,0:T(8,128)(2,1)S(1)}, bf16[3,80,3072]{2,1,0:T(8,128)(2,1)S(1)}, bf16[3,80,3072]{2,1,0:T...) custom-call(s32[1,4]{1,0:T(1,128)} %counts_ref.1, ...), custom_call_target="tpu_custom_call" | custom-call | flops 1000 | bytes 1000 | tf_op jit(solution)/shard_map/pallas_call | solution.py:170
  8.8 12.7 %collective-permute-done.from_ref = bf16[80,3072]{1,0:T(8,128)(2,1)S(1)} collective-permute-done((bf16[80,3072]{1,0:T(8,128)(2,1)S(1)}, bf16[80,3072]{1,0:T(8,128)(2,1)S(1)}, u32[]{:S(2)}, u32[]{:S(2)}) %collective-permute-start) | collective-permute-done | bytes 491552 | tf_op jit(solution)/shard_map/ppermute | solution.py:614
  21.5 4.3 %shard_map.86 = (bf16[3072,3072]{1,0:T(8,128)(2,1)S(1)}, bf16[3,80,3072]{2,1,0:T(8,128)(2,1)S(1)}, bf16[80,768]{1,0:T(8,128)(2,1)S(1)}, bf16[80,768]{1,0:T(8,128...) custom-call(bf16[80,3072]{1,0:T(8,128)(2,1)S(1)} %collective-permute, ...), custom_call_target="tpu_custom_call", output_to_operand_aliasing={{0}: (2, {}), {1}: (3, {}), {2}: (4, {}), {3}: (5, {}), {4}... | custom-call | flops 1000 | bytes 1000 | tf_op jit(solution)/shard_map/pallas_call | solution.py:230
  27.7 11.1 %collective-permute-done.1.from_ref = bf16[80,3072]{1,0:T(8,128)(2,1)S(1)} collective-permute-done((bf16[80,3072]{1,0:T(8,128)(2,1)S(1)}, bf16[80,3072]{1,0:T(8,128)(2,1)S(1)}, u32[]{:S(2)}, u32[]{:S(2)}) %collective-permute-start.1) | collective-permute-done | bytes 491552 | tf_op jit(solution)/shard_map/ppermute | solution.py:614
  38.8 4.3 %shard_map.87 = (bf16[3072,3072]{1,0:T(8,128)(2,1)S(1)}, bf16[3,80,3072]{2,1,0:T(8,128)(2,1)S(1)}, bf16[80,768]{1,0:T(8,128)(2,1)S(1)}, bf16[80,768]{1,0:T(8,128...) custom-call(bf16[80,3072]{1,0:T(8,128)(2,1)S(1)} %collective-permute, ...), custom_call_target="tpu_custom_call", output_to_operand_aliasing={{0}: (2, {}), {1}: (3, {}), {2}: (4, {}), {3}: (5, {}), {4}... | custom-call | flops 1000 | bytes 1000 | tf_op jit(solution)/shard_map/pallas_call | solution.py:230
  45.4 7.3 %shard_map.88 = (bf16[3072,3072]{1,0:T(8,128)(2,1)S(1)}, bf16[3072,3072]{1,0:T(8,128)(2,1)S(1)}) custom-call(bf16[3072,3072]{1,0:T(8,128)(2,1)S(1)} %get-tuple-element.153.w_ref), custom_call_target="tpu_custom_call", output_to_operand_aliasing={{0}: (0, {})} | custom-call | flops 1000 | bytes 1000 | tf_op jit(solution)/shard_map/pallas_call | solution.py:272
  52.7 2.6 %collective-permute-done.2.from_ref = bf16[80,3072]{1,0:T(8,128)(2,1)S(1)} collective-permute-done((bf16[80,3072]{1,0:T(8,128)(2,1)S(1)}, bf16[80,3072]{1,0:T(8,128)(2,1)S(1)}, u32[]{:S(2)}, u32[]{:S(2)}) %collective-permute-start.2) | collective-permute-done | bytes 491552 | tf_op jit(solution)/shard_map/ppermute | solution.py:614
  55.3 4.3 %shard_map.89 = (bf16[3072,3072]{1,0:T(8,128)(2,1)S(1)}, bf16[3,80,3072]{2,1,0:T(8,128)(2,1)S(1)}, bf16[80,768]{1,0:T(8,128)(2,1)S(1)}, bf16[80,768]{1,0:T(8,128...) custom-call(bf16[80,3072]{1,0:T(8,128)(2,1)S(1)} %collective-permute, ...), custom_call_target="tpu_custom_call", output_to_operand_aliasing={{0}: (2, {}), {1}: (3, {}), {2}: (4, {}), {3}: (5, {}), {4}... | custom-call | flops 1000 | bytes 1000 | tf_op jit(solution)/shard_map/pallas_call | solution.py:230
  65.6 3.9 %collective-permute-done.3.from_ref = bf16[80,3072]{1,0:T(8,128)(2,1)S(1)} collective-permute-done((bf16[80,3072]{1,0:T(8,128)(2,1)S(1)}, bf16[80,3072]{1,0:T(8,128)(2,1)S(1)}, u32[]{:S(2)}, u32[]{:S(2)}) %collective-permute-start.3) | collective-permute-done | bytes 491552 | tf_op jit(solution)/shard_map/ppermute | solution.py:614
  78.8 13.2 %collective-permute-done.15.refs_9_ = bf16[80,3072]{1,0:T(8,128)(2,1)S(1)} collective-permute-done((bf16[80,3072]{1,0:T(8,128)(2,1)S(1)}, bf16[80,3072]{1,0:T(8,128)(2,1)S(1)}, u32[]{:S(2)}, u32[]{:S(2)}) %collective-permute-start.15) | collective-permute-done | bytes 491552 | tf_op jit(solution)/shard_map/ppermute | solution.py:622
  92.0 3.9 %shard_map.94 = (bf16[3072,3072]{1,0:T(8,128)(2,1)S(1)}, bf16[80,3072]{1,0:T(8,128)(2,1)S(1)}, bf16[80,3072]{1,0:T(8,128)(2,1)S(1)}, bf16[80,3072]{1,0:T(8,128)(2,1)S(1)}, bf16[80,3072]{1,0:T(8,128)(2,1)S(1)}) custom-call(bf16[80,768]{1,0:T(8,128)(2,1)S(1)} %collective-permute-done.8.refs_0_., ...), custom_call_target="tpu_custom_call", output_to_operand_aliasing={{0}: (3, {}), {1}: (6, {}), {2}: (7, {}), {3}: (8, {})} | custom-call | flops 1000 | bytes 1000 | tf_op jit(solution)/shard_map/pallas_call | solution.py:338
  105.9 3.9 %shard_map.95 = (bf16[3072,3072]{1,0:T(8,128)(2,1)S(1)}, bf16[80,3072]{1,0:T(8,128)(2,1)S(1)}, bf16[80,3072]{1,0:T(8,128)(2,1)S(1)}, bf16[80,3072]{1,0:T(8,128)(2,1)S(1)}, bf16[80,3072]{1,0:T(8,128)(2,1)S(1)}) custom-call(bf16[80,768]{1,0:T(8,128)(2,1)S(1)} %collective-permute-done.5.refs_0_., ...), custom_call_target="tpu_custom_call", output_to_operand_aliasing={{0}: (3, {}), {1}: (5, {}), {2}: (6, {}), {3}: (7, {})} | custom-call | flops 1000 | bytes 1000 | tf_op jit(solution)/shard_map/pallas_call | solution.py:338
  114.2 3.3 %collective-permute-done.21.refs_1_ = bf16[80,3072]{1,0:T(8,128)(2,1)S(1)} collective-permute-done((bf16[80,3072]{1,0:T(8,128)(2,1)S(1)}, bf16[80,3072]{1,0:T(8,128)(2,1)S(1)}, u32[]{:S(2)}, u32[]{:S(2)}) %collective-permute-start.21) | collective-permute-done | bytes 491552 | tf_op jit(solution)/shard_map/ppermute | solution.py:61
  120.9 3.9 %shard_map.96 = (bf16[3072,3072]{1,0:T(8,128)(2,1)S(1)}, bf16[80,3072]{1,0:T(8,128)(2,1)S(1)}, bf16[80,3072]{1,0:T(8,128)(2,1)S(1)}, bf16[80,3072]{1,0:T(8,128)(2,1)S(1)}) custom-call(bf16[3072,3072]{1,0:T(8,128)(2,1)S(1)} %get-tuple-element.213.refs_0_, ...), custom_call_target="tpu_custom_call", output_to_operand_aliasing={{0}: (0, {}), {1}: (2, {}), {2}: (3, {})} | custom-call | flops 1000 | bytes 1000 | tf_op jit(solution)/shard_map/pallas_call | solution.py:338
  127.7 2.8 %shard_map.97 = (f32[768,192]{1,0:T(8,128)S(1)}, bf16[2,192,192]{2,1,0:T(8,128)(2,1)S(1)}, bf16[8,384,384]{2,1,0:T(8,128)(2,1)S(1)}, bf16[768,320]{1,0:T(8,128)(...) custom-call(bf16[80,768]{1,0:T(8,128)(2,1)S(1)} %get-tuple-element.219.refs_0_, ...), custom_call_target="tpu_custom_call" | custom-call | flops 1000 | bytes 1000 | tf_op jit(solution)/shard_map/pallas_call | solution.py:402
  130.5 5.0 %shard_map.98 = (f32[384,3072]{1,0:T(8,128)S(1)}, f32[384,3072]{1,0:T(8,128)S(1)}, f32[768,192]{1,0:T(8,128)S(1)}) custom-call(bf16[80,3072]{1,0:T(8,128)(2,1)S(1)} %get-tuple-element.218.refs_0_, bf16[80,3072]{1,0:T(8,128)(2,1)S(1)} %collective-permute-done.21.refs_1_, bf16[80,3072]{1,0:T(8,128)(2,1)S(1)} %collective-permute-done.22.refs_2_, ...), custom_call_target="tpu_custom_call" | custom-call | flops 1000 | bytes 1000 | tf_op jit(solution)/shard_map/pallas_call | solution.py:460
  135.5 5.4 %collective-permute-done.18.refs_1_.refs_2_ = bf16[80,3072]{1,0:T(8,128)(2,1)S(1)} collective-permute-done((bf16[80,3072]{1,0:T(8,128)(2,1)S(1)}, bf16[80,3072]{1,0:T(8,128)(2,1)S(1)}, u32[]{:S(2)}, u32[]{:S(2)}) %collective-permute-start.18) | collective-permute-done | bytes 491552 | tf_op jit(solution)/shard_map/ppermute | solution.py:61
  143.6 5.3 %collective-permute-done.25.refs_1_ = bf16[80,3072]{1,0:T(8,128)(2,1)S(1)} collective-permute-done((bf16[80,3072]{1,0:T(8,128)(2,1)S(1)}, bf16[80,3072]{1,0:T(8,128)(2,1)S(1)}, u32[]{:S(2)}, u32[]{:S(2)}) %collective-permute-start.25) | collective-permute-done | bytes 491552 | tf_op jit(solution)/shard_map/ppermute | solution.py:61
  150.1 3.6 %shard_map.100 = (f32[384,3072]{1,0:T(8,128)S(1)}, f32[384,3072]{1,0:T(8,128)S(1)}, f32[768,192]{1,0:T(8,128)S(1)}) custom-call(bf16[80,3072]{1,0:T(8,128)(2,1)S(1)} %get-tuple-element.217.refs_0_, bf16[80,3072]{1,0:T(8,128)(2,1)S(1)} %collective-permute-done.20.refs_0_.refs_1_, ...), custom_call_target="tpu_custom_call", output_to_operand_aliasing={{0}: (4, {}), {1}: (5, {}), {2}: (6, {})} | custom-call | flops 1000 | bytes 1000 | tf_op jit(solution)/shard_map/pallas_call | solution.py:460
  153.8 3.7 %shard_map.101 = (f32[384,3072]{1,0:T(8,128)S(1)}, f32[384,3072]{1,0:T(8,128)S(1)}, f32[768,192]{1,0:T(8,128)S(1)}) custom-call(bf16[80,3072]{1,0:T(8,128)(2,1)S(1)} %get-tuple-element.227.refs_0_, bf16[80,3072]{1,0:T(8,128)(2,1)S(1)} %collective-permute-done.25.refs_1_, ...), custom_call_target="tpu_custom_call", output_to_operand_aliasing={{0}: (4, {}), {1}: (5, {}), {2}: (6, {})} | custom-call | flops 1000 | bytes 1000 | tf_op jit(solution)/shard_map/pallas_call | solution.py:460
  157.5 4.0 %collective-permute-done.26.second = bf16[80,3072]{1,0:T(8,128)(2,1)S(1)} collective-permute-done((bf16[80,3072]{1,0:T(8,128)(2,1)S(1)}, bf16[80,3072]{1,0:T(8,128)(2,1)S(1)}, u32[]{:S(2)}, u32[]{:S(2)}) %collective-permute-start.26) | collective-permute-done | bytes 491552 | tf_op jit(solution)/shard_map/ppermute | solution.py:61
  163.5 7.4 %collective-permute-start.28 = (bf16[384,3584]{1,0:T(8,128)(2,1)S(1)}, bf16[384,3584]{1,0:T(8,128)(2,1)S(1)}, u32[]{:S(2)}, u32[]{:S(2)}) collective-permute-start(bf16[384,3584]{1,0:T(8,128)(2,1)S(1)} %get-tuple-element.240), channel_id=1, source_target_pairs={{0,1},{1,0},{2,3},{3,2},{4,5},{5,4},{6,7},{7,6},{8,9},{9,8},{10,11... | collective-permute-start | bytes 8257544 | tf_op jit(solution)/shard_map/ppermute | solution.py:61
  172.5 3.1 %collective-permute-done.28.other_ref = bf16[384,3584]{1,0:T(8,128)(2,1)S(1)} collective-permute-done((bf16[384,3584]{1,0:T(8,128)(2,1)S(1)}, bf16[384,3584]{1,0:T(8,128)(2,1)S(1)}, u32[]{:S(2)}, u32[]{:S(2)}) %collective-permute-start.28) | collective-permute-done | bytes 2752544 | tf_op jit(solution)/shard_map/ppermute | solution.py:61
  175.6 3.2 %shard_map.104 = (bf16[384,3072]{1,0:T(8,128)(2,1)}, f32[2,192,192]{2,1,0:T(8,128)}, f32[2,192,192]{2,1,0:T(8,128)}) custom-call(f32[384,3072]{1,0:T(8,128)S(1)} %shard_map.102.own_ref, bf16[384,3584]{1,0:T(8,128)(2,1)S(1)} %collective-permute-done.28.other_ref, bf16[2,192,192]{2,1,0:T(8,128)(2,1)S(1)} %get-tuple-element.241.left_ref, ...), custom_call_target="tpu_custom_call" | custom-call | flops 1000 | bytes 1000 | tf_op jit(solution)/shard_map/pallas_call | solution.py:573
  (58 shorter events, 48.9 us)
Async XLA Ops:
  7.5 14.0 %collective-permute-start = (bf16[80,3072]{1,0:T(8,128)(2,1)S(1)}, bf16[80,3072]{1,0:T(8,128)(2,1)S(1)}, u32[]{:S(2)}, u32[]{:S(2)}) collective-permute-start(bf16[80,3072]{1,0:T(8,128)(2,1)S(1)} %get-tuple-element.125), channel_id=1, source_target_pairs={{0,8},{1,9},{2,10},{3,11},{4,12},{5,13},{6,14},{7,15}} | collective-permute-start | bytes 1474568 | tf_op jit(solution)/shard_map/ppermute | solution.py:614
  25.8 13.1 %collective-permute-start.1 = (bf16[80,3072]{1,0:T(8,128)(2,1)S(1)}, bf16[80,3072]{1,0:T(8,128)(2,1)S(1)}, u32[]{:S(2)}, u32[]{:S(2)}) collective-permute-start(bf16[80,3072]{1,0:T(8,128)(2,1)S(1)} %get-tuple-element.137), channel_id=1, source_target_pairs={{0,8},{8,16},{1,9},{9,17},{2,10},{10,18},{3,11},{11,19},{4,12},{12... | collective-permute-start | bytes 1474568 | tf_op jit(solution)/shard_map/ppermute | solution.py:614
  43.2 12.1 %collective-permute-start.2 = (bf16[80,3072]{1,0:T(8,128)(2,1)S(1)}, bf16[80,3072]{1,0:T(8,128)(2,1)S(1)}, u32[]{:S(2)}, u32[]{:S(2)}) collective-permute-start(bf16[80,3072]{1,0:T(8,128)(2,1)S(1)} %get-tuple-element.152), channel_id=1, source_target_pairs={{0,8},{8,16},{16,24},{1,9},{9,17},{17,25},{2,10},{10,18},{18,26},{... | collective-permute-start | bytes 1474568 | tf_op jit(solution)/shard_map/ppermute | solution.py:614
  59.6 9.8 %collective-permute-start.3 = (bf16[80,3072]{1,0:T(8,128)(2,1)S(1)}, bf16[80,3072]{1,0:T(8,128)(2,1)S(1)}, u32[]{:S(2)}, u32[]{:S(2)}) collective-permute-start(bf16[80,3072]{1,0:T(8,128)(2,1)S(1)} %get-tuple-element.168), channel_id=1, source_target_pairs={{8,16},{16,24},{9,17},{17,25},{10,18},{18,26},{11,19},{19,27},{12,... | collective-permute-start | bytes 1474568 | tf_op jit(solution)/shard_map/ppermute | solution.py:614
  62.2 8.0 %collective-permute-start.14 = (bf16[80,3072]{1,0:T(8,128)(2,1)S(1)}, bf16[80,3072]{1,0:T(8,128)(2,1)S(1)}, u32[]{:S(2)}, u32[]{:S(2)}) collective-permute-start(bf16[80,3072]{1,0:T(8,128)(2,1)S(1)} %get-tuple-element.201), channel_id=1, source_target_pairs={{24,16},{25,17},{26,18},{27,19},{28,20},{29,21},{30,22},{31,23}} | collective-permute-start | bytes 1474568 | tf_op jit(solution)/shard_map/ppermute | solution.py:622
  62.9 7.3 %collective-permute-start.11 = (bf16[80,768]{1,0:T(8,128)(2,1)S(1)}, bf16[80,768]{1,0:T(8,128)(2,1)S(1)}, u32[]{:S(2)}, u32[]{:S(2)}) collective-permute-start(bf16[80,768]{1,0:T(8,128)(2,1)S(1)} %get-tuple-element.192), channel_id=1, source_target_pairs={{0,2},{1,3},{2,0},{3,1},{4,6},{5,7},{6,4},{7,5},{8,10},{9,11},{10,... | collective-permute-start | bytes 368648 | tf_op jit(solution)/shard_map/ppermute | solution.py:61
  64.1 6.0 %collective-permute-start.12 = (bf16[80,768]{1,0:T(8,128)(2,1)S(1)}, bf16[80,768]{1,0:T(8,128)(2,1)S(1)}, u32[]{:S(2)}, u32[]{:S(2)}) collective-permute-start(bf16[80,768]{1,0:T(8,128)(2,1)S(1)} %get-tuple-element.193), channel_id=1, source_target_pairs={{0,4},{1,5},{2,6},{3,7},{4,0},{5,1},{6,2},{7,3},{8,12},{9,13},{10,... | collective-permute-start | bytes 368648 | tf_op jit(solution)/shard_map/ppermute | solution.py:61
  65.4 4.8 %collective-permute-start.13 = (bf16[80,768]{1,0:T(8,128)(2,1)S(1)}, bf16[80,768]{1,0:T(8,128)(2,1)S(1)}, u32[]{:S(2)}, u32[]{:S(2)}) collective-permute-start(bf16[80,768]{1,0:T(8,128)(2,1)S(1)} %get-tuple-element.194), channel_id=1, source_target_pairs={{0,6},{1,7},{2,4},{3,5},{4,2},{5,3},{6,0},{7,1},{8,14},{9,15},{10,... | collective-permute-start | bytes 368648 | tf_op jit(solution)/shard_map/ppermute | solution.py:61
  69.5 5.0 %collective-permute-start.4 = (bf16[80,3072]{1,0:T(8,128)(2,1)S(1)}, bf16[80,3072]{1,0:T(8,128)(2,1)S(1)}, u32[]{:S(2)}, u32[]{:S(2)}) collective-permute-start(bf16[80,3072]{1,0:T(8,128)(2,1)S(1)} %get-tuple-element.179), channel_id=1, source_target_pairs={{16,24},{17,25},{18,26},{19,27},{20,28},{21,29},{22,30},{23,31}} | collective-permute-start | bytes 1474568 | tf_op jit(solution)/shard_map/ppermute | solution.py:614
  70.4 21.6 %collective-permute-start.15 = (bf16[80,3072]{1,0:T(8,128)(2,1)S(1)}, bf16[80,3072]{1,0:T(8,128)(2,1)S(1)}, u32[]{:S(2)}, u32[]{:S(2)}) collective-permute-start(bf16[80,3072]{1,0:T(8,128)(2,1)S(1)} %get-tuple-element.207), channel_id=1, source_target_pairs={{16,8},{24,16},{17,9},{25,17},{18,10},{26,18},{19,11},{27,19},{20,... | collective-permute-start | bytes 1474568 | tf_op jit(solution)/shard_map/ppermute | solution.py:622
  95.9 9.9 %collective-permute-start.16 = (bf16[80,3072]{1,0:T(8,128)(2,1)S(1)}, bf16[80,3072]{1,0:T(8,128)(2,1)S(1)}, u32[]{:S(2)}, u32[]{:S(2)}) collective-permute-start(bf16[80,3072]{1,0:T(8,128)(2,1)S(1)} %get-tuple-element.212), channel_id=1, source_target_pairs={{8,0},{16,8},{24,16},{9,1},{17,9},{25,17},{10,2},{18,10},{26,18},{... | collective-permute-start | bytes 1474568 | tf_op jit(solution)/shard_map/ppermute | solution.py:622
  100.4 4.6 %collective-permute-start.7 = (bf16[80,768]{1,0:T(8,128)(2,1)S(1)}, bf16[80,768]{1,0:T(8,128)(2,1)S(1)}, u32[]{:S(2)}, u32[]{:S(2)}) collective-permute-start(bf16[80,768]{1,0:T(8,128)(2,1)S(1)} %get-tuple-element.188), channel_id=1, source_target_pairs={{0,6},{1,7},{2,4},{3,5},{4,2},{5,3},{6,0},{7,1},{8,14},{9,15},{10,... | collective-permute-start | bytes 368648 | tf_op jit(solution)/shard_map/ppermute | solution.py:61
  109.8 7.7 %collective-permute-start.21 = (bf16[80,3072]{1,0:T(8,128)(2,1)S(1)}, bf16[80,3072]{1,0:T(8,128)(2,1)S(1)}, u32[]{:S(2)}, u32[]{:S(2)}) collective-permute-start(bf16[80,3072]{1,0:T(8,128)(2,1)S(1)} %get-tuple-element.218.refs_0_), channel_id=1, source_target_pairs={{0,2},{1,3},{2,0},{3,1},{4,6},{5,7},{6,4},{7,5},{8,10},{9,11},{10,... | collective-permute-start | bytes 1474568 | tf_op jit(solution)/shard_map/ppermute | solution.py:61
  111.0 9.9 %collective-permute-start.17 = (bf16[80,3072]{1,0:T(8,128)(2,1)S(1)}, bf16[80,3072]{1,0:T(8,128)(2,1)S(1)}, u32[]{:S(2)}, u32[]{:S(2)}) collective-permute-start(bf16[80,3072]{1,0:T(8,128)(2,1)S(1)} %get-tuple-element.216), channel_id=1, source_target_pairs={{8,0},{16,8},{9,1},{17,9},{10,2},{18,10},{11,3},{19,11},{12,4},{20... | collective-permute-start | bytes 1474568 | tf_op jit(solution)/shard_map/ppermute | solution.py:622
  112.9 17.5 %collective-permute-start.22 = (bf16[80,3072]{1,0:T(8,128)(2,1)S(1)}, bf16[80,3072]{1,0:T(8,128)(2,1)S(1)}, u32[]{:S(2)}, u32[]{:S(2)}) collective-permute-start(bf16[80,3072]{1,0:T(8,128)(2,1)S(1)} %get-tuple-element.218.refs_0_), channel_id=1, source_target_pairs={{0,4},{1,5},{2,6},{3,7},{4,0},{5,1},{6,2},{7,3},{8,12},{9,13},{10,... | collective-permute-start | bytes 1474568 | tf_op jit(solution)/shard_map/ppermute | solution.py:61
  117.5 13.0 %collective-permute-start.23 = (bf16[80,3072]{1,0:T(8,128)(2,1)S(1)}, bf16[80,3072]{1,0:T(8,128)(2,1)S(1)}, u32[]{:S(2)}, u32[]{:S(2)}) collective-permute-start(bf16[80,3072]{1,0:T(8,128)(2,1)S(1)} %collective-permute-done.21.refs_1_), channel_id=1, source_target_pairs={{0,4},{1,5},{2,6},{3,7},{4,0},{5,1},{6,2},{7,3},{8,12},{9,13},{10,... | collective-permute-start | bytes 1474568 | tf_op jit(solution)/shard_map/ppermute | solution.py:61
  124.8 10.7 %collective-permute-start.24 = (bf16[80,3072]{1,0:T(8,128)(2,1)S(1)}, bf16[80,3072]{1,0:T(8,128)(2,1)S(1)}, u32[]{:S(2)}, u32[]{:S(2)}) collective-permute-start(bf16[80,3072]{1,0:T(8,128)(2,1)S(1)} %get-tuple-element.226), channel_id=1, source_target_pairs={{8,0},{9,1},{10,2},{11,3},{12,4},{13,5},{14,6},{15,7}} | collective-permute-start | bytes 1474568 | tf_op jit(solution)/shard_map/ppermute | solution.py:622
  126.1 9.4 %collective-permute-start.20 = (bf16[80,3072]{1,0:T(8,128)(2,1)S(1)}, bf16[80,3072]{1,0:T(8,128)(2,1)S(1)}, u32[]{:S(2)}, u32[]{:S(2)}) collective-permute-start(bf16[80,3072]{1,0:T(8,128)(2,1)S(1)} %get-tuple-element.217.refs_0_), channel_id=1, source_target_pairs={{0,2},{1,3},{2,0},{3,1},{4,6},{5,7},{6,4},{7,5},{8,10},{9,11},{10,... | collective-permute-start | bytes 1474568 | tf_op jit(solution)/shard_map/ppermute | solution.py:61
  126.4 14.5 %collective-permute-start.18 = (bf16[80,3072]{1,0:T(8,128)(2,1)S(1)}, bf16[80,3072]{1,0:T(8,128)(2,1)S(1)}, u32[]{:S(2)}, u32[]{:S(2)}) collective-permute-start(bf16[80,3072]{1,0:T(8,128)(2,1)S(1)} %get-tuple-element.217.refs_0_), channel_id=1, source_target_pairs={{0,4},{1,5},{2,6},{3,7},{4,0},{5,1},{6,2},{7,3},{8,12},{9,13},{10,... | collective-permute-start | bytes 1474568 | tf_op jit(solution)/shard_map/ppermute | solution.py:61
  140.9 8.0 %collective-permute-start.25 = (bf16[80,3072]{1,0:T(8,128)(2,1)S(1)}, bf16[80,3072]{1,0:T(8,128)(2,1)S(1)}, u32[]{:S(2)}, u32[]{:S(2)}) collective-permute-start(bf16[80,3072]{1,0:T(8,128)(2,1)S(1)} %get-tuple-element.227.refs_0_), channel_id=1, source_target_pairs={{0,2},{1,3},{2,0},{3,1},{4,6},{5,7},{6,4},{7,5},{8,10},{9,11},{10,... | collective-permute-start | bytes 1474568 | tf_op jit(solution)/shard_map/ppermute | solution.py:61
  141.6 12.2 %collective-permute-start.27 = (bf16[80,3072]{1,0:T(8,128)(2,1)S(1)}, bf16[80,3072]{1,0:T(8,128)(2,1)S(1)}, u32[]{:S(2)}, u32[]{:S(2)}) collective-permute-start(bf16[80,3072]{1,0:T(8,128)(2,1)S(1)} %get-tuple-element.227.refs_0_), channel_id=1, source_target_pairs={{0,4},{1,5},{2,6},{3,7},{4,0},{5,1},{6,2},{7,3},{8,12},{9,13},{10,... | collective-permute-start | bytes 1474568 | tf_op jit(solution)/shard_map/ppermute | solution.py:61
  142.8 14.6 %collective-permute-start.19 = (bf16[80,3072]{1,0:T(8,128)(2,1)S(1)}, bf16[80,3072]{1,0:T(8,128)(2,1)S(1)}, u32[]{:S(2)}, u32[]{:S(2)}) collective-permute-start(bf16[80,3072]{1,0:T(8,128)(2,1)S(1)} %collective-permute-done.18.refs_1_.refs_2_), channel_id=1, source_target_pairs={{0,2},{1,3},{2,0},{3,1},{4,6},{5,7},{6,4},{7,5},{8,10},{9,11},{10,... | collective-permute-start | bytes 1474568 | tf_op jit(solution)/shard_map/ppermute | solution.py:61
  148.9 12.6 %collective-permute-start.26 = (bf16[80,3072]{1,0:T(8,128)(2,1)S(1)}, bf16[80,3072]{1,0:T(8,128)(2,1)S(1)}, u32[]{:S(2)}, u32[]{:S(2)}) collective-permute-start(bf16[80,3072]{1,0:T(8,128)(2,1)S(1)} %collective-permute-done.25.refs_1_), channel_id=1, source_target_pairs={{0,4},{1,5},{2,6},{3,7},{4,0},{5,1},{6,2},{7,3},{8,12},{9,13},{10,... | collective-permute-start | bytes 1474568 | tf_op jit(solution)/shard_map/ppermute | solution.py:61
  163.5 12.1 %collective-permute-start.28 = (bf16[384,3584]{1,0:T(8,128)(2,1)S(1)}, bf16[384,3584]{1,0:T(8,128)(2,1)S(1)}, u32[]{:S(2)}, u32[]{:S(2)}) collective-permute-start(bf16[384,3584]{1,0:T(8,128)(2,1)S(1)} %get-tuple-element.240), channel_id=1, source_target_pairs={{0,1},{1,0},{2,3},{3,2},{4,5},{5,4},{6,7},{7,6},{8,9},{9,8},{10,11... | collective-permute-start | bytes 8257544 | tf_op jit(solution)/shard_map/ppermute | solution.py:61
  (7 other events, 33.2 us)

commit v8 on v7

--- a/solution.py
+++ b/solution.py
@@ -129,32 +129,29 @@
             load.start()
         copy_counts.wait()
         copy_tokens.wait()
+        for load in loads[2:FLIGHT]:
+            load.start()
+        pack(tok_out)
+        held[...] = tok_out[0]
+        for k, load in enumerate(loads):
+            load.wait()
+            if k + FLIGHT < len(loads):
+                loads[k + FLIGHT].start()
+            forward_columns(pl.ds(k * LOAD, LOAD), held, w_ref, next_ref, slope_ref, 0)
+        keep_columns(0, [0], held, stores)
 
     @pl.when(here > 0)
     def _():
-        for load in loads[:2]:
-            load.start()
-
-    for load in loads[2:FLIGHT]:
-        load.start()
-
-    @pl.when(here == 0)
-    def _():
-        pack(tok_out)
-        held[...] = tok_out[0]
-
-    for k, load in enumerate(loads):
-        load.wait()
-        if k + FLIGHT < len(loads):
-            loads[k + FLIGHT].start()
-
-        @pl.when(here == 0)
-        def _():
-            forward_columns(pl.ds(k * LOAD, LOAD), held, w_ref, next_ref, slope_ref, 0)
-
-    @pl.when(here == 0)
-    def _():
-        keep_columns(0, [0], held, stores)
+        blocks = [
+            pltpu.make_async_copy(
+                weight_ref.at[pl.ds(k * LOAD, LOAD)], w_ref.at[pl.ds(k * LOAD, LOAD)], sems.at[k]
+            )
+            for k in range(D // LOAD)
+        ]
+        for block in blocks:
+            block.start()
+        for block in blocks:
+            block.wait()
 
     @pl.when(jnp.logical_and(here == sections - 1, sections > 1))
     def _():
@@ -366,14 +363,22 @@
     pin_ref, pout_ref, gram_ref, left_ref, right_ref = refs[chips * PIECES : chips * PIECES + 5]
     turned = refs[chips * PIECES + 5 :]
     final = []
+    width = gram_ref.shape[0]
+
+    def keep(ref, some):
+        columns = jnp.concatenate(some, axis=0).T
+        for block in range(width // BLOCK):
+            rows = slice(block * BLOCK, (block + 1) * BLOCK)
+            ref[own_first(block * BLOCK, width // 2), :] = columns[rows]
+
     for piece in range(PIECES):
         some = [part[...] for part in parts[piece * chips : (piece + 1) * chips]]
         if piece < PIECES - 2:
-            turned[piece][...] = jnp.concatenate(some, axis=0).T
+            keep(turned[piece], some)
         else:
-            turned[piece][...] = jnp.concatenate(some[:-1], axis=0).T
+            keep(turned[piece], some[:-1])
             final.append(some[-1])
-    turned[PIECES][...] = jnp.concatenate(final, axis=0).T
+    keep(turned[PIECES], final)
     for block in range(2 * blocks):
         rows = slice(block * BLOCK, (block + 1) * BLOCK)
         gram = jnp.zeros((BLOCK, BLOCK), F32)
@@ -416,6 +421,12 @@
     )(*[resident(p) for p in flat], inverse_in, inverse_out)
 
 
+def own_first(chunk, own):
+    core = lax.rem(lax.axis_index("dp"), 2)
+    first = lax.rem(chunk // own + core, 2) * own + chunk % own
+    return pl.ds(pl.multiple_of(first, 16), min(own, BLOCK))
+
+
 def add_gram(every, gram_ref, begins):
     width = gram_ref.shape[0]
     chip = lax.div(lax.axis_index("dp"), 2)
@@ -423,18 +434,14 @@
     turned = every[:, columns].T
     for block in range(width // BLOCK):
         rows = slice(block * BLOCK, (block + 1) * BLOCK)
+        place = own_first(block * BLOCK, width // 2)
         gram = contract_last(turned[rows], turned[rows])
-        gram_ref[rows, :] = gram if begins else gram + gram_ref[rows, :]
+        gram_ref[place, :] = gram if begins else gram + gram_ref[place, :]
 
 
 def fill(parts, every):
     for k, part in enumerate(parts):
         every[k * PIECE : (k + 1) * PIECE, :] = part[...]
-
-
-def half_rows(mine, own):
-    core = lax.rem(lax.axis_index("dp"), 2)
-    return pl.ds(pl.multiple_of((core if mine else 1 - core) * own, 16), own)
 
 
 def gather_kernel(count, begins, *refs):
@@ -443,14 +450,14 @@
     own_ref, other_ref, gram_ref, every = refs[-4:]
     fill(parts, every)
     add_gram(every, gram_ref, begins)
-    for mine, acc_ref in ((True, own_ref), (False, other_ref)):
-        rows = half_rows(mine, acc_ref.shape[0])
-
-        @pl.loop(0, D // LOAD)
-        def _(step):
-            columns = pl.ds(pl.multiple_of(step * LOAD, LOAD), LOAD)
-            term = jnp.dot(xt_ref[rows, :], every[:, columns], preferred_element_type=F32)
-            acc_ref[:, columns] = term if begins else acc_ref[:, columns] + term
+    own = own_ref.shape[0]
+
+    @pl.loop(0, D // LOAD)
+    def _(step):
+        columns = pl.ds(pl.multiple_of(step * LOAD, LOAD), LOAD)
+        term = jnp.dot(xt_ref[...], every[:, columns], preferred_element_type=F32)
+        for acc_ref, some in ((own_ref, term[:own]), (other_ref, term[own:])):
+            acc_ref[:, columns] = some if begins else acc_ref[:, columns] + some
 
 
 def gather(parts, turned, so_far):
@@ -470,7 +477,7 @@
 
 
 def other_kernel(first, second, xt_ref, acc_ref, gram_in_ref, gram_ref, _, out_ref, part):
-    rows = half_rows(False, acc_ref.shape[0])
+    rows = slice(acc_ref.shape[0], 2 * acc_ref.shape[0])
     fill((first, second), part)
     add_gram(part, gram_ref, False)
     out_ref[:, D : D + BLOCK] = gram_ref[rows, :].astype(BF)
@@ -504,7 +511,7 @@
 
 
 def own_kernel(first, second, xt_ref, acc_ref, out_ref, part):
-    rows = half_rows(True, acc_ref.shape[0])
+    rows = slice(0, acc_ref.shape[0])
     fill((first, second), part)
 
     @pl.loop(0, D // LOAD)
@@ -529,14 +536,12 @@
 
 def finish_kernel(blocks, total, own_ref, other_ref, left_ref, right_ref, *refs):
     gram_in_ref, gram_out_ref, update_ref, factor_in_ref, factor_out_ref, ready, grams, sems = refs
-    core = lax.rem(lax.axis_index("dp"), 2)
     scale = 1.0 / math.sqrt(total)
     pairs = D // PAIR
     copies = []
     for block in range(blocks):
         rows = slice(block * BLOCK, (block + 1) * BLOCK)
-        start = pl.multiple_of((core * blocks + block) * BLOCK, BLOCK)
-        mine = pl.ds(start, BLOCK)
+        mine = rows
         grams[1, block] = (
             gram_out_ref[mine, :] + other_ref[rows, D : D + BLOCK].astype(F32)
         ) * (1.0 / total)

time: 180 us -> 180 us (level)
  Pallas kernels: 60.9 us -> 58.2 us
  waiting for transfers between devices: 76.4 us -> 78.9 us
    pallas_call x3, Pallas kernels: 12.3 us -> 9.46 us  [gather(): pl.pallas_call(functools.partial(gather_kernel, count, not so_far), out_s...]
    ppermute x19, waiting for transfers between devices: 29.8 us -> 32.3 us  [swap(): return lax.ppermute(x, 'dp', [(r, r ^ flip) for r in range(ranks)])]
  transfers between devices with their start and end apart: 29 -> 29, of which waited for: 18 -> 18; matrix products, arithmetic and copies ran while one was open for 0% -> 0% of each run, Pallas kernels for 16% -> 14%
where the time goes in v8:
time: 180 us; the launch traced here: 179 us
  waiting for transfers between devices  78.9 us (44%)
  Pallas kernels  58.2 us (32%)
  starting transfers between devices  40.6 us (23%)
    ppermute x19, waiting for transfers between devices, swap(): return lax.ppermute(x, 'dp', [(r, r ^ flip) for r in range(ranks)])  32.3 us
    ppermute x5, waiting for transfers between devices, shards(): arrived_ahead = lax.ppermute(ahead, 'section', pairs)  30.4 us
    ppermute x19, starting transfers between devices, swap(): return lax.ppermute(x, 'dp', [(r, r ^ flip) for r in range(ranks)])  24.9 us
    ppermute x5, waiting for transfers between devices, shards(): arrived_behind = lax.ppermute(behind, 'section', pairs)  16.2 us
    pallas_call x5, Pallas kernels, forward(): pl.pallas_call(functools.partial(forward_kernel, tick, span, count, sends...  12.9 us
    pallas_call x6, Pallas kernels, backward(): pl.pallas_call(functools.partial(backward_kernel, tick, sections, span, l...  11.9 us
    pallas_call x3, Pallas kernels, gather(): pl.pallas_call(functools.partial(gather_kernel, count, not so_far), out_s...  9.46 us
    ppermute x5, starting transfers between devices, shards(): arrived_ahead = lax.ppermute(ahead, 'section', pairs)  8.58 us
  transfers between devices with their start and end apart: 29, of which 18 were waited for; matrix products, arithmetic and copies ran while one was open for 0% of the time, Pallas kernels for 14%

profile of v8, /device:TPU:9, one launch (start us, length us, event | category | flops | bytes accessed | tf_op | source)
XLA Modules:
  0.0 178.8 jit_solution(16907143832873892103)
XLA Ops:
  0.6 6.5 %shard_map.85 = (bf16[3072,3072]{1,0:T(8,128)(2,1)S(1)}, bf16[80,3072]{1,0:T(8,128)(2,1)S(1)}, bf16[3,80,3072]{2,1,0:T(8,128)(2,1)S(1)}, bf16[3,80,3072]{2,1,0:T...) custom-call(s32[1,4]{1,0:T(1,128)} %counts_ref.1, ...), custom_call_target="tpu_custom_call" | custom-call | flops 1000 | bytes 1000 | tf_op jit(solution)/shard_map/pallas_call | solution.py:167
  8.5 12.7 %collective-permute-done.from_ref = bf16[80,3072]{1,0:T(8,128)(2,1)S(1)} collective-permute-done((bf16[80,3072]{1,0:T(8,128)(2,1)S(1)}, bf16[80,3072]{1,0:T(8,128)(2,1)S(1)}, u32[]{:S(2)}, u32[]{:S(2)}) %collective-permute-start) | collective-permute-done | bytes 491552 | tf_op jit(solution)/shard_map/ppermute | solution.py:619
  21.2 4.3 %shard_map.86 = (bf16[3072,3072]{1,0:T(8,128)(2,1)S(1)}, bf16[3,80,3072]{2,1,0:T(8,128)(2,1)S(1)}, bf16[80,768]{1,0:T(8,128)(2,1)S(1)}, bf16[80,768]{1,0:T(8,128...) custom-call(bf16[80,3072]{1,0:T(8,128)(2,1)S(1)} %collective-permute, ...), custom_call_target="tpu_custom_call", output_to_operand_aliasing={{0}: (2, {}), {1}: (3, {}), {2}: (4, {}), {3}: (5, {}), {4}... | custom-call | flops 1000 | bytes 1000 | tf_op jit(solution)/shard_map/pallas_call | solution.py:227
  27.4 11.1 %collective-permute-done.1.from_ref = bf16[80,3072]{1,0:T(8,128)(2,1)S(1)} collective-permute-done((bf16[80,3072]{1,0:T(8,128)(2,1)S(1)}, bf16[80,3072]{1,0:T(8,128)(2,1)S(1)}, u32[]{:S(2)}, u32[]{:S(2)}) %collective-permute-start.1) | collective-permute-done | bytes 491552 | tf_op jit(solution)/shard_map/ppermute | solution.py:619
  38.5 4.3 %shard_map.87 = (bf16[3072,3072]{1,0:T(8,128)(2,1)S(1)}, bf16[3,80,3072]{2,1,0:T(8,128)(2,1)S(1)}, bf16[80,768]{1,0:T(8,128)(2,1)S(1)}, bf16[80,768]{1,0:T(8,128...) custom-call(bf16[80,3072]{1,0:T(8,128)(2,1)S(1)} %collective-permute, ...), custom_call_target="tpu_custom_call", output_to_operand_aliasing={{0}: (2, {}), {1}: (3, {}), {2}: (4, {}), {3}: (5, {}), {4}... | custom-call | flops 1000 | bytes 1000 | tf_op jit(solution)/shard_map/pallas_call | solution.py:227
  45.1 7.3 %shard_map.88 = (bf16[3072,3072]{1,0:T(8,128)(2,1)S(1)}, bf16[3072,3072]{1,0:T(8,128)(2,1)S(1)}) custom-call(bf16[3072,3072]{1,0:T(8,128)(2,1)S(1)} %get-tuple-element.153.w_ref), custom_call_target="tpu_custom_call", output_to_operand_aliasing={{0}: (0, {})} | custom-call | flops 1000 | bytes 1000 | tf_op jit(solution)/shard_map/pallas_call | solution.py:269
  52.4 2.6 %collective-permute-done.2.from_ref = bf16[80,3072]{1,0:T(8,128)(2,1)S(1)} collective-permute-done((bf16[80,3072]{1,0:T(8,128)(2,1)S(1)}, bf16[80,3072]{1,0:T(8,128)(2,1)S(1)}, u32[]{:S(2)}, u32[]{:S(2)}) %collective-permute-start.2) | collective-permute-done | bytes 491552 | tf_op jit(solution)/shard_map/ppermute | solution.py:619
  55.0 4.3 %shard_map.89 = (bf16[3072,3072]{1,0:T(8,128)(2,1)S(1)}, bf16[3,80,3072]{2,1,0:T(8,128)(2,1)S(1)}, bf16[80,768]{1,0:T(8,128)(2,1)S(1)}, bf16[80,768]{1,0:T(8,128...) custom-call(bf16[80,3072]{1,0:T(8,128)(2,1)S(1)} %collective-permute, ...), custom_call_target="tpu_custom_call", output_to_operand_aliasing={{0}: (2, {}), {1}: (3, {}), {2}: (4, {}), {3}: (5, {}), {4}... | custom-call | flops 1000 | bytes 1000 | tf_op jit(solution)/shard_map/pallas_call | solution.py:227
  65.3 3.9 %collective-permute-done.3.from_ref = bf16[80,3072]{1,0:T(8,128)(2,1)S(1)} collective-permute-done((bf16[80,3072]{1,0:T(8,128)(2,1)S(1)}, bf16[80,3072]{1,0:T(8,128)(2,1)S(1)}, u32[]{:S(2)}, u32[]{:S(2)}) %collective-permute-start.3) | collective-permute-done | bytes 491552 | tf_op jit(solution)/shard_map/ppermute | solution.py:619
  78.5 13.2 %collective-permute-done.15.refs_9_ = bf16[80,3072]{1,0:T(8,128)(2,1)S(1)} collective-permute-done((bf16[80,3072]{1,0:T(8,128)(2,1)S(1)}, bf16[80,3072]{1,0:T(8,128)(2,1)S(1)}, u32[]{:S(2)}, u32[]{:S(2)}) %collective-permute-start.15) | collective-permute-done | bytes 491552 | tf_op jit(solution)/shard_map/ppermute | solution.py:627
  91.7 3.9 %shard_map.94 = (bf16[3072,3072]{1,0:T(8,128)(2,1)S(1)}, bf16[80,3072]{1,0:T(8,128)(2,1)S(1)}, bf16[80,3072]{1,0:T(8,128)(2,1)S(1)}, bf16[80,3072]{1,0:T(8,128)(2,1)S(1)}, bf16[80,3072]{1,0:T(8,128)(2,1)S(1)}) custom-call(bf16[80,768]{1,0:T(8,128)(2,1)S(1)} %collective-permute-done.8.refs_0_., ...), custom_call_target="tpu_custom_call", output_to_operand_aliasing={{0}: (3, {}), {1}: (6, {}), {2}: (7, {}), {3}: (8, {})} | custom-call | flops 1000 | bytes 1000 | tf_op jit(solution)/shard_map/pallas_call | solution.py:335
  105.6 3.9 %shard_map.95 = (bf16[3072,3072]{1,0:T(8,128)(2,1)S(1)}, bf16[80,3072]{1,0:T(8,128)(2,1)S(1)}, bf16[80,3072]{1,0:T(8,128)(2,1)S(1)}, bf16[80,3072]{1,0:T(8,128)(2,1)S(1)}, bf16[80,3072]{1,0:T(8,128)(2,1)S(1)}) custom-call(bf16[80,768]{1,0:T(8,128)(2,1)S(1)} %collective-permute-done.5.refs_0_., ...), custom_call_target="tpu_custom_call", output_to_operand_aliasing={{0}: (3, {}), {1}: (5, {}), {2}: (6, {}), {3}: (7, {})} | custom-call | flops 1000 | bytes 1000 | tf_op jit(solution)/shard_map/pallas_call | solution.py:335
  113.9 3.3 %collective-permute-done.21.refs_1_ = bf16[80,3072]{1,0:T(8,128)(2,1)S(1)} collective-permute-done((bf16[80,3072]{1,0:T(8,128)(2,1)S(1)}, bf16[80,3072]{1,0:T(8,128)(2,1)S(1)}, u32[]{:S(2)}, u32[]{:S(2)}) %collective-permute-start.21) | collective-permute-done | bytes 491552 | tf_op jit(solution)/shard_map/ppermute | solution.py:61
  120.6 3.9 %shard_map.96 = (bf16[3072,3072]{1,0:T(8,128)(2,1)S(1)}, bf16[80,3072]{1,0:T(8,128)(2,1)S(1)}, bf16[80,3072]{1,0:T(8,128)(2,1)S(1)}, bf16[80,3072]{1,0:T(8,128)(2,1)S(1)}) custom-call(bf16[3072,3072]{1,0:T(8,128)(2,1)S(1)} %get-tuple-element.213.refs_0_, ...), custom_call_target="tpu_custom_call", output_to_operand_aliasing={{0}: (0, {}), {1}: (2, {}), {2}: (3, {})} | custom-call | flops 1000 | bytes 1000 | tf_op jit(solution)/shard_map/pallas_call | solution.py:335
  127.4 3.2 %shard_map.97 = (f32[768,192]{1,0:T(8,128)S(1)}, bf16[2,192,192]{2,1,0:T(8,128)(2,1)S(1)}, bf16[8,384,384]{2,1,0:T(8,128)(2,1)S(1)}, bf16[768,320]{1,0:T(8,128)(...) custom-call(bf16[80,768]{1,0:T(8,128)(2,1)S(1)} %get-tuple-element.219.refs_0_, ...), custom_call_target="tpu_custom_call" | custom-call | flops 1000 | bytes 1000 | tf_op jit(solution)/shard_map/pallas_call | solution.py:407
  130.6 4.0 %shard_map.98 = (f32[384,3072]{1,0:T(8,128)S(1)}, f32[384,3072]{1,0:T(8,128)S(1)}, f32[768,192]{1,0:T(8,128)S(1)}) custom-call(bf16[80,3072]{1,0:T(8,128)(2,1)S(1)} %get-tuple-element.218.refs_0_, bf16[80,3072]{1,0:T(8,128)(2,1)S(1)} %collective-permute-done.21.refs_1_, bf16[80,3072]{1,0:T(8,128)(2,1)S(1)} %collective-permute-done.22.refs_2_, ...), custom_call_target="tpu_custom_call" | custom-call | flops 1000 | bytes 1000 | tf_op jit(solution)/shard_map/pallas_call | solution.py:467
  134.6 6.0 %collective-permute-done.18.refs_1_.refs_2_ = bf16[80,3072]{1,0:T(8,128)(2,1)S(1)} collective-permute-done((bf16[80,3072]{1,0:T(8,128)(2,1)S(1)}, bf16[80,3072]{1,0:T(8,128)(2,1)S(1)}, u32[]{:S(2)}, u32[]{:S(2)}) %collective-permute-start.18) | collective-permute-done | bytes 491552 | tf_op jit(solution)/shard_map/ppermute | solution.py:61
  143.3 5.3 %collective-permute-done.25.refs_1_ = bf16[80,3072]{1,0:T(8,128)(2,1)S(1)} collective-permute-done((bf16[80,3072]{1,0:T(8,128)(2,1)S(1)}, bf16[80,3072]{1,0:T(8,128)(2,1)S(1)}, u32[]{:S(2)}, u32[]{:S(2)}) %collective-permute-start.25) | collective-permute-done | bytes 491552 | tf_op jit(solution)/shard_map/ppermute | solution.py:61
  149.8 2.7 %shard_map.100 = (f32[384,3072]{1,0:T(8,128)S(1)}, f32[384,3072]{1,0:T(8,128)S(1)}, f32[768,192]{1,0:T(8,128)S(1)}) custom-call(bf16[80,3072]{1,0:T(8,128)(2,1)S(1)} %get-tuple-element.217.refs_0_, bf16[80,3072]{1,0:T(8,128)(2,1)S(1)} %collective-permute-done.20.refs_0_.refs_1_, ...), custom_call_target="tpu_custom_call", output_to_operand_aliasing={{0}: (4, {}), {1}: (5, {}), {2}: (6, {})} | custom-call | flops 1000 | bytes 1000 | tf_op jit(solution)/shard_map/pallas_call | solution.py:467
  152.6 2.7 %shard_map.101 = (f32[384,3072]{1,0:T(8,128)S(1)}, f32[384,3072]{1,0:T(8,128)S(1)}, f32[768,192]{1,0:T(8,128)S(1)}) custom-call(bf16[80,3072]{1,0:T(8,128)(2,1)S(1)} %get-tuple-element.227.refs_0_, bf16[80,3072]{1,0:T(8,128)(2,1)S(1)} %collective-permute-done.25.refs_1_, ...), custom_call_target="tpu_custom_call", output_to_operand_aliasing={{0}: (4, {}), {1}: (5, {}), {2}: (6, {})} | custom-call | flops 1000 | bytes 1000 | tf_op jit(solution)/shard_map/pallas_call | solution.py:467
  155.3 5.8 %collective-permute-done.26.second = bf16[80,3072]{1,0:T(8,128)(2,1)S(1)} collective-permute-done((bf16[80,3072]{1,0:T(8,128)(2,1)S(1)}, bf16[80,3072]{1,0:T(8,128)(2,1)S(1)}, u32[]{:S(2)}, u32[]{:S(2)}) %collective-permute-start.26) | collective-permute-done | bytes 491552 | tf_op jit(solution)/shard_map/ppermute | solution.py:61
  163.2 7.4 %collective-permute-start.28 = (bf16[384,3584]{1,0:T(8,128)(2,1)S(1)}, bf16[384,3584]{1,0:T(8,128)(2,1)S(1)}, u32[]{:S(2)}, u32[]{:S(2)}) collective-permute-start(bf16[384,3584]{1,0:T(8,128)(2,1)S(1)} %get-tuple-element.240), channel_id=1, source_target_pairs={{0,1},{1,0},{2,3},{3,2},{4,5},{5,4},{6,7},{7,6},{8,9},{9,8},{10,11... | collective-permute-start | bytes 8257544 | tf_op jit(solution)/shard_map/ppermute | solution.py:61
  172.3 3.1 %collective-permute-done.28.other_ref = bf16[384,3584]{1,0:T(8,128)(2,1)S(1)} collective-permute-done((bf16[384,3584]{1,0:T(8,128)(2,1)S(1)}, bf16[384,3584]{1,0:T(8,128)(2,1)S(1)}, u32[]{:S(2)}, u32[]{:S(2)}) %collective-permute-start.28) | collective-permute-done | bytes 2752544 | tf_op jit(solution)/shard_map/ppermute | solution.py:61
  175.4 3.2 %shard_map.104 = (bf16[384,3072]{1,0:T(8,128)(2,1)}, f32[2,192,192]{2,1,0:T(8,128)}, f32[2,192,192]{2,1,0:T(8,128)}) custom-call(f32[384,3072]{1,0:T(8,128)S(1)} %shard_map.102.own_ref, bf16[384,3584]{1,0:T(8,128)(2,1)S(1)} %collective-permute-done.28.other_ref, bf16[2,192,192]{2,1,0:T(8,128)(2,1)S(1)} %get-tuple-element.241.left_ref, ...), custom_call_target="tpu_custom_call" | custom-call | flops 1000 | bytes 1000 | tf_op jit(solution)/shard_map/pallas_call | solution.py:578
  (58 shorter events, 49.0 us)
Async XLA Ops:
  7.2 14.0 %collective-permute-start = (bf16[80,3072]{1,0:T(8,128)(2,1)S(1)}, bf16[80,3072]{1,0:T(8,128)(2,1)S(1)}, u32[]{:S(2)}, u32[]{:S(2)}) collective-permute-start(bf16[80,3072]{1,0:T(8,128)(2,1)S(1)} %get-tuple-element.125), channel_id=1, source_target_pairs={{0,8},{1,9},{2,10},{3,11},{4,12},{5,13},{6,14},{7,15}} | collective-permute-start | bytes 1474568 | tf_op jit(solution)/shard_map/ppermute | solution.py:619
  25.5 13.1 %collective-permute-start.1 = (bf16[80,3072]{1,0:T(8,128)(2,1)S(1)}, bf16[80,3072]{1,0:T(8,128)(2,1)S(1)}, u32[]{:S(2)}, u32[]{:S(2)}) collective-permute-start(bf16[80,3072]{1,0:T(8,128)(2,1)S(1)} %get-tuple-element.137), channel_id=1, source_target_pairs={{0,8},{8,16},{1,9},{9,17},{2,10},{10,18},{3,11},{11,19},{4,12},{12... | collective-permute-start | bytes 1474568 | tf_op jit(solution)/shard_map/ppermute | solution.py:619
  42.9 12.1 %collective-permute-start.2 = (bf16[80,3072]{1,0:T(8,128)(2,1)S(1)}, bf16[80,3072]{1,0:T(8,128)(2,1)S(1)}, u32[]{:S(2)}, u32[]{:S(2)}) collective-permute-start(bf16[80,3072]{1,0:T(8,128)(2,1)S(1)} %get-tuple-element.152), channel_id=1, source_target_pairs={{0,8},{8,16},{16,24},{1,9},{9,17},{17,25},{2,10},{10,18},{18,26},{... | collective-permute-start | bytes 1474568 | tf_op jit(solution)/shard_map/ppermute | solution.py:619
  59.3 9.8 %collective-permute-start.3 = (bf16[80,3072]{1,0:T(8,128)(2,1)S(1)}, bf16[80,3072]{1,0:T(8,128)(2,1)S(1)}, u32[]{:S(2)}, u32[]{:S(2)}) collective-permute-start(bf16[80,3072]{1,0:T(8,128)(2,1)S(1)} %get-tuple-element.168), channel_id=1, source_target_pairs={{8,16},{16,24},{9,17},{17,25},{10,18},{18,26},{11,19},{19,27},{12,... | collective-permute-start | bytes 1474568 | tf_op jit(solution)/shard_map/ppermute | solution.py:619
  61.8 8.0 %collective-permute-start.14 = (bf16[80,3072]{1,0:T(8,128)(2,1)S(1)}, bf16[80,3072]{1,0:T(8,128)(2,1)S(1)}, u32[]{:S(2)}, u32[]{:S(2)}) collective-permute-start(bf16[80,3072]{1,0:T(8,128)(2,1)S(1)} %get-tuple-element.201), channel_id=1, source_target_pairs={{24,16},{25,17},{26,18},{27,19},{28,20},{29,21},{30,22},{31,23}} | collective-permute-start | bytes 1474568 | tf_op jit(solution)/shard_map/ppermute | solution.py:627
  62.5 7.3 %collective-permute-start.11 = (bf16[80,768]{1,0:T(8,128)(2,1)S(1)}, bf16[80,768]{1,0:T(8,128)(2,1)S(1)}, u32[]{:S(2)}, u32[]{:S(2)}) collective-permute-start(bf16[80,768]{1,0:T(8,128)(2,1)S(1)} %get-tuple-element.192), channel_id=1, source_target_pairs={{0,2},{1,3},{2,0},{3,1},{4,6},{5,7},{6,4},{7,5},{8,10},{9,11},{10,... | collective-permute-start | bytes 368648 | tf_op jit(solution)/shard_map/ppermute | solution.py:61
  63.8 6.0 %collective-permute-start.12 = (bf16[80,768]{1,0:T(8,128)(2,1)S(1)}, bf16[80,768]{1,0:T(8,128)(2,1)S(1)}, u32[]{:S(2)}, u32[]{:S(2)}) collective-permute-start(bf16[80,768]{1,0:T(8,128)(2,1)S(1)} %get-tuple-element.193), channel_id=1, source_target_pairs={{0,4},{1,5},{2,6},{3,7},{4,0},{5,1},{6,2},{7,3},{8,12},{9,13},{10,... | collective-permute-start | bytes 368648 | tf_op jit(solution)/shard_map/ppermute | solution.py:61
  65.1 4.8 %collective-permute-start.13 = (bf16[80,768]{1,0:T(8,128)(2,1)S(1)}, bf16[80,768]{1,0:T(8,128)(2,1)S(1)}, u32[]{:S(2)}, u32[]{:S(2)}) collective-permute-start(bf16[80,768]{1,0:T(8,128)(2,1)S(1)} %get-tuple-element.194), channel_id=1, source_target_pairs={{0,6},{1,7},{2,4},{3,5},{4,2},{5,3},{6,0},{7,1},{8,14},{9,15},{10,... | collective-permute-start | bytes 368648 | tf_op jit(solution)/shard_map/ppermute | solution.py:61
  69.2 5.0 %collective-permute-start.4 = (bf16[80,3072]{1,0:T(8,128)(2,1)S(1)}, bf16[80,3072]{1,0:T(8,128)(2,1)S(1)}, u32[]{:S(2)}, u32[]{:S(2)}) collective-permute-start(bf16[80,3072]{1,0:T(8,128)(2,1)S(1)} %get-tuple-element.179), channel_id=1, source_target_pairs={{16,24},{17,25},{18,26},{19,27},{20,28},{21,29},{22,30},{23,31}} | collective-permute-start | bytes 1474568 | tf_op jit(solution)/shard_map/ppermute | solution.py:619
  70.1 21.6 %collective-permute-start.15 = (bf16[80,3072]{1,0:T(8,128)(2,1)S(1)}, bf16[80,3072]{1,0:T(8,128)(2,1)S(1)}, u32[]{:S(2)}, u32[]{:S(2)}) collective-permute-start(bf16[80,3072]{1,0:T(8,128)(2,1)S(1)} %get-tuple-element.207), channel_id=1, source_target_pairs={{16,8},{24,16},{17,9},{25,17},{18,10},{26,18},{19,11},{27,19},{20,... | collective-permute-start | bytes 1474568 | tf_op jit(solution)/shard_map/ppermute | solution.py:627
  73.9 4.6 %collective-permute-start.10 = (bf16[80,768]{1,0:T(8,128)(2,1)S(1)}, bf16[80,768]{1,0:T(8,128)(2,1)S(1)}, u32[]{:S(2)}, u32[]{:S(2)}) collective-permute-start(bf16[80,768]{1,0:T(8,128)(2,1)S(1)} %get-tuple-element.191), channel_id=1, source_target_pairs={{0,6},{1,7},{2,4},{3,5},{4,2},{5,3},{6,0},{7,1},{8,14},{9,15},{10,... | collective-permute-start | bytes 368648 | tf_op jit(solution)/shard_map/ppermute | solution.py:61
  95.6 9.9 %collective-permute-start.16 = (bf16[80,3072]{1,0:T(8,128)(2,1)S(1)}, bf16[80,3072]{1,0:T(8,128)(2,1)S(1)}, u32[]{:S(2)}, u32[]{:S(2)}) collective-permute-start(bf16[80,3072]{1,0:T(8,128)(2,1)S(1)} %get-tuple-element.212), channel_id=1, source_target_pairs={{8,0},{16,8},{24,16},{9,1},{17,9},{25,17},{10,2},{18,10},{26,18},{... | collective-permute-start | bytes 1474568 | tf_op jit(solution)/shard_map/ppermute | solution.py:627
  109.4 7.7 %collective-permute-start.21 = (bf16[80,3072]{1,0:T(8,128)(2,1)S(1)}, bf16[80,3072]{1,0:T(8,128)(2,1)S(1)}, u32[]{:S(2)}, u32[]{:S(2)}) collective-permute-start(bf16[80,3072]{1,0:T(8,128)(2,1)S(1)} %get-tuple-element.218.refs_0_), channel_id=1, source_target_pairs={{0,2},{1,3},{2,0},{3,1},{4,6},{5,7},{6,4},{7,5},{8,10},{9,11},{10,... | collective-permute-start | bytes 1474568 | tf_op jit(solution)/shard_map/ppermute | solution.py:61
  110.7 9.9 %collective-permute-start.17 = (bf16[80,3072]{1,0:T(8,128)(2,1)S(1)}, bf16[80,3072]{1,0:T(8,128)(2,1)S(1)}, u32[]{:S(2)}, u32[]{:S(2)}) collective-permute-start(bf16[80,3072]{1,0:T(8,128)(2,1)S(1)} %get-tuple-element.216), channel_id=1, source_target_pairs={{8,0},{16,8},{9,1},{17,9},{10,2},{18,10},{11,3},{19,11},{12,4},{20... | collective-permute-start | bytes 1474568 | tf_op jit(solution)/shard_map/ppermute | solution.py:627
  112.6 17.9 %collective-permute-start.22 = (bf16[80,3072]{1,0:T(8,128)(2,1)S(1)}, bf16[80,3072]{1,0:T(8,128)(2,1)S(1)}, u32[]{:S(2)}, u32[]{:S(2)}) collective-permute-start(bf16[80,3072]{1,0:T(8,128)(2,1)S(1)} %get-tuple-element.218.refs_0_), channel_id=1, source_target_pairs={{0,4},{1,5},{2,6},{3,7},{4,0},{5,1},{6,2},{7,3},{8,12},{9,13},{10,... | collective-permute-start | bytes 1474568 | tf_op jit(solution)/shard_map/ppermute | solution.py:61
  117.2 13.4 %collective-permute-start.23 = (bf16[80,3072]{1,0:T(8,128)(2,1)S(1)}, bf16[80,3072]{1,0:T(8,128)(2,1)S(1)}, u32[]{:S(2)}, u32[]{:S(2)}) collective-permute-start(bf16[80,3072]{1,0:T(8,128)(2,1)S(1)} %collective-permute-done.21.refs_1_), channel_id=1, source_target_pairs={{0,4},{1,5},{2,6},{3,7},{4,0},{5,1},{6,2},{7,3},{8,12},{9,13},{10,... | collective-permute-start | bytes 1474568 | tf_op jit(solution)/shard_map/ppermute | solution.py:61
  124.5 10.1 %collective-permute-start.24 = (bf16[80,3072]{1,0:T(8,128)(2,1)S(1)}, bf16[80,3072]{1,0:T(8,128)(2,1)S(1)}, u32[]{:S(2)}, u32[]{:S(2)}) collective-permute-start(bf16[80,3072]{1,0:T(8,128)(2,1)S(1)} %get-tuple-element.226), channel_id=1, source_target_pairs={{8,0},{9,1},{10,2},{11,3},{12,4},{13,5},{14,6},{15,7}} | collective-permute-start | bytes 1474568 | tf_op jit(solution)/shard_map/ppermute | solution.py:627
  125.8 8.8 %collective-permute-start.20 = (bf16[80,3072]{1,0:T(8,128)(2,1)S(1)}, bf16[80,3072]{1,0:T(8,128)(2,1)S(1)}, u32[]{:S(2)}, u32[]{:S(2)}) collective-permute-start(bf16[80,3072]{1,0:T(8,128)(2,1)S(1)} %get-tuple-element.217.refs_0_), channel_id=1, source_target_pairs={{0,2},{1,3},{2,0},{3,1},{4,6},{5,7},{6,4},{7,5},{8,10},{9,11},{10,... | collective-permute-start | bytes 1474568 | tf_op jit(solution)/shard_map/ppermute | solution.py:61
  126.1 14.5 %collective-permute-start.18 = (bf16[80,3072]{1,0:T(8,128)(2,1)S(1)}, bf16[80,3072]{1,0:T(8,128)(2,1)S(1)}, u32[]{:S(2)}, u32[]{:S(2)}) collective-permute-start(bf16[80,3072]{1,0:T(8,128)(2,1)S(1)} %get-tuple-element.217.refs_0_), channel_id=1, source_target_pairs={{0,4},{1,5},{2,6},{3,7},{4,0},{5,1},{6,2},{7,3},{8,12},{9,13},{10,... | collective-permute-start | bytes 1474568 | tf_op jit(solution)/shard_map/ppermute | solution.py:61
  140.6 8.0 %collective-permute-start.25 = (bf16[80,3072]{1,0:T(8,128)(2,1)S(1)}, bf16[80,3072]{1,0:T(8,128)(2,1)S(1)}, u32[]{:S(2)}, u32[]{:S(2)}) collective-permute-start(bf16[80,3072]{1,0:T(8,128)(2,1)S(1)} %get-tuple-element.227.refs_0_), channel_id=1, source_target_pairs={{0,2},{1,3},{2,0},{3,1},{4,6},{5,7},{6,4},{7,5},{8,10},{9,11},{10,... | collective-permute-start | bytes 1474568 | tf_op jit(solution)/shard_map/ppermute | solution.py:61
  141.3 11.3 %collective-permute-start.27 = (bf16[80,3072]{1,0:T(8,128)(2,1)S(1)}, bf16[80,3072]{1,0:T(8,128)(2,1)S(1)}, u32[]{:S(2)}, u32[]{:S(2)}) collective-permute-start(bf16[80,3072]{1,0:T(8,128)(2,1)S(1)} %get-tuple-element.227.refs_0_), channel_id=1, source_target_pairs={{0,4},{1,5},{2,6},{3,7},{4,0},{5,1},{6,2},{7,3},{8,12},{9,13},{10,... | collective-permute-start | bytes 1474568 | tf_op jit(solution)/shard_map/ppermute | solution.py:61
  142.5 12.8 %collective-permute-start.19 = (bf16[80,3072]{1,0:T(8,128)(2,1)S(1)}, bf16[80,3072]{1,0:T(8,128)(2,1)S(1)}, u32[]{:S(2)}, u32[]{:S(2)}) collective-permute-start(bf16[80,3072]{1,0:T(8,128)(2,1)S(1)} %collective-permute-done.18.refs_1_.refs_2_), channel_id=1, source_target_pairs={{0,2},{1,3},{2,0},{3,1},{4,6},{5,7},{6,4},{7,5},{8,10},{9,11},{10,... | collective-permute-start | bytes 1474568 | tf_op jit(solution)/shard_map/ppermute | solution.py:61
  148.6 12.6 %collective-permute-start.26 = (bf16[80,3072]{1,0:T(8,128)(2,1)S(1)}, bf16[80,3072]{1,0:T(8,128)(2,1)S(1)}, u32[]{:S(2)}, u32[]{:S(2)}) collective-permute-start(bf16[80,3072]{1,0:T(8,128)(2,1)S(1)} %collective-permute-done.25.refs_1_), channel_id=1, source_target_pairs={{0,4},{1,5},{2,6},{3,7},{4,0},{5,1},{6,2},{7,3},{8,12},{9,13},{10,... | collective-permute-start | bytes 1474568 | tf_op jit(solution)/shard_map/ppermute | solution.py:61
  163.2 12.2 %collective-permute-start.28 = (bf16[384,3584]{1,0:T(8,128)(2,1)S(1)}, bf16[384,3584]{1,0:T(8,128)(2,1)S(1)}, u32[]{:S(2)}, u32[]{:S(2)}) collective-permute-start(bf16[384,3584]{1,0:T(8,128)(2,1)S(1)} %get-tuple-element.240), channel_id=1, source_target_pairs={{0,1},{1,0},{2,3},{3,2},{4,5},{5,4},{6,7},{7,6},{8,9},{9,8},{10,11... | collective-permute-start | bytes 8257544 | tf_op jit(solution)/shard_map/ppermute | solution.py:61
  (7 other events, 33.2 us)

commit v9 on v8

--- a/solution.py
+++ b/solution.py
@@ -634,7 +634,7 @@
                     crossed, inverse_in[0], inverse_out[0]
                 )
             if 1 <= done == PIECES - 1:
-                after = after + [parts[done - 1][o] for o in single]
+                after = after + [parts[done - 1][o] for o in reversed(single)]
             if done >= 2:
                 acc = gather(parts[done - 2], rows_turned[done - 2], acc)
                 after = after + [acc[2]]
@@ -648,6 +648,8 @@
             piece = [kept[done]]
             for offset in range(1, chips):
                 bit = offset & -offset if done % 2 else 1 << (offset.bit_length() - 1)
+                if done < PIECES - 2:
+                    bit = offset
                 piece.append(swap(piece[offset ^ bit], ranks, 2 * bit))
             parts.append(piece)
     for index in range(PIECES - 2, PIECES):

time: 180 us -> 181 us (level)
  waiting for transfers between devices: 78.9 us -> 83.2 us
  starting transfers between devices: 40.6 us -> 38.6 us
    ppermute x5, waiting for transfers between devices: 16.2 us -> 19 us  [shards(): arrived_behind = lax.ppermute(behind, 'section', pairs)]
    ppermute x19, starting transfers between devices: 24.9 us -> 22.9 us  [swap(): return lax.ppermute(x, 'dp', [(r, r ^ flip) for r in range(ranks)])]
  transfers between devices with their start and end apart: 29 -> 29, of which waited for: 18 -> 19; matrix products, arithmetic and copies ran while one was open for 0% -> 0% of each run, Pallas kernels for 14% -> 14%
where the time goes in v9:
time: 181 us
  waiting for transfers between devices  83.2 us (46%)
  Pallas kernels  58.2 us (32%)
  starting transfers between devices  38.6 us (21%)
    ppermute x19, waiting for transfers between devices, swap(): return lax.ppermute(x, 'dp', [(r, r ^ flip) for r in range(ranks)])  33.9 us
    ppermute x5, waiting for transfers between devices, shards(): arrived_ahead = lax.ppermute(ahead, 'section', pairs)  30.4 us
    ppermute x19, starting transfers between devices, swap(): return lax.ppermute(x, 'dp', [(r, r ^ flip) for r in range(ranks)])  22.9 us
    ppermute x5, waiting for transfers between devices, shards(): arrived_behind = lax.ppermute(behind, 'section', pairs)  19 us
    pallas_call x5, Pallas kernels, forward(): pl.pallas_call(functools.partial(forward_kernel, tick, span, count, sends...  12.9 us
    pallas_call x6, Pallas kernels, backward(): pl.pallas_call(functools.partial(backward_kernel, tick, sections, span, l...  11.9 us
    pallas_call x3, Pallas kernels, gather(): pl.pallas_call(functools.partial(gather_kernel, count, not so_far), out_s...  9.45 us
    ppermute x5, starting transfers between devices, shards(): arrived_ahead = lax.ppermute(ahead, 'section', pairs)  8.58 us
  transfers between devices with their start and end apart: 29, of which 19 were waited for; matrix products, arithmetic and copies ran while one was open for 0% of the time, Pallas kernels for 14%

profile of v9, /device:TPU:9, one launch (start us, length us, event | category | flops | bytes accessed | tf_op | source)
XLA Modules:
  0.0 181.1 jit_solution(4716194540638766377)
XLA Ops:
  0.6 6.5 %shard_map.85 = (bf16[3072,3072]{1,0:T(8,128)(2,1)S(1)}, bf16[80,3072]{1,0:T(8,128)(2,1)S(1)}, bf16[3,80,3072]{2,1,0:T(8,128)(2,1)S(1)}, bf16[3,80,3072]{2,1,0:T...) custom-call(s32[1,4]{1,0:T(1,128)} %counts_ref.1, ...), custom_call_target="tpu_custom_call" | custom-call | flops 1000 | bytes 1000 | tf_op jit(solution)/shard_map/pallas_call | solution.py:167
  8.5 12.7 %collective-permute-done.from_ref = bf16[80,3072]{1,0:T(8,128)(2,1)S(1)} collective-permute-done((bf16[80,3072]{1,0:T(8,128)(2,1)S(1)}, bf16[80,3072]{1,0:T(8,128)(2,1)S(1)}, u32[]{:S(2)}, u32[]{:S(2)}) %collective-permute-start) | collective-permute-done | bytes 491552 | tf_op jit(solution)/shard_map/ppermute | solution.py:619
  21.2 4.3 %shard_map.86 = (bf16[3072,3072]{1,0:T(8,128)(2,1)S(1)}, bf16[3,80,3072]{2,1,0:T(8,128)(2,1)S(1)}, bf16[80,768]{1,0:T(8,128)(2,1)S(1)}, bf16[80,768]{1,0:T(8,128...) custom-call(bf16[80,3072]{1,0:T(8,128)(2,1)S(1)} %collective-permute, ...), custom_call_target="tpu_custom_call", output_to_operand_aliasing={{0}: (2, {}), {1}: (3, {}), {2}: (4, {}), {3}: (5, {}), {4}... | custom-call | flops 1000 | bytes 1000 | tf_op jit(solution)/shard_map/pallas_call | solution.py:227
  27.4 11.1 %collective-permute-done.1.from_ref = bf16[80,3072]{1,0:T(8,128)(2,1)S(1)} collective-permute-done((bf16[80,3072]{1,0:T(8,128)(2,1)S(1)}, bf16[80,3072]{1,0:T(8,128)(2,1)S(1)}, u32[]{:S(2)}, u32[]{:S(2)}) %collective-permute-start.1) | collective-permute-done | bytes 491552 | tf_op jit(solution)/shard_map/ppermute | solution.py:619
  38.5 4.3 %shard_map.87 = (bf16[3072,3072]{1,0:T(8,128)(2,1)S(1)}, bf16[3,80,3072]{2,1,0:T(8,128)(2,1)S(1)}, bf16[80,768]{1,0:T(8,128)(2,1)S(1)}, bf16[80,768]{1,0:T(8,128...) custom-call(bf16[80,3072]{1,0:T(8,128)(2,1)S(1)} %collective-permute, ...), custom_call_target="tpu_custom_call", output_to_operand_aliasing={{0}: (2, {}), {1}: (3, {}), {2}: (4, {}), {3}: (5, {}), {4}... | custom-call | flops 1000 | bytes 1000 | tf_op jit(solution)/shard_map/pallas_call | solution.py:227
  45.1 7.3 %shard_map.88 = (bf16[3072,3072]{1,0:T(8,128)(2,1)S(1)}, bf16[3072,3072]{1,0:T(8,128)(2,1)S(1)}) custom-call(bf16[3072,3072]{1,0:T(8,128)(2,1)S(1)} %get-tuple-element.153.w_ref), custom_call_target="tpu_custom_call", output_to_operand_aliasing={{0}: (0, {})} | custom-call | flops 1000 | bytes 1000 | tf_op jit(solution)/shard_map/pallas_call | solution.py:269
  55.0 4.3 %shard_map.89 = (bf16[3072,3072]{1,0:T(8,128)(2,1)S(1)}, bf16[3,80,3072]{2,1,0:T(8,128)(2,1)S(1)}, bf16[80,768]{1,0:T(8,128)(2,1)S(1)}, bf16[80,768]{1,0:T(8,128...) custom-call(bf16[80,3072]{1,0:T(8,128)(2,1)S(1)} %collective-permute, ...), custom_call_target="tpu_custom_call", output_to_operand_aliasing={{0}: (2, {}), {1}: (3, {}), {2}: (4, {}), {3}: (5, {}), {4}... | custom-call | flops 1000 | bytes 1000 | tf_op jit(solution)/shard_map/pallas_call | solution.py:227
  65.3 3.9 %collective-permute-done.3.from_ref = bf16[80,3072]{1,0:T(8,128)(2,1)S(1)} collective-permute-done((bf16[80,3072]{1,0:T(8,128)(2,1)S(1)}, bf16[80,3072]{1,0:T(8,128)(2,1)S(1)}, u32[]{:S(2)}, u32[]{:S(2)}) %collective-permute-start.3) | collective-permute-done | bytes 491552 | tf_op jit(solution)/shard_map/ppermute | solution.py:619
  78.5 13.2 %collective-permute-done.15.refs_9_ = bf16[80,3072]{1,0:T(8,128)(2,1)S(1)} collective-permute-done((bf16[80,3072]{1,0:T(8,128)(2,1)S(1)}, bf16[80,3072]{1,0:T(8,128)(2,1)S(1)}, u32[]{:S(2)}, u32[]{:S(2)}) %collective-permute-start.15) | collective-permute-done | bytes 491552 | tf_op jit(solution)/shard_map/ppermute | solution.py:627
  91.7 3.9 %shard_map.94 = (bf16[3072,3072]{1,0:T(8,128)(2,1)S(1)}, bf16[80,3072]{1,0:T(8,128)(2,1)S(1)}, bf16[80,3072]{1,0:T(8,128)(2,1)S(1)}, bf16[80,3072]{1,0:T(8,128)(2,1)S(1)}, bf16[80,3072]{1,0:T(8,128)(2,1)S(1)}) custom-call(bf16[80,768]{1,0:T(8,128)(2,1)S(1)} %collective-permute-done.8.refs_0_., ...), custom_call_target="tpu_custom_call", output_to_operand_aliasing={{0}: (3, {}), {1}: (6, {}), {2}: (7, {}), {3}: (8, {})} | custom-call | flops 1000 | bytes 1000 | tf_op jit(solution)/shard_map/pallas_call | solution.py:335
  105.6 3.9 %shard_map.95 = (bf16[3072,3072]{1,0:T(8,128)(2,1)S(1)}, bf16[80,3072]{1,0:T(8,128)(2,1)S(1)}, bf16[80,3072]{1,0:T(8,128)(2,1)S(1)}, bf16[80,3072]{1,0:T(8,128)(2,1)S(1)}, bf16[80,3072]{1,0:T(8,128)(2,1)S(1)}) custom-call(bf16[80,768]{1,0:T(8,128)(2,1)S(1)} %collective-permute-done.5.refs_0_., ...), custom_call_target="tpu_custom_call", output_to_operand_aliasing={{0}: (3, {}), {1}: (5, {}), {2}: (6, {}), {3}: (7, {})} | custom-call | flops 1000 | bytes 1000 | tf_op jit(solution)/shard_map/pallas_call | solution.py:335
  114.1 4.9 %collective-permute-done.17.refs_4_ = bf16[80,3072]{1,0:T(8,128)(2,1)S(1)} collective-permute-done((bf16[80,3072]{1,0:T(8,128)(2,1)S(1)}, bf16[80,3072]{1,0:T(8,128)(2,1)S(1)}, u32[]{:S(2)}, u32[]{:S(2)}) %collective-permute-start.17) | collective-permute-done | bytes 491552 | tf_op jit(solution)/shard_map/ppermute | solution.py:627
  119.0 3.9 %shard_map.96 = (bf16[3072,3072]{1,0:T(8,128)(2,1)S(1)}, bf16[80,3072]{1,0:T(8,128)(2,1)S(1)}, bf16[80,3072]{1,0:T(8,128)(2,1)S(1)}, bf16[80,3072]{1,0:T(8,128)(2,1)S(1)}) custom-call(bf16[3072,3072]{1,0:T(8,128)(2,1)S(1)} %get-tuple-element.213.refs_0_, ...), custom_call_target="tpu_custom_call", output_to_operand_aliasing={{0}: (0, {}), {1}: (2, {}), {2}: (3, {})} | custom-call | flops 1000 | bytes 1000 | tf_op jit(solution)/shard_map/pallas_call | solution.py:335
  126.8 3.2 %shard_map.97 = (f32[768,192]{1,0:T(8,128)S(1)}, bf16[2,192,192]{2,1,0:T(8,128)(2,1)S(1)}, bf16[8,384,384]{2,1,0:T(8,128)(2,1)S(1)}, bf16[768,320]{1,0:T(8,128)(...) custom-call(bf16[80,768]{1,0:T(8,128)(2,1)S(1)} %get-tuple-element.219.refs_0_, ...), custom_call_target="tpu_custom_call" | custom-call | flops 1000 | bytes 1000 | tf_op jit(solution)/shard_map/pallas_call | solution.py:407
  130.0 4.5 %collective-permute-done.22.refs_2_ = bf16[80,3072]{1,0:T(8,128)(2,1)S(1)} collective-permute-done((bf16[80,3072]{1,0:T(8,128)(2,1)S(1)}, bf16[80,3072]{1,0:T(8,128)(2,1)S(1)}, u32[]{:S(2)}, u32[]{:S(2)}) %collective-permute-start.22) | collective-permute-done | bytes 491552 | tf_op jit(solution)/shard_map/ppermute | solution.py:61
  134.4 4.0 %shard_map.98 = (f32[384,3072]{1,0:T(8,128)S(1)}, f32[384,3072]{1,0:T(8,128)S(1)}, f32[768,192]{1,0:T(8,128)S(1)}) custom-call(bf16[80,3072]{1,0:T(8,128)(2,1)S(1)} %get-tuple-element.218.refs_0_, bf16[80,3072]{1,0:T(8,128)(2,1)S(1)} %collective-permute-done.21.refs_1_, bf16[80,3072]{1,0:T(8,128)(2,1)S(1)} %collective-permute-done.22.refs_2_, ...), custom_call_target="tpu_custom_call" | custom-call | flops 1000 | bytes 1000 | tf_op jit(solution)/shard_map/pallas_call | solution.py:467
  140.7 4.3 %collective-permute-done.18.refs_0_.refs_2_ = bf16[80,3072]{1,0:T(8,128)(2,1)S(1)} collective-permute-done((bf16[80,3072]{1,0:T(8,128)(2,1)S(1)}, bf16[80,3072]{1,0:T(8,128)(2,1)S(1)}, u32[]{:S(2)}, u32[]{:S(2)}) %collective-permute-start.18) | collective-permute-done | bytes 491552 | tf_op jit(solution)/shard_map/ppermute | solution.py:61
  148.2 7.8 %collective-permute-done.25.refs_1_ = bf16[80,3072]{1,0:T(8,128)(2,1)S(1)} collective-permute-done((bf16[80,3072]{1,0:T(8,128)(2,1)S(1)}, bf16[80,3072]{1,0:T(8,128)(2,1)S(1)}, u32[]{:S(2)}, u32[]{:S(2)}) %collective-permute-start.25) | collective-permute-done | bytes 491552 | tf_op jit(solution)/shard_map/ppermute | solution.py:61
  157.9 2.7 %shard_map.100 = (f32[384,3072]{1,0:T(8,128)S(1)}, f32[384,3072]{1,0:T(8,128)S(1)}, f32[768,192]{1,0:T(8,128)S(1)}) custom-call(bf16[80,3072]{1,0:T(8,128)(2,1)S(1)} %get-tuple-element.217.refs_0_, bf16[80,3072]{1,0:T(8,128)(2,1)S(1)} %collective-permute-done.20.refs_1_, ...), custom_call_target="tpu_custom_call", output_to_operand_aliasing={{0}: (4, {}), {1}: (5, {}), {2}: (6, {})} | custom-call | flops 1000 | bytes 1000 | tf_op jit(solution)/shard_map/pallas_call | solution.py:467
  160.6 2.7 %shard_map.101 = (f32[384,3072]{1,0:T(8,128)S(1)}, f32[384,3072]{1,0:T(8,128)S(1)}, f32[768,192]{1,0:T(8,128)S(1)}) custom-call(bf16[80,3072]{1,0:T(8,128)(2,1)S(1)} %get-tuple-element.227.refs_0_, bf16[80,3072]{1,0:T(8,128)(2,1)S(1)} %collective-permute-done.25.refs_1_, ...), custom_call_target="tpu_custom_call", output_to_operand_aliasing={{0}: (4, {}), {1}: (5, {}), {2}: (6, {})} | custom-call | flops 1000 | bytes 1000 | tf_op jit(solution)/shard_map/pallas_call | solution.py:467
  163.4 3.1 %collective-permute-done.19.first = bf16[80,3072]{1,0:T(8,128)(2,1)S(1)} collective-permute-done((bf16[80,3072]{1,0:T(8,128)(2,1)S(1)}, bf16[80,3072]{1,0:T(8,128)(2,1)S(1)}, u32[]{:S(2)}, u32[]{:S(2)}) %collective-permute-start.19) | collective-permute-done | bytes 491552 | tf_op jit(solution)/shard_map/ppermute | solution.py:61
  168.6 4.4 %collective-permute-start.28 = (bf16[384,3584]{1,0:T(8,128)(2,1)S(1)}, bf16[384,3584]{1,0:T(8,128)(2,1)S(1)}, u32[]{:S(2)}, u32[]{:S(2)}) collective-permute-start(bf16[384,3584]{1,0:T(8,128)(2,1)S(1)} %get-tuple-element.240), channel_id=1, source_target_pairs={{0,1},{1,0},{2,3},{3,2},{4,5},{5,4},{6,7},{7,6},{8,9},{9,8},{10,11... | collective-permute-start | bytes 8257544 | tf_op jit(solution)/shard_map/ppermute | solution.py:61
  174.6 3.1 %collective-permute-done.28.other_ref = bf16[384,3584]{1,0:T(8,128)(2,1)S(1)} collective-permute-done((bf16[384,3584]{1,0:T(8,128)(2,1)S(1)}, bf16[384,3584]{1,0:T(8,128)(2,1)S(1)}, u32[]{:S(2)}, u32[]{:S(2)}) %collective-permute-start.28) | collective-permute-done | bytes 2752544 | tf_op jit(solution)/shard_map/ppermute | solution.py:61
  177.7 3.2 %shard_map.104 = (bf16[384,3072]{1,0:T(8,128)(2,1)}, f32[2,192,192]{2,1,0:T(8,128)}, f32[2,192,192]{2,1,0:T(8,128)}) custom-call(f32[384,3072]{1,0:T(8,128)S(1)} %shard_map.102.own_ref, bf16[384,3584]{1,0:T(8,128)(2,1)S(1)} %collective-permute-done.28.other_ref, bf16[2,192,192]{2,1,0:T(8,128)(2,1)S(1)} %get-tuple-element.241.left_ref, ...), custom_call_target="tpu_custom_call" | custom-call | flops 1000 | bytes 1000 | tf_op jit(solution)/shard_map/pallas_call | solution.py:578
  (58 shorter events, 52.7 us)
Async XLA Ops:
  7.2 14.0 %collective-permute-start = (bf16[80,3072]{1,0:T(8,128)(2,1)S(1)}, bf16[80,3072]{1,0:T(8,128)(2,1)S(1)}, u32[]{:S(2)}, u32[]{:S(2)}) collective-permute-start(bf16[80,3072]{1,0:T(8,128)(2,1)S(1)} %get-tuple-element.125), channel_id=1, source_target_pairs={{0,8},{1,9},{2,10},{3,11},{4,12},{5,13},{6,14},{7,15}} | collective-permute-start | bytes 1474568 | tf_op jit(solution)/shard_map/ppermute | solution.py:619
  25.5 13.1 %collective-permute-start.1 = (bf16[80,3072]{1,0:T(8,128)(2,1)S(1)}, bf16[80,3072]{1,0:T(8,128)(2,1)S(1)}, u32[]{:S(2)}, u32[]{:S(2)}) collective-permute-start(bf16[80,3072]{1,0:T(8,128)(2,1)S(1)} %get-tuple-element.137), channel_id=1, source_target_pairs={{0,8},{8,16},{1,9},{9,17},{2,10},{10,18},{3,11},{11,19},{4,12},{12... | collective-permute-start | bytes 1474568 | tf_op jit(solution)/shard_map/ppermute | solution.py:619
  42.9 12.1 %collective-permute-start.2 = (bf16[80,3072]{1,0:T(8,128)(2,1)S(1)}, bf16[80,3072]{1,0:T(8,128)(2,1)S(1)}, u32[]{:S(2)}, u32[]{:S(2)}) collective-permute-start(bf16[80,3072]{1,0:T(8,128)(2,1)S(1)} %get-tuple-element.152), channel_id=1, source_target_pairs={{0,8},{8,16},{16,24},{1,9},{9,17},{17,25},{2,10},{10,18},{18,26},{... | collective-permute-start | bytes 1474568 | tf_op jit(solution)/shard_map/ppermute | solution.py:619
  59.3 9.8 %collective-permute-start.3 = (bf16[80,3072]{1,0:T(8,128)(2,1)S(1)}, bf16[80,3072]{1,0:T(8,128)(2,1)S(1)}, u32[]{:S(2)}, u32[]{:S(2)}) collective-permute-start(bf16[80,3072]{1,0:T(8,128)(2,1)S(1)} %get-tuple-element.168), channel_id=1, source_target_pairs={{8,16},{16,24},{9,17},{17,25},{10,18},{18,26},{11,19},{19,27},{12,... | collective-permute-start | bytes 1474568 | tf_op jit(solution)/shard_map/ppermute | solution.py:619
  61.8 8.0 %collective-permute-start.14 = (bf16[80,3072]{1,0:T(8,128)(2,1)S(1)}, bf16[80,3072]{1,0:T(8,128)(2,1)S(1)}, u32[]{:S(2)}, u32[]{:S(2)}) collective-permute-start(bf16[80,3072]{1,0:T(8,128)(2,1)S(1)} %get-tuple-element.201), channel_id=1, source_target_pairs={{24,16},{25,17},{26,18},{27,19},{28,20},{29,21},{30,22},{31,23}} | collective-permute-start | bytes 1474568 | tf_op jit(solution)/shard_map/ppermute | solution.py:627
  62.5 7.3 %collective-permute-start.11 = (bf16[80,768]{1,0:T(8,128)(2,1)S(1)}, bf16[80,768]{1,0:T(8,128)(2,1)S(1)}, u32[]{:S(2)}, u32[]{:S(2)}) collective-permute-start(bf16[80,768]{1,0:T(8,128)(2,1)S(1)} %get-tuple-element.192), channel_id=1, source_target_pairs={{0,2},{1,3},{2,0},{3,1},{4,6},{5,7},{6,4},{7,5},{8,10},{9,11},{10,... | collective-permute-start | bytes 368648 | tf_op jit(solution)/shard_map/ppermute | solution.py:61
  63.8 6.0 %collective-permute-start.12 = (bf16[80,768]{1,0:T(8,128)(2,1)S(1)}, bf16[80,768]{1,0:T(8,128)(2,1)S(1)}, u32[]{:S(2)}, u32[]{:S(2)}) collective-permute-start(bf16[80,768]{1,0:T(8,128)(2,1)S(1)} %get-tuple-element.193), channel_id=1, source_target_pairs={{0,4},{1,5},{2,6},{3,7},{4,0},{5,1},{6,2},{7,3},{8,12},{9,13},{10,... | collective-permute-start | bytes 368648 | tf_op jit(solution)/shard_map/ppermute | solution.py:61
  65.1 4.8 %collective-permute-start.13 = (bf16[80,768]{1,0:T(8,128)(2,1)S(1)}, bf16[80,768]{1,0:T(8,128)(2,1)S(1)}, u32[]{:S(2)}, u32[]{:S(2)}) collective-permute-start(bf16[80,768]{1,0:T(8,128)(2,1)S(1)} %get-tuple-element.194), channel_id=1, source_target_pairs={{0,6},{1,7},{2,4},{3,5},{4,2},{5,3},{6,0},{7,1},{8,14},{9,15},{10,... | collective-permute-start | bytes 368648 | tf_op jit(solution)/shard_map/ppermute | solution.py:61
  69.2 5.0 %collective-permute-start.4 = (bf16[80,3072]{1,0:T(8,128)(2,1)S(1)}, bf16[80,3072]{1,0:T(8,128)(2,1)S(1)}, u32[]{:S(2)}, u32[]{:S(2)}) collective-permute-start(bf16[80,3072]{1,0:T(8,128)(2,1)S(1)} %get-tuple-element.179), channel_id=1, source_target_pairs={{16,24},{17,25},{18,26},{19,27},{20,28},{21,29},{22,30},{23,31}} | collective-permute-start | bytes 1474568 | tf_op jit(solution)/shard_map/ppermute | solution.py:619
  70.1 21.6 %collective-permute-start.15 = (bf16[80,3072]{1,0:T(8,128)(2,1)S(1)}, bf16[80,3072]{1,0:T(8,128)(2,1)S(1)}, u32[]{:S(2)}, u32[]{:S(2)}) collective-permute-start(bf16[80,3072]{1,0:T(8,128)(2,1)S(1)} %get-tuple-element.207), channel_id=1, source_target_pairs={{16,8},{24,16},{17,9},{25,17},{18,10},{26,18},{19,11},{27,19},{20,... | collective-permute-start | bytes 1474568 | tf_op jit(solution)/shard_map/ppermute | solution.py:627
  73.9 4.6 %collective-permute-start.10 = (bf16[80,768]{1,0:T(8,128)(2,1)S(1)}, bf16[80,768]{1,0:T(8,128)(2,1)S(1)}, u32[]{:S(2)}, u32[]{:S(2)}) collective-permute-start(bf16[80,768]{1,0:T(8,128)(2,1)S(1)} %get-tuple-element.191), channel_id=1, source_target_pairs={{0,6},{1,7},{2,4},{3,5},{4,2},{5,3},{6,0},{7,1},{8,14},{9,15},{10,... | collective-permute-start | bytes 368648 | tf_op jit(solution)/shard_map/ppermute | solution.py:61
  95.6 9.9 %collective-permute-start.16 = (bf16[80,3072]{1,0:T(8,128)(2,1)S(1)}, bf16[80,3072]{1,0:T(8,128)(2,1)S(1)}, u32[]{:S(2)}, u32[]{:S(2)}) collective-permute-start(bf16[80,3072]{1,0:T(8,128)(2,1)S(1)} %get-tuple-element.212), channel_id=1, source_target_pairs={{8,0},{16,8},{24,16},{9,1},{17,9},{25,17},{10,2},{18,10},{26,18},{... | collective-permute-start | bytes 1474568 | tf_op jit(solution)/shard_map/ppermute | solution.py:627
  109.4 9.6 %collective-permute-start.17 = (bf16[80,3072]{1,0:T(8,128)(2,1)S(1)}, bf16[80,3072]{1,0:T(8,128)(2,1)S(1)}, u32[]{:S(2)}, u32[]{:S(2)}) collective-permute-start(bf16[80,3072]{1,0:T(8,128)(2,1)S(1)} %get-tuple-element.216), channel_id=1, source_target_pairs={{8,0},{16,8},{9,1},{17,9},{10,2},{18,10},{11,3},{19,11},{12,4},{20... | collective-permute-start | bytes 1474568 | tf_op jit(solution)/shard_map/ppermute | solution.py:627
  111.4 14.2 %collective-permute-start.23 = (bf16[80,3072]{1,0:T(8,128)(2,1)S(1)}, bf16[80,3072]{1,0:T(8,128)(2,1)S(1)}, u32[]{:S(2)}, u32[]{:S(2)}) collective-permute-start(bf16[80,3072]{1,0:T(8,128)(2,1)S(1)} %get-tuple-element.218.refs_0_), channel_id=1, source_target_pairs={{0,6},{1,7},{2,4},{3,5},{4,2},{5,3},{6,0},{7,1},{8,14},{9,15},{10,... | collective-permute-start | bytes 1474568 | tf_op jit(solution)/shard_map/ppermute | solution.py:61
  113.6 20.8 %collective-permute-start.22 = (bf16[80,3072]{1,0:T(8,128)(2,1)S(1)}, bf16[80,3072]{1,0:T(8,128)(2,1)S(1)}, u32[]{:S(2)}, u32[]{:S(2)}) collective-permute-start(bf16[80,3072]{1,0:T(8,128)(2,1)S(1)} %get-tuple-element.218.refs_0_), channel_id=1, source_target_pairs={{0,4},{1,5},{2,6},{3,7},{4,0},{5,1},{6,2},{7,3},{8,12},{9,13},{10,... | collective-permute-start | bytes 1474568 | tf_op jit(solution)/shard_map/ppermute | solution.py:61
  113.8 20.6 %collective-permute-start.21 = (bf16[80,3072]{1,0:T(8,128)(2,1)S(1)}, bf16[80,3072]{1,0:T(8,128)(2,1)S(1)}, u32[]{:S(2)}, u32[]{:S(2)}) collective-permute-start(bf16[80,3072]{1,0:T(8,128)(2,1)S(1)} %get-tuple-element.218.refs_0_), channel_id=1, source_target_pairs={{0,2},{1,3},{2,0},{3,1},{4,6},{5,7},{6,4},{7,5},{8,10},{9,11},{10,... | collective-permute-start | bytes 1474568 | tf_op jit(solution)/shard_map/ppermute | solution.py:61
  122.9 15.5 %collective-permute-start.24 = (bf16[80,3072]{1,0:T(8,128)(2,1)S(1)}, bf16[80,3072]{1,0:T(8,128)(2,1)S(1)}, u32[]{:S(2)}, u32[]{:S(2)}) collective-permute-start(bf16[80,3072]{1,0:T(8,128)(2,1)S(1)} %get-tuple-element.226), channel_id=1, source_target_pairs={{8,0},{9,1},{10,2},{11,3},{12,4},{13,5},{14,6},{15,7}} | collective-permute-start | bytes 1474568 | tf_op jit(solution)/shard_map/ppermute | solution.py:627
  124.2 16.4 %collective-permute-start.20 = (bf16[80,3072]{1,0:T(8,128)(2,1)S(1)}, bf16[80,3072]{1,0:T(8,128)(2,1)S(1)}, u32[]{:S(2)}, u32[]{:S(2)}) collective-permute-start(bf16[80,3072]{1,0:T(8,128)(2,1)S(1)} %get-tuple-element.217.refs_0_), channel_id=1, source_target_pairs={{0,2},{1,3},{2,0},{3,1},{4,6},{5,7},{6,4},{7,5},{8,10},{9,11},{10,... | collective-permute-start | bytes 1474568 | tf_op jit(solution)/shard_map/ppermute | solution.py:61
  125.5 19.4 %collective-permute-start.18 = (bf16[80,3072]{1,0:T(8,128)(2,1)S(1)}, bf16[80,3072]{1,0:T(8,128)(2,1)S(1)}, u32[]{:S(2)}, u32[]{:S(2)}) collective-permute-start(bf16[80,3072]{1,0:T(8,128)(2,1)S(1)} %get-tuple-element.217.refs_0_), channel_id=1, source_target_pairs={{0,4},{1,5},{2,6},{3,7},{4,0},{5,1},{6,2},{7,3},{8,12},{9,13},{10,... | collective-permute-start | bytes 1474568 | tf_op jit(solution)/shard_map/ppermute | solution.py:61
  145.0 11.0 %collective-permute-start.25 = (bf16[80,3072]{1,0:T(8,128)(2,1)S(1)}, bf16[80,3072]{1,0:T(8,128)(2,1)S(1)}, u32[]{:S(2)}, u32[]{:S(2)}) collective-permute-start(bf16[80,3072]{1,0:T(8,128)(2,1)S(1)} %get-tuple-element.227.refs_0_), channel_id=1, source_target_pairs={{0,2},{1,3},{2,0},{3,1},{4,6},{5,7},{6,4},{7,5},{8,10},{9,11},{10,... | collective-permute-start | bytes 1474568 | tf_op jit(solution)/shard_map/ppermute | solution.py:61
  146.7 14.0 %collective-permute-start.27 = (bf16[80,3072]{1,0:T(8,128)(2,1)S(1)}, bf16[80,3072]{1,0:T(8,128)(2,1)S(1)}, u32[]{:S(2)}, u32[]{:S(2)}) collective-permute-start(bf16[80,3072]{1,0:T(8,128)(2,1)S(1)} %get-tuple-element.227.refs_0_), channel_id=1, source_target_pairs={{0,4},{1,5},{2,6},{3,7},{4,0},{5,1},{6,2},{7,3},{8,12},{9,13},{10,... | collective-permute-start | bytes 1474568 | tf_op jit(solution)/shard_map/ppermute | solution.py:61
  147.3 19.2 %collective-permute-start.19 = (bf16[80,3072]{1,0:T(8,128)(2,1)S(1)}, bf16[80,3072]{1,0:T(8,128)(2,1)S(1)}, u32[]{:S(2)}, u32[]{:S(2)}) collective-permute-start(bf16[80,3072]{1,0:T(8,128)(2,1)S(1)} %collective-permute-done.18.refs_0_.refs_2_), channel_id=1, source_target_pairs={{0,2},{1,3},{2,0},{3,1},{4,6},{5,7},{6,4},{7,5},{8,10},{9,11},{10,... | collective-permute-start | bytes 1474568 | tf_op jit(solution)/shard_map/ppermute | solution.py:61
  156.0 10.5 %collective-permute-start.26 = (bf16[80,3072]{1,0:T(8,128)(2,1)S(1)}, bf16[80,3072]{1,0:T(8,128)(2,1)S(1)}, u32[]{:S(2)}, u32[]{:S(2)}) collective-permute-start(bf16[80,3072]{1,0:T(8,128)(2,1)S(1)} %collective-permute-done.25.refs_1_), channel_id=1, source_target_pairs={{0,4},{1,5},{2,6},{3,7},{4,0},{5,1},{6,2},{7,3},{8,12},{9,13},{10,... | collective-permute-start | bytes 1474568 | tf_op jit(solution)/shard_map/ppermute | solution.py:61
  168.6 9.1 %collective-permute-start.28 = (bf16[384,3584]{1,0:T(8,128)(2,1)S(1)}, bf16[384,3584]{1,0:T(8,128)(2,1)S(1)}, u32[]{:S(2)}, u32[]{:S(2)}) collective-permute-start(bf16[384,3584]{1,0:T(8,128)(2,1)S(1)} %get-tuple-element.240), channel_id=1, source_target_pairs={{0,1},{1,0},{2,3},{3,2},{4,5},{5,4},{6,7},{7,6},{8,9},{9,8},{10,11... | collective-permute-start | bytes 8257544 | tf_op jit(solution)/shard_map/ppermute | solution.py:61
  (7 other events, 35.2 us)

commit v10 on v9

--- a/solution.py
+++ b/solution.py
@@ -437,6 +437,22 @@
         place = own_first(block * BLOCK, width // 2)
         gram = contract_last(turned[rows], turned[rows])
         gram_ref[place, :] = gram if begins else gram + gram_ref[place, :]
+
+
+def hold_kernel(*refs):
+    pass
+
+
+def hold(x, after):
+    return pl.pallas_call(
+        hold_kernel,
+        out_shape=near(*x.shape),
+        in_specs=[VM, HB],
+        out_specs=VM,
+        input_output_aliases={0: 0},
+        compiler_params=limit(1),
+        cost_estimate=SMALL,
+    )(resident(x), after)
 
 
 def fill(parts, every):
@@ -645,13 +661,26 @@
             swapped = [swap(stores[known][o], ranks, 2 * o) for o in range(1, chips)]
             crossed.append([stores[known][0]] + swapped)
         if 0 <= done < PIECES:
-            piece = [kept[done]]
-            for offset in range(1, chips):
-                bit = offset & -offset if done % 2 else 1 << (offset.bit_length() - 1)
-                if done < PIECES - 2:
-                    bit = offset
-                piece.append(swap(piece[offset ^ bit], ranks, 2 * bit))
+            piece = [kept[done]] + [None] * (chips - 1)
+            for bit in single:
+                piece[bit] = swap(kept[done], ranks, 2 * bit)
             parts.append(piece)
+            ready = [done]
+            if done == PIECES - 2:
+                ready = []
+            elif done == PIECES - 1:
+                for bit in single:
+                    parts[-2][bit] = hold(parts[-2][bit], piece[1])
+                ready = [PIECES - 1, PIECES - 2]
+            for index in ready:
+                piece = parts[index]
+                for offset in range(1, chips):
+                    if offset in single:
+                        continue
+                    bit = offset & -offset if index % 2 else 1 << (offset.bit_length() - 1)
+                    if index < PIECES - 2:
+                        bit = offset
+                    piece[offset] = swap(piece[offset ^ bit], ranks, 2 * bit)
     for index in range(PIECES - 2, PIECES):
         acc = gather(parts[index][:-1], rows_turned[index], acc)
     final = [parts[-2][-1], parts[-1][-1]]

time: 181 us -> 182 us (level)
  transfers between devices with their start and end apart: 29 -> 29, of which waited for: 19 -> 20; matrix products, arithmetic and copies ran while one was open for 0% -> 0% of each run, Pallas kernels for 14% -> 14%
where the time goes in v10:
time: 182 us
  waiting for transfers between devices  84.6 us (46%)
  Pallas kernels  58.2 us (32%)
  starting transfers between devices  37.7 us (21%)
    ppermute x19, waiting for transfers between devices, swap(): return lax.ppermute(x, 'dp', [(r, r ^ flip) for r in range(ranks)])  35.3 us
    ppermute x5, waiting for transfers between devices, shards(): arrived_ahead = lax.ppermute(ahead, 'section', pairs)  30.4 us
    ppermute x19, starting transfers between devices, swap(): return lax.ppermute(x, 'dp', [(r, r ^ flip) for r in range(ranks)])  22 us
    ppermute x5, waiting for transfers between devices, shards(): arrived_behind = lax.ppermute(behind, 'section', pairs)  19 us
    pallas_call x5, Pallas kernels, forward(): pl.pallas_call(functools.partial(forward_kernel, tick, span, count, sends...  12.9 us
    pallas_call x6, Pallas kernels, backward(): pl.pallas_call(functools.partial(backward_kernel, tick, sections, span, l...  11.9 us
    pallas_call x3, Pallas kernels, gather(): pl.pallas_call(functools.partial(gather_kernel, count, not so_far), out_s...  9.45 us
    ppermute x5, starting transfers between devices, shards(): arrived_ahead = lax.ppermute(ahead, 'section', pairs)  8.58 us
  transfers between devices with their start and end apart: 29, of which 20 were waited for; matrix products, arithmetic and copies ran while one was open for 0% of the time, Pallas kernels for 14%

profile of v10, /device:TPU:9, one launch (start us, length us, event | category | flops | bytes accessed | tf_op | source)
XLA Modules:
  0.0 181.6 jit_solution(15518719144752643045)
XLA Ops:
  0.6 6.5 %shard_map.85 = (bf16[3072,3072]{1,0:T(8,128)(2,1)S(1)}, bf16[80,3072]{1,0:T(8,128)(2,1)S(1)}, bf16[3,80,3072]{2,1,0:T(8,128)(2,1)S(1)}, bf16[3,80,3072]{2,1,0:T...) custom-call(s32[1,4]{1,0:T(1,128)} %counts_ref.1, ...), custom_call_target="tpu_custom_call" | custom-call | flops 1000 | bytes 1000 | tf_op jit(solution)/shard_map/pallas_call | solution.py:167
  8.5 12.7 %collective-permute-done.from_ref = bf16[80,3072]{1,0:T(8,128)(2,1)S(1)} collective-permute-done((bf16[80,3072]{1,0:T(8,128)(2,1)S(1)}, bf16[80,3072]{1,0:T(8,128)(2,1)S(1)}, u32[]{:S(2)}, u32[]{:S(2)}) %collective-permute-start) | collective-permute-done | bytes 491552 | tf_op jit(solution)/shard_map/ppermute | solution.py:635
  21.2 4.3 %shard_map.86 = (bf16[3072,3072]{1,0:T(8,128)(2,1)S(1)}, bf16[3,80,3072]{2,1,0:T(8,128)(2,1)S(1)}, bf16[80,768]{1,0:T(8,128)(2,1)S(1)}, bf16[80,768]{1,0:T(8,128...) custom-call(bf16[80,3072]{1,0:T(8,128)(2,1)S(1)} %collective-permute, ...), custom_call_target="tpu_custom_call", output_to_operand_aliasing={{0}: (2, {}), {1}: (3, {}), {2}: (4, {}), {3}: (5, {}), {4}... | custom-call | flops 1000 | bytes 1000 | tf_op jit(solution)/shard_map/pallas_call | solution.py:227
  27.4 11.1 %collective-permute-done.1.from_ref = bf16[80,3072]{1,0:T(8,128)(2,1)S(1)} collective-permute-done((bf16[80,3072]{1,0:T(8,128)(2,1)S(1)}, bf16[80,3072]{1,0:T(8,128)(2,1)S(1)}, u32[]{:S(2)}, u32[]{:S(2)}) %collective-permute-start.1) | collective-permute-done | bytes 491552 | tf_op jit(solution)/shard_map/ppermute | solution.py:635
  38.5 4.3 %shard_map.87 = (bf16[3072,3072]{1,0:T(8,128)(2,1)S(1)}, bf16[3,80,3072]{2,1,0:T(8,128)(2,1)S(1)}, bf16[80,768]{1,0:T(8,128)(2,1)S(1)}, bf16[80,768]{1,0:T(8,128...) custom-call(bf16[80,3072]{1,0:T(8,128)(2,1)S(1)} %collective-permute, ...), custom_call_target="tpu_custom_call", output_to_operand_aliasing={{0}: (2, {}), {1}: (3, {}), {2}: (4, {}), {3}: (5, {}), {4}... | custom-call | flops 1000 | bytes 1000 | tf_op jit(solution)/shard_map/pallas_call | solution.py:227
  45.1 7.3 %shard_map.88 = (bf16[3072,3072]{1,0:T(8,128)(2,1)S(1)}, bf16[3072,3072]{1,0:T(8,128)(2,1)S(1)}) custom-call(bf16[3072,3072]{1,0:T(8,128)(2,1)S(1)} %get-tuple-element.153.w_ref), custom_call_target="tpu_custom_call", output_to_operand_aliasing={{0}: (0, {})} | custom-call | flops 1000 | bytes 1000 | tf_op jit(solution)/shard_map/pallas_call | solution.py:269
  52.4 2.6 %collective-permute-done.2.from_ref = bf16[80,3072]{1,0:T(8,128)(2,1)S(1)} collective-permute-done((bf16[80,3072]{1,0:T(8,128)(2,1)S(1)}, bf16[80,3072]{1,0:T(8,128)(2,1)S(1)}, u32[]{:S(2)}, u32[]{:S(2)}) %collective-permute-start.2) | collective-permute-done | bytes 491552 | tf_op jit(solution)/shard_map/ppermute | solution.py:635
  55.0 4.3 %shard_map.89 = (bf16[3072,3072]{1,0:T(8,128)(2,1)S(1)}, bf16[3,80,3072]{2,1,0:T(8,128)(2,1)S(1)}, bf16[80,768]{1,0:T(8,128)(2,1)S(1)}, bf16[80,768]{1,0:T(8,128...) custom-call(bf16[80,3072]{1,0:T(8,128)(2,1)S(1)} %collective-permute, ...), custom_call_target="tpu_custom_call", output_to_operand_aliasing={{0}: (2, {}), {1}: (3, {}), {2}: (4, {}), {3}: (5, {}), {4}... | custom-call | flops 1000 | bytes 1000 | tf_op jit(solution)/shard_map/pallas_call | solution.py:227
  65.3 3.9 %collective-permute-done.3.from_ref = bf16[80,3072]{1,0:T(8,128)(2,1)S(1)} collective-permute-done((bf16[80,3072]{1,0:T(8,128)(2,1)S(1)}, bf16[80,3072]{1,0:T(8,128)(2,1)S(1)}, u32[]{:S(2)}, u32[]{:S(2)}) %collective-permute-start.3) | collective-permute-done | bytes 491552 | tf_op jit(solution)/shard_map/ppermute | solution.py:635
  78.5 13.2 %collective-permute-done.15.refs_9_ = bf16[80,3072]{1,0:T(8,128)(2,1)S(1)} collective-permute-done((bf16[80,3072]{1,0:T(8,128)(2,1)S(1)}, bf16[80,3072]{1,0:T(8,128)(2,1)S(1)}, u32[]{:S(2)}, u32[]{:S(2)}) %collective-permute-start.15) | collective-permute-done | bytes 491552 | tf_op jit(solution)/shard_map/ppermute | solution.py:643
  91.7 3.9 %shard_map.94 = (bf16[3072,3072]{1,0:T(8,128)(2,1)S(1)}, bf16[80,3072]{1,0:T(8,128)(2,1)S(1)}, bf16[80,3072]{1,0:T(8,128)(2,1)S(1)}, bf16[80,3072]{1,0:T(8,128)(2,1)S(1)}, bf16[80,3072]{1,0:T(8,128)(2,1)S(1)}) custom-call(bf16[80,768]{1,0:T(8,128)(2,1)S(1)} %collective-permute-done.8.refs_0_., ...), custom_call_target="tpu_custom_call", output_to_operand_aliasing={{0}: (3, {}), {1}: (6, {}), {2}: (7, {}), {3}: (8, {})} | custom-call | flops 1000 | bytes 1000 | tf_op jit(solution)/shard_map/pallas_call | solution.py:335
  105.6 3.9 %shard_map.95 = (bf16[3072,3072]{1,0:T(8,128)(2,1)S(1)}, bf16[80,3072]{1,0:T(8,128)(2,1)S(1)}, bf16[80,3072]{1,0:T(8,128)(2,1)S(1)}, bf16[80,3072]{1,0:T(8,128)(2,1)S(1)}, bf16[80,3072]{1,0:T(8,128)(2,1)S(1)}) custom-call(bf16[80,768]{1,0:T(8,128)(2,1)S(1)} %collective-permute-done.5.refs_0_., ...), custom_call_target="tpu_custom_call", output_to_operand_aliasing={{0}: (3, {}), {1}: (5, {}), {2}: (6, {}), {3}: (7, {})} | custom-call | flops 1000 | bytes 1000 | tf_op jit(solution)/shard_map/pallas_call | solution.py:335
  114.1 4.9 %collective-permute-done.17.refs_4_ = bf16[80,3072]{1,0:T(8,128)(2,1)S(1)} collective-permute-done((bf16[80,3072]{1,0:T(8,128)(2,1)S(1)}, bf16[80,3072]{1,0:T(8,128)(2,1)S(1)}, u32[]{:S(2)}, u32[]{:S(2)}) %collective-permute-start.17) | collective-permute-done | bytes 491552 | tf_op jit(solution)/shard_map/ppermute | solution.py:643
  119.0 3.9 %shard_map.96 = (bf16[3072,3072]{1,0:T(8,128)(2,1)S(1)}, bf16[80,3072]{1,0:T(8,128)(2,1)S(1)}, bf16[80,3072]{1,0:T(8,128)(2,1)S(1)}, bf16[80,3072]{1,0:T(8,128)(2,1)S(1)}) custom-call(bf16[3072,3072]{1,0:T(8,128)(2,1)S(1)} %get-tuple-element.213.refs_0_, ...), custom_call_target="tpu_custom_call", output_to_operand_aliasing={{0}: (0, {}), {1}: (2, {}), {2}: (3, {})} | custom-call | flops 1000 | bytes 1000 | tf_op jit(solution)/shard_map/pallas_call | solution.py:335
  126.8 3.2 %shard_map.97 = (f32[768,192]{1,0:T(8,128)S(1)}, bf16[2,192,192]{2,1,0:T(8,128)(2,1)S(1)}, bf16[8,384,384]{2,1,0:T(8,128)(2,1)S(1)}, bf16[768,320]{1,0:T(8,128)(...) custom-call(bf16[80,768]{1,0:T(8,128)(2,1)S(1)} %get-tuple-element.219.refs_0_, ...), custom_call_target="tpu_custom_call" | custom-call | flops 1000 | bytes 1000 | tf_op jit(solution)/shard_map/pallas_call | solution.py:407
  130.0 4.5 %collective-permute-done.21.refs_2_ = bf16[80,3072]{1,0:T(8,128)(2,1)S(1)} collective-permute-done((bf16[80,3072]{1,0:T(8,128)(2,1)S(1)}, bf16[80,3072]{1,0:T(8,128)(2,1)S(1)}, u32[]{:S(2)}, u32[]{:S(2)}) %collective-permute-start.21) | collective-permute-done | bytes 491552 | tf_op jit(solution)/shard_map/ppermute | solution.py:61
  134.4 4.0 %shard_map.98 = (f32[384,3072]{1,0:T(8,128)S(1)}, f32[384,3072]{1,0:T(8,128)S(1)}, f32[768,192]{1,0:T(8,128)S(1)}) custom-call(bf16[80,3072]{1,0:T(8,128)(2,1)S(1)} %get-tuple-element.218.refs_0_, bf16[80,3072]{1,0:T(8,128)(2,1)S(1)} %collective-permute-done.20.refs_1_, bf16[80,3072]{1,0:T(8,128)(2,1)S(1)} %collective-permute-done.21.refs_2_, ...), custom_call_target="tpu_custom_call" | custom-call | flops 1000 | bytes 1000 | tf_op jit(solution)/shard_map/pallas_call | solution.py:483
  140.7 4.3 %collective-permute-done.18.refs_0_ = bf16[80,3072]{1,0:T(8,128)(2,1)S(1)} collective-permute-done((bf16[80,3072]{1,0:T(8,128)(2,1)S(1)}, bf16[80,3072]{1,0:T(8,128)(2,1)S(1)}, u32[]{:S(2)}, u32[]{:S(2)}) %collective-permute-start.18) | collective-permute-done | bytes 491552 | tf_op jit(solution)/shard_map/ppermute | solution.py:61
  147.3 8.7 %collective-permute-done.24.refs_1_ = bf16[80,3072]{1,0:T(8,128)(2,1)S(1)} collective-permute-done((bf16[80,3072]{1,0:T(8,128)(2,1)S(1)}, bf16[80,3072]{1,0:T(8,128)(2,1)S(1)}, u32[]{:S(2)}, u32[]{:S(2)}) %collective-permute-start.24) | collective-permute-done | bytes 491552 | tf_op jit(solution)/shard_map/ppermute | solution.py:61
  158.4 2.7 %shard_map.102 = (f32[384,3072]{1,0:T(8,128)S(1)}, f32[384,3072]{1,0:T(8,128)S(1)}, f32[768,192]{1,0:T(8,128)S(1)}) custom-call(bf16[80,3072]{1,0:T(8,128)(2,1)S(1)} %get-tuple-element.217.refs_0_, bf16[80,3072]{1,0:T(8,128)(2,1)S(1)} %shard_map.101.refs_1_, ...), custom_call_target="tpu_custom_call", output_to_operand_aliasing={{0}: (4, {}), {1}: (5, {}), {2}: (6, {})} | custom-call | flops 1000 | bytes 1000 | tf_op jit(solution)/shard_map/pallas_call | solution.py:483
  161.2 2.7 %shard_map.103 = (f32[384,3072]{1,0:T(8,128)S(1)}, f32[384,3072]{1,0:T(8,128)S(1)}, f32[768,192]{1,0:T(8,128)S(1)}) custom-call(bf16[80,3072]{1,0:T(8,128)(2,1)S(1)} %get-tuple-element.227.refs_0_, bf16[80,3072]{1,0:T(8,128)(2,1)S(1)} %collective-permute-done.24.refs_1_, ...), custom_call_target="tpu_custom_call", output_to_operand_aliasing={{0}: (4, {}), {1}: (5, {}), {2}: (6, {})} | custom-call | flops 1000 | bytes 1000 | tf_op jit(solution)/shard_map/pallas_call | solution.py:483
  169.6 3.9 %collective-permute-start.28 = (bf16[384,3584]{1,0:T(8,128)(2,1)S(1)}, bf16[384,3584]{1,0:T(8,128)(2,1)S(1)}, u32[]{:S(2)}, u32[]{:S(2)}) collective-permute-start(bf16[384,3584]{1,0:T(8,128)(2,1)S(1)} %get-tuple-element.240), channel_id=1, source_target_pairs={{0,1},{1,0},{2,3},{3,2},{4,5},{5,4},{6,7},{7,6},{8,9},{9,8},{10,11... | collective-permute-start | bytes 8257544 | tf_op jit(solution)/shard_map/ppermute | solution.py:61
  175.1 3.1 %collective-permute-done.28.other_ref = bf16[384,3584]{1,0:T(8,128)(2,1)S(1)} collective-permute-done((bf16[384,3584]{1,0:T(8,128)(2,1)S(1)}, bf16[384,3584]{1,0:T(8,128)(2,1)S(1)}, u32[]{:S(2)}, u32[]{:S(2)}) %collective-permute-start.28) | collective-permute-done | bytes 2752544 | tf_op jit(solution)/shard_map/ppermute | solution.py:61
  178.2 3.2 %shard_map.106 = (bf16[384,3072]{1,0:T(8,128)(2,1)}, f32[2,192,192]{2,1,0:T(8,128)}, f32[2,192,192]{2,1,0:T(8,128)}) custom-call(f32[384,3072]{1,0:T(8,128)S(1)} %shard_map.104.own_ref, bf16[384,3584]{1,0:T(8,128)(2,1)S(1)} %collective-permute-done.28.other_ref, bf16[2,192,192]{2,1,0:T(8,128)(2,1)S(1)} %get-tuple-element.241.left_ref, ...), custom_call_target="tpu_custom_call" | custom-call | flops 1000 | bytes 1000 | tf_op jit(solution)/shard_map/pallas_call | solution.py:594
  (60 shorter events, 53.3 us)
Async XLA Ops:
  7.2 14.0 %collective-permute-start = (bf16[80,3072]{1,0:T(8,128)(2,1)S(1)}, bf16[80,3072]{1,0:T(8,128)(2,1)S(1)}, u32[]{:S(2)}, u32[]{:S(2)}) collective-permute-start(bf16[80,3072]{1,0:T(8,128)(2,1)S(1)} %get-tuple-element.125), channel_id=1, source_target_pairs={{0,8},{1,9},{2,10},{3,11},{4,12},{5,13},{6,14},{7,15}} | collective-permute-start | bytes 1474568 | tf_op jit(solution)/shard_map/ppermute | solution.py:635
  25.5 13.1 %collective-permute-start.1 = (bf16[80,3072]{1,0:T(8,128)(2,1)S(1)}, bf16[80,3072]{1,0:T(8,128)(2,1)S(1)}, u32[]{:S(2)}, u32[]{:S(2)}) collective-permute-start(bf16[80,3072]{1,0:T(8,128)(2,1)S(1)} %get-tuple-element.137), channel_id=1, source_target_pairs={{0,8},{8,16},{1,9},{9,17},{2,10},{10,18},{3,11},{11,19},{4,12},{12... | collective-permute-start | bytes 1474568 | tf_op jit(solution)/shard_map/ppermute | solution.py:635
  42.9 12.1 %collective-permute-start.2 = (bf16[80,3072]{1,0:T(8,128)(2,1)S(1)}, bf16[80,3072]{1,0:T(8,128)(2,1)S(1)}, u32[]{:S(2)}, u32[]{:S(2)}) collective-permute-start(bf16[80,3072]{1,0:T(8,128)(2,1)S(1)} %get-tuple-element.152), channel_id=1, source_target_pairs={{0,8},{8,16},{16,24},{1,9},{9,17},{17,25},{2,10},{10,18},{18,26},{... | collective-permute-start | bytes 1474568 | tf_op jit(solution)/shard_map/ppermute | solution.py:635
  59.3 9.8 %collective-permute-start.3 = (bf16[80,3072]{1,0:T(8,128)(2,1)S(1)}, bf16[80,3072]{1,0:T(8,128)(2,1)S(1)}, u32[]{:S(2)}, u32[]{:S(2)}) collective-permute-start(bf16[80,3072]{1,0:T(8,128)(2,1)S(1)} %get-tuple-element.168), channel_id=1, source_target_pairs={{8,16},{16,24},{9,17},{17,25},{10,18},{18,26},{11,19},{19,27},{12,... | collective-permute-start | bytes 1474568 | tf_op jit(solution)/shard_map/ppermute | solution.py:635
  61.8 8.0 %collective-permute-start.14 = (bf16[80,3072]{1,0:T(8,128)(2,1)S(1)}, bf16[80,3072]{1,0:T(8,128)(2,1)S(1)}, u32[]{:S(2)}, u32[]{:S(2)}) collective-permute-start(bf16[80,3072]{1,0:T(8,128)(2,1)S(1)} %get-tuple-element.201), channel_id=1, source_target_pairs={{24,16},{25,17},{26,18},{27,19},{28,20},{29,21},{30,22},{31,23}} | collective-permute-start | bytes 1474568 | tf_op jit(solution)/shard_map/ppermute | solution.py:643
  62.5 7.3 %collective-permute-start.11 = (bf16[80,768]{1,0:T(8,128)(2,1)S(1)}, bf16[80,768]{1,0:T(8,128)(2,1)S(1)}, u32[]{:S(2)}, u32[]{:S(2)}) collective-permute-start(bf16[80,768]{1,0:T(8,128)(2,1)S(1)} %get-tuple-element.192), channel_id=1, source_target_pairs={{0,2},{1,3},{2,0},{3,1},{4,6},{5,7},{6,4},{7,5},{8,10},{9,11},{10,... | collective-permute-start | bytes 368648 | tf_op jit(solution)/shard_map/ppermute | solution.py:61
  63.8 6.0 %collective-permute-start.12 = (bf16[80,768]{1,0:T(8,128)(2,1)S(1)}, bf16[80,768]{1,0:T(8,128)(2,1)S(1)}, u32[]{:S(2)}, u32[]{:S(2)}) collective-permute-start(bf16[80,768]{1,0:T(8,128)(2,1)S(1)} %get-tuple-element.193), channel_id=1, source_target_pairs={{0,4},{1,5},{2,6},{3,7},{4,0},{5,1},{6,2},{7,3},{8,12},{9,13},{10,... | collective-permute-start | bytes 368648 | tf_op jit(solution)/shard_map/ppermute | solution.py:61
  65.1 4.8 %collective-permute-start.13 = (bf16[80,768]{1,0:T(8,128)(2,1)S(1)}, bf16[80,768]{1,0:T(8,128)(2,1)S(1)}, u32[]{:S(2)}, u32[]{:S(2)}) collective-permute-start(bf16[80,768]{1,0:T(8,128)(2,1)S(1)} %get-tuple-element.194), channel_id=1, source_target_pairs={{0,6},{1,7},{2,4},{3,5},{4,2},{5,3},{6,0},{7,1},{8,14},{9,15},{10,... | collective-permute-start | bytes 368648 | tf_op jit(solution)/shard_map/ppermute | solution.py:61
  69.2 5.0 %collective-permute-start.4 = (bf16[80,3072]{1,0:T(8,128)(2,1)S(1)}, bf16[80,3072]{1,0:T(8,128)(2,1)S(1)}, u32[]{:S(2)}, u32[]{:S(2)}) collective-permute-start(bf16[80,3072]{1,0:T(8,128)(2,1)S(1)} %get-tuple-element.179), channel_id=1, source_target_pairs={{16,24},{17,25},{18,26},{19,27},{20,28},{21,29},{22,30},{23,31}} | collective-permute-start | bytes 1474568 | tf_op jit(solution)/shard_map/ppermute | solution.py:635
  70.1 21.6 %collective-permute-start.15 = (bf16[80,3072]{1,0:T(8,128)(2,1)S(1)}, bf16[80,3072]{1,0:T(8,128)(2,1)S(1)}, u32[]{:S(2)}, u32[]{:S(2)}) collective-permute-start(bf16[80,3072]{1,0:T(8,128)(2,1)S(1)} %get-tuple-element.207), channel_id=1, source_target_pairs={{16,8},{24,16},{17,9},{25,17},{18,10},{26,18},{19,11},{27,19},{20,... | collective-permute-start | bytes 1474568 | tf_op jit(solution)/shard_map/ppermute | solution.py:643
  95.6 9.9 %collective-permute-start.16 = (bf16[80,3072]{1,0:T(8,128)(2,1)S(1)}, bf16[80,3072]{1,0:T(8,128)(2,1)S(1)}, u32[]{:S(2)}, u32[]{:S(2)}) collective-permute-start(bf16[80,3072]{1,0:T(8,128)(2,1)S(1)} %get-tuple-element.212), channel_id=1, source_target_pairs={{8,0},{16,8},{24,16},{9,1},{17,9},{25,17},{10,2},{18,10},{26,18},{... | collective-permute-start | bytes 1474568 | tf_op jit(solution)/shard_map/ppermute | solution.py:643
  100.1 4.6 %collective-permute-start.7 = (bf16[80,768]{1,0:T(8,128)(2,1)S(1)}, bf16[80,768]{1,0:T(8,128)(2,1)S(1)}, u32[]{:S(2)}, u32[]{:S(2)}) collective-permute-start(bf16[80,768]{1,0:T(8,128)(2,1)S(1)} %get-tuple-element.188), channel_id=1, source_target_pairs={{0,6},{1,7},{2,4},{3,5},{4,2},{5,3},{6,0},{7,1},{8,14},{9,15},{10,... | collective-permute-start | bytes 368648 | tf_op jit(solution)/shard_map/ppermute | solution.py:61
  109.4 9.6 %collective-permute-start.17 = (bf16[80,3072]{1,0:T(8,128)(2,1)S(1)}, bf16[80,3072]{1,0:T(8,128)(2,1)S(1)}, u32[]{:S(2)}, u32[]{:S(2)}) collective-permute-start(bf16[80,3072]{1,0:T(8,128)(2,1)S(1)} %get-tuple-element.216), channel_id=1, source_target_pairs={{8,0},{16,8},{9,1},{17,9},{10,2},{18,10},{11,3},{19,11},{12,4},{20... | collective-permute-start | bytes 1474568 | tf_op jit(solution)/shard_map/ppermute | solution.py:643
  111.4 14.2 %collective-permute-start.22 = (bf16[80,3072]{1,0:T(8,128)(2,1)S(1)}, bf16[80,3072]{1,0:T(8,128)(2,1)S(1)}, u32[]{:S(2)}, u32[]{:S(2)}) collective-permute-start(bf16[80,3072]{1,0:T(8,128)(2,1)S(1)} %get-tuple-element.218.refs_0_), channel_id=1, source_target_pairs={{0,6},{1,7},{2,4},{3,5},{4,2},{5,3},{6,0},{7,1},{8,14},{9,15},{10,... | collective-permute-start | bytes 1474568 | tf_op jit(solution)/shard_map/ppermute | solution.py:61
  113.6 20.8 %collective-permute-start.21 = (bf16[80,3072]{1,0:T(8,128)(2,1)S(1)}, bf16[80,3072]{1,0:T(8,128)(2,1)S(1)}, u32[]{:S(2)}, u32[]{:S(2)}) collective-permute-start(bf16[80,3072]{1,0:T(8,128)(2,1)S(1)} %get-tuple-element.218.refs_0_), channel_id=1, source_target_pairs={{0,4},{1,5},{2,6},{3,7},{4,0},{5,1},{6,2},{7,3},{8,12},{9,13},{10,... | collective-permute-start | bytes 1474568 | tf_op jit(solution)/shard_map/ppermute | solution.py:61
  113.8 20.6 %collective-permute-start.20 = (bf16[80,3072]{1,0:T(8,128)(2,1)S(1)}, bf16[80,3072]{1,0:T(8,128)(2,1)S(1)}, u32[]{:S(2)}, u32[]{:S(2)}) collective-permute-start(bf16[80,3072]{1,0:T(8,128)(2,1)S(1)} %get-tuple-element.218.refs_0_), channel_id=1, source_target_pairs={{0,2},{1,3},{2,0},{3,1},{4,6},{5,7},{6,4},{7,5},{8,10},{9,11},{10,... | collective-permute-start | bytes 1474568 | tf_op jit(solution)/shard_map/ppermute | solution.py:61
  122.9 15.5 %collective-permute-start.23 = (bf16[80,3072]{1,0:T(8,128)(2,1)S(1)}, bf16[80,3072]{1,0:T(8,128)(2,1)S(1)}, u32[]{:S(2)}, u32[]{:S(2)}) collective-permute-start(bf16[80,3072]{1,0:T(8,128)(2,1)S(1)} %get-tuple-element.226), channel_id=1, source_target_pairs={{8,0},{9,1},{10,2},{11,3},{12,4},{13,5},{14,6},{15,7}} | collective-permute-start | bytes 1474568 | tf_op jit(solution)/shard_map/ppermute | solution.py:643
  124.2 16.4 %collective-permute-start.19 = (bf16[80,3072]{1,0:T(8,128)(2,1)S(1)}, bf16[80,3072]{1,0:T(8,128)(2,1)S(1)}, u32[]{:S(2)}, u32[]{:S(2)}) collective-permute-start(bf16[80,3072]{1,0:T(8,128)(2,1)S(1)} %get-tuple-element.217.refs_0_), channel_id=1, source_target_pairs={{0,2},{1,3},{2,0},{3,1},{4,6},{5,7},{6,4},{7,5},{8,10},{9,11},{10,... | collective-permute-start | bytes 1474568 | tf_op jit(solution)/shard_map/ppermute | solution.py:61
  125.5 19.4 %collective-permute-start.18 = (bf16[80,3072]{1,0:T(8,128)(2,1)S(1)}, bf16[80,3072]{1,0:T(8,128)(2,1)S(1)}, u32[]{:S(2)}, u32[]{:S(2)}) collective-permute-start(bf16[80,3072]{1,0:T(8,128)(2,1)S(1)} %get-tuple-element.217.refs_0_), channel_id=1, source_target_pairs={{0,4},{1,5},{2,6},{3,7},{4,0},{5,1},{6,2},{7,3},{8,12},{9,13},{10,... | collective-permute-start | bytes 1474568 | tf_op jit(solution)/shard_map/ppermute | solution.py:61
  145.0 11.0 %collective-permute-start.24 = (bf16[80,3072]{1,0:T(8,128)(2,1)S(1)}, bf16[80,3072]{1,0:T(8,128)(2,1)S(1)}, u32[]{:S(2)}, u32[]{:S(2)}) collective-permute-start(bf16[80,3072]{1,0:T(8,128)(2,1)S(1)} %get-tuple-element.227.refs_0_), channel_id=1, source_target_pairs={{0,2},{1,3},{2,0},{3,1},{4,6},{5,7},{6,4},{7,5},{8,10},{9,11},{10,... | collective-permute-start | bytes 1474568 | tf_op jit(solution)/shard_map/ppermute | solution.py:61
  146.7 14.5 %collective-permute-start.27 = (bf16[80,3072]{1,0:T(8,128)(2,1)S(1)}, bf16[80,3072]{1,0:T(8,128)(2,1)S(1)}, u32[]{:S(2)}, u32[]{:S(2)}) collective-permute-start(bf16[80,3072]{1,0:T(8,128)(2,1)S(1)} %get-tuple-element.227.refs_0_), channel_id=1, source_target_pairs={{0,4},{1,5},{2,6},{3,7},{4,0},{5,1},{6,2},{7,3},{8,12},{9,13},{10,... | collective-permute-start | bytes 1474568 | tf_op jit(solution)/shard_map/ppermute | solution.py:61
  156.0 10.3 %collective-permute-start.25 = (bf16[80,3072]{1,0:T(8,128)(2,1)S(1)}, bf16[80,3072]{1,0:T(8,128)(2,1)S(1)}, u32[]{:S(2)}, u32[]{:S(2)}) collective-permute-start(bf16[80,3072]{1,0:T(8,128)(2,1)S(1)} %shard_map.100.refs_2_), channel_id=1, source_target_pairs={{0,2},{1,3},{2,0},{3,1},{4,6},{5,7},{6,4},{7,5},{8,10},{9,11},{10,... | collective-permute-start | bytes 1474568 | tf_op jit(solution)/shard_map/ppermute | solution.py:61
  157.7 9.8 %collective-permute-start.26 = (bf16[80,3072]{1,0:T(8,128)(2,1)S(1)}, bf16[80,3072]{1,0:T(8,128)(2,1)S(1)}, u32[]{:S(2)}, u32[]{:S(2)}) collective-permute-start(bf16[80,3072]{1,0:T(8,128)(2,1)S(1)} %collective-permute-done.24.refs_1_), channel_id=1, source_target_pairs={{0,4},{1,5},{2,6},{3,7},{4,0},{5,1},{6,2},{7,3},{8,12},{9,13},{10,... | collective-permute-start | bytes 1474568 | tf_op jit(solution)/shard_map/ppermute | solution.py:61
  169.6 8.6 %collective-permute-start.28 = (bf16[384,3584]{1,0:T(8,128)(2,1)S(1)}, bf16[384,3584]{1,0:T(8,128)(2,1)S(1)}, u32[]{:S(2)}, u32[]{:S(2)}) collective-permute-start(bf16[384,3584]{1,0:T(8,128)(2,1)S(1)} %get-tuple-element.240), channel_id=1, source_target_pairs={{0,1},{1,0},{2,3},{3,2},{4,5},{5,4},{6,7},{7,6},{8,9},{9,8},{10,11... | collective-permute-start | bytes 8257544 | tf_op jit(solution)/shard_map/ppermute | solution.py:61
  (7 other events, 35.2 us)

commit v11 on v8

--- a/solution.py
+++ b/solution.py
@@ -634,7 +634,7 @@
                     crossed, inverse_in[0], inverse_out[0]
                 )
             if 1 <= done == PIECES - 1:
-                after = after + [parts[done - 1][o] for o in single]
+                after = after + [parts[done - 1][1]]
             if done >= 2:
                 acc = gather(parts[done - 2], rows_turned[done - 2], acc)
                 after = after + [acc[2]]

time: 180 us -> 179 us (level)
  starting transfers between devices: 40.6 us -> 37.7 us
  waiting for transfers between devices: 78.9 us -> 81.6 us
    ppermute x19, starting transfers between devices: 24.9 us -> 21.9 us  [swap(): return lax.ppermute(x, 'dp', [(r, r ^ flip) for r in range(ranks)])]
    ppermute x19, waiting for transfers between devices: 32.3 us -> 35.1 us  [swap(): return lax.ppermute(x, 'dp', [(r, r ^ flip) for r in range(ranks)])]
  transfers between devices with their start and end apart: 29 -> 29, of which waited for: 18 -> 19; matrix products, arithmetic and copies ran while one was open for 0% -> 0% of each run, Pallas kernels for 14% -> 14%
where the time goes in v11:
time: 179 us
  waiting for transfers between devices  81.6 us (46%)
  Pallas kernels  58.4 us (33%)
  starting transfers between devices  37.7 us (21%)
    ppermute x19, waiting for transfers between devices, swap(): return lax.ppermute(x, 'dp', [(r, r ^ flip) for r in range(ranks)])  35.1 us
    ppermute x5, waiting for transfers between devices, shards(): arrived_ahead = lax.ppermute(ahead, 'section', pairs)  30.4 us
    ppermute x19, starting transfers between devices, swap(): return lax.ppermute(x, 'dp', [(r, r ^ flip) for r in range(ranks)])  21.9 us
    ppermute x5, waiting for transfers between devices, shards(): arrived_behind = lax.ppermute(behind, 'section', pairs)  16.2 us
    pallas_call x5, Pallas kernels, forward(): pl.pallas_call(functools.partial(forward_kernel, tick, span, count, sends...  12.9 us
    pallas_call x6, Pallas kernels, backward(): pl.pallas_call(functools.partial(backward_kernel, tick, sections, span, l...  12.1 us
    pallas_call x3, Pallas kernels, gather(): pl.pallas_call(functools.partial(gather_kernel, count, not so_far), out_s...  9.45 us
    ppermute x5, starting transfers between devices, shards(): arrived_ahead = lax.ppermute(ahead, 'section', pairs)  8.58 us
  transfers between devices with their start and end apart: 29, of which 19 were waited for; matrix products, arithmetic and copies ran while one was open for 0% of the time, Pallas kernels for 14%

profile of v11, /device:TPU:9, one launch (start us, length us, event | category | flops | bytes accessed | tf_op | source)
XLA Modules:
  0.0 178.8 jit_solution(3992461504584484855)
XLA Ops:
  0.6 6.5 %shard_map.85 = (bf16[3072,3072]{1,0:T(8,128)(2,1)S(1)}, bf16[80,3072]{1,0:T(8,128)(2,1)S(1)}, bf16[3,80,3072]{2,1,0:T(8,128)(2,1)S(1)}, bf16[3,80,3072]{2,1,0:T...) custom-call(s32[1,4]{1,0:T(1,128)} %counts_ref.1, ...), custom_call_target="tpu_custom_call" | custom-call | flops 1000 | bytes 1000 | tf_op jit(solution)/shard_map/pallas_call | solution.py:167
  8.5 12.7 %collective-permute-done.from_ref = bf16[80,3072]{1,0:T(8,128)(2,1)S(1)} collective-permute-done((bf16[80,3072]{1,0:T(8,128)(2,1)S(1)}, bf16[80,3072]{1,0:T(8,128)(2,1)S(1)}, u32[]{:S(2)}, u32[]{:S(2)}) %collective-permute-start) | collective-permute-done | bytes 491552 | tf_op jit(solution)/shard_map/ppermute | solution.py:619
  21.2 4.3 %shard_map.86 = (bf16[3072,3072]{1,0:T(8,128)(2,1)S(1)}, bf16[3,80,3072]{2,1,0:T(8,128)(2,1)S(1)}, bf16[80,768]{1,0:T(8,128)(2,1)S(1)}, bf16[80,768]{1,0:T(8,128...) custom-call(bf16[80,3072]{1,0:T(8,128)(2,1)S(1)} %collective-permute, ...), custom_call_target="tpu_custom_call", output_to_operand_aliasing={{0}: (2, {}), {1}: (3, {}), {2}: (4, {}), {3}: (5, {}), {4}... | custom-call | flops 1000 | bytes 1000 | tf_op jit(solution)/shard_map/pallas_call | solution.py:227
  27.4 11.1 %collective-permute-done.1.from_ref = bf16[80,3072]{1,0:T(8,128)(2,1)S(1)} collective-permute-done((bf16[80,3072]{1,0:T(8,128)(2,1)S(1)}, bf16[80,3072]{1,0:T(8,128)(2,1)S(1)}, u32[]{:S(2)}, u32[]{:S(2)}) %collective-permute-start.1) | collective-permute-done | bytes 491552 | tf_op jit(solution)/shard_map/ppermute | solution.py:619
  38.5 4.3 %shard_map.87 = (bf16[3072,3072]{1,0:T(8,128)(2,1)S(1)}, bf16[3,80,3072]{2,1,0:T(8,128)(2,1)S(1)}, bf16[80,768]{1,0:T(8,128)(2,1)S(1)}, bf16[80,768]{1,0:T(8,128...) custom-call(bf16[80,3072]{1,0:T(8,128)(2,1)S(1)} %collective-permute, ...), custom_call_target="tpu_custom_call", output_to_operand_aliasing={{0}: (2, {}), {1}: (3, {}), {2}: (4, {}), {3}: (5, {}), {4}... | custom-call | flops 1000 | bytes 1000 | tf_op jit(solution)/shard_map/pallas_call | solution.py:227
  45.1 7.3 %shard_map.88 = (bf16[3072,3072]{1,0:T(8,128)(2,1)S(1)}, bf16[3072,3072]{1,0:T(8,128)(2,1)S(1)}) custom-call(bf16[3072,3072]{1,0:T(8,128)(2,1)S(1)} %get-tuple-element.153.w_ref), custom_call_target="tpu_custom_call", output_to_operand_aliasing={{0}: (0, {})} | custom-call | flops 1000 | bytes 1000 | tf_op jit(solution)/shard_map/pallas_call | solution.py:269
  55.0 4.3 %shard_map.89 = (bf16[3072,3072]{1,0:T(8,128)(2,1)S(1)}, bf16[3,80,3072]{2,1,0:T(8,128)(2,1)S(1)}, bf16[80,768]{1,0:T(8,128)(2,1)S(1)}, bf16[80,768]{1,0:T(8,128...) custom-call(bf16[80,3072]{1,0:T(8,128)(2,1)S(1)} %collective-permute, ...), custom_call_target="tpu_custom_call", output_to_operand_aliasing={{0}: (2, {}), {1}: (3, {}), {2}: (4, {}), {3}: (5, {}), {4}... | custom-call | flops 1000 | bytes 1000 | tf_op jit(solution)/shard_map/pallas_call | solution.py:227
  65.3 3.9 %collective-permute-done.3.from_ref = bf16[80,3072]{1,0:T(8,128)(2,1)S(1)} collective-permute-done((bf16[80,3072]{1,0:T(8,128)(2,1)S(1)}, bf16[80,3072]{1,0:T(8,128)(2,1)S(1)}, u32[]{:S(2)}, u32[]{:S(2)}) %collective-permute-start.3) | collective-permute-done | bytes 491552 | tf_op jit(solution)/shard_map/ppermute | solution.py:619
  78.5 13.2 %collective-permute-done.15.refs_9_ = bf16[80,3072]{1,0:T(8,128)(2,1)S(1)} collective-permute-done((bf16[80,3072]{1,0:T(8,128)(2,1)S(1)}, bf16[80,3072]{1,0:T(8,128)(2,1)S(1)}, u32[]{:S(2)}, u32[]{:S(2)}) %collective-permute-start.15) | collective-permute-done | bytes 491552 | tf_op jit(solution)/shard_map/ppermute | solution.py:627
  91.7 3.9 %shard_map.94 = (bf16[3072,3072]{1,0:T(8,128)(2,1)S(1)}, bf16[80,3072]{1,0:T(8,128)(2,1)S(1)}, bf16[80,3072]{1,0:T(8,128)(2,1)S(1)}, bf16[80,3072]{1,0:T(8,128)(2,1)S(1)}, bf16[80,3072]{1,0:T(8,128)(2,1)S(1)}) custom-call(bf16[80,768]{1,0:T(8,128)(2,1)S(1)} %collective-permute-done.8.refs_0_., ...), custom_call_target="tpu_custom_call", output_to_operand_aliasing={{0}: (3, {}), {1}: (6, {}), {2}: (7, {}), {3}: (8, {})} | custom-call | flops 1000 | bytes 1000 | tf_op jit(solution)/shard_map/pallas_call | solution.py:335
  105.6 3.9 %shard_map.95 = (bf16[3072,3072]{1,0:T(8,128)(2,1)S(1)}, bf16[80,3072]{1,0:T(8,128)(2,1)S(1)}, bf16[80,3072]{1,0:T(8,128)(2,1)S(1)}, bf16[80,3072]{1,0:T(8,128)(2,1)S(1)}, bf16[80,3072]{1,0:T(8,128)(2,1)S(1)}) custom-call(bf16[80,768]{1,0:T(8,128)(2,1)S(1)} %collective-permute-done.5.refs_0_., ...), custom_call_target="tpu_custom_call", output_to_operand_aliasing={{0}: (3, {}), {1}: (5, {}), {2}: (6, {}), {3}: (7, {})} | custom-call | flops 1000 | bytes 1000 | tf_op jit(solution)/shard_map/pallas_call | solution.py:335
  113.9 3.3 %collective-permute-done.21.refs_1_ = bf16[80,3072]{1,0:T(8,128)(2,1)S(1)} collective-permute-done((bf16[80,3072]{1,0:T(8,128)(2,1)S(1)}, bf16[80,3072]{1,0:T(8,128)(2,1)S(1)}, u32[]{:S(2)}, u32[]{:S(2)}) %collective-permute-start.21) | collective-permute-done | bytes 491552 | tf_op jit(solution)/shard_map/ppermute | solution.py:61
  120.6 3.9 %shard_map.96 = (bf16[3072,3072]{1,0:T(8,128)(2,1)S(1)}, bf16[80,3072]{1,0:T(8,128)(2,1)S(1)}, bf16[80,3072]{1,0:T(8,128)(2,1)S(1)}, bf16[80,3072]{1,0:T(8,128)(2,1)S(1)}) custom-call(bf16[3072,3072]{1,0:T(8,128)(2,1)S(1)} %get-tuple-element.213.refs_0_, ...), custom_call_target="tpu_custom_call", output_to_operand_aliasing={{0}: (0, {}), {1}: (2, {}), {2}: (3, {})} | custom-call | flops 1000 | bytes 1000 | tf_op jit(solution)/shard_map/pallas_call | solution.py:335
  126.1 3.2 %shard_map.97 = (f32[768,192]{1,0:T(8,128)S(1)}, bf16[2,192,192]{2,1,0:T(8,128)(2,1)S(1)}, bf16[8,384,384]{2,1,0:T(8,128)(2,1)S(1)}, bf16[768,320]{1,0:T(8,128)(...) custom-call(bf16[80,768]{1,0:T(8,128)(2,1)S(1)} %get-tuple-element.219.refs_0_, ...), custom_call_target="tpu_custom_call" | custom-call | flops 1000 | bytes 1000 | tf_op jit(solution)/shard_map/pallas_call | solution.py:407
  130.6 4.0 %shard_map.98 = (f32[384,3072]{1,0:T(8,128)S(1)}, f32[384,3072]{1,0:T(8,128)S(1)}, f32[768,192]{1,0:T(8,128)S(1)}) custom-call(bf16[80,3072]{1,0:T(8,128)(2,1)S(1)} %get-tuple-element.218.refs_0_, bf16[80,3072]{1,0:T(8,128)(2,1)S(1)} %collective-permute-done.21.refs_1_, bf16[80,3072]{1,0:T(8,128)(2,1)S(1)} %collective-permute-done.22.refs_2_, ...), custom_call_target="tpu_custom_call" | custom-call | flops 1000 | bytes 1000 | tf_op jit(solution)/shard_map/pallas_call | solution.py:467
  136.4 6.3 %collective-permute-done.18.refs_2_ = bf16[80,3072]{1,0:T(8,128)(2,1)S(1)} collective-permute-done((bf16[80,3072]{1,0:T(8,128)(2,1)S(1)}, bf16[80,3072]{1,0:T(8,128)(2,1)S(1)}, u32[]{:S(2)}, u32[]{:S(2)}) %collective-permute-start.18) | collective-permute-done | bytes 491552 | tf_op jit(solution)/shard_map/ppermute | solution.py:61
  143.5 2.8 %collective-permute-done.25.refs_1_ = bf16[80,3072]{1,0:T(8,128)(2,1)S(1)} collective-permute-done((bf16[80,3072]{1,0:T(8,128)(2,1)S(1)}, bf16[80,3072]{1,0:T(8,128)(2,1)S(1)}, u32[]{:S(2)}, u32[]{:S(2)}) %collective-permute-start.25) | collective-permute-done | bytes 491552 | tf_op jit(solution)/shard_map/ppermute | solution.py:61
  147.6 2.7 %shard_map.100 = (f32[384,3072]{1,0:T(8,128)S(1)}, f32[384,3072]{1,0:T(8,128)S(1)}, f32[768,192]{1,0:T(8,128)S(1)}) custom-call(bf16[80,3072]{1,0:T(8,128)(2,1)S(1)} %get-tuple-element.217.refs_0_, bf16[80,3072]{1,0:T(8,128)(2,1)S(1)} %collective-permute-done.20.refs_0_.refs_1_, ...), custom_call_target="tpu_custom_call", output_to_operand_aliasing={{0}: (4, {}), {1}: (5, {}), {2}: (6, {})} | custom-call | flops 1000 | bytes 1000 | tf_op jit(solution)/shard_map/pallas_call | solution.py:467
  150.3 2.9 %collective-permute-done.27.refs_2_ = bf16[80,3072]{1,0:T(8,128)(2,1)S(1)} collective-permute-done((bf16[80,3072]{1,0:T(8,128)(2,1)S(1)}, bf16[80,3072]{1,0:T(8,128)(2,1)S(1)}, u32[]{:S(2)}, u32[]{:S(2)}) %collective-permute-start.27) | collective-permute-done | bytes 491552 | tf_op jit(solution)/shard_map/ppermute | solution.py:61
  153.2 2.7 %shard_map.101 = (f32[384,3072]{1,0:T(8,128)S(1)}, f32[384,3072]{1,0:T(8,128)S(1)}, f32[768,192]{1,0:T(8,128)S(1)}) custom-call(bf16[80,3072]{1,0:T(8,128)(2,1)S(1)} %get-tuple-element.227.refs_0_, bf16[80,3072]{1,0:T(8,128)(2,1)S(1)} %collective-permute-done.25.refs_1_, ...), custom_call_target="tpu_custom_call", output_to_operand_aliasing={{0}: (4, {}), {1}: (5, {}), {2}: (6, {})} | custom-call | flops 1000 | bytes 1000 | tf_op jit(solution)/shard_map/pallas_call | solution.py:467
  156.0 7.8 %collective-permute-done.26.second = bf16[80,3072]{1,0:T(8,128)(2,1)S(1)} collective-permute-done((bf16[80,3072]{1,0:T(8,128)(2,1)S(1)}, bf16[80,3072]{1,0:T(8,128)(2,1)S(1)}, u32[]{:S(2)}, u32[]{:S(2)}) %collective-permute-start.26) | collective-permute-done | bytes 491552 | tf_op jit(solution)/shard_map/ppermute | solution.py:61
  165.9 4.8 %collective-permute-start.28 = (bf16[384,3584]{1,0:T(8,128)(2,1)S(1)}, bf16[384,3584]{1,0:T(8,128)(2,1)S(1)}, u32[]{:S(2)}, u32[]{:S(2)}) collective-permute-start(bf16[384,3584]{1,0:T(8,128)(2,1)S(1)} %get-tuple-element.240), channel_id=1, source_target_pairs={{0,1},{1,0},{2,3},{3,2},{4,5},{5,4},{6,7},{7,6},{8,9},{9,8},{10,11... | collective-permute-start | bytes 8257544 | tf_op jit(solution)/shard_map/ppermute | solution.py:61
  172.3 3.1 %collective-permute-done.28.other_ref = bf16[384,3584]{1,0:T(8,128)(2,1)S(1)} collective-permute-done((bf16[384,3584]{1,0:T(8,128)(2,1)S(1)}, bf16[384,3584]{1,0:T(8,128)(2,1)S(1)}, u32[]{:S(2)}, u32[]{:S(2)}) %collective-permute-start.28) | collective-permute-done | bytes 2752544 | tf_op jit(solution)/shard_map/ppermute | solution.py:61
  175.4 3.2 %shard_map.104 = (bf16[384,3072]{1,0:T(8,128)(2,1)}, f32[2,192,192]{2,1,0:T(8,128)}, f32[2,192,192]{2,1,0:T(8,128)}) custom-call(f32[384,3072]{1,0:T(8,128)S(1)} %shard_map.102.own_ref, bf16[384,3584]{1,0:T(8,128)(2,1)S(1)} %collective-permute-done.28.other_ref, bf16[2,192,192]{2,1,0:T(8,128)(2,1)S(1)} %get-tuple-element.241.left_ref, ...), custom_call_target="tpu_custom_call" | custom-call | flops 1000 | bytes 1000 | tf_op jit(solution)/shard_map/pallas_call | solution.py:578
  (58 shorter events, 51.5 us)
Async XLA Ops:
  7.2 14.0 %collective-permute-start = (bf16[80,3072]{1,0:T(8,128)(2,1)S(1)}, bf16[80,3072]{1,0:T(8,128)(2,1)S(1)}, u32[]{:S(2)}, u32[]{:S(2)}) collective-permute-start(bf16[80,3072]{1,0:T(8,128)(2,1)S(1)} %get-tuple-element.125), channel_id=1, source_target_pairs={{0,8},{1,9},{2,10},{3,11},{4,12},{5,13},{6,14},{7,15}} | collective-permute-start | bytes 1474568 | tf_op jit(solution)/shard_map/ppermute | solution.py:619
  25.5 13.1 %collective-permute-start.1 = (bf16[80,3072]{1,0:T(8,128)(2,1)S(1)}, bf16[80,3072]{1,0:T(8,128)(2,1)S(1)}, u32[]{:S(2)}, u32[]{:S(2)}) collective-permute-start(bf16[80,3072]{1,0:T(8,128)(2,1)S(1)} %get-tuple-element.137), channel_id=1, source_target_pairs={{0,8},{8,16},{1,9},{9,17},{2,10},{10,18},{3,11},{11,19},{4,12},{12... | collective-permute-start | bytes 1474568 | tf_op jit(solution)/shard_map/ppermute | solution.py:619
  42.9 12.1 %collective-permute-start.2 = (bf16[80,3072]{1,0:T(8,128)(2,1)S(1)}, bf16[80,3072]{1,0:T(8,128)(2,1)S(1)}, u32[]{:S(2)}, u32[]{:S(2)}) collective-permute-start(bf16[80,3072]{1,0:T(8,128)(2,1)S(1)} %get-tuple-element.152), channel_id=1, source_target_pairs={{0,8},{8,16},{16,24},{1,9},{9,17},{17,25},{2,10},{10,18},{18,26},{... | collective-permute-start | bytes 1474568 | tf_op jit(solution)/shard_map/ppermute | solution.py:619
  59.3 9.8 %collective-permute-start.3 = (bf16[80,3072]{1,0:T(8,128)(2,1)S(1)}, bf16[80,3072]{1,0:T(8,128)(2,1)S(1)}, u32[]{:S(2)}, u32[]{:S(2)}) collective-permute-start(bf16[80,3072]{1,0:T(8,128)(2,1)S(1)} %get-tuple-element.168), channel_id=1, source_target_pairs={{8,16},{16,24},{9,17},{17,25},{10,18},{18,26},{11,19},{19,27},{12,... | collective-permute-start | bytes 1474568 | tf_op jit(solution)/shard_map/ppermute | solution.py:619
  61.8 8.0 %collective-permute-start.14 = (bf16[80,3072]{1,0:T(8,128)(2,1)S(1)}, bf16[80,3072]{1,0:T(8,128)(2,1)S(1)}, u32[]{:S(2)}, u32[]{:S(2)}) collective-permute-start(bf16[80,3072]{1,0:T(8,128)(2,1)S(1)} %get-tuple-element.201), channel_id=1, source_target_pairs={{24,16},{25,17},{26,18},{27,19},{28,20},{29,21},{30,22},{31,23}} | collective-permute-start | bytes 1474568 | tf_op jit(solution)/shard_map/ppermute | solution.py:627
  62.5 7.3 %collective-permute-start.11 = (bf16[80,768]{1,0:T(8,128)(2,1)S(1)}, bf16[80,768]{1,0:T(8,128)(2,1)S(1)}, u32[]{:S(2)}, u32[]{:S(2)}) collective-permute-start(bf16[80,768]{1,0:T(8,128)(2,1)S(1)} %get-tuple-element.192), channel_id=1, source_target_pairs={{0,2},{1,3},{2,0},{3,1},{4,6},{5,7},{6,4},{7,5},{8,10},{9,11},{10,... | collective-permute-start | bytes 368648 | tf_op jit(solution)/shard_map/ppermute | solution.py:61
  63.8 6.0 %collective-permute-start.12 = (bf16[80,768]{1,0:T(8,128)(2,1)S(1)}, bf16[80,768]{1,0:T(8,128)(2,1)S(1)}, u32[]{:S(2)}, u32[]{:S(2)}) collective-permute-start(bf16[80,768]{1,0:T(8,128)(2,1)S(1)} %get-tuple-element.193), channel_id=1, source_target_pairs={{0,4},{1,5},{2,6},{3,7},{4,0},{5,1},{6,2},{7,3},{8,12},{9,13},{10,... | collective-permute-start | bytes 368648 | tf_op jit(solution)/shard_map/ppermute | solution.py:61
  65.1 4.8 %collective-permute-start.13 = (bf16[80,768]{1,0:T(8,128)(2,1)S(1)}, bf16[80,768]{1,0:T(8,128)(2,1)S(1)}, u32[]{:S(2)}, u32[]{:S(2)}) collective-permute-start(bf16[80,768]{1,0:T(8,128)(2,1)S(1)} %get-tuple-element.194), channel_id=1, source_target_pairs={{0,6},{1,7},{2,4},{3,5},{4,2},{5,3},{6,0},{7,1},{8,14},{9,15},{10,... | collective-permute-start | bytes 368648 | tf_op jit(solution)/shard_map/ppermute | solution.py:61
  69.2 5.0 %collective-permute-start.4 = (bf16[80,3072]{1,0:T(8,128)(2,1)S(1)}, bf16[80,3072]{1,0:T(8,128)(2,1)S(1)}, u32[]{:S(2)}, u32[]{:S(2)}) collective-permute-start(bf16[80,3072]{1,0:T(8,128)(2,1)S(1)} %get-tuple-element.179), channel_id=1, source_target_pairs={{16,24},{17,25},{18,26},{19,27},{20,28},{21,29},{22,30},{23,31}} | collective-permute-start | bytes 1474568 | tf_op jit(solution)/shard_map/ppermute | solution.py:619
  70.1 21.6 %collective-permute-start.15 = (bf16[80,3072]{1,0:T(8,128)(2,1)S(1)}, bf16[80,3072]{1,0:T(8,128)(2,1)S(1)}, u32[]{:S(2)}, u32[]{:S(2)}) collective-permute-start(bf16[80,3072]{1,0:T(8,128)(2,1)S(1)} %get-tuple-element.207), channel_id=1, source_target_pairs={{16,8},{24,16},{17,9},{25,17},{18,10},{26,18},{19,11},{27,19},{20,... | collective-permute-start | bytes 1474568 | tf_op jit(solution)/shard_map/ppermute | solution.py:627
  73.9 4.6 %collective-permute-start.10 = (bf16[80,768]{1,0:T(8,128)(2,1)S(1)}, bf16[80,768]{1,0:T(8,128)(2,1)S(1)}, u32[]{:S(2)}, u32[]{:S(2)}) collective-permute-start(bf16[80,768]{1,0:T(8,128)(2,1)S(1)} %get-tuple-element.191), channel_id=1, source_target_pairs={{0,6},{1,7},{2,4},{3,5},{4,2},{5,3},{6,0},{7,1},{8,14},{9,15},{10,... | collective-permute-start | bytes 368648 | tf_op jit(solution)/shard_map/ppermute | solution.py:61
  95.6 9.9 %collective-permute-start.16 = (bf16[80,3072]{1,0:T(8,128)(2,1)S(1)}, bf16[80,3072]{1,0:T(8,128)(2,1)S(1)}, u32[]{:S(2)}, u32[]{:S(2)}) collective-permute-start(bf16[80,3072]{1,0:T(8,128)(2,1)S(1)} %get-tuple-element.212), channel_id=1, source_target_pairs={{8,0},{16,8},{24,16},{9,1},{17,9},{25,17},{10,2},{18,10},{26,18},{... | collective-permute-start | bytes 1474568 | tf_op jit(solution)/shard_map/ppermute | solution.py:627
  109.4 7.7 %collective-permute-start.21 = (bf16[80,3072]{1,0:T(8,128)(2,1)S(1)}, bf16[80,3072]{1,0:T(8,128)(2,1)S(1)}, u32[]{:S(2)}, u32[]{:S(2)}) collective-permute-start(bf16[80,3072]{1,0:T(8,128)(2,1)S(1)} %get-tuple-element.218.refs_0_), channel_id=1, source_target_pairs={{0,2},{1,3},{2,0},{3,1},{4,6},{5,7},{6,4},{7,5},{8,10},{9,11},{10,... | collective-permute-start | bytes 1474568 | tf_op jit(solution)/shard_map/ppermute | solution.py:61
  110.7 9.9 %collective-permute-start.17 = (bf16[80,3072]{1,0:T(8,128)(2,1)S(1)}, bf16[80,3072]{1,0:T(8,128)(2,1)S(1)}, u32[]{:S(2)}, u32[]{:S(2)}) collective-permute-start(bf16[80,3072]{1,0:T(8,128)(2,1)S(1)} %get-tuple-element.216), channel_id=1, source_target_pairs={{8,0},{16,8},{9,1},{17,9},{10,2},{18,10},{11,3},{19,11},{12,4},{20... | collective-permute-start | bytes 1474568 | tf_op jit(solution)/shard_map/ppermute | solution.py:627
  112.6 18.0 %collective-permute-start.22 = (bf16[80,3072]{1,0:T(8,128)(2,1)S(1)}, bf16[80,3072]{1,0:T(8,128)(2,1)S(1)}, u32[]{:S(2)}, u32[]{:S(2)}) collective-permute-start(bf16[80,3072]{1,0:T(8,128)(2,1)S(1)} %get-tuple-element.218.refs_0_), channel_id=1, source_target_pairs={{0,4},{1,5},{2,6},{3,7},{4,0},{5,1},{6,2},{7,3},{8,12},{9,13},{10,... | collective-permute-start | bytes 1474568 | tf_op jit(solution)/shard_map/ppermute | solution.py:61
  117.2 13.4 %collective-permute-start.23 = (bf16[80,3072]{1,0:T(8,128)(2,1)S(1)}, bf16[80,3072]{1,0:T(8,128)(2,1)S(1)}, u32[]{:S(2)}, u32[]{:S(2)}) collective-permute-start(bf16[80,3072]{1,0:T(8,128)(2,1)S(1)} %collective-permute-done.21.refs_1_), channel_id=1, source_target_pairs={{0,4},{1,5},{2,6},{3,7},{4,0},{5,1},{6,2},{7,3},{8,12},{9,13},{10,... | collective-permute-start | bytes 1474568 | tf_op jit(solution)/shard_map/ppermute | solution.py:61
  124.5 10.2 %collective-permute-start.24 = (bf16[80,3072]{1,0:T(8,128)(2,1)S(1)}, bf16[80,3072]{1,0:T(8,128)(2,1)S(1)}, u32[]{:S(2)}, u32[]{:S(2)}) collective-permute-start(bf16[80,3072]{1,0:T(8,128)(2,1)S(1)} %get-tuple-element.226), channel_id=1, source_target_pairs={{8,0},{9,1},{10,2},{11,3},{12,4},{13,5},{14,6},{15,7}} | collective-permute-start | bytes 1474568 | tf_op jit(solution)/shard_map/ppermute | solution.py:627
  125.8 8.8 %collective-permute-start.20 = (bf16[80,3072]{1,0:T(8,128)(2,1)S(1)}, bf16[80,3072]{1,0:T(8,128)(2,1)S(1)}, u32[]{:S(2)}, u32[]{:S(2)}) collective-permute-start(bf16[80,3072]{1,0:T(8,128)(2,1)S(1)} %get-tuple-element.217.refs_0_), channel_id=1, source_target_pairs={{0,2},{1,3},{2,0},{3,1},{4,6},{5,7},{6,4},{7,5},{8,10},{9,11},{10,... | collective-permute-start | bytes 1474568 | tf_op jit(solution)/shard_map/ppermute | solution.py:61
  129.3 13.4 %collective-permute-start.18 = (bf16[80,3072]{1,0:T(8,128)(2,1)S(1)}, bf16[80,3072]{1,0:T(8,128)(2,1)S(1)}, u32[]{:S(2)}, u32[]{:S(2)}) collective-permute-start(bf16[80,3072]{1,0:T(8,128)(2,1)S(1)} %get-tuple-element.217.refs_0_), channel_id=1, source_target_pairs={{0,4},{1,5},{2,6},{3,7},{4,0},{5,1},{6,2},{7,3},{8,12},{9,13},{10,... | collective-permute-start | bytes 1474568 | tf_op jit(solution)/shard_map/ppermute | solution.py:61
  134.9 11.4 %collective-permute-start.25 = (bf16[80,3072]{1,0:T(8,128)(2,1)S(1)}, bf16[80,3072]{1,0:T(8,128)(2,1)S(1)}, u32[]{:S(2)}, u32[]{:S(2)}) collective-permute-start(bf16[80,3072]{1,0:T(8,128)(2,1)S(1)} %get-tuple-element.227.refs_0_), channel_id=1, source_target_pairs={{0,2},{1,3},{2,0},{3,1},{4,6},{5,7},{6,4},{7,5},{8,10},{9,11},{10,... | collective-permute-start | bytes 1474568 | tf_op jit(solution)/shard_map/ppermute | solution.py:61
  136.2 17.1 %collective-permute-start.27 = (bf16[80,3072]{1,0:T(8,128)(2,1)S(1)}, bf16[80,3072]{1,0:T(8,128)(2,1)S(1)}, u32[]{:S(2)}, u32[]{:S(2)}) collective-permute-start(bf16[80,3072]{1,0:T(8,128)(2,1)S(1)} %get-tuple-element.227.refs_0_), channel_id=1, source_target_pairs={{0,4},{1,5},{2,6},{3,7},{4,0},{5,1},{6,2},{7,3},{8,12},{9,13},{10,... | collective-permute-start | bytes 1474568 | tf_op jit(solution)/shard_map/ppermute | solution.py:61
  142.7 13.3 %collective-permute-start.19 = (bf16[80,3072]{1,0:T(8,128)(2,1)S(1)}, bf16[80,3072]{1,0:T(8,128)(2,1)S(1)}, u32[]{:S(2)}, u32[]{:S(2)}) collective-permute-start(bf16[80,3072]{1,0:T(8,128)(2,1)S(1)} %collective-permute-done.18.refs_2_), channel_id=1, source_target_pairs={{0,2},{1,3},{2,0},{3,1},{4,6},{5,7},{6,4},{7,5},{8,10},{9,11},{10,... | collective-permute-start | bytes 1474568 | tf_op jit(solution)/shard_map/ppermute | solution.py:61
  146.3 17.4 %collective-permute-start.26 = (bf16[80,3072]{1,0:T(8,128)(2,1)S(1)}, bf16[80,3072]{1,0:T(8,128)(2,1)S(1)}, u32[]{:S(2)}, u32[]{:S(2)}) collective-permute-start(bf16[80,3072]{1,0:T(8,128)(2,1)S(1)} %collective-permute-done.25.refs_1_), channel_id=1, source_target_pairs={{0,4},{1,5},{2,6},{3,7},{4,0},{5,1},{6,2},{7,3},{8,12},{9,13},{10,... | collective-permute-start | bytes 1474568 | tf_op jit(solution)/shard_map/ppermute | solution.py:61
  165.9 9.5 %collective-permute-start.28 = (bf16[384,3584]{1,0:T(8,128)(2,1)S(1)}, bf16[384,3584]{1,0:T(8,128)(2,1)S(1)}, u32[]{:S(2)}, u32[]{:S(2)}) collective-permute-start(bf16[384,3584]{1,0:T(8,128)(2,1)S(1)} %get-tuple-element.240), channel_id=1, source_target_pairs={{0,1},{1,0},{2,3},{3,2},{4,5},{5,4},{6,7},{7,6},{8,9},{9,8},{10,11... | collective-permute-start | bytes 8257544 | tf_op jit(solution)/shard_map/ppermute | solution.py:61
  (7 other events, 30.8 us)

commit v12 on v11

--- a/solution.py
+++ b/solution.py
@@ -22,6 +22,7 @@
 LOAD = 512
 PAIR = 2 * BLOCK
 SIDE = 256
+HALF = D // 2
 FLIGHT = 4
 
 C_ZERO = 0.7978845608028654
@@ -476,38 +477,44 @@
     )(*[resident(p) for p in parts], resident(turned), *[resident(a) for a in so_far])
 
 
-def other_kernel(first, second, xt_ref, acc_ref, gram_in_ref, gram_ref, _, out_ref, part):
-    rows = slice(acc_ref.shape[0], 2 * acc_ref.shape[0])
+def other_kernel(side, first, second, xt_ref, acc_ref, *refs):
+    out_ref, part = refs[-2:]
+    own = acc_ref.shape[0]
+    rows = slice(own, 2 * own)
     fill((first, second), part)
-    add_gram(part, gram_ref, False)
-    out_ref[:, D : D + BLOCK] = gram_ref[rows, :].astype(BF)
-    out_ref[:, D + SIDE : D + SIDE + BLOCK] = gram_in_ref[rows, :].astype(BF)
-
-    @pl.loop(0, D // LOAD)
+    if side:
+        gram_in_ref, gram_ref = refs[0], refs[2]
+        add_gram(part, gram_ref, False)
+        out_ref[:, HALF : HALF + BLOCK] = gram_ref[rows, :].astype(BF)
+        out_ref[:, HALF + SIDE : HALF + SIDE + BLOCK] = gram_in_ref[rows, :].astype(BF)
+
+    @pl.loop(0, HALF // LOAD)
     def _(step):
-        columns = pl.ds(pl.multiple_of(step * LOAD, LOAD), LOAD)
+        place = pl.ds(pl.multiple_of(step * LOAD, LOAD), LOAD)
+        columns = pl.ds(pl.multiple_of(side * HALF + step * LOAD, LOAD), LOAD)
         term = jnp.dot(xt_ref[rows, :], part[:, columns], preferred_element_type=F32)
-        out_ref[:, columns] = (term + acc_ref[:, columns]).astype(BF)
-
-
-def other_half(parts, turned, acc, gram_in, gram_out):
-    width = turned.shape[0]
-    return pl.pallas_call(
-        other_kernel,
-        out_shape=(near(width, BLOCK, kind=F32), near(width // 2, D + 2 * SIDE)),
-        in_specs=[VM] * 6,
-        out_specs=(VM, VM),
+        out_ref[:, place] = (term + acc_ref[:, columns]).astype(BF)
+
+
+def other_half(side, parts, turned, acc, grams):
+    own = acc.shape[0]
+    outs = pl.pallas_call(
+        functools.partial(other_kernel, side),
+        out_shape=[near(*g.shape, kind=F32) for g in grams[1:]]
+        + [near(own, HALF + 2 * SIDE * side)],
+        in_specs=[VM] * (4 + len(grams)),
+        out_specs=[VM] * max(1, len(grams)),
         scratch_shapes=[pltpu.VMEM((2 * PIECE, D), BF)],
-        input_output_aliases={5: 0},
+        input_output_aliases={5: 0} if side else {},
         compiler_params=limit(8),
         cost_estimate=SMALL,
     )(
         *[resident(p) for p in parts],
         resident(turned),
         resident(acc),
-        resident(gram_in),
-        resident(gram_out),
+        *[resident(g) for g in grams],
     )
+    return outs
 
 
 def own_kernel(first, second, xt_ref, acc_ref, out_ref, part):
@@ -534,27 +541,31 @@
     )(*[resident(p) for p in parts], resident(turned), resident(acc))
 
 
-def finish_kernel(blocks, total, own_ref, other_ref, left_ref, right_ref, *refs):
-    gram_in_ref, gram_out_ref, update_ref, factor_in_ref, factor_out_ref, ready, grams, sems = refs
+def finish_kernel(side, blocks, total, own_ref, other_ref, left_ref, right_ref, *refs):
     scale = 1.0 / math.sqrt(total)
-    pairs = D // PAIR
+    pairs = HALF // PAIR
+    base = side * HALF
     copies = []
-    for block in range(blocks):
-        rows = slice(block * BLOCK, (block + 1) * BLOCK)
-        mine = rows
-        grams[1, block] = (
-            gram_out_ref[mine, :] + other_ref[rows, D : D + BLOCK].astype(F32)
-        ) * (1.0 / total)
-        grams[0, block] = (
-            gram_in_ref[mine, :] + other_ref[rows, D + SIDE : D + SIDE + BLOCK].astype(F32)
-        ) * (1.0 / total)
-    for k, ref in enumerate((factor_in_ref, factor_out_ref)):
-        copy = pltpu.make_async_copy(grams.at[k], ref, sems.at[pairs + k])
-        copy.start()
-        copies.append(copy)
-    for step in range(D // (2 * PAIR)):
+    if side:
+        gram_in_ref, gram_out_ref, update_ref, factor_in_ref, factor_out_ref = refs[:5]
+        ready, grams, sems = refs[5:]
+        for block in range(blocks):
+            rows = slice(block * BLOCK, (block + 1) * BLOCK)
+            for k, (gram, begins) in enumerate(((gram_in_ref, SIDE), (gram_out_ref, 0))):
+                columns = slice(HALF + begins, HALF + begins + BLOCK)
+                grams[k, block] = (gram[rows, :] + other_ref[rows, columns].astype(F32)) * (
+                    1.0 / total
+                )
+        for k, ref in enumerate((factor_in_ref, factor_out_ref)):
+            copy = pltpu.make_async_copy(grams.at[k], ref, sems.at[pairs + k])
+            copy.start()
+            copies.append(copy)
+    else:
+        update_ref, ready, sems = refs[1:]
+    for step in range(pairs // 2):
         columns = slice(step * 2 * PAIR, (step + 1) * 2 * PAIR)
-        grad = (own_ref[:, columns] + other_ref[:, columns].astype(F32)).astype(BF)
+        wide = slice(base + step * 2 * PAIR, base + (step + 1) * 2 * PAIR)
+        grad = (own_ref[:, wide] + other_ref[:, columns].astype(F32)).astype(BF)
         for block in range(blocks):
             rows = slice(block * BLOCK, (block + 1) * BLOCK)
             ready[rows, columns] = jnp.dot(
@@ -562,29 +573,30 @@
             ).astype(BF)
     for pair in range(pairs):
         columns = slice(pair * PAIR, (pair + 1) * PAIR)
-        right = jnp.dot(ready[:, columns], right_ref[pair], preferred_element_type=F32)
+        wide = slice(base + pair * PAIR, base + (pair + 1) * PAIR)
+        right = jnp.dot(
+            ready[:, columns], right_ref[side * pairs + pair], preferred_element_type=F32
+        )
         ready[:, columns] = (right * scale).astype(BF)
-        copy = pltpu.make_async_copy(
-            ready.at[:, columns], update_ref.at[:, columns], sems.at[pair]
-        )
+        copy = pltpu.make_async_copy(ready.at[:, columns], update_ref.at[:, wide], sems.at[pair])
         copy.start()
         copies.append(copy)
     for copy in copies:
         copy.wait()
 
 
-def finish(blocks, total, own, other, left, right, gram_in, gram_out):
+def finish(side, blocks, total, own, other, left, right, grams, update):
     factor = shape(blocks, BLOCK, BLOCK, kind=F32)
+    scratch = [pltpu.VMEM((blocks * BLOCK, HALF), BF)]
+    if side:
+        scratch.append(pltpu.VMEM((2, blocks, BLOCK, BLOCK), F32))
     return pl.pallas_call(
-        functools.partial(finish_kernel, blocks, total),
-        out_shape=(shape(blocks * BLOCK, D), factor, factor),
-        in_specs=[VM] * 6,
-        out_specs=(HB, HB, HB),
-        scratch_shapes=[
-            pltpu.VMEM((blocks * BLOCK, D), BF),
-            pltpu.VMEM((2, blocks, BLOCK, BLOCK), F32),
-            pltpu.SemaphoreType.DMA((D // PAIR + 2,)),
-        ],
+        functools.partial(finish_kernel, side, blocks, total),
+        out_shape=[shape(blocks * BLOCK, D)] + [factor, factor] * side,
+        in_specs=[VM] * (4 + len(grams)) + [HB] * len(update),
+        out_specs=[HB] * (1 + 2 * side),
+        scratch_shapes=[*scratch, pltpu.SemaphoreType.DMA((HALF // PAIR + 2,))],
+        input_output_aliases={} if side else {4: 0},
         compiler_params=limit(8),
         cost_estimate=SMALL,
     )(
@@ -592,8 +604,8 @@
         resident(other),
         resident(left),
         resident(right),
-        resident(gram_in),
-        resident(gram_out),
+        *[resident(g) for g in grams],
+        *[distant(u) for u in update],
     )
 
 
@@ -653,12 +665,16 @@
     for index in range(PIECES - 2, PIECES):
         acc = gather(parts[index][:-1], rows_turned[index], acc)
     final = [parts[-2][-1], parts[-1][-1]]
-    gram_out, other = other_half(final, rows_turned[-1], acc[1], gram_in, acc[2])
-    other = swap(other, ranks, 1)
+    (first,) = other_half(0, final, rows_turned[-1], acc[1], [])
+    first = swap(first, ranks, 1)
+    gram_out, second = other_half(1, final, rows_turned[-1], acc[1], [gram_in, acc[2]])
+    second = swap(second, ranks, 1)
     own = own_half(final, rows_turned[-1], acc[0])
+    blocks = inverse_in.shape[1]
     update, factor_in, factor_out = finish(
-        inverse_in.shape[1], total, own, other, left, right, gram_in, gram_out
+        1, blocks, total, own, second, left, right, [gram_in, gram_out], []
     )
+    (update,) = finish(0, blocks, total, own, first, left, right, [], [update])
     return (update[None], factor_in[None], factor_out[None])
 
 

time: 179 us -> 178 us (level)
  waiting for transfers between devices: 81.6 us -> 79 us
    ppermute x19 -> x20, waiting for transfers between devices: 35.1 us -> 32.4 us  [swap(): return lax.ppermute(x, 'dp', [(r, r ^ flip) for r in range(ranks)])]
    pallas_call x2 -> x4, Pallas kernels: 5.33 us -> 6.42 us  [the longest x2 4.26 us: finish(): pl.pallas_call(functools.partial(finish_kernel, side, blocks, total), out...]
    ppermute x19 -> x20, starting transfers between devices: 21.9 us -> 22 us  [swap(): return lax.ppermute(x, 'dp', [(r, r ^ flip) for r in range(ranks)])]
  transfers between devices with their start and end apart: 29 -> 30, of which waited for: 19 -> 19; matrix products, arithmetic and copies ran while one was open for 0% -> 0% of each run, Pallas kernels for 14% -> 16%
where the time goes in v12:
time: 178 us; the launch traced here: 177 us
  waiting for transfers between devices  79 us (44%)
  Pallas kernels  59.5 us (33%)
  starting transfers between devices  37.8 us (21%)
    ppermute x20, waiting for transfers between devices, swap(): return lax.ppermute(x, 'dp', [(r, r ^ flip) for r in range(ranks)])  32.4 us
    ppermute x5, waiting for transfers between devices, shards(): arrived_ahead = lax.ppermute(ahead, 'section', pairs)  30.4 us
    ppermute x20, starting transfers between devices, swap(): return lax.ppermute(x, 'dp', [(r, r ^ flip) for r in range(ranks)])  22 us
    ppermute x5, waiting for transfers between devices, shards(): arrived_behind = lax.ppermute(behind, 'section', pairs)  16.2 us
    pallas_call x5, Pallas kernels, forward(): pl.pallas_call(functools.partial(forward_kernel, tick, span, count, sends...  12.9 us
    pallas_call x6, Pallas kernels, backward(): pl.pallas_call(functools.partial(backward_kernel, tick, sections, span, l...  12.1 us
    pallas_call x3, Pallas kernels, gather(): pl.pallas_call(functools.partial(gather_kernel, count, not so_far), out_s...  9.46 us
    ppermute x5, starting transfers between devices, shards(): arrived_ahead = lax.ppermute(ahead, 'section', pairs)  8.58 us
  transfers between devices with their start and end apart: 30, of which 19 were waited for; matrix products, arithmetic and copies ran while one was open for 0% of the time, Pallas kernels for 16%

profile of v12, /device:TPU:9, one launch (start us, length us, event | category | flops | bytes accessed | tf_op | source)
XLA Modules:
  0.0 177.4 jit_solution(10498434565163627609)
XLA Ops:
  0.6 6.5 %shard_map.85 = (bf16[3072,3072]{1,0:T(8,128)(2,1)S(1)}, bf16[80,3072]{1,0:T(8,128)(2,1)S(1)}, bf16[3,80,3072]{2,1,0:T(8,128)(2,1)S(1)}, bf16[3,80,3072]{2,1,0:T...) custom-call(s32[1,4]{1,0:T(1,128)} %counts_ref.1, ...), custom_call_target="tpu_custom_call" | custom-call | flops 1000 | bytes 1000 | tf_op jit(solution)/shard_map/pallas_call | solution.py:168
  8.5 12.7 %collective-permute-done.from_ref = bf16[80,3072]{1,0:T(8,128)(2,1)S(1)} collective-permute-done((bf16[80,3072]{1,0:T(8,128)(2,1)S(1)}, bf16[80,3072]{1,0:T(8,128)(2,1)S(1)}, u32[]{:S(2)}, u32[]{:S(2)}) %collective-permute-start) | collective-permute-done | bytes 491552 | tf_op jit(solution)/shard_map/ppermute | solution.py:631
  21.2 4.3 %shard_map.86 = (bf16[3072,3072]{1,0:T(8,128)(2,1)S(1)}, bf16[3,80,3072]{2,1,0:T(8,128)(2,1)S(1)}, bf16[80,768]{1,0:T(8,128)(2,1)S(1)}, bf16[80,768]{1,0:T(8,128...) custom-call(bf16[80,3072]{1,0:T(8,128)(2,1)S(1)} %collective-permute, ...), custom_call_target="tpu_custom_call", output_to_operand_aliasing={{0}: (2, {}), {1}: (3, {}), {2}: (4, {}), {3}: (5, {}), {4}... | custom-call | flops 1000 | bytes 1000 | tf_op jit(solution)/shard_map/pallas_call | solution.py:228
  27.4 11.1 %collective-permute-done.1.from_ref = bf16[80,3072]{1,0:T(8,128)(2,1)S(1)} collective-permute-done((bf16[80,3072]{1,0:T(8,128)(2,1)S(1)}, bf16[80,3072]{1,0:T(8,128)(2,1)S(1)}, u32[]{:S(2)}, u32[]{:S(2)}) %collective-permute-start.1) | collective-permute-done | bytes 491552 | tf_op jit(solution)/shard_map/ppermute | solution.py:631
  38.5 4.3 %shard_map.87 = (bf16[3072,3072]{1,0:T(8,128)(2,1)S(1)}, bf16[3,80,3072]{2,1,0:T(8,128)(2,1)S(1)}, bf16[80,768]{1,0:T(8,128)(2,1)S(1)}, bf16[80,768]{1,0:T(8,128...) custom-call(bf16[80,3072]{1,0:T(8,128)(2,1)S(1)} %collective-permute, ...), custom_call_target="tpu_custom_call", output_to_operand_aliasing={{0}: (2, {}), {1}: (3, {}), {2}: (4, {}), {3}: (5, {}), {4}... | custom-call | flops 1000 | bytes 1000 | tf_op jit(solution)/shard_map/pallas_call | solution.py:228
  45.1 7.3 %shard_map.88 = (bf16[3072,3072]{1,0:T(8,128)(2,1)S(1)}, bf16[3072,3072]{1,0:T(8,128)(2,1)S(1)}) custom-call(bf16[3072,3072]{1,0:T(8,128)(2,1)S(1)} %get-tuple-element.153.w_ref), custom_call_target="tpu_custom_call", output_to_operand_aliasing={{0}: (0, {})} | custom-call | flops 1000 | bytes 1000 | tf_op jit(solution)/shard_map/pallas_call | solution.py:270
  52.4 2.6 %collective-permute-done.2.from_ref = bf16[80,3072]{1,0:T(8,128)(2,1)S(1)} collective-permute-done((bf16[80,3072]{1,0:T(8,128)(2,1)S(1)}, bf16[80,3072]{1,0:T(8,128)(2,1)S(1)}, u32[]{:S(2)}, u32[]{:S(2)}) %collective-permute-start.2) | collective-permute-done | bytes 491552 | tf_op jit(solution)/shard_map/ppermute | solution.py:631
  55.0 4.3 %shard_map.89 = (bf16[3072,3072]{1,0:T(8,128)(2,1)S(1)}, bf16[3,80,3072]{2,1,0:T(8,128)(2,1)S(1)}, bf16[80,768]{1,0:T(8,128)(2,1)S(1)}, bf16[80,768]{1,0:T(8,128...) custom-call(bf16[80,3072]{1,0:T(8,128)(2,1)S(1)} %collective-permute, ...), custom_call_target="tpu_custom_call", output_to_operand_aliasing={{0}: (2, {}), {1}: (3, {}), {2}: (4, {}), {3}: (5, {}), {4}... | custom-call | flops 1000 | bytes 1000 | tf_op jit(solution)/shard_map/pallas_call | solution.py:228
  59.3 2.5 %collective-permute-start.3 = (bf16[80,3072]{1,0:T(8,128)(2,1)S(1)}, bf16[80,3072]{1,0:T(8,128)(2,1)S(1)}, u32[]{:S(2)}, u32[]{:S(2)}) collective-permute-start(bf16[80,3072]{1,0:T(8,128)(2,1)S(1)} %get-tuple-element.168), channel_id=1, source_target_pairs={{8,16},{16,24},{9,17},{17,25},{10,18},{18,26},{11,19},{19,27},{12,... | collective-permute-start | bytes 1474568 | tf_op jit(solution)/shard_map/ppermute | solution.py:631
  65.3 3.9 %collective-permute-done.3.from_ref = bf16[80,3072]{1,0:T(8,128)(2,1)S(1)} collective-permute-done((bf16[80,3072]{1,0:T(8,128)(2,1)S(1)}, bf16[80,3072]{1,0:T(8,128)(2,1)S(1)}, u32[]{:S(2)}, u32[]{:S(2)}) %collective-permute-start.3) | collective-permute-done | bytes 491552 | tf_op jit(solution)/shard_map/ppermute | solution.py:631
  78.5 13.2 %collective-permute-done.15.refs_9_ = bf16[80,3072]{1,0:T(8,128)(2,1)S(1)} collective-permute-done((bf16[80,3072]{1,0:T(8,128)(2,1)S(1)}, bf16[80,3072]{1,0:T(8,128)(2,1)S(1)}, u32[]{:S(2)}, u32[]{:S(2)}) %collective-permute-start.15) | collective-permute-done | bytes 491552 | tf_op jit(solution)/shard_map/ppermute | solution.py:639
  91.7 3.9 %shard_map.94 = (bf16[3072,3072]{1,0:T(8,128)(2,1)S(1)}, bf16[80,3072]{1,0:T(8,128)(2,1)S(1)}, bf16[80,3072]{1,0:T(8,128)(2,1)S(1)}, bf16[80,3072]{1,0:T(8,128)(2,1)S(1)}, bf16[80,3072]{1,0:T(8,128)(2,1)S(1)}) custom-call(bf16[80,768]{1,0:T(8,128)(2,1)S(1)} %collective-permute-done.8.refs_0_., ...), custom_call_target="tpu_custom_call", output_to_operand_aliasing={{0}: (3, {}), {1}: (6, {}), {2}: (7, {}), {3}: (8, {})} | custom-call | flops 1000 | bytes 1000 | tf_op jit(solution)/shard_map/pallas_call | solution.py:336
  105.6 3.9 %shard_map.95 = (bf16[3072,3072]{1,0:T(8,128)(2,1)S(1)}, bf16[80,3072]{1,0:T(8,128)(2,1)S(1)}, bf16[80,3072]{1,0:T(8,128)(2,1)S(1)}, bf16[80,3072]{1,0:T(8,128)(2,1)S(1)}, bf16[80,3072]{1,0:T(8,128)(2,1)S(1)}) custom-call(bf16[80,768]{1,0:T(8,128)(2,1)S(1)} %collective-permute-done.5.refs_0_., ...), custom_call_target="tpu_custom_call", output_to_operand_aliasing={{0}: (3, {}), {1}: (5, {}), {2}: (6, {}), {3}: (7, {})} | custom-call | flops 1000 | bytes 1000 | tf_op jit(solution)/shard_map/pallas_call | solution.py:336
  113.9 3.3 %collective-permute-done.21.refs_1_ = bf16[80,3072]{1,0:T(8,128)(2,1)S(1)} collective-permute-done((bf16[80,3072]{1,0:T(8,128)(2,1)S(1)}, bf16[80,3072]{1,0:T(8,128)(2,1)S(1)}, u32[]{:S(2)}, u32[]{:S(2)}) %collective-permute-start.21) | collective-permute-done | bytes 491552 | tf_op jit(solution)/shard_map/ppermute | solution.py:62
  120.6 3.9 %shard_map.96 = (bf16[3072,3072]{1,0:T(8,128)(2,1)S(1)}, bf16[80,3072]{1,0:T(8,128)(2,1)S(1)}, bf16[80,3072]{1,0:T(8,128)(2,1)S(1)}, bf16[80,3072]{1,0:T(8,128)(2,1)S(1)}) custom-call(bf16[3072,3072]{1,0:T(8,128)(2,1)S(1)} %get-tuple-element.213.refs_0_, ...), custom_call_target="tpu_custom_call", output_to_operand_aliasing={{0}: (0, {}), {1}: (2, {}), {2}: (3, {})} | custom-call | flops 1000 | bytes 1000 | tf_op jit(solution)/shard_map/pallas_call | solution.py:336
  126.1 3.2 %shard_map.97 = (f32[768,192]{1,0:T(8,128)S(1)}, bf16[2,192,192]{2,1,0:T(8,128)(2,1)S(1)}, bf16[8,384,384]{2,1,0:T(8,128)(2,1)S(1)}, bf16[768,320]{1,0:T(8,128)(...) custom-call(bf16[80,768]{1,0:T(8,128)(2,1)S(1)} %get-tuple-element.219.refs_0_, ...), custom_call_target="tpu_custom_call" | custom-call | flops 1000 | bytes 1000 | tf_op jit(solution)/shard_map/pallas_call | solution.py:408
  130.6 4.0 %shard_map.98 = (f32[384,3072]{1,0:T(8,128)S(1)}, f32[384,3072]{1,0:T(8,128)S(1)}, f32[768,192]{1,0:T(8,128)S(1)}) custom-call(bf16[80,3072]{1,0:T(8,128)(2,1)S(1)} %get-tuple-element.218.refs_0_, bf16[80,3072]{1,0:T(8,128)(2,1)S(1)} %collective-permute-done.21.refs_1_, bf16[80,3072]{1,0:T(8,128)(2,1)S(1)} %collective-permute-done.22.refs_2_, ...), custom_call_target="tpu_custom_call" | custom-call | flops 1000 | bytes 1000 | tf_op jit(solution)/shard_map/pallas_call | solution.py:468
  136.4 6.3 %collective-permute-done.18.refs_2_ = bf16[80,3072]{1,0:T(8,128)(2,1)S(1)} collective-permute-done((bf16[80,3072]{1,0:T(8,128)(2,1)S(1)}, bf16[80,3072]{1,0:T(8,128)(2,1)S(1)}, u32[]{:S(2)}, u32[]{:S(2)}) %collective-permute-start.18) | collective-permute-done | bytes 491552 | tf_op jit(solution)/shard_map/ppermute | solution.py:62
  143.5 2.8 %collective-permute-done.25.refs_1_ = bf16[80,3072]{1,0:T(8,128)(2,1)S(1)} collective-permute-done((bf16[80,3072]{1,0:T(8,128)(2,1)S(1)}, bf16[80,3072]{1,0:T(8,128)(2,1)S(1)}, u32[]{:S(2)}, u32[]{:S(2)}) %collective-permute-start.25) | collective-permute-done | bytes 491552 | tf_op jit(solution)/shard_map/ppermute | solution.py:62
  147.6 2.7 %shard_map.100 = (f32[384,3072]{1,0:T(8,128)S(1)}, f32[384,3072]{1,0:T(8,128)S(1)}, f32[768,192]{1,0:T(8,128)S(1)}) custom-call(bf16[80,3072]{1,0:T(8,128)(2,1)S(1)} %get-tuple-element.217.refs_0_, bf16[80,3072]{1,0:T(8,128)(2,1)S(1)} %collective-permute-done.20.refs_0_.refs_1_, ...), custom_call_target="tpu_custom_call", output_to_operand_aliasing={{0}: (4, {}), {1}: (5, {}), {2}: (6, {})} | custom-call | flops 1000 | bytes 1000 | tf_op jit(solution)/shard_map/pallas_call | solution.py:468
  150.3 2.9 %collective-permute-done.27.refs_2_ = bf16[80,3072]{1,0:T(8,128)(2,1)S(1)} collective-permute-done((bf16[80,3072]{1,0:T(8,128)(2,1)S(1)}, bf16[80,3072]{1,0:T(8,128)(2,1)S(1)}, u32[]{:S(2)}, u32[]{:S(2)}) %collective-permute-start.27) | collective-permute-done | bytes 491552 | tf_op jit(solution)/shard_map/ppermute | solution.py:62
  153.2 2.7 %shard_map.101 = (f32[384,3072]{1,0:T(8,128)S(1)}, f32[384,3072]{1,0:T(8,128)S(1)}, f32[768,192]{1,0:T(8,128)S(1)}) custom-call(bf16[80,3072]{1,0:T(8,128)(2,1)S(1)} %get-tuple-element.227.refs_0_, bf16[80,3072]{1,0:T(8,128)(2,1)S(1)} %collective-permute-done.25.refs_1_, ...), custom_call_target="tpu_custom_call", output_to_operand_aliasing={{0}: (4, {}), {1}: (5, {}), {2}: (6, {})} | custom-call | flops 1000 | bytes 1000 | tf_op jit(solution)/shard_map/pallas_call | solution.py:468
  156.0 7.8 %collective-permute-done.26.second = bf16[80,3072]{1,0:T(8,128)(2,1)S(1)} collective-permute-done((bf16[80,3072]{1,0:T(8,128)(2,1)S(1)}, bf16[80,3072]{1,0:T(8,128)(2,1)S(1)}, u32[]{:S(2)}, u32[]{:S(2)}) %collective-permute-start.26) | collective-permute-done | bytes 491552 | tf_op jit(solution)/shard_map/ppermute | solution.py:62
  165.1 4.8 %collective-permute-start.29 = (bf16[384,2048]{1,0:T(8,128)(2,1)S(1)}, bf16[384,2048]{1,0:T(8,128)(2,1)S(1)}, u32[]{:S(2)}, u32[]{:S(2)}) collective-permute-start(bf16[384,2048]{1,0:T(8,128)(2,1)S(1)} %get-tuple-element.242), channel_id=1, source_target_pairs={{0,1},{1,0},{2,3},{3,2},{4,5},{5,4},{6,7},{7,6},{8,9},{9,8},{10,11... | collective-permute-start | bytes 4718600 | tf_op jit(solution)/shard_map/ppermute | solution.py:62
  (62 shorter events, 51.3 us)
Async XLA Ops:
  7.2 14.0 %collective-permute-start = (bf16[80,3072]{1,0:T(8,128)(2,1)S(1)}, bf16[80,3072]{1,0:T(8,128)(2,1)S(1)}, u32[]{:S(2)}, u32[]{:S(2)}) collective-permute-start(bf16[80,3072]{1,0:T(8,128)(2,1)S(1)} %get-tuple-element.125), channel_id=1, source_target_pairs={{0,8},{1,9},{2,10},{3,11},{4,12},{5,13},{6,14},{7,15}} | collective-permute-start | bytes 1474568 | tf_op jit(solution)/shard_map/ppermute | solution.py:631
  25.5 13.1 %collective-permute-start.1 = (bf16[80,3072]{1,0:T(8,128)(2,1)S(1)}, bf16[80,3072]{1,0:T(8,128)(2,1)S(1)}, u32[]{:S(2)}, u32[]{:S(2)}) collective-permute-start(bf16[80,3072]{1,0:T(8,128)(2,1)S(1)} %get-tuple-element.137), channel_id=1, source_target_pairs={{0,8},{8,16},{1,9},{9,17},{2,10},{10,18},{3,11},{11,19},{4,12},{12... | collective-permute-start | bytes 1474568 | tf_op jit(solution)/shard_map/ppermute | solution.py:631
  42.9 12.1 %collective-permute-start.2 = (bf16[80,3072]{1,0:T(8,128)(2,1)S(1)}, bf16[80,3072]{1,0:T(8,128)(2,1)S(1)}, u32[]{:S(2)}, u32[]{:S(2)}) collective-permute-start(bf16[80,3072]{1,0:T(8,128)(2,1)S(1)} %get-tuple-element.152), channel_id=1, source_target_pairs={{0,8},{8,16},{16,24},{1,9},{9,17},{17,25},{2,10},{10,18},{18,26},{... | collective-permute-start | bytes 1474568 | tf_op jit(solution)/shard_map/ppermute | solution.py:631
  59.3 9.8 %collective-permute-start.3 = (bf16[80,3072]{1,0:T(8,128)(2,1)S(1)}, bf16[80,3072]{1,0:T(8,128)(2,1)S(1)}, u32[]{:S(2)}, u32[]{:S(2)}) collective-permute-start(bf16[80,3072]{1,0:T(8,128)(2,1)S(1)} %get-tuple-element.168), channel_id=1, source_target_pairs={{8,16},{16,24},{9,17},{17,25},{10,18},{18,26},{11,19},{19,27},{12,... | collective-permute-start | bytes 1474568 | tf_op jit(solution)/shard_map/ppermute | solution.py:631
  61.8 8.0 %collective-permute-start.14 = (bf16[80,3072]{1,0:T(8,128)(2,1)S(1)}, bf16[80,3072]{1,0:T(8,128)(2,1)S(1)}, u32[]{:S(2)}, u32[]{:S(2)}) collective-permute-start(bf16[80,3072]{1,0:T(8,128)(2,1)S(1)} %get-tuple-element.201), channel_id=1, source_target_pairs={{24,16},{25,17},{26,18},{27,19},{28,20},{29,21},{30,22},{31,23}} | collective-permute-start | bytes 1474568 | tf_op jit(solution)/shard_map/ppermute | solution.py:639
  62.5 7.3 %collective-permute-start.11 = (bf16[80,768]{1,0:T(8,128)(2,1)S(1)}, bf16[80,768]{1,0:T(8,128)(2,1)S(1)}, u32[]{:S(2)}, u32[]{:S(2)}) collective-permute-start(bf16[80,768]{1,0:T(8,128)(2,1)S(1)} %get-tuple-element.192), channel_id=1, source_target_pairs={{0,2},{1,3},{2,0},{3,1},{4,6},{5,7},{6,4},{7,5},{8,10},{9,11},{10,... | collective-permute-start | bytes 368648 | tf_op jit(solution)/shard_map/ppermute | solution.py:62
  63.8 6.0 %collective-permute-start.12 = (bf16[80,768]{1,0:T(8,128)(2,1)S(1)}, bf16[80,768]{1,0:T(8,128)(2,1)S(1)}, u32[]{:S(2)}, u32[]{:S(2)}) collective-permute-start(bf16[80,768]{1,0:T(8,128)(2,1)S(1)} %get-tuple-element.193), channel_id=1, source_target_pairs={{0,4},{1,5},{2,6},{3,7},{4,0},{5,1},{6,2},{7,3},{8,12},{9,13},{10,... | collective-permute-start | bytes 368648 | tf_op jit(solution)/shard_map/ppermute | solution.py:62
  65.1 4.8 %collective-permute-start.13 = (bf16[80,768]{1,0:T(8,128)(2,1)S(1)}, bf16[80,768]{1,0:T(8,128)(2,1)S(1)}, u32[]{:S(2)}, u32[]{:S(2)}) collective-permute-start(bf16[80,768]{1,0:T(8,128)(2,1)S(1)} %get-tuple-element.194), channel_id=1, source_target_pairs={{0,6},{1,7},{2,4},{3,5},{4,2},{5,3},{6,0},{7,1},{8,14},{9,15},{10,... | collective-permute-start | bytes 368648 | tf_op jit(solution)/shard_map/ppermute | solution.py:62
  69.2 5.0 %collective-permute-start.4 = (bf16[80,3072]{1,0:T(8,128)(2,1)S(1)}, bf16[80,3072]{1,0:T(8,128)(2,1)S(1)}, u32[]{:S(2)}, u32[]{:S(2)}) collective-permute-start(bf16[80,3072]{1,0:T(8,128)(2,1)S(1)} %get-tuple-element.179), channel_id=1, source_target_pairs={{16,24},{17,25},{18,26},{19,27},{20,28},{21,29},{22,30},{23,31}} | collective-permute-start | bytes 1474568 | tf_op jit(solution)/shard_map/ppermute | solution.py:631
  70.1 21.6 %collective-permute-start.15 = (bf16[80,3072]{1,0:T(8,128)(2,1)S(1)}, bf16[80,3072]{1,0:T(8,128)(2,1)S(1)}, u32[]{:S(2)}, u32[]{:S(2)}) collective-permute-start(bf16[80,3072]{1,0:T(8,128)(2,1)S(1)} %get-tuple-element.207), channel_id=1, source_target_pairs={{16,8},{24,16},{17,9},{25,17},{18,10},{26,18},{19,11},{27,19},{20,... | collective-permute-start | bytes 1474568 | tf_op jit(solution)/shard_map/ppermute | solution.py:639
  73.9 4.6 %collective-permute-start.10 = (bf16[80,768]{1,0:T(8,128)(2,1)S(1)}, bf16[80,768]{1,0:T(8,128)(2,1)S(1)}, u32[]{:S(2)}, u32[]{:S(2)}) collective-permute-start(bf16[80,768]{1,0:T(8,128)(2,1)S(1)} %get-tuple-element.191), channel_id=1, source_target_pairs={{0,6},{1,7},{2,4},{3,5},{4,2},{5,3},{6,0},{7,1},{8,14},{9,15},{10,... | collective-permute-start | bytes 368648 | tf_op jit(solution)/shard_map/ppermute | solution.py:62
  95.6 9.9 %collective-permute-start.16 = (bf16[80,3072]{1,0:T(8,128)(2,1)S(1)}, bf16[80,3072]{1,0:T(8,128)(2,1)S(1)}, u32[]{:S(2)}, u32[]{:S(2)}) collective-permute-start(bf16[80,3072]{1,0:T(8,128)(2,1)S(1)} %get-tuple-element.212), channel_id=1, source_target_pairs={{8,0},{16,8},{24,16},{9,1},{17,9},{25,17},{10,2},{18,10},{26,18},{... | collective-permute-start | bytes 1474568 | tf_op jit(solution)/shard_map/ppermute | solution.py:639
  109.4 7.7 %collective-permute-start.21 = (bf16[80,3072]{1,0:T(8,128)(2,1)S(1)}, bf16[80,3072]{1,0:T(8,128)(2,1)S(1)}, u32[]{:S(2)}, u32[]{:S(2)}) collective-permute-start(bf16[80,3072]{1,0:T(8,128)(2,1)S(1)} %get-tuple-element.218.refs_0_), channel_id=1, source_target_pairs={{0,2},{1,3},{2,0},{3,1},{4,6},{5,7},{6,4},{7,5},{8,10},{9,11},{10,... | collective-permute-start | bytes 1474568 | tf_op jit(solution)/shard_map/ppermute | solution.py:62
  110.7 9.9 %collective-permute-start.17 = (bf16[80,3072]{1,0:T(8,128)(2,1)S(1)}, bf16[80,3072]{1,0:T(8,128)(2,1)S(1)}, u32[]{:S(2)}, u32[]{:S(2)}) collective-permute-start(bf16[80,3072]{1,0:T(8,128)(2,1)S(1)} %get-tuple-element.216), channel_id=1, source_target_pairs={{8,0},{16,8},{9,1},{17,9},{10,2},{18,10},{11,3},{19,11},{12,4},{20... | collective-permute-start | bytes 1474568 | tf_op jit(solution)/shard_map/ppermute | solution.py:639
  112.6 18.0 %collective-permute-start.22 = (bf16[80,3072]{1,0:T(8,128)(2,1)S(1)}, bf16[80,3072]{1,0:T(8,128)(2,1)S(1)}, u32[]{:S(2)}, u32[]{:S(2)}) collective-permute-start(bf16[80,3072]{1,0:T(8,128)(2,1)S(1)} %get-tuple-element.218.refs_0_), channel_id=1, source_target_pairs={{0,4},{1,5},{2,6},{3,7},{4,0},{5,1},{6,2},{7,3},{8,12},{9,13},{10,... | collective-permute-start | bytes 1474568 | tf_op jit(solution)/shard_map/ppermute | solution.py:62
  117.2 13.4 %collective-permute-start.23 = (bf16[80,3072]{1,0:T(8,128)(2,1)S(1)}, bf16[80,3072]{1,0:T(8,128)(2,1)S(1)}, u32[]{:S(2)}, u32[]{:S(2)}) collective-permute-start(bf16[80,3072]{1,0:T(8,128)(2,1)S(1)} %collective-permute-done.21.refs_1_), channel_id=1, source_target_pairs={{0,4},{1,5},{2,6},{3,7},{4,0},{5,1},{6,2},{7,3},{8,12},{9,13},{10,... | collective-permute-start | bytes 1474568 | tf_op jit(solution)/shard_map/ppermute | solution.py:62
  124.5 10.1 %collective-permute-start.24 = (bf16[80,3072]{1,0:T(8,128)(2,1)S(1)}, bf16[80,3072]{1,0:T(8,128)(2,1)S(1)}, u32[]{:S(2)}, u32[]{:S(2)}) collective-permute-start(bf16[80,3072]{1,0:T(8,128)(2,1)S(1)} %get-tuple-element.226), channel_id=1, source_target_pairs={{8,0},{9,1},{10,2},{11,3},{12,4},{13,5},{14,6},{15,7}} | collective-permute-start | bytes 1474568 | tf_op jit(solution)/shard_map/ppermute | solution.py:639
  125.8 8.8 %collective-permute-start.20 = (bf16[80,3072]{1,0:T(8,128)(2,1)S(1)}, bf16[80,3072]{1,0:T(8,128)(2,1)S(1)}, u32[]{:S(2)}, u32[]{:S(2)}) collective-permute-start(bf16[80,3072]{1,0:T(8,128)(2,1)S(1)} %get-tuple-element.217.refs_0_), channel_id=1, source_target_pairs={{0,2},{1,3},{2,0},{3,1},{4,6},{5,7},{6,4},{7,5},{8,10},{9,11},{10,... | collective-permute-start | bytes 1474568 | tf_op jit(solution)/shard_map/ppermute | solution.py:62
  129.3 13.4 %collective-permute-start.18 = (bf16[80,3072]{1,0:T(8,128)(2,1)S(1)}, bf16[80,3072]{1,0:T(8,128)(2,1)S(1)}, u32[]{:S(2)}, u32[]{:S(2)}) collective-permute-start(bf16[80,3072]{1,0:T(8,128)(2,1)S(1)} %get-tuple-element.217.refs_0_), channel_id=1, source_target_pairs={{0,4},{1,5},{2,6},{3,7},{4,0},{5,1},{6,2},{7,3},{8,12},{9,13},{10,... | collective-permute-start | bytes 1474568 | tf_op jit(solution)/shard_map/ppermute | solution.py:62
  134.9 11.4 %collective-permute-start.25 = (bf16[80,3072]{1,0:T(8,128)(2,1)S(1)}, bf16[80,3072]{1,0:T(8,128)(2,1)S(1)}, u32[]{:S(2)}, u32[]{:S(2)}) collective-permute-start(bf16[80,3072]{1,0:T(8,128)(2,1)S(1)} %get-tuple-element.227.refs_0_), channel_id=1, source_target_pairs={{0,2},{1,3},{2,0},{3,1},{4,6},{5,7},{6,4},{7,5},{8,10},{9,11},{10,... | collective-permute-start | bytes 1474568 | tf_op jit(solution)/shard_map/ppermute | solution.py:62
  136.2 17.0 %collective-permute-start.27 = (bf16[80,3072]{1,0:T(8,128)(2,1)S(1)}, bf16[80,3072]{1,0:T(8,128)(2,1)S(1)}, u32[]{:S(2)}, u32[]{:S(2)}) collective-permute-start(bf16[80,3072]{1,0:T(8,128)(2,1)S(1)} %get-tuple-element.227.refs_0_), channel_id=1, source_target_pairs={{0,4},{1,5},{2,6},{3,7},{4,0},{5,1},{6,2},{7,3},{8,12},{9,13},{10,... | collective-permute-start | bytes 1474568 | tf_op jit(solution)/shard_map/ppermute | solution.py:62
  142.7 13.3 %collective-permute-start.19 = (bf16[80,3072]{1,0:T(8,128)(2,1)S(1)}, bf16[80,3072]{1,0:T(8,128)(2,1)S(1)}, u32[]{:S(2)}, u32[]{:S(2)}) collective-permute-start(bf16[80,3072]{1,0:T(8,128)(2,1)S(1)} %collective-permute-done.18.refs_2_), channel_id=1, source_target_pairs={{0,2},{1,3},{2,0},{3,1},{4,6},{5,7},{6,4},{7,5},{8,10},{9,11},{10,... | collective-permute-start | bytes 1474568 | tf_op jit(solution)/shard_map/ppermute | solution.py:62
  146.3 17.4 %collective-permute-start.26 = (bf16[80,3072]{1,0:T(8,128)(2,1)S(1)}, bf16[80,3072]{1,0:T(8,128)(2,1)S(1)}, u32[]{:S(2)}, u32[]{:S(2)}) collective-permute-start(bf16[80,3072]{1,0:T(8,128)(2,1)S(1)} %collective-permute-done.25.refs_1_), channel_id=1, source_target_pairs={{0,4},{1,5},{2,6},{3,7},{4,0},{5,1},{6,2},{7,3},{8,12},{9,13},{10,... | collective-permute-start | bytes 1474568 | tf_op jit(solution)/shard_map/ppermute | solution.py:62
  165.1 7.8 %collective-permute-start.29 = (bf16[384,2048]{1,0:T(8,128)(2,1)S(1)}, bf16[384,2048]{1,0:T(8,128)(2,1)S(1)}, u32[]{:S(2)}, u32[]{:S(2)}) collective-permute-start(bf16[384,2048]{1,0:T(8,128)(2,1)S(1)} %get-tuple-element.242), channel_id=1, source_target_pairs={{0,1},{1,0},{2,3},{3,2},{4,5},{5,4},{6,7},{7,6},{8,9},{9,8},{10,11... | collective-permute-start | bytes 4718600 | tf_op jit(solution)/shard_map/ppermute | solution.py:62
  (8 other events, 35.2 us)
